TPU v7x, 32 devices: a whole 2x2x4 slice. The times are simulated.
32 devices in a mesh: group: 1, chan: 32 (over z, y, x, core).
Axes of the slice: x: 2, y: 2, z: 4, core: 2. Of those that a mesh axis runs over, the one named last changes fastest.
Arguments:
- records: bfloat16 [8, 128, 16384], P('group', None, 'chan'), may hold values from -6 to 6
- valid_flags: int32 [8, 128], P('group', 'chan'), may hold values 0 or 1
- source_ids: int32 [64], P('group'), may hold values from 0 to 127, as said below
Outputs:
- correlations: float32 [64, 128, 1001], P('group', 'chan')
Inputs may be any that keep to these rules, and one draw needn't show every extreme that they name: `source_ids`: 64 distinct channel indices.
All inputs are finite; a program needn't handle non-finite values. No bound on the sum of `valid_flags` on one device may be relied on, other than what follows from the above.
Results may differ from a plain program's by a relative error of at most 0.00035.
The roundings to bfloat16 on the way count: a program that leaves them out, or rounds other values in their place, can miss the bound.
Values may be sent and summed in bfloat16 or wider, within the bound.
No kernel may reach another device: no remote copies, remote signals or barrier semaphores. Data moves between devices by JAX's collectives and lax.ppermute only.
A program may use at most 64 MiB of HBM per device.

v0:
```python
import functools
import math

import jax
import jax.numpy as jnp
import ml_dtypes
import numpy as np
from jax import lax
from jax.experimental import pallas as pl
from jax.experimental.pallas import tpu as pltpu
from jax.sharding import PartitionSpec as P

BAND = 600
SOURCES = 64
HALF_LAG = 500

lowest_bin = 8
floor_share = 0.05
epsilon = 1e-06

PART = 640
WIDTH = 2 * PART
LAGS = 2 * HALF_LAG + 1
SHARES = 2
FLAG_TILE = BAND // 128 * 128
FLAG_LANE = BAND - FLAG_TILE


def angles(phase, samples):
    step = np.float32(2.0 * math.pi / samples)
    return (phase.astype(np.float32) * step).astype(np.float64)


def cos_sin(samples):
    angle = angles(np.arange(samples), samples)
    return np.cos(angle).astype(np.float32), (-np.sin(angle)).astype(np.float32)


def lane_tiles(table):
    tiled = table.reshape(*table.shape[:-1], -1, 128)
    return np.ascontiguousarray(np.moveaxis(tiled, -2, -3))


@functools.lru_cache(maxsize=None)
def forward_table(samples):
    cosine, sine = (part.astype(ml_dtypes.bfloat16) for part in cos_sin(samples))
    bins = lowest_bin + np.arange(BAND)
    phase = np.arange(samples)[:, None] * bins[None, :] % samples
    table = np.zeros((samples, WIDTH), ml_dtypes.bfloat16)
    table[:, :BAND] = cosine[phase]
    table[:, PART : PART + BAND] = sine[phase]
    return lane_tiles(table.T)


@functools.lru_cache(maxsize=None)
def inverse_table(samples):
    factor = np.float32(1.0 / math.sqrt(BAND))
    cosine, sine = ((part * factor).astype(ml_dtypes.bfloat16) for part in cos_sin(samples))
    bins = lowest_bin + np.arange(BAND)
    shifts = np.arange(LAGS) - HALF_LAG
    phase = bins[:, None] * shifts[None, :] % samples
    table = np.zeros((WIDTH, -(-LAGS // 128) * 128), ml_dtypes.bfloat16)
    table[:BAND, :LAGS] = cosine[phase]
    table[PART : PART + BAND, :LAGS] = sine[phase]
    return lane_tiles(table)


def transform_kernel(half_ref, records_ref, table_ref, out_ref, total_ref):
    step = pl.program_id(0)

    @pl.when(step == 0)
    def _():
        total_ref[...] = jnp.zeros_like(total_ref)

    tiles = jnp.concatenate([table_ref[tile] for tile in range(table_ref.shape[0])], axis=1)
    records = jnp.concatenate([records_ref[i] for i in range(records_ref.shape[0])], axis=1)
    total_ref[...] += lax.dot_general(
        tiles, records, (((1,), (1,)), ((), ())), preferred_element_type=jnp.float32
    )

    @pl.when(step == pl.num_programs(0) - 1)
    def _():
        out_ref[...] = total_ref[...].T


def transform(half, records, table):
    senders, rows, span = records.shape
    depth = senders * span
    block = max(span, min(1024, depth))
    steps = depth // block
    return pl.pallas_call(
        transform_kernel,
        grid_spec=pltpu.PrefetchScalarGridSpec(
            num_scalar_prefetch=1,
            grid=(steps,),
            in_specs=[
                pl.BlockSpec((block // span, rows, span), lambda k, half: (k, 0, 0)),
                pl.BlockSpec((block // 128, WIDTH, 128), lambda k, half: (half[0] * steps + k, 0, 0)),
            ],
            out_specs=pl.BlockSpec((rows, WIDTH), lambda k, half: (0, 0)),
            scratch_shapes=[pltpu.VMEM((WIDTH, rows), jnp.float32)],
        ),
        out_shape=jax.ShapeDtypeStruct((rows, WIDTH), jnp.float32),
        compiler_params=pltpu.CompilerParams(vmem_limit_bytes=24 * 2**20),
        cost_estimate=pl.CostEstimate(
            flops=2 * rows * depth * WIDTH,
            bytes_accessed=2 * depth * WIDTH,
            transcendentals=0,
        ),
        name="transform",
    )(half, records, table)


def whiten_kernel(flags_ref, *rest):
    parts, white_ref = rest[:-1], rest[-1]
    total = parts[0][...]
    for part in parts[1:]:
        total += part[...]
    real_part, imag_part = total[:, :PART], total[:, PART:]
    power = real_part * real_part + imag_part * imag_part
    level = jnp.sum(power, axis=1, keepdims=True) * (1.0 / BAND)
    factor = lax.rsqrt(power + floor_share * level + epsilon)
    white_ref[:, :PART] = (real_part * factor).astype(jnp.bfloat16)
    white_ref[:, PART:] = (imag_part * factor).astype(jnp.bfloat16)
    rows = total.shape[0]
    lane = lax.broadcasted_iota(jnp.int32, (rows, 128), 1)
    held = (lane >= FLAG_LANE) & (lane < FLAG_LANE + flags_ref.shape[1])
    tile = (real_part * factor)[:, FLAG_TILE : FLAG_TILE + 128]
    flags = jnp.concatenate(
        [
            jnp.zeros((1, FLAG_LANE), jnp.float32),
            flags_ref[...],
            jnp.zeros((1, 128 - FLAG_LANE - flags_ref.shape[1]), jnp.float32),
        ],
        axis=1,
    )
    white_ref[:, FLAG_TILE : FLAG_TILE + 128] = jnp.where(held, flags, tile).astype(jnp.bfloat16)


def whiten(flags, parts):
    return pl.pallas_call(
        whiten_kernel,
        out_shape=jax.ShapeDtypeStruct(parts[0].shape, jnp.bfloat16),
        compiler_params=pltpu.CompilerParams(vmem_limit_bytes=16 * 2**20),
        name="whiten",
    )(flags, *parts)


def correlate_kernel(segments, channels, shares, place_ref, flags_ref, ids_ref, table_ref, *rest):
    blocks, rest = rest[:-7], rest[-7:]
    out_ref, held_ref, inverse_ref, panel_ref, receivers_ref, stacked_ref, sems = rest
    far, near = held_ref.shape[0], held_ref.shape[1]
    rows = held_ref.shape[3]
    copies = []
    for index, block in enumerate(blocks):
        copies.append(
            pltpu.make_async_copy(block, held_ref.at[:, index // 2, index % 2], sems.at[index])
        )
        copies[-1].start()
    fetch = pltpu.make_async_copy(table_ref, inverse_ref, sems.at[len(blocks)])
    fetch.start()
    devices = far * near * 2
    members = devices // shares
    ch_local = channels // devices
    place = place_ref[0]
    ids = ids_ref[...]
    sources = ids.shape[0]
    for copy in copies:
        copy.wait()

    tails = held_ref[:, :, :, :, FLAG_TILE : FLAG_TILE + 128].reshape(devices * rows, 128)
    column = lax.broadcasted_iota(jnp.int32, (sources, devices * rows), 1)
    choice = (column == ((ids // ch_local) ^ place) * rows).astype(jnp.bfloat16)
    tail = jnp.dot(choice, tails, preferred_element_type=jnp.float32)
    lane = lax.broadcasted_iota(jnp.int32, (sources, 128), 1)

    channel = lax.broadcasted_iota(jnp.int32, (sources, channels), 1)
    pick_sources = (channel == ids).astype(jnp.bfloat16)
    line = lax.broadcasted_iota(jnp.int32, (16, channels), 0)
    channel = lax.broadcasted_iota(jnp.int32, (16, channels), 1)
    pick_own = ((channel == place * ch_local + line) & (line < ch_local)).astype(jnp.bfloat16)
    pick = jnp.concatenate([pick_sources, pick_own], axis=0)

    counts = [jnp.zeros((sources, 1), jnp.float32) for _ in range(ch_local)]
    for g in range(segments):
        parts = []
        for first in range(0, channels, rows):
            block = (g * channels + first) // rows
            index = place ^ (block % shares * members + block // shares)
            parts.append(held_ref[index // (2 * near), index // 2 % near, index % 2])
        segment = jnp.concatenate(parts, axis=0)
        picked = jnp.dot(pick, segment, preferred_element_type=jnp.float32)
        mine = lane == FLAG_LANE + g * ch_local + ids % ch_local
        weight = jnp.sum(jnp.where(mine, tail, 0.0), axis=1, keepdims=True)
        panel_ref[g] = picked[:sources] * weight
        receivers_ref[g] = picked[sources:]
        for c in range(ch_local):
            counts[c] += weight * flags_ref[g, c]

    for c in range(ch_local):
        share = 1.0 / jnp.maximum(counts[c], 1.0)
        lines = slice(c * sources, (c + 1) * sources)
        for start in range(0, PART, 128):
            re = slice(start, start + 128)
            im = slice(PART + start, PART + start + 128)
            real_sum = jnp.zeros((sources, 128), jnp.float32)
            imag_sum = jnp.zeros((sources, 128), jnp.float32)
            for g in range(segments):
                rec_real = receivers_ref[g, c : c + 1, re] * flags_ref[g, c]
                rec_imag = receivers_ref[g, c : c + 1, im] * flags_ref[g, c]
                src_real, src_imag = panel_ref[g, :, re], panel_ref[g, :, im]
                real_sum += src_real * rec_real + src_imag * rec_imag
                imag_sum += src_imag * rec_real - src_real * rec_imag
            stacked_ref[lines, re] = (real_sum * share).astype(jnp.bfloat16)
            stacked_ref[lines, im] = (imag_sum * share).astype(jnp.bfloat16)
    fetch.wait()
    inverse = jnp.concatenate([inverse_ref[tile] for tile in range(inverse_ref.shape[0])], axis=1)
    lags = jnp.dot(stacked_ref[...], inverse, preferred_element_type=jnp.float32)
    for c in range(ch_local):
        out_ref[:, c, :] = lags[c * sources : (c + 1) * sources, :LAGS]


def correlate(place, weights, source_ids, inverse, blocks, segments, channels, shares):
    far, rows, _ = blocks[0].shape
    near = len(blocks) // 2
    devices = far * near * 2
    ch_local = channels // devices
    sources = source_ids.shape[0]
    smem = pl.BlockSpec(memory_space=pltpu.SMEM)
    vmem = pl.BlockSpec(memory_space=pltpu.VMEM)
    anywhere = pl.BlockSpec(memory_space=pl.ANY)
    return pl.pallas_call(
        functools.partial(correlate_kernel, segments, channels, shares),
        in_specs=[smem, smem, vmem, pl.BlockSpec(memory_space=pltpu.HBM)] + [anywhere] * len(blocks),
        out_specs=vmem,
        out_shape=jax.ShapeDtypeStruct((sources, ch_local, LAGS), jnp.float32),
        scratch_shapes=[
            pltpu.VMEM((far, near, 2, rows, WIDTH), jnp.bfloat16),
            pltpu.VMEM(inverse.shape, jnp.bfloat16),
            pltpu.VMEM((segments, sources, WIDTH), jnp.float32),
            pltpu.VMEM((segments, 16, WIDTH), jnp.float32),
            pltpu.VMEM((ch_local * sources, WIDTH), jnp.bfloat16),
            pltpu.SemaphoreType.DMA((len(blocks) + 1,)),
        ],
        compiler_params=pltpu.CompilerParams(vmem_limit_bytes=40 * 2**20),
        name="correlate",
    )(place, weights, source_ids.reshape(sources, 1), inverse, *blocks)


def per_device(records, valid_flags, source_ids):
    segments, channels, span = records.shape
    devices = lax.axis_size("chan")
    members = devices // SHARES
    samples = span * devices
    place = lax.axis_index("chan")
    weights = valid_flags.astype(jnp.float32)

    def exchange(block, bits):
        return lax.ppermute(block, "chan", [(i, i ^ bits) for i in range(devices)])

    half = place // members
    groups = [list(range(members)), list(range(members, devices))]
    rows = segments * channels // devices
    grouped = records.reshape(members, SHARES, rows, span)
    table = forward_table(samples)

    def partial(owner):
        chosen = lax.dynamic_index_in_dim(grouped, owner, 1, keepdims=False)
        regrouped = lax.all_to_all(
            chosen, "chan", split_axis=0, concat_axis=0, axis_index_groups=groups, tiled=True
        )
        return transform(half.reshape(1), regrouped, table)

    received = exchange(partial(1 - half), members)
    white = whiten(weights.reshape(1, -1), [partial(half), received])

    far = devices // 8
    line = jnp.stack([white] + [exchange(white, 8 * k) for k in range(1, far)])
    plane = [line] + [exchange(line, 2 * k) for k in range(1, 4)]
    blocks = [b for block in plane for b in (block, exchange(block, 1))]
    return correlate(
        place.reshape(1),
        weights,
        source_ids,
        inverse_table(samples),
        blocks,
        segments,
        channels,
        SHARES,
    )


def solution(mesh):
    return jax.shard_map(
        per_device,
        mesh=mesh,
        in_specs=(P("group", None, "chan"), P("group", "chan"), P("group")),
        out_specs=P("group", "chan", None),
        check_vma=False,
    )
```

profile of v0, /device:TPU:0, one launch (start us, length us, event | category | flops | bytes accessed | tf_op | source)
XLA Modules:
  0.0 87.5 jit_solution(18020144328188647508)
XLA Ops:
  0.0 2.1 %dynamic-slice_bitcast_fusion = (bf16[16,32,512]{2,1,0:T(8,128)(2,1)S(1)}, bf16[16,32,512]{2,1,0:T(8,128)(2,1)}) fusion(bf16[16,2,32,512]{3,2,1,0:T(8,128)(2,1)} %bitcast.17, s32[]{:T(128)S(6)} %select_n.14, s32[]{:T(128)S(6)} %select_n.13), kind=kLoop, calls=%fused_computation | loop fusion | bytes 2097160 | tf_op jit(solution)/shard_map/jit(dynamic_index_in_dim)/squeeze | solution.py:268
  2.1 16.7 %all_to_all.10.records_ref = bf16[16,32,512]{2,1,0:T(8,128)(2,1)} all-to-all(bf16[16,32,512]{2,1,0:T(8,128)(2,1)S(1)} %get-tuple-element.5), channel_id=1, replica_groups={{0,1,2,3,4,5,6,7,8,9,10,11,12,13,14,15},{16,17,18,19,20,21,22,23,24,25,..., dimensions={0} | all-to-all | bytes 1048576 | tf_op jit(solution)/shard_map/all_to_all | solution.py:269
  18.8 3.6 %all-to-all-start = ((bf16[16,32,512]{2,1,0:T(8,128)(2,1)}), bf16[16,32,512]{2,1,0:T(8,128)(2,1)S(1)}, u32[]{:S(2)}, u32[]{:S(2)}) async-start(bf16[16,32,512]{2,1,0:T(8,128)(2,1)} %get-tuple-element.6), calls=%async_computation | async-start | bytes 1048576 | tf_op jit(solution)/shard_map/all_to_all | solution.py:269
  22.4 1.0 %copy-done.1 = bf16[16,32,512]{2,1,0:T(8,128)(2,1)S(1)} copy-done((bf16[16,32,512]{2,1,0:T(8,128)(2,1)S(1)}, bf16[16,32,512]{2,1,0:T(8,128)(2,1)}, u32[]{:S(2)}) %copy-start.1) | copy-done | bytes 524312
  23.5 12.0 %transform.3 = f32[32,1280]{1,0:T(8,128)S(1)} custom-call(s32[1]{0:T(128)} %bitcast.2.half_ref, bf16[16,32,512]{2,1,0:T(8,128)(2,1)S(1)} %copy-done.1, bf16[128,1280,128]{2,1,0:T(8,128)(2,1)} %constant.34.clone.table_ref), custom_call_target="tpu_custom_call" | custom-call | flops 671088640 | bytes 20971520 | tf_op jit(solution)/shard_map/transform/pallas_call | solution.py:91
  35.5 2.7 %collective-permute-start = (f32[32,1280]{1,0:T(8,128)S(1)}, f32[32,1280]{1,0:T(8,128)S(1)}, u32[]{:S(2)}, u32[]{:S(2)}) collective-permute-start(f32[32,1280]{1,0:T(8,128)S(1)} %transform.3), channel_id=1, source_target_pairs={{0,16},{1,17},{2,18},{3,19},{4,20},{5,21},{6,22},{7,23},{8,24},{9,... | collective-permute-start | bytes 491528 | tf_op jit(solution)/shard_map/ppermute | solution.py:259
  38.2 0.1 reshape.18.flags_ref
  38.3 11.9 %transform.2.rest_0_ = f32[32,1280]{1,0:T(8,128)S(1)} custom-call(s32[1]{0:T(128)} %bitcast.2.half_ref, bf16[16,32,512]{2,1,0:T(8,128)(2,1)S(1)} %all-to-all-done.records_ref, bf16[128,1280,128]{2,1,0:T(8,128)(2,1)} %constant.34.clone.table_ref), custom_call_target="tpu_custom_call" | custom-call | flops 671088640 | bytes 20971520 | tf_op jit(solution)/shard_map/transform/pallas_call | solution.py:91
  50.2 0.1 whiten.1
  50.4 1.7 %collective-permute-start.3 = (bf16[32,1280]{1,0:T(8,128)(2,1)S(1)}, bf16[32,1280]{1,0:T(8,128)(2,1)S(1)}, u32[]{:S(2)}, u32[]{:S(2)}) collective-permute-start(bf16[32,1280]{1,0:T(8,128)(2,1)S(1)} %whiten.1), channel_id=1, source_target_pairs={{0,24},{1,25},{2,26},{3,27},{4,28},{5,29},{6,30},{7,31},{8,16},{9,... | collective-permute-start | bytes 245768 | tf_op jit(solution)/shard_map/ppermute | solution.py:259
  52.0 1.7 %collective-permute-start.2 = (bf16[32,1280]{1,0:T(8,128)(2,1)S(1)}, bf16[32,1280]{1,0:T(8,128)(2,1)S(1)}, u32[]{:S(2)}, u32[]{:S(2)}) collective-permute-start(bf16[32,1280]{1,0:T(8,128)(2,1)S(1)} %whiten.1), channel_id=1, source_target_pairs={{0,16},{1,17},{2,18},{3,19},{4,20},{5,21},{6,22},{7,23},{8,24},{9,... | collective-permute-start | bytes 245768 | tf_op jit(solution)/shard_map/ppermute | solution.py:259
  53.7 1.1 %collective-permute-start.1 = (bf16[32,1280]{1,0:T(8,128)(2,1)S(1)}, bf16[32,1280]{1,0:T(8,128)(2,1)S(1)}, u32[]{:S(2)}, u32[]{:S(2)}) collective-permute-start(bf16[32,1280]{1,0:T(8,128)(2,1)S(1)} %whiten.1), channel_id=1, source_target_pairs={{0,8},{1,9},{2,10},{3,11},{4,12},{5,13},{6,14},{7,15},{8,0},{9,1},... | collective-permute-start | bytes 245768 | tf_op jit(solution)/shard_map/ppermute | solution.py:259
  54.8 2.8 %collective-permute-done.3 = bf16[32,1280]{1,0:T(8,128)(2,1)S(1)} collective-permute-done((bf16[32,1280]{1,0:T(8,128)(2,1)S(1)}, bf16[32,1280]{1,0:T(8,128)(2,1)S(1)}, u32[]{:S(2)}, u32[]{:S(2)}) %collective-permute-start.3) | collective-permute-done | bytes 81952 | tf_op jit(solution)/shard_map/ppermute | solution.py:259
  57.6 3.6 %collective-permute-done.2 = bf16[32,1280]{1,0:T(8,128)(2,1)S(1)} collective-permute-done((bf16[32,1280]{1,0:T(8,128)(2,1)S(1)}, bf16[32,1280]{1,0:T(8,128)(2,1)S(1)}, u32[]{:S(2)}, u32[]{:S(2)}) %collective-permute-start.2) | collective-permute-done | bytes 81952 | tf_op jit(solution)/shard_map/ppermute | solution.py:259
  61.2 2.4 %collective-permute-start.9 = (bf16[4,32,1280]{2,1,0:T(8,128)(2,1)S(1)}, bf16[4,32,1280]{2,1,0:T(8,128)(2,1)S(1)}, u32[]{:S(2)}, u32[]{:S(2)}) collective-permute-start(bf16[4,32,1280]{2,1,0:T(8,128)(2,1)S(1)} %pad_maximum_fusion.rest_0_), channel_id=1, source_target_pairs={{0,6},{1,7},{2,4},{3,5},{4,2},{5,3},{6,0},{7,1},{8,14},{9,15},{10,... | collective-permute-start | bytes 983048 | tf_op jit(solution)/shard_map/ppermute | solution.py:259
  63.7 0.5 collective-permute-start.7
  64.2 0.6 collective-permute-start.5
  64.8 8.1 %collective-permute-done.9.rest_6_ = bf16[4,32,1280]{2,1,0:T(8,128)(2,1)S(1)} collective-permute-done((bf16[4,32,1280]{2,1,0:T(8,128)(2,1)S(1)}, bf16[4,32,1280]{2,1,0:T(8,128)(2,1)S(1)}, u32[]{:S(2)}, u32[]{:S(2)}) %collective-permute-start.9) | collective-permute-done | bytes 327712 | tf_op jit(solution)/shard_map/ppermute | solution.py:259
  72.9 5.4 %collective-permute-done.7.rest_4_ = bf16[4,32,1280]{2,1,0:T(8,128)(2,1)} collective-permute-done((bf16[4,32,1280]{2,1,0:T(8,128)(2,1)S(1)}, bf16[4,32,1280]{2,1,0:T(8,128)(2,1)}, u32[]{:S(2)}, u32[]{:S(2)}) %collective-permute-start.7) | collective-permute-done | bytes 327712 | tf_op jit(solution)/shard_map/ppermute | solution.py:259
  78.3 0.5 collective-permute-start.6
  78.8 0.1 copy.13.ids_ref
  78.9 1.3 %collective-permute-done.8.rest_5_ = bf16[4,32,1280]{2,1,0:T(8,128)(2,1)} collective-permute-done((bf16[4,32,1280]{2,1,0:T(8,128)(2,1)}, bf16[4,32,1280]{2,1,0:T(8,128)(2,1)}, u32[]{:S(2)}, u32[]{:S(2)}) %collective-permute-start.8) | collective-permute-done | bytes 327712 | tf_op jit(solution)/shard_map/ppermute | solution.py:259
  80.3 0.5 collective-permute-done.6.rest_3_
  80.8 6.8 %correlate.1 = f32[64,4,1001]{2,1,0:T(4,128)} custom-call(s32[1]{0:T(128)} %bitcast.place_ref, f32[8,4]{1,0:T(8,128)S(1)} %convert_element_type.3.flags_ref, s32[64,1]{1,0:T(8,128)S(1)} %copy.13.ids_ref, bf16[8,1280,128]{2,1,0:T(8,128)(2,1)S(1)} %copy-done, bf16[4,32,1280]{2,1,0:T(8,128)(2,1)S(1)} %pad_maximum_fusion.rest_0_, ...), custom_call_target="tpu_custom_call" | custom-call | tf_op jit(solution)/shard_map/correlate/pallas_call | solution.py:232
  (19 shorter events, 0.2 us)
Async XLA Ops:
  0.0 38.1 %copy-start.2 = (s32[8,4]{0,1:T(4,128)S(1)}, s32[8,4]{0,1:T(4,128)}, u32[]{:S(2)}) copy-start(s32[8,4]{0,1:T(4,128)} %param.6) | copy-start | bytes 388
  18.8 19.5 %all-to-all-start = ((bf16[16,32,512]{2,1,0:T(8,128)(2,1)}), bf16[16,32,512]{2,1,0:T(8,128)(2,1)S(1)}, u32[]{:S(2)}, u32[]{:S(2)}) async-start(bf16[16,32,512]{2,1,0:T(8,128)(2,1)} %get-tuple-element.6), calls=%async_computation | async-start | bytes 1048576 | tf_op jit(solution)/shard_map/all_to_all | solution.py:269
  22.4 1.0 %copy-start.1 = (bf16[16,32,512]{2,1,0:T(8,128)(2,1)S(1)}, bf16[16,32,512]{2,1,0:T(8,128)(2,1)}, u32[]{:S(2)}) copy-start(bf16[16,32,512]{2,1,0:T(8,128)(2,1)} %all_to_all.10.records_ref) | copy-start | bytes 1572868
  23.5 55.4 %copy-start.3 = (s32[64]{0:T(128)S(1)}, s32[64]{0:T(128)}, u32[]{:S(2)}) copy-start(s32[64]{0:T(128)} %param.7) | copy-start | bytes 772
  23.5 57.3 %copy-start = (bf16[8,1280,128]{2,1,0:T(8,128)(2,1)S(1)}, bf16[8,1280,128]{2,1,0:T(8,128)(2,1)}, u32[]{:S(2)}) copy-start(bf16[8,1280,128]{2,1,0:T(8,128)(2,1)} %constant.35.clone.table_ref) | copy-start | bytes 7864324
  35.5 14.7 %collective-permute-start = (f32[32,1280]{1,0:T(8,128)S(1)}, f32[32,1280]{1,0:T(8,128)S(1)}, u32[]{:S(2)}, u32[]{:S(2)}) collective-permute-start(f32[32,1280]{1,0:T(8,128)S(1)} %transform.3), channel_id=1, source_target_pairs={{0,16},{1,17},{2,18},{3,19},{4,20},{5,21},{6,22},{7,23},{8,24},{9,... | collective-permute-start | bytes 491528 | tf_op jit(solution)/shard_map/ppermute | solution.py:259
  50.4 7.2 %collective-permute-start.3 = (bf16[32,1280]{1,0:T(8,128)(2,1)S(1)}, bf16[32,1280]{1,0:T(8,128)(2,1)S(1)}, u32[]{:S(2)}, u32[]{:S(2)}) collective-permute-start(bf16[32,1280]{1,0:T(8,128)(2,1)S(1)} %whiten.1), channel_id=1, source_target_pairs={{0,24},{1,25},{2,26},{3,27},{4,28},{5,29},{6,30},{7,31},{8,16},{9,... | collective-permute-start | bytes 245768 | tf_op jit(solution)/shard_map/ppermute | solution.py:259
  52.0 9.2 %collective-permute-start.2 = (bf16[32,1280]{1,0:T(8,128)(2,1)S(1)}, bf16[32,1280]{1,0:T(8,128)(2,1)S(1)}, u32[]{:S(2)}, u32[]{:S(2)}) collective-permute-start(bf16[32,1280]{1,0:T(8,128)(2,1)S(1)} %whiten.1), channel_id=1, source_target_pairs={{0,16},{1,17},{2,18},{3,19},{4,20},{5,21},{6,22},{7,23},{8,24},{9,... | collective-permute-start | bytes 245768 | tf_op jit(solution)/shard_map/ppermute | solution.py:259
  53.7 7.5 %collective-permute-start.1 = (bf16[32,1280]{1,0:T(8,128)(2,1)S(1)}, bf16[32,1280]{1,0:T(8,128)(2,1)S(1)}, u32[]{:S(2)}, u32[]{:S(2)}) collective-permute-start(bf16[32,1280]{1,0:T(8,128)(2,1)S(1)} %whiten.1), channel_id=1, source_target_pairs={{0,8},{1,9},{2,10},{3,11},{4,12},{5,13},{6,14},{7,15},{8,0},{9,1},... | collective-permute-start | bytes 245768 | tf_op jit(solution)/shard_map/ppermute | solution.py:259
  61.2 11.7 %collective-permute-start.9 = (bf16[4,32,1280]{2,1,0:T(8,128)(2,1)S(1)}, bf16[4,32,1280]{2,1,0:T(8,128)(2,1)S(1)}, u32[]{:S(2)}, u32[]{:S(2)}) collective-permute-start(bf16[4,32,1280]{2,1,0:T(8,128)(2,1)S(1)} %pad_maximum_fusion.rest_0_), channel_id=1, source_target_pairs={{0,6},{1,7},{2,4},{3,5},{4,2},{5,3},{6,0},{7,1},{8,14},{9,15},{10,... | collective-permute-start | bytes 983048 | tf_op jit(solution)/shard_map/ppermute | solution.py:259
  63.7 14.6 %collective-permute-start.7 = (bf16[4,32,1280]{2,1,0:T(8,128)(2,1)S(1)}, bf16[4,32,1280]{2,1,0:T(8,128)(2,1)}, u32[]{:S(2)}, u32[]{:S(2)}) collective-permute-start(bf16[4,32,1280]{2,1,0:T(8,128)(2,1)S(1)} %pad_maximum_fusion.rest_0_), channel_id=1, source_target_pairs={{0,4},{1,5},{2,6},{3,7},{4,0},{5,1},{6,2},{7,3},{8,12},{9,13},{10,... | collective-permute-start | bytes 983048 | tf_op jit(solution)/shard_map/ppermute | solution.py:259
  64.2 14.1 %collective-permute-start.5 = (bf16[4,32,1280]{2,1,0:T(8,128)(2,1)S(1)}, bf16[4,32,1280]{2,1,0:T(8,128)(2,1)}, u32[]{:S(2)}, u32[]{:S(2)}) collective-permute-start(bf16[4,32,1280]{2,1,0:T(8,128)(2,1)S(1)} %pad_maximum_fusion.rest_0_), channel_id=1, source_target_pairs={{0,2},{1,3},{2,0},{3,1},{4,6},{5,7},{6,4},{7,5},{8,10},{9,11},{10,... | collective-permute-start | bytes 983048 | tf_op jit(solution)/shard_map/ppermute | solution.py:259
  64.8 14.1 %collective-permute-start.4 = (bf16[4,32,1280]{2,1,0:T(8,128)(2,1)S(1)}, bf16[4,32,1280]{2,1,0:T(8,128)(2,1)}, u32[]{:S(2)}, u32[]{:S(2)}) collective-permute-start(bf16[4,32,1280]{2,1,0:T(8,128)(2,1)S(1)} %pad_maximum_fusion.rest_0_), channel_id=1, source_target_pairs={{0,1},{1,0},{2,3},{3,2},{4,5},{5,4},{6,7},{7,6},{8,9},{9,8},{10,11... | collective-permute-start | bytes 983048 | tf_op jit(solution)/shard_map/ppermute | solution.py:259
  72.9 6.0 %collective-permute-start.10 = (bf16[4,32,1280]{2,1,0:T(8,128)(2,1)S(1)}, bf16[4,32,1280]{2,1,0:T(8,128)(2,1)}, u32[]{:S(2)}, u32[]{:S(2)}) collective-permute-start(bf16[4,32,1280]{2,1,0:T(8,128)(2,1)S(1)} %collective-permute-done.9.rest_6_), channel_id=1, source_target_pairs={{0,1},{1,0},{2,3},{3,2},{4,5},{5,4},{6,7},{7,6},{8,9},{9,8},{10,11... | collective-permute-start | bytes 983048 | tf_op jit(solution)/shard_map/ppermute | solution.py:259
  78.3 2.0 %collective-permute-start.8 = (bf16[4,32,1280]{2,1,0:T(8,128)(2,1)}, bf16[4,32,1280]{2,1,0:T(8,128)(2,1)}, u32[]{:S(2)}, u32[]{:S(2)}) collective-permute-start(bf16[4,32,1280]{2,1,0:T(8,128)(2,1)} %collective-permute-done.7.rest_4_), channel_id=1, source_target_pairs={{0,1},{1,0},{2,3},{3,2},{4,5},{5,4},{6,7},{7,6},{8,9},{9,8},{10,11... | collective-permute-start | bytes 983048 | tf_op jit(solution)/shard_map/ppermute | solution.py:259
  78.3 2.4 %collective-permute-start.6 = (bf16[4,32,1280]{2,1,0:T(8,128)(2,1)}, bf16[4,32,1280]{2,1,0:T(8,128)(2,1)}, u32[]{:S(2)}, u32[]{:S(2)}) collective-permute-start(bf16[4,32,1280]{2,1,0:T(8,128)(2,1)} %collective-permute-done.5.rest_2_), channel_id=1, source_target_pairs={{0,1},{1,0},{2,3},{3,2},{4,5},{5,4},{6,7},{7,6},{8,9},{9,8},{10,11... | collective-permute-start | bytes 983048 | tf_op jit(solution)/shard_map/ppermute | solution.py:259
where the time goes:
time: 88.1 us; the launch traced here: 87.5 us
  Pallas kernels  30.8 us (35%)
  waiting for transfers between devices  21.7 us (25%)
  blocking collectives  16.7 us (19%)
  starting transfers between devices  14.8 us (17%)
  local copies, waits for them, and re-layouts  3.4 us (4%)
    pallas_call x2, Pallas kernels, transform(): pl.pallas_call(transform_kernel, grid_spec=pltpu.PrefetchScalarGridSpec(n...  23.9 us
    ppermute x11, waiting for transfers between devices, exchange(): return lax.ppermute(block, 'chan', [(i, i ^ bits) for i in range(devices)])  21.7 us
    all_to_all x1, blocking collectives, partial(): lax.all_to_all(chosen, 'chan', split_axis=0, concat_axis=0, axis_index_gr...  16.7 us
    ppermute x11, starting transfers between devices, exchange(): return lax.ppermute(block, 'chan', [(i, i ^ bits) for i in range(devices)])  11.2 us
    pallas_call x1, Pallas kernels, correlate(): pl.pallas_call(functools.partial(correlate_kernel, segments, channels, sh...  6.76 us
    all_to_all x1, starting transfers between devices, partial(): lax.all_to_all(chosen, 'chan', split_axis=0, concat_axis=0, axis_index_gr...  3.57 us
    squeeze x1, local copies, waits for them, and re-layouts, partial(): chosen = lax.dynamic_index_in_dim(grouped, owner, 1, keepdims=False)  2.1 us
  transfers between devices with their start and end apart: 12, of which 6 were waited for; matrix products, arithmetic and copies ran while one was open for 0% of the time, Pallas kernels for 27%

commit v1 on v0

v1 whole, which is shorter than its diff:
```python
import functools
import math

import jax
import jax.numpy as jnp
import ml_dtypes
import numpy as np
from jax import lax
from jax.experimental import pallas as pl
from jax.experimental.pallas import tpu as pltpu
from jax.sharding import PartitionSpec as P

BAND = 600
SOURCES = 64
HALF_LAG = 500

lowest_bin = 8
floor_share = 0.05
epsilon = 1e-06

PART = 640
WIDTH = 2 * PART
LAGS = 2 * HALF_LAG + 1
LAG_TILES = -(-LAGS // 128)
BLOCK = 512
SHARES = 2
FIRST_TILES = 6
FLAG_TILE = BAND // 128 * 128
FLAG_LANE = BAND - FLAG_TILE


def angles(phase, samples):
    step = np.float32(2.0 * math.pi / samples)
    return (phase.astype(np.float32) * step).astype(np.float64)


def cos_sin(samples):
    angle = angles(np.arange(samples), samples)
    return np.cos(angle).astype(np.float32), (-np.sin(angle)).astype(np.float32)


def lane_tiles(table):
    tiled = table.reshape(*table.shape[:-1], -1, 128)
    return np.ascontiguousarray(np.moveaxis(tiled, -2, -3))


@functools.lru_cache(maxsize=None)
def tables(samples):
    bins = lowest_bin + np.arange(BAND)
    cosine, sine = cos_sin(samples)
    phase = np.arange(samples)[:, None] * bins[None, :] % samples
    forward = np.zeros((samples, WIDTH), ml_dtypes.bfloat16)
    forward[:, :BAND] = cosine.astype(ml_dtypes.bfloat16)[phase]
    forward[:, PART : PART + BAND] = sine.astype(ml_dtypes.bfloat16)[phase]
    factor = np.float32(1.0 / math.sqrt(BAND))
    phase = bins[:, None] * (np.arange(LAGS) - HALF_LAG)[None, :] % samples
    inverse = np.zeros((WIDTH, LAG_TILES * 128), ml_dtypes.bfloat16)
    inverse[:BAND, :LAGS] = (cosine * factor).astype(ml_dtypes.bfloat16)[phase]
    inverse[PART : PART + BAND, :LAGS] = (sine * factor).astype(ml_dtypes.bfloat16)[phase]
    parts = [lane_tiles(forward.reshape(-1, BLOCK, WIDTH)), lane_tiles(inverse)]
    return np.concatenate([part.reshape(-1, 128) for part in parts])


def transform_kernel(first, share_ref, records_ref, table_ref, *rest):
    own_ref, other_ref, tiles_ref, sems = rest
    senders, rows, span = records_ref.shape
    blocks, lines, _ = tiles_ref.shape
    columns = lines // BLOCK
    copies = []
    for index in range(blocks):
        block = share_ref[0] * blocks + index
        start = (block * (WIDTH // 128) + first) * BLOCK
        source = table_ref.at[pl.ds(pl.multiple_of(start, BLOCK), lines)]
        copies.append(pltpu.make_async_copy(source, tiles_ref.at[index], sems.at[index]))
        copies[-1].start()
    total = jnp.zeros((rows, columns * 128), jnp.float32)
    pieces = BLOCK // span
    for index in range(blocks):
        copies[index].wait()
        tiles = [tiles_ref[index, tile * BLOCK : (tile + 1) * BLOCK] for tile in range(columns)]
        records = [records_ref[index * pieces + piece] for piece in range(pieces)]
        total += jnp.dot(
            jnp.concatenate(records, axis=1),
            jnp.concatenate(tiles, axis=1),
            preferred_element_type=jnp.float32,
        )
    low, high = total[: rows // 2], total[rows // 2 :]
    mine = share_ref[0] == 0
    own_ref[...] = jnp.where(mine, low, high)
    other_ref[...] = jnp.where(mine, high, low)


def transform(share, records, table, first, last):
    senders, rows, span = records.shape
    columns = last - first
    depth = senders * span
    blocks = depth // BLOCK
    vmem = pl.BlockSpec(memory_space=pltpu.VMEM)
    shape = jax.ShapeDtypeStruct((rows // 2, columns * 128), jnp.float32)
    return pl.pallas_call(
        functools.partial(transform_kernel, first),
        in_specs=[
            pl.BlockSpec(memory_space=pltpu.SMEM),
            vmem,
            pl.BlockSpec(memory_space=pltpu.HBM),
        ],
        out_specs=[vmem, vmem],
        out_shape=[shape, shape],
        scratch_shapes=[
            pltpu.VMEM((blocks, columns * BLOCK, 128), jnp.bfloat16),
            pltpu.SemaphoreType.DMA((blocks,)),
        ],
        compiler_params=pltpu.CompilerParams(vmem_limit_bytes=32 * 2**20),
        cost_estimate=pl.CostEstimate(
            flops=2 * rows * depth * columns * 128,
            bytes_accessed=2 * depth * columns * 128,
            transcendentals=0,
        ),
        name="transform",
    )(share, records, table)


def whiten_kernel(flags_ref, *rest):
    parts, white_ref = rest[:-1], rest[-1]
    sums = [mine[...] + other[...] for mine, other in zip(parts[::2], parts[1::2])]
    total = jnp.concatenate(sums, axis=1)
    real_part, imag_part = total[:, :PART], total[:, PART:]
    power = real_part * real_part + imag_part * imag_part
    level = jnp.sum(power, axis=1, keepdims=True) * (1.0 / BAND)
    factor = lax.rsqrt(power + floor_share * level + epsilon)
    white_ref[:, :PART] = (real_part * factor).astype(jnp.bfloat16)
    white_ref[:, PART:] = (imag_part * factor).astype(jnp.bfloat16)
    rows = total.shape[0]
    lane = lax.broadcasted_iota(jnp.int32, (rows, 128), 1)
    held = (lane >= FLAG_LANE) & (lane < FLAG_LANE + flags_ref.shape[1])
    tile = (real_part * factor)[:, FLAG_TILE : FLAG_TILE + 128]
    flags = jnp.concatenate(
        [
            jnp.zeros((1, FLAG_LANE), jnp.float32),
            flags_ref[...],
            jnp.zeros((1, 128 - FLAG_LANE - flags_ref.shape[1]), jnp.float32),
        ],
        axis=1,
    )
    white_ref[:, FLAG_TILE : FLAG_TILE + 128] = jnp.where(held, flags, tile).astype(jnp.bfloat16)


def whiten(flags, parts):
    return pl.pallas_call(
        whiten_kernel,
        out_shape=jax.ShapeDtypeStruct((parts[0].shape[0], WIDTH), jnp.bfloat16),
        compiler_params=pltpu.CompilerParams(vmem_limit_bytes=16 * 2**20),
        name="whiten",
    )(flags, *parts)


def correlate_kernel(segments, channels, shares, place_ref, flags_ref, ids_ref, table_ref, *rest):
    blocks, rest = rest[:-7], rest[-7:]
    out_ref, held_ref, inverse_ref, panel_ref, receivers_ref, stacked_ref, sem = rest
    lines = inverse_ref.shape[0]
    fetch = pltpu.make_async_copy(
        table_ref.at[pl.ds(table_ref.shape[0] - lines, lines)], inverse_ref, sem
    )
    fetch.start()
    devices, rows, _ = held_ref.shape
    members = devices // shares
    ch_local = channels // devices
    place = place_ref[0]
    ids = ids_ref[...]
    sources = ids.shape[0]

    def position(device):
        return device % members * shares + device // members

    for index, block in enumerate(blocks):
        for line in range(block.shape[0]):
            held_ref[position(place ^ (line * len(blocks) + index))] = block[line]

    tails = held_ref[:, :, FLAG_TILE : FLAG_TILE + 128].reshape(devices * rows, 128)
    column = lax.broadcasted_iota(jnp.int32, (sources, devices * rows), 1)
    choice = (column == position(ids // ch_local) * rows).astype(jnp.bfloat16)
    tail = jnp.dot(choice, tails, preferred_element_type=jnp.float32)
    lane = lax.broadcasted_iota(jnp.int32, (sources, 128), 1)

    channel = lax.broadcasted_iota(jnp.int32, (sources, channels), 1)
    pick_sources = (channel == ids).astype(jnp.bfloat16)
    line = lax.broadcasted_iota(jnp.int32, (16, channels), 0)
    channel = lax.broadcasted_iota(jnp.int32, (16, channels), 1)
    pick_own = ((channel == place * ch_local + line) & (line < ch_local)).astype(jnp.bfloat16)
    pick = jnp.concatenate([pick_sources, pick_own], axis=0)

    counts = [jnp.zeros((sources, 1), jnp.float32) for _ in range(ch_local)]
    for g in range(segments):
        blocks_per = channels // rows
        segment = held_ref[g * blocks_per : (g + 1) * blocks_per].reshape(channels, WIDTH)
        picked = jnp.dot(pick, segment, preferred_element_type=jnp.float32)
        mine = lane == FLAG_LANE + g * ch_local + ids % ch_local
        weight = jnp.sum(jnp.where(mine, tail, 0.0), axis=1, keepdims=True)
        panel_ref[g] = picked[:sources] * weight
        receivers_ref[g] = picked[sources:]
        for c in range(ch_local):
            counts[c] += weight * flags_ref[g, c]

    for c in range(ch_local):
        share = 1.0 / jnp.maximum(counts[c], 1.0)
        lines = slice(c * sources, (c + 1) * sources)
        for start in range(0, PART, 128):
            re = slice(start, start + 128)
            im = slice(PART + start, PART + start + 128)
            real_sum = jnp.zeros((sources, 128), jnp.float32)
            imag_sum = jnp.zeros((sources, 128), jnp.float32)
            for g in range(segments):
                rec_real = receivers_ref[g, c : c + 1, re] * flags_ref[g, c]
                rec_imag = receivers_ref[g, c : c + 1, im] * flags_ref[g, c]
                src_real, src_imag = panel_ref[g, :, re], panel_ref[g, :, im]
                real_sum += src_real * rec_real + src_imag * rec_imag
                imag_sum += src_imag * rec_real - src_real * rec_imag
            stacked_ref[lines, re] = (real_sum * share).astype(jnp.bfloat16)
            stacked_ref[lines, im] = (imag_sum * share).astype(jnp.bfloat16)
    fetch.wait()
    tiles = [inverse_ref[tile * WIDTH : (tile + 1) * WIDTH] for tile in range(LAG_TILES)]
    inverse = jnp.concatenate(tiles, axis=1)
    lags = jnp.dot(stacked_ref[...], inverse, preferred_element_type=jnp.float32)
    for c in range(ch_local):
        out_ref[:, c, :] = lags[c * sources : (c + 1) * sources, :LAGS]


def correlate(place, weights, source_ids, table, blocks, segments, channels, shares):
    far, rows, _ = blocks[0].shape
    devices = far * len(blocks)
    ch_local = channels // devices
    sources = source_ids.shape[0]
    smem = pl.BlockSpec(memory_space=pltpu.SMEM)
    vmem = pl.BlockSpec(memory_space=pltpu.VMEM)
    return pl.pallas_call(
        functools.partial(correlate_kernel, segments, channels, shares),
        in_specs=[smem, smem, vmem, pl.BlockSpec(memory_space=pltpu.HBM)] + [vmem] * len(blocks),
        out_specs=vmem,
        out_shape=jax.ShapeDtypeStruct((sources, ch_local, LAGS), jnp.float32),
        scratch_shapes=[
            pltpu.VMEM((devices, rows, WIDTH), jnp.bfloat16),
            pltpu.VMEM((LAG_TILES * WIDTH, 128), jnp.bfloat16),
            pltpu.VMEM((segments, sources, WIDTH), jnp.float32),
            pltpu.VMEM((segments, 16, WIDTH), jnp.float32),
            pltpu.VMEM((ch_local * sources, WIDTH), jnp.bfloat16),
            pltpu.SemaphoreType.DMA,
        ],
        compiler_params=pltpu.CompilerParams(vmem_limit_bytes=40 * 2**20),
        name="correlate",
    )(place, weights, source_ids.reshape(sources, 1), table, *blocks)


def per_device(records, valid_flags, source_ids):
    segments, channels, span = records.shape
    devices = lax.axis_size("chan")
    members = devices // SHARES
    samples = span * devices
    place = lax.axis_index("chan")
    weights = valid_flags.astype(jnp.float32)

    def exchange(block, bits):
        return lax.ppermute(block, "chan", [(i, i ^ bits) for i in range(devices)])

    share = (place // members).reshape(1)
    groups = [list(range(members)), list(range(members, devices))]
    grouped = records.reshape(members, segments * channels // members, span)
    regrouped = lax.all_to_all(
        grouped, "chan", split_axis=0, concat_axis=0, axis_index_groups=groups, tiled=True
    )
    table = tables(samples)
    parts = []
    for first, last in ((0, FIRST_TILES), (FIRST_TILES, WIDTH // 128)):
        own, other = transform(share, regrouped, table, first, last)
        parts += [own, exchange(other, members)]
    white = whiten(weights.reshape(1, -1), parts)

    far = devices // 8
    line = jnp.stack([white] + [exchange(white, 8 * k) for k in range(1, far)])
    plane = [line] + [exchange(line, 2 * k) for k in range(1, 4)]
    blocks = [b for block in plane for b in (block, exchange(block, 1))]
    return correlate(
        place.reshape(1),
        weights,
        source_ids,
        table,
        blocks,
        segments,
        channels,
        SHARES,
    )


def solution(mesh):
    return jax.shard_map(
        per_device,
        mesh=mesh,
        in_specs=(P("group", None, "chan"), P("group", "chan"), P("group")),
        out_specs=P("group", "chan", None),
        check_vma=False,
    )
```

time: 88.1 us -> 73.4 us (0.83)
  waiting for transfers between devices: 21.7 us -> 40.3 us
  blocking collectives: 16.7 us -> 0 us
  Pallas kernels: 30.8 us -> 14.6 us
  local copies, waits for them, and re-layouts: 3.4 us -> 0.26 us
  starting transfers between devices: 14.8 us -> 17.9 us
    all_to_all x1 -> x0, blocking collectives: 16.7 us -> none  [partial(): lax.all_to_all(chosen, 'chan', split_axis=0, concat_axis=0, axis_index_gr...]
    all_to_all x1, waiting for transfers between devices: 0.01 us -> 16.2 us  [per_device(): lax.all_to_all(grouped, 'chan', split_axis=0, concat_axis=0, axis_index_g...]
    pallas_call x3, Pallas kernels: 24 us -> 8.86 us  [the longest x2 8.75 us: transform(): pl.pallas_call(functools.partial(transform_kernel, first), in_specs=[pl.B...]
    all_to_all x1, starting transfers between devices: 3.57 us -> 6.29 us  [per_device(): lax.all_to_all(grouped, 'chan', split_axis=0, concat_axis=0, axis_index_g...]
    ppermute x11 -> x12, waiting for transfers between devices: 21.7 us -> 24.2 us  [exchange(): return lax.ppermute(block, 'chan', [(i, i ^ bits) for i in range(devices)])]
    squeeze x1 -> x0, local copies, waits for them, and re-layouts: 2.1 us -> none  [partial(): chosen = lax.dynamic_index_in_dim(grouped, owner, 1, keepdims=False)]
    pallas_call x1, Pallas kernels: 6.76 us -> 5.72 us  [correlate(): pl.pallas_call(functools.partial(correlate_kernel, segments, channels, sh...]
    unnamed x9 -> x5, local copies, waits for them, and re-layouts: 1.13 us -> 0.09 us
  transfers between devices with their start and end apart: 12 -> 13, of which waited for: 6 -> 8; matrix products, arithmetic and copies ran while one was open for 0% -> 0% of each run, Pallas kernels for 27% -> 5%
where the time goes in v1:
time: 73.4 us; the launch traced here: 73.2 us
  waiting for transfers between devices  40.3 us (55%)
  starting transfers between devices  17.9 us (24%)
  Pallas kernels  14.6 us (20%)
    ppermute x12, waiting for transfers between devices, exchange(): return lax.ppermute(block, 'chan', [(i, i ^ bits) for i in range(devices)])  24.2 us
    all_to_all x1, waiting for transfers between devices, per_device(): lax.all_to_all(grouped, 'chan', split_axis=0, concat_axis=0, axis_index_g...  16.2 us
    ppermute x12, starting transfers between devices, exchange(): return lax.ppermute(block, 'chan', [(i, i ^ bits) for i in range(devices)])  11.6 us
    pallas_call x2, Pallas kernels, transform(): pl.pallas_call(functools.partial(transform_kernel, first), in_specs=[pl.B...  8.75 us
    all_to_all x1, starting transfers between devices, per_device(): lax.all_to_all(grouped, 'chan', split_axis=0, concat_axis=0, axis_index_g...  6.29 us
    pallas_call x1, Pallas kernels, correlate(): pl.pallas_call(functools.partial(correlate_kernel, segments, channels, sh...  5.72 us
  transfers between devices with their start and end apart: 13, of which 8 were waited for; matrix products, arithmetic and copies ran while one was open for 0% of the time, Pallas kernels for 5%

profile of v1, /device:TPU:0, one launch (start us, length us, event | category | flops | bytes accessed | tf_op | source)
XLA Modules:
  0.0 73.2 jit_solution(7670155563907746845)
XLA Ops:
  0.0 6.3 %all-to-all-start = ((bf16[16,64,512]{2,1,0:T(8,128)(2,1)}), bf16[16,64,512]{2,1,0:T(8,128)(2,1)S(1)}, u32[]{:S(2)}, u32[]{:S(2)}) async-start(bf16[16,64,512]{2,1,0:T(8,128)(2,1)} %bitcast.9), calls=%async_computation | async-start | bytes 2097152 | tf_op jit(solution)/shard_map/all_to_all | solution.py:267
  6.3 16.2 %all-to-all-done.records_ref = bf16[16,64,512]{2,1,0:T(8,128)(2,1)S(1)} async-done(((bf16[16,64,512]{2,1,0:T(8,128)(2,1)}), bf16[16,64,512]{2,1,0:T(8,128)(2,1)S(1)}, u32[]{:S(2)}, u32[]{:S(2)}) %all-to-all-start) | async-done | bytes 1048608 | tf_op jit(solution)/shard_map/all_to_all | solution.py:267
  22.5 5.0 %transform.2 = (f32[32,768]{1,0:T(8,128)S(1)}, f32[32,768]{1,0:T(8,128)S(1)}) custom-call(s32[1]{0:T(128)} %bitcast.2.share_ref, bf16[16,64,512]{2,1,0:T(8,128)(2,1)S(1)} %all-to-all-done.records_ref, bf16[174080,128]{1,0:T(8,128)(2,1)} %constant.22.clone.table_ref), custom_call_target="tpu_custom_call" | custom-call | flops 805306368 | bytes 12582912 | tf_op jit(solution)/shard_map/transform/pallas_call | solution.py:100
  27.5 2.7 %collective-permute-start = (f32[32,768]{1,0:T(8,128)S(1)}, f32[32,768]{1,0:T(8,128)S(1)}, u32[]{:S(2)}, u32[]{:S(2)}) collective-permute-start(f32[32,768]{1,0:T(8,128)S(1)} %get-tuple-element.10), channel_id=1, source_target_pairs={{0,16},{1,17},{2,18},{3,19},{4,20},{5,21},{6,22},{7,23},{8,24},{9,... | collective-permute-start | bytes 294920 | tf_op jit(solution)/shard_map/ppermute | solution.py:262
  30.2 3.7 %transform.3 = (f32[32,512]{1,0:T(8,128)S(1)}, f32[32,512]{1,0:T(8,128)S(1)}) custom-call(s32[1]{0:T(128)} %bitcast.2.share_ref, bf16[16,64,512]{2,1,0:T(8,128)(2,1)S(1)} %all-to-all-done.records_ref, bf16[174080,128]{1,0:T(8,128)(2,1)} %constant.22.clone.table_ref), custom_call_target="tpu_custom_call" | custom-call | flops 536870912 | bytes 8388608 | tf_op jit(solution)/shard_map/transform/pallas_call | solution.py:100
  33.9 0.4 collective-permute-start.1
  34.3 0.1 copy.7
  34.4 0.1 reshape.17.flags_ref
  34.5 5.4 %collective-permute-done.1.rest_3_ = f32[32,512]{1,0:T(8,128)S(1)} collective-permute-done((f32[32,512]{1,0:T(8,128)S(1)}, f32[32,512]{1,0:T(8,128)S(1)}, u32[]{:S(2)}, u32[]{:S(2)}) %collective-permute-start.1) | collective-permute-done | bytes 65568 | tf_op jit(solution)/shard_map/ppermute | solution.py:262
  39.8 0.1 whiten.1
  40.0 0.1 collective-permute-start.4
  40.0 1.5 %collective-permute-start.3 = (bf16[32,1280]{1,0:T(8,128)(2,1)S(1)}, bf16[32,1280]{1,0:T(8,128)(2,1)S(1)}, u32[]{:S(2)}, u32[]{:S(2)}) collective-permute-start(bf16[32,1280]{1,0:T(8,128)(2,1)S(1)} %whiten.1), channel_id=1, source_target_pairs={{0,16},{1,17},{2,18},{3,19},{4,20},{5,21},{6,22},{7,23},{8,24},{9,... | collective-permute-start | bytes 245768 | tf_op jit(solution)/shard_map/ppermute | solution.py:262
  41.5 2.9 %collective-permute-start.2 = (bf16[32,1280]{1,0:T(8,128)(2,1)S(1)}, bf16[32,1280]{1,0:T(8,128)(2,1)S(1)}, u32[]{:S(2)}, u32[]{:S(2)}) collective-permute-start(bf16[32,1280]{1,0:T(8,128)(2,1)S(1)} %whiten.1), channel_id=1, source_target_pairs={{0,8},{1,9},{2,10},{3,11},{4,12},{5,13},{6,14},{7,15},{8,0},{9,1},... | collective-permute-start | bytes 245768 | tf_op jit(solution)/shard_map/ppermute | solution.py:262
  44.4 2.0 %collective-permute-done.4 = bf16[32,1280]{1,0:T(8,128)(2,1)S(1)} collective-permute-done((bf16[32,1280]{1,0:T(8,128)(2,1)S(1)}, bf16[32,1280]{1,0:T(8,128)(2,1)S(1)}, u32[]{:S(2)}, u32[]{:S(2)}) %collective-permute-start.4) | collective-permute-done | bytes 81952 | tf_op jit(solution)/shard_map/ppermute | solution.py:262
  46.4 1.9 %collective-permute-done.3 = bf16[32,1280]{1,0:T(8,128)(2,1)S(1)} collective-permute-done((bf16[32,1280]{1,0:T(8,128)(2,1)S(1)}, bf16[32,1280]{1,0:T(8,128)(2,1)S(1)}, u32[]{:S(2)}, u32[]{:S(2)}) %collective-permute-start.3) | collective-permute-done | bytes 81952 | tf_op jit(solution)/shard_map/ppermute | solution.py:262
  48.3 2.8 %collective-permute-start.10 = (bf16[4,32,1280]{2,1,0:T(8,128)(2,1)S(1)}, bf16[4,32,1280]{2,1,0:T(8,128)(2,1)S(1)}, u32[]{:S(2)}, u32[]{:S(2)}) collective-permute-start(bf16[4,32,1280]{2,1,0:T(8,128)(2,1)S(1)} %pad_maximum_fusion.rest_0_), channel_id=1, source_target_pairs={{0,6},{1,7},{2,4},{3,5},{4,2},{5,3},{6,0},{7,1},{8,14},{9,15},{10,... | collective-permute-start | bytes 983048 | tf_op jit(solution)/shard_map/ppermute | solution.py:262
  51.2 0.7 collective-permute-start.6
  51.9 8.1 %collective-permute-done.10.rest_6_ = bf16[4,32,1280]{2,1,0:T(8,128)(2,1)S(1)} collective-permute-done((bf16[4,32,1280]{2,1,0:T(8,128)(2,1)S(1)}, bf16[4,32,1280]{2,1,0:T(8,128)(2,1)S(1)}, u32[]{:S(2)}, u32[]{:S(2)}) %collective-permute-start.10) | collective-permute-done | bytes 327712 | tf_op jit(solution)/shard_map/ppermute | solution.py:262
  60.0 5.4 %collective-permute-done.8.rest_4_ = bf16[4,32,1280]{2,1,0:T(8,128)(2,1)S(1)} collective-permute-done((bf16[4,32,1280]{2,1,0:T(8,128)(2,1)S(1)}, bf16[4,32,1280]{2,1,0:T(8,128)(2,1)S(1)}, u32[]{:S(2)}, u32[]{:S(2)}) %collective-permute-start.8) | collective-permute-done | bytes 327712 | tf_op jit(solution)/shard_map/ppermute | solution.py:262
  65.4 0.5 collective-permute-start.7
  65.9 0.1 copy.8.ids_ref
  66.0 1.0 %collective-permute-done.9.rest_5_ = bf16[4,32,1280]{2,1,0:T(8,128)(2,1)S(1)} collective-permute-done((bf16[4,32,1280]{2,1,0:T(8,128)(2,1)S(1)}, bf16[4,32,1280]{2,1,0:T(8,128)(2,1)S(1)}, u32[]{:S(2)}, u32[]{:S(2)}) %collective-permute-start.9) | collective-permute-done | bytes 327712 | tf_op jit(solution)/shard_map/ppermute | solution.py:262
  67.0 0.5 collective-permute-done.7.rest_3_
  67.4 5.7 %correlate.1 = f32[64,4,1001]{2,1,0:T(4,128)} custom-call(s32[1]{0:T(128)} %bitcast.place_ref, f32[8,4]{1,0:T(8,128)S(1)} %convert_element_type.3.flags_ref, s32[64,1]{1,0:T(8,128)S(1)} %copy.8.ids_ref, bf16[174080,128]{1,0:T(8,128)(2,1)} %constant.22.clone.table_ref, bf16[4,32,1280]{2,1,0:T(8,128)(2,1)S(1)} %pad_maximum_fusion.rest_0_, ...), custom_call_target="tpu_custom_call" | custom-call | tf_op jit(solution)/shard_map/correlate/pallas_call | solution.py:235
  (15 shorter events, 0.1 us)
Async XLA Ops:
  0.0 22.5 %all-to-all-start = ((bf16[16,64,512]{2,1,0:T(8,128)(2,1)}), bf16[16,64,512]{2,1,0:T(8,128)(2,1)S(1)}, u32[]{:S(2)}, u32[]{:S(2)}) async-start(bf16[16,64,512]{2,1,0:T(8,128)(2,1)} %bitcast.9), calls=%async_computation | async-start | bytes 2097152 | tf_op jit(solution)/shard_map/all_to_all | solution.py:267
  22.5 11.8 %copy-start = (s32[8,4]{0,1:T(4,128)S(1)}, s32[8,4]{0,1:T(4,128)}, u32[]{:S(2)}) copy-start(s32[8,4]{0,1:T(4,128)} %param.5) | copy-start | bytes 388
  22.5 43.4 %copy-start.1 = (s32[64]{0:T(128)S(1)}, s32[64]{0:T(128)}, u32[]{:S(2)}) copy-start(s32[64]{0:T(128)} %param.6) | copy-start | bytes 772
  27.5 12.3 %collective-permute-start = (f32[32,768]{1,0:T(8,128)S(1)}, f32[32,768]{1,0:T(8,128)S(1)}, u32[]{:S(2)}, u32[]{:S(2)}) collective-permute-start(f32[32,768]{1,0:T(8,128)S(1)} %get-tuple-element.10), channel_id=1, source_target_pairs={{0,16},{1,17},{2,18},{3,19},{4,20},{5,21},{6,22},{7,23},{8,24},{9,... | collective-permute-start | bytes 294920 | tf_op jit(solution)/shard_map/ppermute | solution.py:262
  33.9 5.9 %collective-permute-start.1 = (f32[32,512]{1,0:T(8,128)S(1)}, f32[32,512]{1,0:T(8,128)S(1)}, u32[]{:S(2)}, u32[]{:S(2)}) collective-permute-start(f32[32,512]{1,0:T(8,128)S(1)} %get-tuple-element.12), channel_id=1, source_target_pairs={{0,16},{1,17},{2,18},{3,19},{4,20},{5,21},{6,22},{7,23},{8,24},{9,... | collective-permute-start | bytes 196616 | tf_op jit(solution)/shard_map/ppermute | solution.py:262
  40.0 6.5 %collective-permute-start.4 = (bf16[32,1280]{1,0:T(8,128)(2,1)S(1)}, bf16[32,1280]{1,0:T(8,128)(2,1)S(1)}, u32[]{:S(2)}, u32[]{:S(2)}) collective-permute-start(bf16[32,1280]{1,0:T(8,128)(2,1)S(1)} %whiten.1), channel_id=1, source_target_pairs={{0,24},{1,25},{2,26},{3,27},{4,28},{5,29},{6,30},{7,31},{8,16},{9,... | collective-permute-start | bytes 245768 | tf_op jit(solution)/shard_map/ppermute | solution.py:262
  40.0 8.2 %collective-permute-start.3 = (bf16[32,1280]{1,0:T(8,128)(2,1)S(1)}, bf16[32,1280]{1,0:T(8,128)(2,1)S(1)}, u32[]{:S(2)}, u32[]{:S(2)}) collective-permute-start(bf16[32,1280]{1,0:T(8,128)(2,1)S(1)} %whiten.1), channel_id=1, source_target_pairs={{0,16},{1,17},{2,18},{3,19},{4,20},{5,21},{6,22},{7,23},{8,24},{9,... | collective-permute-start | bytes 245768 | tf_op jit(solution)/shard_map/ppermute | solution.py:262
  41.5 6.7 %collective-permute-start.2 = (bf16[32,1280]{1,0:T(8,128)(2,1)S(1)}, bf16[32,1280]{1,0:T(8,128)(2,1)S(1)}, u32[]{:S(2)}, u32[]{:S(2)}) collective-permute-start(bf16[32,1280]{1,0:T(8,128)(2,1)S(1)} %whiten.1), channel_id=1, source_target_pairs={{0,8},{1,9},{2,10},{3,11},{4,12},{5,13},{6,14},{7,15},{8,0},{9,1},... | collective-permute-start | bytes 245768 | tf_op jit(solution)/shard_map/ppermute | solution.py:262
  48.3 11.7 %collective-permute-start.10 = (bf16[4,32,1280]{2,1,0:T(8,128)(2,1)S(1)}, bf16[4,32,1280]{2,1,0:T(8,128)(2,1)S(1)}, u32[]{:S(2)}, u32[]{:S(2)}) collective-permute-start(bf16[4,32,1280]{2,1,0:T(8,128)(2,1)S(1)} %pad_maximum_fusion.rest_0_), channel_id=1, source_target_pairs={{0,6},{1,7},{2,4},{3,5},{4,2},{5,3},{6,0},{7,1},{8,14},{9,15},{10,... | collective-permute-start | bytes 983048 | tf_op jit(solution)/shard_map/ppermute | solution.py:262
  51.2 14.2 %collective-permute-start.8 = (bf16[4,32,1280]{2,1,0:T(8,128)(2,1)S(1)}, bf16[4,32,1280]{2,1,0:T(8,128)(2,1)S(1)}, u32[]{:S(2)}, u32[]{:S(2)}) collective-permute-start(bf16[4,32,1280]{2,1,0:T(8,128)(2,1)S(1)} %pad_maximum_fusion.rest_0_), channel_id=1, source_target_pairs={{0,4},{1,5},{2,6},{3,7},{4,0},{5,1},{6,2},{7,3},{8,12},{9,13},{10,... | collective-permute-start | bytes 983048 | tf_op jit(solution)/shard_map/ppermute | solution.py:262
  51.2 14.2 %collective-permute-start.6 = (bf16[4,32,1280]{2,1,0:T(8,128)(2,1)S(1)}, bf16[4,32,1280]{2,1,0:T(8,128)(2,1)S(1)}, u32[]{:S(2)}, u32[]{:S(2)}) collective-permute-start(bf16[4,32,1280]{2,1,0:T(8,128)(2,1)S(1)} %pad_maximum_fusion.rest_0_), channel_id=1, source_target_pairs={{0,2},{1,3},{2,0},{3,1},{4,6},{5,7},{6,4},{7,5},{8,10},{9,11},{10,... | collective-permute-start | bytes 983048 | tf_op jit(solution)/shard_map/ppermute | solution.py:262
  51.9 14.1 %collective-permute-start.5 = (bf16[4,32,1280]{2,1,0:T(8,128)(2,1)S(1)}, bf16[4,32,1280]{2,1,0:T(8,128)(2,1)S(1)}, u32[]{:S(2)}, u32[]{:S(2)}) collective-permute-start(bf16[4,32,1280]{2,1,0:T(8,128)(2,1)S(1)} %pad_maximum_fusion.rest_0_), channel_id=1, source_target_pairs={{0,1},{1,0},{2,3},{3,2},{4,5},{5,4},{6,7},{7,6},{8,9},{9,8},{10,11... | collective-permute-start | bytes 983048 | tf_op jit(solution)/shard_map/ppermute | solution.py:262
  60.0 6.0 %collective-permute-start.11 = (bf16[4,32,1280]{2,1,0:T(8,128)(2,1)S(1)}, bf16[4,32,1280]{2,1,0:T(8,128)(2,1)S(1)}, u32[]{:S(2)}, u32[]{:S(2)}) collective-permute-start(bf16[4,32,1280]{2,1,0:T(8,128)(2,1)S(1)} %collective-permute-done.10.rest_6_), channel_id=1, source_target_pairs={{0,1},{1,0},{2,3},{3,2},{4,5},{5,4},{6,7},{7,6},{8,9},{9,8},{10,11... | collective-permute-start | bytes 983048 | tf_op jit(solution)/shard_map/ppermute | solution.py:262
  65.3 1.6 %collective-permute-start.9 = (bf16[4,32,1280]{2,1,0:T(8,128)(2,1)S(1)}, bf16[4,32,1280]{2,1,0:T(8,128)(2,1)S(1)}, u32[]{:S(2)}, u32[]{:S(2)}) collective-permute-start(bf16[4,32,1280]{2,1,0:T(8,128)(2,1)S(1)} %collective-permute-done.8.rest_4_), channel_id=1, source_target_pairs={{0,1},{1,0},{2,3},{3,2},{4,5},{5,4},{6,7},{7,6},{8,9},{9,8},{10,11... | collective-permute-start | bytes 983048 | tf_op jit(solution)/shard_map/ppermute | solution.py:262
  65.4 2.1 %collective-permute-start.7 = (bf16[4,32,1280]{2,1,0:T(8,128)(2,1)S(1)}, bf16[4,32,1280]{2,1,0:T(8,128)(2,1)S(1)}, u32[]{:S(2)}, u32[]{:S(2)}) collective-permute-start(bf16[4,32,1280]{2,1,0:T(8,128)(2,1)S(1)} %collective-permute-done.6.rest_2_), channel_id=1, source_target_pairs={{0,1},{1,0},{2,3},{3,2},{4,5},{5,4},{6,7},{7,6},{8,9},{9,8},{10,11... | collective-permute-start | bytes 983048 | tf_op jit(solution)/shard_map/ppermute | solution.py:262

commit v2 on v1

--- a/solution.py
+++ b/solution.py
@@ -22,8 +22,8 @@
 WIDTH = 2 * PART
 LAGS = 2 * HALF_LAG + 1
 LAG_TILES = -(-LAGS // 128)
-BLOCK = 512
 SHARES = 2
+COLUMN_TILES = WIDTH // 128
 FIRST_TILES = 6
 FLAG_TILE = BAND // 128 * 128
 FLAG_LANE = BAND - FLAG_TILE
@@ -45,7 +45,7 @@
 
 
 @functools.lru_cache(maxsize=None)
-def tables(samples):
+def tables(samples, span):
     bins = lowest_bin + np.arange(BAND)
     cosine, sine = cos_sin(samples)
     phase = np.arange(samples)[:, None] * bins[None, :] % samples
@@ -57,67 +57,91 @@
     inverse = np.zeros((WIDTH, LAG_TILES * 128), ml_dtypes.bfloat16)
     inverse[:BAND, :LAGS] = (cosine * factor).astype(ml_dtypes.bfloat16)[phase]
     inverse[PART : PART + BAND, :LAGS] = (sine * factor).astype(ml_dtypes.bfloat16)[phase]
-    parts = [lane_tiles(forward.reshape(-1, BLOCK, WIDTH)), lane_tiles(inverse)]
+    parts = [lane_tiles(forward.reshape(-1, span, WIDTH)), lane_tiles(inverse)]
     return np.concatenate([part.reshape(-1, 128) for part in parts])
 
 
-def transform_kernel(first, share_ref, records_ref, table_ref, *rest):
-    own_ref, other_ref, tiles_ref, sems = rest
-    senders, rows, span = records_ref.shape
-    blocks, lines, _ = tiles_ref.shape
-    columns = lines // BLOCK
+def fetch_kernel(share_ref, table_ref, after_ref, out_ref, sems):
+    blocks, lines, _ = out_ref.shape
+    batch = blocks // sems.shape[0]
     copies = []
-    for index in range(blocks):
-        block = share_ref[0] * blocks + index
-        start = (block * (WIDTH // 128) + first) * BLOCK
-        source = table_ref.at[pl.ds(pl.multiple_of(start, BLOCK), lines)]
-        copies.append(pltpu.make_async_copy(source, tiles_ref.at[index], sems.at[index]))
-        copies[-1].start()
-    total = jnp.zeros((rows, columns * 128), jnp.float32)
-    pieces = BLOCK // span
-    for index in range(blocks):
-        copies[index].wait()
-        tiles = [tiles_ref[index, tile * BLOCK : (tile + 1) * BLOCK] for tile in range(columns)]
-        records = [records_ref[index * pieces + piece] for piece in range(pieces)]
-        total += jnp.dot(
-            jnp.concatenate(records, axis=1),
-            jnp.concatenate(tiles, axis=1),
-            preferred_element_type=jnp.float32,
-        )
-    low, high = total[: rows // 2], total[rows // 2 :]
-    mine = share_ref[0] == 0
-    own_ref[...] = jnp.where(mine, low, high)
-    other_ref[...] = jnp.where(mine, high, low)
-
-
-def transform(share, records, table, first, last):
-    senders, rows, span = records.shape
-    columns = last - first
-    depth = senders * span
-    blocks = depth // BLOCK
-    vmem = pl.BlockSpec(memory_space=pltpu.VMEM)
-    shape = jax.ShapeDtypeStruct((rows // 2, columns * 128), jnp.float32)
+    for index in range(sems.shape[0]):
+        for block in range(index * batch, (index + 1) * batch):
+            start = (share_ref[0] * blocks + block) * lines
+            source = table_ref.at[pl.ds(pl.multiple_of(start, lines), lines)]
+            copies.append(pltpu.make_async_copy(source, out_ref.at[block], sems.at[block]))
+            copies[-1].start()
+    for copy in copies:
+        copy.wait()
+
+
+def fetch(share, table, members, span, after):
+    shape = (members, COLUMN_TILES * span, 128)
     return pl.pallas_call(
-        functools.partial(transform_kernel, first),
+        fetch_kernel,
         in_specs=[
             pl.BlockSpec(memory_space=pltpu.SMEM),
-            vmem,
             pl.BlockSpec(memory_space=pltpu.HBM),
+            pl.BlockSpec(memory_space=pl.ANY),
         ],
-        out_specs=[vmem, vmem],
-        out_shape=[shape, shape],
-        scratch_shapes=[
-            pltpu.VMEM((blocks, columns * BLOCK, 128), jnp.bfloat16),
-            pltpu.SemaphoreType.DMA((blocks,)),
-        ],
-        compiler_params=pltpu.CompilerParams(vmem_limit_bytes=32 * 2**20),
+        out_specs=pl.BlockSpec(memory_space=pltpu.VMEM),
+        out_shape=jax.ShapeDtypeStruct(shape, jnp.bfloat16),
+        scratch_shapes=[pltpu.SemaphoreType.DMA((members,))],
+        compiler_params=pltpu.CompilerParams(vmem_limit_bytes=8 * 2**20),
         cost_estimate=pl.CostEstimate(
-            flops=2 * rows * depth * columns * 128,
-            bytes_accessed=2 * depth * columns * 128,
+            flops=0, bytes_accessed=4 * math.prod(shape), transcendentals=0
+        ),
+        name="fetch",
+    )(share, table, after)
+
+
+def transform_kernel(steps, first, started, place_ref, table_ref, *rest):
+    records, rest = rest[: len(steps)], rest[len(steps) :]
+    span = records[0].shape[1]
+    members = table_ref.shape[0]
+    if started:
+        total, outs = rest[0][...], rest[1:]
+    else:
+        total, outs = None, rest
+    columns = outs[0].shape[1] // 128
+    for step, block in zip(steps, records):
+        member = place_ref[0] % members ^ step
+        tiles = [
+            table_ref[member, (first + tile) * span : (first + tile + 1) * span]
+            for tile in range(columns)
+        ]
+        product = jnp.dot(
+            block[...], jnp.concatenate(tiles, axis=1), preferred_element_type=jnp.float32
+        )
+        total = product if total is None else total + product
+    if len(outs) == 1:
+        outs[0][...] = total
+    else:
+        rows = outs[0].shape[0]
+        mine = place_ref[0] < members
+        outs[0][...] = jnp.where(mine, total[:rows], total[rows:])
+        outs[1][...] = jnp.where(mine, total[rows:], total[:rows])
+
+
+def transform(place, table, steps, records, first, last, before, split):
+    rows, span = records[0].shape
+    columns = (last - first) * 128
+    vmem = pl.BlockSpec(memory_space=pltpu.VMEM)
+    outs = 2 if split else 1
+    started = before is not None
+    return pl.pallas_call(
+        functools.partial(transform_kernel, steps, first, started),
+        in_specs=[pl.BlockSpec(memory_space=pltpu.SMEM)] + [vmem] * (1 + len(steps) + started),
+        out_specs=[vmem] * outs,
+        out_shape=[jax.ShapeDtypeStruct((rows // outs, columns), jnp.float32)] * outs,
+        compiler_params=pltpu.CompilerParams(vmem_limit_bytes=8 * 2**20),
+        cost_estimate=pl.CostEstimate(
+            flops=2 * rows * len(steps) * span * columns,
+            bytes_accessed=2 * len(steps) * span * columns,
             transcendentals=0,
         ),
         name="transform",
-    )(share, records, table)
+    )(place, table, *records, *([before] if started else []))
 
 
 def whiten_kernel(flags_ref, *rest):
@@ -250,6 +274,13 @@
     )(place, weights, source_ids.reshape(sources, 1), table, *blocks)
 
 
+def balanced_steps(members):
+    chips = members // 2
+    masks = [m for low in range(1, chips // 2) for m in (low, low ^ (chips - 1))] + [chips - 1]
+    first = [2 * m for m in masks]
+    return [0] + first[5:] + first[:5] + [2 * m + 1 for m in masks] + [1]
+
+
 def per_device(records, valid_flags, source_ids):
     segments, channels, span = records.shape
     devices = lax.axis_size("chan")
@@ -261,16 +292,27 @@
     def exchange(block, bits):
         return lax.ppermute(block, "chan", [(i, i ^ bits) for i in range(devices)])
 
-    share = (place // members).reshape(1)
-    groups = [list(range(members)), list(range(members, devices))]
+    me = place.reshape(1)
     grouped = records.reshape(members, segments * channels // members, span)
-    regrouped = lax.all_to_all(
-        grouped, "chan", split_axis=0, concat_axis=0, axis_index_groups=groups, tiled=True
-    )
-    table = tables(samples)
+    sent = [
+        lax.dynamic_index_in_dim(grouped, place % members ^ step, 0, keepdims=False)
+        for step in range(members)
+    ]
+    arrived = {step: exchange(sent[step], step) if step else sent[0] for step in range(members)}
+    table = tables(samples, span)
+    near = fetch(me // members, table, members, span, sent[0])
+    steps = balanced_steps(members)
+    early, late = steps[: members // 2], steps[members // 2 :]
     parts = []
-    for first, last in ((0, FIRST_TILES), (FIRST_TILES, WIDTH // 128)):
-        own, other = transform(share, regrouped, table, first, last)
+    spans = (0, FIRST_TILES), (FIRST_TILES, COLUMN_TILES)
+    begun = [
+        transform(me, near, early, [arrived[k] for k in early], first, last, None, False)[0]
+        for first, last in spans
+    ]
+    for (first, last), before in zip(spans, begun):
+        own, other = transform(
+            me, near, late, [arrived[k] for k in late], first, last, before, True
+        )
         parts += [own, exchange(other, members)]
     white = whiten(weights.reshape(1, -1), parts)
 

time: 73.4 us -> 76.7 us (1.045)
  waiting for transfers between devices: 40.3 us -> 25.7 us
  starting transfers between devices: 17.9 us -> 31.4 us
  Pallas kernels: 14.6 us -> 17 us
  local copies, waits for them, and re-layouts: 0.26 us -> 1.58 us
    ppermute x12 -> x27, starting transfers between devices: 11.6 us -> 31.4 us  [exchange(): return lax.ppermute(block, 'chan', [(i, i ^ bits) for i in range(devices)])]
    all_to_all x1 -> x0, waiting for transfers between devices: 16.2 us -> none  [per_device(): lax.all_to_all(grouped, 'chan', split_axis=0, concat_axis=0, axis_index_g...]
    all_to_all x1 -> x0, starting transfers between devices: 6.29 us -> none  [per_device(): lax.all_to_all(grouped, 'chan', split_axis=0, concat_axis=0, axis_index_g...]
    pallas_call x2 -> x5, Pallas kernels: 8.75 us -> 11.2 us  [the longest x1 7.14 us: fetch(): pl.pallas_call(fetch_kernel, in_specs=[pl.BlockSpec(memory_space=pltpu.SM...]
    ppermute x12 -> x27, waiting for transfers between devices: 24.2 us -> 25.7 us  [exchange(): return lax.ppermute(block, 'chan', [(i, i ^ bits) for i in range(devices)])]
    squeeze x0 -> x1, local copies, waits for them, and re-layouts: none -> 1.31 us  [per_device(): lax.dynamic_index_in_dim(grouped, place % members ^ step, 0, keepdims=False)]
  transfers between devices with their start and end apart: 13 -> 27, of which waited for: 8 -> 9; matrix products, arithmetic and copies ran while one was open for 0% -> 0% of each run, Pallas kernels for 5% -> 13%
where the time goes in v2:
time: 76.7 us; the launch traced here: 75.9 us
  starting transfers between devices  31.4 us (41%)
  waiting for transfers between devices  25.7 us (34%)
  Pallas kernels  17 us (22%)
  local copies, waits for them, and re-layouts  1.58 us (2%)
    ppermute x27, starting transfers between devices, exchange(): return lax.ppermute(block, 'chan', [(i, i ^ bits) for i in range(devices)])  31.4 us
    ppermute x27, waiting for transfers between devices, exchange(): return lax.ppermute(block, 'chan', [(i, i ^ bits) for i in range(devices)])  25.7 us
    pallas_call x1, Pallas kernels, fetch(): pl.pallas_call(fetch_kernel, in_specs=[pl.BlockSpec(memory_space=pltpu.SM...  7.14 us
    pallas_call x1, Pallas kernels, correlate(): pl.pallas_call(functools.partial(correlate_kernel, segments, channels, sh...  5.72 us
    pallas_call x4, Pallas kernels, transform(): pl.pallas_call(functools.partial(transform_kernel, steps, first, started)...  4.08 us
  transfers between devices with their start and end apart: 27, of which 9 were waited for; matrix products, arithmetic and copies ran while one was open for 0% of the time, Pallas kernels for 13%

profile of v2, /device:TPU:0, one launch (start us, length us, event | category | flops | bytes accessed | tf_op | source)
XLA Modules:
  0.0 75.9 jit_solution(14338603892002297102)
XLA Ops:
  0.0 1.3 %dynamic-slice_bitcast_fusion = (bf16[64,512]{1,0:T(8,128)(2,1)S(1)}, bf16[64,512]{1,0:T(8,128)(2,1)S(1)}, bf16[64,512]{1,0:T(8,128)(2,1)S(1)}, bf16[64,512]{1,0...) fusion(bf16[16,64,512]{2,1,0:T(8,128)(2,1)} %bitcast.40, ...), kind=kLoop, calls=%fused_computation.1 | loop fusion | bytes 2097216 | tf_op jit(solution)/shard_map/jit(dynamic_index_in_dim)/squeeze | solution.py:298
  1.3 3.0 %collective-permute-start.10 = (bf16[64,512]{1,0:T(8,128)(2,1)S(1)}, bf16[64,512]{1,0:T(8,128)(2,1)S(1)}, u32[]{:S(2)}, u32[]{:S(2)}) collective-permute-start(bf16[64,512]{1,0:T(8,128)(2,1)S(1)} %get-tuple-element.17), channel_id=1, source_target_pairs={{0,2},{1,3},{2,0},{3,1},{4,6},{5,7},{6,4},{7,5},{8,10},{9,11},{10,... | collective-permute-start | bytes 196616 | tf_op jit(solution)/shard_map/ppermute | solution.py:293
  4.3 2.5 %collective-permute-start.11 = (bf16[64,512]{1,0:T(8,128)(2,1)S(1)}, bf16[64,512]{1,0:T(8,128)(2,1)S(1)}, u32[]{:S(2)}, u32[]{:S(2)}) collective-permute-start(bf16[64,512]{1,0:T(8,128)(2,1)S(1)} %get-tuple-element.16), channel_id=1, source_target_pairs={{0,12},{1,13},{2,14},{3,15},{4,8},{5,9},{6,10},{7,11},{8,4},{9,5},... | collective-permute-start | bytes 196616 | tf_op jit(solution)/shard_map/ppermute | solution.py:293
  7.4 2.8 %collective-permute-start.14 = (bf16[64,512]{1,0:T(8,128)(2,1)S(1)}, bf16[64,512]{1,0:T(8,128)(2,1)S(1)}, u32[]{:S(2)}, u32[]{:S(2)}) collective-permute-start(bf16[64,512]{1,0:T(8,128)(2,1)S(1)} %get-tuple-element.13), channel_id=1, source_target_pairs={{0,6},{1,7},{2,4},{3,5},{4,2},{5,3},{6,0},{7,1},{8,14},{9,15},{10,... | collective-permute-start | bytes 196616 | tf_op jit(solution)/shard_map/ppermute | solution.py:293
  10.2 1.6 %collective-permute-start.8 = (bf16[64,512]{1,0:T(8,128)(2,1)S(1)}, bf16[64,512]{1,0:T(8,128)(2,1)S(1)}, u32[]{:S(2)}, u32[]{:S(2)}) collective-permute-start(bf16[64,512]{1,0:T(8,128)(2,1)S(1)} %get-tuple-element.19), channel_id=1, source_target_pairs={{0,8},{1,9},{2,10},{3,11},{4,12},{5,13},{6,14},{7,15},{8,0},{9,1},... | collective-permute-start | bytes 196616 | tf_op jit(solution)/shard_map/ppermute | solution.py:293
  12.7 3.3 %collective-permute-start.1 = (bf16[64,512]{1,0:T(8,128)(2,1)S(1)}, bf16[64,512]{1,0:T(8,128)(2,1)S(1)}, u32[]{:S(2)}, u32[]{:S(2)}) collective-permute-start(bf16[64,512]{1,0:T(8,128)(2,1)S(1)} %get-tuple-element.26), channel_id=1, source_target_pairs={{0,13},{1,12},{2,15},{3,14},{4,9},{5,8},{6,11},{7,10},{8,5},{9,4},... | collective-permute-start | bytes 196616 | tf_op jit(solution)/shard_map/ppermute | solution.py:293
  15.9 1.1 %collective-permute-start.3 = (bf16[64,512]{1,0:T(8,128)(2,1)S(1)}, bf16[64,512]{1,0:T(8,128)(2,1)S(1)}, u32[]{:S(2)}, u32[]{:S(2)}) collective-permute-start(bf16[64,512]{1,0:T(8,128)(2,1)S(1)} %get-tuple-element.24), channel_id=1, source_target_pairs={{0,11},{1,10},{2,9},{3,8},{4,15},{5,14},{6,13},{7,12},{8,3},{9,2},... | collective-permute-start | bytes 196616 | tf_op jit(solution)/shard_map/ppermute | solution.py:293
  17.0 2.2 %collective-permute-done.9.rest_2_ = bf16[64,512]{1,0:T(8,128)(2,1)S(1)} collective-permute-done((bf16[64,512]{1,0:T(8,128)(2,1)S(1)}, bf16[64,512]{1,0:T(8,128)(2,1)S(1)}, u32[]{:S(2)}, u32[]{:S(2)}) %collective-permute-start.9) | collective-permute-done | bytes 65568 | tf_op jit(solution)/shard_map/ppermute | solution.py:293
  19.2 1.1 %collective-permute-start.5 = (bf16[64,512]{1,0:T(8,128)(2,1)S(1)}, bf16[64,512]{1,0:T(8,128)(2,1)S(1)}, u32[]{:S(2)}, u32[]{:S(2)}) collective-permute-start(bf16[64,512]{1,0:T(8,128)(2,1)S(1)} %get-tuple-element.22), channel_id=1, source_target_pairs={{0,9},{1,8},{2,11},{3,10},{4,13},{5,12},{6,15},{7,14},{8,1},{9,0},... | collective-permute-start | bytes 196616 | tf_op jit(solution)/shard_map/ppermute | solution.py:293
  21.1 2.3 %collective-permute-start.7 = (bf16[64,512]{1,0:T(8,128)(2,1)S(1)}, bf16[64,512]{1,0:T(8,128)(2,1)S(1)}, u32[]{:S(2)}, u32[]{:S(2)}) collective-permute-start(bf16[64,512]{1,0:T(8,128)(2,1)S(1)} %get-tuple-element.20), channel_id=1, source_target_pairs={{0,1},{1,0},{2,3},{3,2},{4,5},{5,4},{6,7},{7,6},{8,9},{9,8},{10,11... | collective-permute-start | bytes 196616 | tf_op jit(solution)/shard_map/ppermute | solution.py:293
  23.5 7.1 %fetch.1.table_ref = bf16[16,5120,128]{2,1,0:T(8,128)(2,1)S(1)} custom-call(s32[1]{0:T(128)S(6)} %select_n.91.share_ref, bf16[174080,128]{1,0:T(8,128)(2,1)} %constant.133.clone.table_ref, bf16[64,512]{1,0:T(8,128)(2,1)S(1)} %get-tuple-element.28.after_ref.rest_0_), custom_call_target="tpu_custom_call" | custom-call | bytes 41943040 | tf_op jit(solution)/shard_map/fetch/pallas_call | solution.py:80
  30.6 1.2 %transform.4.rest_8_ = f32[64,768]{1,0:T(8,128)S(1)} custom-call(s32[1]{0:T(128)} %bitcast.place_ref, bf16[16,5120,128]{2,1,0:T(8,128)(2,1)S(1)} %fetch.1.table_ref, bf16[64,512]{1,0:T(8,128)(2,1)S(1)} %get-tuple-element.28.after_ref.rest_0_, bf16[64,512]{1,0:T(8,128)(2,1)S(1)} %collective-permute-done.8.rest_1_, ...), custom_call_target="tpu_custom_call" | custom-call | flops 402653184 | bytes 6291456 | tf_op jit(solution)/shard_map/transform/pallas_call | solution.py:132
  31.9 1.2 %transform.5 = (f32[32,768]{1,0:T(8,128)S(1)}, f32[32,768]{1,0:T(8,128)S(1)}) custom-call(s32[1]{0:T(128)} %bitcast.place_ref, bf16[16,5120,128]{2,1,0:T(8,128)(2,1)S(1)} %fetch.1.table_ref, bf16[64,512]{1,0:T(8,128)(2,1)S(1)} %collective-permute-done.rest_0_, bf16[64,512]{1,0:T(8,128)(2,1)S(1)} %collective-permute-done.1.rest_1_, ...), custom_call_target="tpu_custom_call" | custom-call | flops 402653184 | bytes 6291456 | tf_op jit(solution)/shard_map/transform/pallas_call | solution.py:132
  33.1 2.7 %collective-permute-start.15 = (f32[32,768]{1,0:T(8,128)S(1)}, f32[32,768]{1,0:T(8,128)S(1)}, u32[]{:S(2)}, u32[]{:S(2)}) collective-permute-start(f32[32,768]{1,0:T(8,128)S(1)} %get-tuple-element.10), channel_id=1, source_target_pairs={{0,16},{1,17},{2,18},{3,19},{4,20},{5,21},{6,22},{7,23},{8,24},{9,... | collective-permute-start | bytes 294920 | tf_op jit(solution)/shard_map/ppermute | solution.py:293
  38.0 5.5 %collective-permute-done.16.rest_3_ = f32[32,512]{1,0:T(8,128)S(1)} collective-permute-done((f32[32,512]{1,0:T(8,128)S(1)}, f32[32,512]{1,0:T(8,128)S(1)}, u32[]{:S(2)}, u32[]{:S(2)}) %collective-permute-start.16) | collective-permute-done | bytes 65568 | tf_op jit(solution)/shard_map/ppermute | solution.py:293
  43.8 3.2 %collective-permute-start.18 = (bf16[32,1280]{1,0:T(8,128)(2,1)S(1)}, bf16[32,1280]{1,0:T(8,128)(2,1)S(1)}, u32[]{:S(2)}, u32[]{:S(2)}) collective-permute-start(bf16[32,1280]{1,0:T(8,128)(2,1)S(1)} %whiten.1), channel_id=1, source_target_pairs={{0,16},{1,17},{2,18},{3,19},{4,20},{5,21},{6,22},{7,23},{8,24},{9,... | collective-permute-start | bytes 245768 | tf_op jit(solution)/shard_map/ppermute | solution.py:293
  46.9 1.2 %collective-permute-start.19 = (bf16[32,1280]{1,0:T(8,128)(2,1)S(1)}, bf16[32,1280]{1,0:T(8,128)(2,1)S(1)}, u32[]{:S(2)}, u32[]{:S(2)}) collective-permute-start(bf16[32,1280]{1,0:T(8,128)(2,1)S(1)} %whiten.1), channel_id=1, source_target_pairs={{0,24},{1,25},{2,26},{3,27},{4,28},{5,29},{6,30},{7,31},{8,16},{9,... | collective-permute-start | bytes 245768 | tf_op jit(solution)/shard_map/ppermute | solution.py:293
  48.1 1.1 %collective-permute-done.17 = bf16[32,1280]{1,0:T(8,128)(2,1)S(1)} collective-permute-done((bf16[32,1280]{1,0:T(8,128)(2,1)S(1)}, bf16[32,1280]{1,0:T(8,128)(2,1)S(1)}, u32[]{:S(2)}, u32[]{:S(2)}) %collective-permute-start.17) | collective-permute-done | bytes 81952 | tf_op jit(solution)/shard_map/ppermute | solution.py:293
  49.3 4.5 %collective-permute-done.18 = bf16[32,1280]{1,0:T(8,128)(2,1)S(1)} collective-permute-done((bf16[32,1280]{1,0:T(8,128)(2,1)S(1)}, bf16[32,1280]{1,0:T(8,128)(2,1)S(1)}, u32[]{:S(2)}, u32[]{:S(2)}) %collective-permute-start.18) | collective-permute-done | bytes 81952 | tf_op jit(solution)/shard_map/ppermute | solution.py:293
  53.9 1.0 %collective-permute-start.23 = (bf16[4,32,1280]{2,1,0:T(8,128)(2,1)S(1)}, bf16[4,32,1280]{2,1,0:T(8,128)(2,1)S(1)}, u32[]{:S(2)}, u32[]{:S(2)}) collective-permute-start(bf16[4,32,1280]{2,1,0:T(8,128)(2,1)S(1)} %pad_maximum_fusion.rest_0_), channel_id=1, source_target_pairs={{0,4},{1,5},{2,6},{3,7},{4,0},{5,1},{6,2},{7,3},{8,12},{9,13},{10,... | collective-permute-start | bytes 983048 | tf_op jit(solution)/shard_map/ppermute | solution.py:293
  54.9 2.5 %collective-permute-start.25 = (bf16[4,32,1280]{2,1,0:T(8,128)(2,1)S(1)}, bf16[4,32,1280]{2,1,0:T(8,128)(2,1)S(1)}, u32[]{:S(2)}, u32[]{:S(2)}) collective-permute-start(bf16[4,32,1280]{2,1,0:T(8,128)(2,1)S(1)} %pad_maximum_fusion.rest_0_), channel_id=1, source_target_pairs={{0,6},{1,7},{2,4},{3,5},{4,2},{5,3},{6,0},{7,1},{8,14},{9,15},{10,... | collective-permute-start | bytes 983048 | tf_op jit(solution)/shard_map/ppermute | solution.py:293
  57.3 7.2 %collective-permute-done.21.rest_2_ = bf16[4,32,1280]{2,1,0:T(8,128)(2,1)S(1)} collective-permute-done((bf16[4,32,1280]{2,1,0:T(8,128)(2,1)S(1)}, bf16[4,32,1280]{2,1,0:T(8,128)(2,1)S(1)}, u32[]{:S(2)}, u32[]{:S(2)}) %collective-permute-start.21) | collective-permute-done | bytes 327712 | tf_op jit(solution)/shard_map/ppermute | solution.py:293
  64.5 3.6 %collective-permute-done.23.rest_4_ = bf16[4,32,1280]{2,1,0:T(8,128)(2,1)S(1)} collective-permute-done((bf16[4,32,1280]{2,1,0:T(8,128)(2,1)S(1)}, bf16[4,32,1280]{2,1,0:T(8,128)(2,1)S(1)}, u32[]{:S(2)}, u32[]{:S(2)}) %collective-permute-start.23) | collective-permute-done | bytes 327712 | tf_op jit(solution)/shard_map/ppermute | solution.py:293
  70.2 5.7 %correlate.1 = f32[64,4,1001]{2,1,0:T(4,128)} custom-call(s32[1]{0:T(128)} %bitcast.place_ref, f32[8,4]{1,0:T(8,128)S(1)} %convert_element_type.3.flags_ref, s32[64,1]{1,0:T(8,128)S(1)} %copy.8.ids_ref, bf16[174080,128]{1,0:T(8,128)(2,1)} %constant.133.clone.table_ref, bf16[4,32,1280]{2,1,0:T(8,128)(2,1)S(1)} %pad_maximum_fusion.rest_0_, ...), custom_call_target="tpu_custom_call" | custom-call | tf_op jit(solution)/shard_map/correlate/pallas_call | solution.py:259
  (47 shorter events, 6.9 us)
Async XLA Ops:
  1.3 8.9 %collective-permute-start.10 = (bf16[64,512]{1,0:T(8,128)(2,1)S(1)}, bf16[64,512]{1,0:T(8,128)(2,1)S(1)}, u32[]{:S(2)}, u32[]{:S(2)}) collective-permute-start(bf16[64,512]{1,0:T(8,128)(2,1)S(1)} %get-tuple-element.17), channel_id=1, source_target_pairs={{0,2},{1,3},{2,0},{3,1},{4,6},{5,7},{6,4},{7,5},{8,10},{9,11},{10,... | collective-permute-start | bytes 196616 | tf_op jit(solution)/shard_map/ppermute | solution.py:293
  4.3 7.5 %collective-permute-start.11 = (bf16[64,512]{1,0:T(8,128)(2,1)S(1)}, bf16[64,512]{1,0:T(8,128)(2,1)S(1)}, u32[]{:S(2)}, u32[]{:S(2)}) collective-permute-start(bf16[64,512]{1,0:T(8,128)(2,1)S(1)} %get-tuple-element.16), channel_id=1, source_target_pairs={{0,12},{1,13},{2,14},{3,15},{4,8},{5,9},{6,10},{7,11},{8,4},{9,5},... | collective-permute-start | bytes 196616 | tf_op jit(solution)/shard_map/ppermute | solution.py:293
  6.8 5.8 %collective-permute-start.12 = (bf16[64,512]{1,0:T(8,128)(2,1)S(1)}, bf16[64,512]{1,0:T(8,128)(2,1)S(1)}, u32[]{:S(2)}, u32[]{:S(2)}) collective-permute-start(bf16[64,512]{1,0:T(8,128)(2,1)S(1)} %get-tuple-element.15), channel_id=1, source_target_pairs={{0,4},{1,5},{2,6},{3,7},{4,0},{5,1},{6,2},{7,3},{8,12},{9,13},{10,... | collective-permute-start | bytes 196616 | tf_op jit(solution)/shard_map/ppermute | solution.py:293
  7.4 5.3 %collective-permute-start.13 = (bf16[64,512]{1,0:T(8,128)(2,1)S(1)}, bf16[64,512]{1,0:T(8,128)(2,1)S(1)}, u32[]{:S(2)}, u32[]{:S(2)}) collective-permute-start(bf16[64,512]{1,0:T(8,128)(2,1)S(1)} %get-tuple-element.14), channel_id=1, source_target_pairs={{0,10},{1,11},{2,8},{3,9},{4,14},{5,15},{6,12},{7,13},{8,2},{9,3},... | collective-permute-start | bytes 196616 | tf_op jit(solution)/shard_map/ppermute | solution.py:293
  7.4 8.5 %collective-permute-start.14 = (bf16[64,512]{1,0:T(8,128)(2,1)S(1)}, bf16[64,512]{1,0:T(8,128)(2,1)S(1)}, u32[]{:S(2)}, u32[]{:S(2)}) collective-permute-start(bf16[64,512]{1,0:T(8,128)(2,1)S(1)} %get-tuple-element.13), channel_id=1, source_target_pairs={{0,6},{1,7},{2,4},{3,5},{4,2},{5,3},{6,0},{7,1},{8,14},{9,15},{10,... | collective-permute-start | bytes 196616 | tf_op jit(solution)/shard_map/ppermute | solution.py:293
  10.2 5.7 %collective-permute-start.8 = (bf16[64,512]{1,0:T(8,128)(2,1)S(1)}, bf16[64,512]{1,0:T(8,128)(2,1)S(1)}, u32[]{:S(2)}, u32[]{:S(2)}) collective-permute-start(bf16[64,512]{1,0:T(8,128)(2,1)S(1)} %get-tuple-element.19), channel_id=1, source_target_pairs={{0,8},{1,9},{2,10},{3,11},{4,12},{5,13},{6,14},{7,15},{8,0},{9,1},... | collective-permute-start | bytes 196616 | tf_op jit(solution)/shard_map/ppermute | solution.py:293
  11.8 7.4 %collective-permute-start.9 = (bf16[64,512]{1,0:T(8,128)(2,1)S(1)}, bf16[64,512]{1,0:T(8,128)(2,1)S(1)}, u32[]{:S(2)}, u32[]{:S(2)}) collective-permute-start(bf16[64,512]{1,0:T(8,128)(2,1)S(1)} %get-tuple-element.18), channel_id=1, source_target_pairs={{0,14},{1,15},{2,12},{3,13},{4,10},{5,11},{6,8},{7,9},{8,6},{9,7},... | collective-permute-start | bytes 196616 | tf_op jit(solution)/shard_map/ppermute | solution.py:293
  12.6 6.6 %collective-permute-start = (bf16[64,512]{1,0:T(8,128)(2,1)S(1)}, bf16[64,512]{1,0:T(8,128)(2,1)S(1)}, u32[]{:S(2)}, u32[]{:S(2)}) collective-permute-start(bf16[64,512]{1,0:T(8,128)(2,1)S(1)} %get-tuple-element.27), channel_id=1, source_target_pairs={{0,3},{1,2},{2,1},{3,0},{4,7},{5,6},{6,5},{7,4},{8,11},{9,10},{10,... | collective-permute-start | bytes 196616 | tf_op jit(solution)/shard_map/ppermute | solution.py:293
  12.7 7.7 %collective-permute-start.1 = (bf16[64,512]{1,0:T(8,128)(2,1)S(1)}, bf16[64,512]{1,0:T(8,128)(2,1)S(1)}, u32[]{:S(2)}, u32[]{:S(2)}) collective-permute-start(bf16[64,512]{1,0:T(8,128)(2,1)S(1)} %get-tuple-element.26), channel_id=1, source_target_pairs={{0,13},{1,12},{2,15},{3,14},{4,9},{5,8},{6,11},{7,10},{8,5},{9,4},... | collective-permute-start | bytes 196616 | tf_op jit(solution)/shard_map/ppermute | solution.py:293
  15.9 5.2 %collective-permute-start.2 = (bf16[64,512]{1,0:T(8,128)(2,1)S(1)}, bf16[64,512]{1,0:T(8,128)(2,1)S(1)}, u32[]{:S(2)}, u32[]{:S(2)}) collective-permute-start(bf16[64,512]{1,0:T(8,128)(2,1)S(1)} %get-tuple-element.25), channel_id=1, source_target_pairs={{0,5},{1,4},{2,7},{3,6},{4,1},{5,0},{6,3},{7,2},{8,13},{9,12},{10,... | collective-permute-start | bytes 196616 | tf_op jit(solution)/shard_map/ppermute | solution.py:293
  15.9 15.9 %collective-permute-start.3 = (bf16[64,512]{1,0:T(8,128)(2,1)S(1)}, bf16[64,512]{1,0:T(8,128)(2,1)S(1)}, u32[]{:S(2)}, u32[]{:S(2)}) collective-permute-start(bf16[64,512]{1,0:T(8,128)(2,1)S(1)} %get-tuple-element.24), channel_id=1, source_target_pairs={{0,11},{1,10},{2,9},{3,8},{4,15},{5,14},{6,13},{7,12},{8,3},{9,2},... | collective-permute-start | bytes 196616 | tf_op jit(solution)/shard_map/ppermute | solution.py:293
  19.2 12.6 %collective-permute-start.4 = (bf16[64,512]{1,0:T(8,128)(2,1)S(1)}, bf16[64,512]{1,0:T(8,128)(2,1)S(1)}, u32[]{:S(2)}, u32[]{:S(2)}) collective-permute-start(bf16[64,512]{1,0:T(8,128)(2,1)S(1)} %get-tuple-element.23), channel_id=1, source_target_pairs={{0,7},{1,6},{2,5},{3,4},{4,3},{5,2},{6,1},{7,0},{8,15},{9,14},{10,... | collective-permute-start | bytes 196616 | tf_op jit(solution)/shard_map/ppermute | solution.py:293
  19.2 12.6 %collective-permute-start.5 = (bf16[64,512]{1,0:T(8,128)(2,1)S(1)}, bf16[64,512]{1,0:T(8,128)(2,1)S(1)}, u32[]{:S(2)}, u32[]{:S(2)}) collective-permute-start(bf16[64,512]{1,0:T(8,128)(2,1)S(1)} %get-tuple-element.22), channel_id=1, source_target_pairs={{0,9},{1,8},{2,11},{3,10},{4,13},{5,12},{6,15},{7,14},{8,1},{9,0},... | collective-permute-start | bytes 196616 | tf_op jit(solution)/shard_map/ppermute | solution.py:293
  20.3 11.5 %collective-permute-start.6 = (bf16[64,512]{1,0:T(8,128)(2,1)S(1)}, bf16[64,512]{1,0:T(8,128)(2,1)S(1)}, u32[]{:S(2)}, u32[]{:S(2)}) collective-permute-start(bf16[64,512]{1,0:T(8,128)(2,1)S(1)} %get-tuple-element.21), channel_id=1, source_target_pairs={{0,15},{1,14},{2,13},{3,12},{4,11},{5,10},{6,9},{7,8},{8,7},{9,6},... | collective-permute-start | bytes 196616 | tf_op jit(solution)/shard_map/ppermute | solution.py:293
  21.1 10.8 %collective-permute-start.7 = (bf16[64,512]{1,0:T(8,128)(2,1)S(1)}, bf16[64,512]{1,0:T(8,128)(2,1)S(1)}, u32[]{:S(2)}, u32[]{:S(2)}) collective-permute-start(bf16[64,512]{1,0:T(8,128)(2,1)S(1)} %get-tuple-element.20), channel_id=1, source_target_pairs={{0,1},{1,0},{2,3},{3,2},{4,5},{5,4},{6,7},{7,6},{8,9},{9,8},{10,11... | collective-permute-start | bytes 196616 | tf_op jit(solution)/shard_map/ppermute | solution.py:293
  33.1 10.5 %collective-permute-start.15 = (f32[32,768]{1,0:T(8,128)S(1)}, f32[32,768]{1,0:T(8,128)S(1)}, u32[]{:S(2)}, u32[]{:S(2)}) collective-permute-start(f32[32,768]{1,0:T(8,128)S(1)} %get-tuple-element.10), channel_id=1, source_target_pairs={{0,16},{1,17},{2,18},{3,19},{4,20},{5,21},{6,22},{7,23},{8,24},{9,... | collective-permute-start | bytes 294920 | tf_op jit(solution)/shard_map/ppermute | solution.py:293
  37.5 6.1 %collective-permute-start.16 = (f32[32,512]{1,0:T(8,128)S(1)}, f32[32,512]{1,0:T(8,128)S(1)}, u32[]{:S(2)}, u32[]{:S(2)}) collective-permute-start(f32[32,512]{1,0:T(8,128)S(1)} %get-tuple-element.12), channel_id=1, source_target_pairs={{0,16},{1,17},{2,18},{3,19},{4,20},{5,21},{6,22},{7,23},{8,24},{9,... | collective-permute-start | bytes 196616 | tf_op jit(solution)/shard_map/ppermute | solution.py:293
  43.7 5.6 %collective-permute-start.17 = (bf16[32,1280]{1,0:T(8,128)(2,1)S(1)}, bf16[32,1280]{1,0:T(8,128)(2,1)S(1)}, u32[]{:S(2)}, u32[]{:S(2)}) collective-permute-start(bf16[32,1280]{1,0:T(8,128)(2,1)S(1)} %whiten.1), channel_id=1, source_target_pairs={{0,8},{1,9},{2,10},{3,11},{4,12},{5,13},{6,14},{7,15},{8,0},{9,1},... | collective-permute-start | bytes 245768 | tf_op jit(solution)/shard_map/ppermute | solution.py:293
  43.8 10.0 %collective-permute-start.18 = (bf16[32,1280]{1,0:T(8,128)(2,1)S(1)}, bf16[32,1280]{1,0:T(8,128)(2,1)S(1)}, u32[]{:S(2)}, u32[]{:S(2)}) collective-permute-start(bf16[32,1280]{1,0:T(8,128)(2,1)S(1)} %whiten.1), channel_id=1, source_target_pairs={{0,16},{1,17},{2,18},{3,19},{4,20},{5,21},{6,22},{7,23},{8,24},{9,... | collective-permute-start | bytes 245768 | tf_op jit(solution)/shard_map/ppermute | solution.py:293
  46.9 6.8 %collective-permute-start.19 = (bf16[32,1280]{1,0:T(8,128)(2,1)S(1)}, bf16[32,1280]{1,0:T(8,128)(2,1)S(1)}, u32[]{:S(2)}, u32[]{:S(2)}) collective-permute-start(bf16[32,1280]{1,0:T(8,128)(2,1)S(1)} %whiten.1), channel_id=1, source_target_pairs={{0,24},{1,25},{2,26},{3,27},{4,28},{5,29},{6,30},{7,31},{8,16},{9,... | collective-permute-start | bytes 245768 | tf_op jit(solution)/shard_map/ppermute | solution.py:293
  53.8 10.7 %collective-permute-start.21 = (bf16[4,32,1280]{2,1,0:T(8,128)(2,1)S(1)}, bf16[4,32,1280]{2,1,0:T(8,128)(2,1)S(1)}, u32[]{:S(2)}, u32[]{:S(2)}) collective-permute-start(bf16[4,32,1280]{2,1,0:T(8,128)(2,1)S(1)} %pad_maximum_fusion.rest_0_), channel_id=1, source_target_pairs={{0,2},{1,3},{2,0},{3,1},{4,6},{5,7},{6,4},{7,5},{8,10},{9,11},{10,... | collective-permute-start | bytes 983048 | tf_op jit(solution)/shard_map/ppermute | solution.py:293
  53.9 14.2 %collective-permute-start.23 = (bf16[4,32,1280]{2,1,0:T(8,128)(2,1)S(1)}, bf16[4,32,1280]{2,1,0:T(8,128)(2,1)S(1)}, u32[]{:S(2)}, u32[]{:S(2)}) collective-permute-start(bf16[4,32,1280]{2,1,0:T(8,128)(2,1)S(1)} %pad_maximum_fusion.rest_0_), channel_id=1, source_target_pairs={{0,4},{1,5},{2,6},{3,7},{4,0},{5,1},{6,2},{7,3},{8,12},{9,13},{10,... | collective-permute-start | bytes 983048 | tf_op jit(solution)/shard_map/ppermute | solution.py:293
  54.9 13.2 %collective-permute-start.25 = (bf16[4,32,1280]{2,1,0:T(8,128)(2,1)S(1)}, bf16[4,32,1280]{2,1,0:T(8,128)(2,1)S(1)}, u32[]{:S(2)}, u32[]{:S(2)}) collective-permute-start(bf16[4,32,1280]{2,1,0:T(8,128)(2,1)S(1)} %pad_maximum_fusion.rest_0_), channel_id=1, source_target_pairs={{0,6},{1,7},{2,4},{3,5},{4,2},{5,3},{6,0},{7,1},{8,14},{9,15},{10,... | collective-permute-start | bytes 983048 | tf_op jit(solution)/shard_map/ppermute | solution.py:293
  57.3 11.4 %collective-permute-start.20 = (bf16[4,32,1280]{2,1,0:T(8,128)(2,1)S(1)}, bf16[4,32,1280]{2,1,0:T(8,128)(2,1)S(1)}, u32[]{:S(2)}, u32[]{:S(2)}) collective-permute-start(bf16[4,32,1280]{2,1,0:T(8,128)(2,1)S(1)} %pad_maximum_fusion.rest_0_), channel_id=1, source_target_pairs={{0,1},{1,0},{2,3},{3,2},{4,5},{5,4},{6,7},{7,6},{8,9},{9,8},{10,11... | collective-permute-start | bytes 983048 | tf_op jit(solution)/shard_map/ppermute | solution.py:293
  (5 other events, 53.2 us)

commit v3 on v1

--- a/solution.py
+++ b/solution.py
@@ -25,6 +25,8 @@
 BLOCK = 512
 SHARES = 2
 FIRST_TILES = 6
+LINE_TILES = 7
+SPLIT = LINE_TILES * 128
 FLAG_TILE = BAND // 128 * 128
 FLAG_LANE = BAND - FLAG_TILE
 
@@ -121,19 +123,16 @@
 
 
 def whiten_kernel(flags_ref, *rest):
-    parts, white_ref = rest[:-1], rest[-1]
+    parts, (first_ref, second_ref) = rest[:-2], rest[-2:]
     sums = [mine[...] + other[...] for mine, other in zip(parts[::2], parts[1::2])]
     total = jnp.concatenate(sums, axis=1)
     real_part, imag_part = total[:, :PART], total[:, PART:]
     power = real_part * real_part + imag_part * imag_part
     level = jnp.sum(power, axis=1, keepdims=True) * (1.0 / BAND)
     factor = lax.rsqrt(power + floor_share * level + epsilon)
-    white_ref[:, :PART] = (real_part * factor).astype(jnp.bfloat16)
-    white_ref[:, PART:] = (imag_part * factor).astype(jnp.bfloat16)
-    rows = total.shape[0]
-    lane = lax.broadcasted_iota(jnp.int32, (rows, 128), 1)
+    real_part, imag_part = real_part * factor, imag_part * factor
+    lane = lax.broadcasted_iota(jnp.int32, (total.shape[0], 128), 1)
     held = (lane >= FLAG_LANE) & (lane < FLAG_LANE + flags_ref.shape[1])
-    tile = (real_part * factor)[:, FLAG_TILE : FLAG_TILE + 128]
     flags = jnp.concatenate(
         [
             jnp.zeros((1, FLAG_LANE), jnp.float32),
@@ -142,19 +141,27 @@
         ],
         axis=1,
     )
-    white_ref[:, FLAG_TILE : FLAG_TILE + 128] = jnp.where(held, flags, tile).astype(jnp.bfloat16)
+    tail = jnp.where(held, flags, real_part[:, FLAG_TILE:])
+    white = jnp.concatenate([real_part[:, :FLAG_TILE], tail, imag_part], axis=1)
+    white = white.astype(jnp.bfloat16)
+    first_ref[...] = white[:, :SPLIT]
+    second_ref[...] = white[:, SPLIT:]
 
 
 def whiten(flags, parts):
+    rows = parts[0].shape[0]
     return pl.pallas_call(
         whiten_kernel,
-        out_shape=jax.ShapeDtypeStruct((parts[0].shape[0], WIDTH), jnp.bfloat16),
+        out_shape=[
+            jax.ShapeDtypeStruct((rows, SPLIT), jnp.bfloat16),
+            jax.ShapeDtypeStruct((rows, WIDTH - SPLIT), jnp.bfloat16),
+        ],
         compiler_params=pltpu.CompilerParams(vmem_limit_bytes=16 * 2**20),
         name="whiten",
     )(flags, *parts)
 
 
-def correlate_kernel(segments, channels, shares, place_ref, flags_ref, ids_ref, table_ref, *rest):
+def correlate_kernel(segments, channels, shares, steps, place_ref, flags_ref, ids_ref, table_ref, *rest):
     blocks, rest = rest[:-7], rest[-7:]
     out_ref, held_ref, inverse_ref, panel_ref, receivers_ref, stacked_ref, sem = rest
     lines = inverse_ref.shape[0]
@@ -172,9 +179,10 @@
     def position(device):
         return device % members * shares + device // members
 
-    for index, block in enumerate(blocks):
+    for (step, stride), block in zip(steps, blocks):
+        columns = slice(0, SPLIT) if block.shape[2] == SPLIT else slice(SPLIT, WIDTH)
         for line in range(block.shape[0]):
-            held_ref[position(place ^ (line * len(blocks) + index))] = block[line]
+            held_ref[position(place ^ (line * stride + step)), :, columns] = block[line]
 
     tails = held_ref[:, :, FLAG_TILE : FLAG_TILE + 128].reshape(devices * rows, 128)
     column = lax.broadcasted_iota(jnp.int32, (sources, devices * rows), 1)
@@ -225,15 +233,14 @@
         out_ref[:, c, :] = lags[c * sources : (c + 1) * sources, :LAGS]
 
 
-def correlate(place, weights, source_ids, table, blocks, segments, channels, shares):
-    far, rows, _ = blocks[0].shape
-    devices = far * len(blocks)
+def correlate(place, weights, source_ids, table, steps, blocks, segments, channels, devices):
+    rows = blocks[0].shape[1]
     ch_local = channels // devices
     sources = source_ids.shape[0]
     smem = pl.BlockSpec(memory_space=pltpu.SMEM)
     vmem = pl.BlockSpec(memory_space=pltpu.VMEM)
     return pl.pallas_call(
-        functools.partial(correlate_kernel, segments, channels, shares),
+        functools.partial(correlate_kernel, segments, channels, SHARES, steps),
         in_specs=[smem, smem, vmem, pl.BlockSpec(memory_space=pltpu.HBM)] + [vmem] * len(blocks),
         out_specs=vmem,
         out_shape=jax.ShapeDtypeStruct((sources, ch_local, LAGS), jnp.float32),
@@ -272,21 +279,27 @@
     for first, last in ((0, FIRST_TILES), (FIRST_TILES, WIDTH // 128)):
         own, other = transform(share, regrouped, table, first, last)
         parts += [own, exchange(other, members)]
-    white = whiten(weights.reshape(1, -1), parts)
-
-    far = devices // 8
-    line = jnp.stack([white] + [exchange(white, 8 * k) for k in range(1, far)])
-    plane = [line] + [exchange(line, 2 * k) for k in range(1, 4)]
-    blocks = [b for block in plane for b in (block, exchange(block, 1))]
+    first, second = whiten(weights.reshape(1, -1), parts)
+
+    far, near = [8 * k for k in range(devices // 8)], [2 * k for k in range(4)]
+    line = jnp.stack([exchange(first, step) if step else first for step in far])
+    plane = jnp.stack([exchange(second, step) if step else second for step in near])
+    steps, blocks = [], []
+    for stacked, stride, others in ((line, 8, near), (plane, 2, far)):
+        for step in others:
+            block = exchange(stacked, step) if step else stacked
+            blocks += [block, exchange(block, 1)]
+            steps += [(step, stride), (step + 1, stride)]
     return correlate(
         place.reshape(1),
         weights,
         source_ids,
         table,
+        steps,
         blocks,
         segments,
         channels,
-        SHARES,
+        devices,
     )
 
 

time: 73.4 us -> 73 us (level)
  waiting for transfers between devices: 40.3 us -> 32.5 us
  starting transfers between devices: 17.9 us -> 25.2 us
    ppermute x12 -> x22, waiting for transfers between devices: 24.2 us -> 16.3 us  [exchange(): return lax.ppermute(block, 'chan', [(i, i ^ bits) for i in range(devices)])]
    ppermute x12 -> x22, starting transfers between devices: 11.6 us -> 18.9 us  [exchange(): return lax.ppermute(block, 'chan', [(i, i ^ bits) for i in range(devices)])]
  transfers between devices with their start and end apart: 13 -> 23, of which waited for: 8 -> 8; matrix products, arithmetic and copies ran while one was open for 0% -> 0% of each run, Pallas kernels for 5% -> 5%
where the time goes in v3:
time: 73 us; the launch traced here: 72.7 us
  waiting for transfers between devices  32.5 us (45%)
  starting transfers between devices  25.2 us (35%)
  Pallas kernels  14.7 us (20%)
    ppermute x22, starting transfers between devices, exchange(): return lax.ppermute(block, 'chan', [(i, i ^ bits) for i in range(devices)])  18.9 us
    ppermute x22, waiting for transfers between devices, exchange(): return lax.ppermute(block, 'chan', [(i, i ^ bits) for i in range(devices)])  16.3 us
    all_to_all x1, waiting for transfers between devices, per_device(): lax.all_to_all(grouped, 'chan', split_axis=0, concat_axis=0, axis_index_g...  16.2 us
    pallas_call x2, Pallas kernels, transform(): pl.pallas_call(functools.partial(transform_kernel, first), in_specs=[pl.B...  8.75 us
    all_to_all x1, starting transfers between devices, per_device(): lax.all_to_all(grouped, 'chan', split_axis=0, concat_axis=0, axis_index_g...  6.29 us
    pallas_call x1, Pallas kernels, correlate(): pl.pallas_call(functools.partial(correlate_kernel, segments, channels, SH...  5.8 us
  transfers between devices with their start and end apart: 23, of which 8 were waited for; matrix products, arithmetic and copies ran while one was open for 0% of the time, Pallas kernels for 5%

profile of v3, /device:TPU:0, one launch (start us, length us, event | category | flops | bytes accessed | tf_op | source)
XLA Modules:
  0.0 72.7 jit_solution(16307832360420999338)
XLA Ops:
  0.0 6.3 %all-to-all-start = ((bf16[16,64,512]{2,1,0:T(8,128)(2,1)}), bf16[16,64,512]{2,1,0:T(8,128)(2,1)S(1)}, u32[]{:S(2)}, u32[]{:S(2)}) async-start(bf16[16,64,512]{2,1,0:T(8,128)(2,1)} %bitcast.14), calls=%async_computation | async-start | bytes 2097152 | tf_op jit(solution)/shard_map/all_to_all | solution.py:274
  6.3 16.2 %all-to-all-done.records_ref = bf16[16,64,512]{2,1,0:T(8,128)(2,1)S(1)} async-done(((bf16[16,64,512]{2,1,0:T(8,128)(2,1)}), bf16[16,64,512]{2,1,0:T(8,128)(2,1)S(1)}, u32[]{:S(2)}, u32[]{:S(2)}) %all-to-all-start) | async-done | bytes 1048608 | tf_op jit(solution)/shard_map/all_to_all | solution.py:274
  22.5 5.0 %transform.2 = (f32[32,768]{1,0:T(8,128)S(1)}, f32[32,768]{1,0:T(8,128)S(1)}) custom-call(s32[1]{0:T(128)} %bitcast.2.share_ref, bf16[16,64,512]{2,1,0:T(8,128)(2,1)S(1)} %all-to-all-done.records_ref, bf16[174080,128]{1,0:T(8,128)(2,1)} %constant.22.clone.table_ref), custom_call_target="tpu_custom_call" | custom-call | flops 805306368 | bytes 12582912 | tf_op jit(solution)/shard_map/transform/pallas_call | solution.py:102
  27.5 2.7 %collective-permute-start = (f32[32,768]{1,0:T(8,128)S(1)}, f32[32,768]{1,0:T(8,128)S(1)}, u32[]{:S(2)}, u32[]{:S(2)}) collective-permute-start(f32[32,768]{1,0:T(8,128)S(1)} %get-tuple-element.12), channel_id=1, source_target_pairs={{0,16},{1,17},{2,18},{3,19},{4,20},{5,21},{6,22},{7,23},{8,24},{9,... | collective-permute-start | bytes 294920 | tf_op jit(solution)/shard_map/ppermute | solution.py:269
  30.2 3.7 %transform.3 = (f32[32,512]{1,0:T(8,128)S(1)}, f32[32,512]{1,0:T(8,128)S(1)}) custom-call(s32[1]{0:T(128)} %bitcast.2.share_ref, bf16[16,64,512]{2,1,0:T(8,128)(2,1)S(1)} %all-to-all-done.records_ref, bf16[174080,128]{1,0:T(8,128)(2,1)} %constant.22.clone.table_ref), custom_call_target="tpu_custom_call" | custom-call | flops 536870912 | bytes 8388608 | tf_op jit(solution)/shard_map/transform/pallas_call | solution.py:102
  33.9 0.4 collective-permute-start.1
  34.5 5.4 %collective-permute-done.1.rest_3_ = f32[32,512]{1,0:T(8,128)S(1)} collective-permute-done((f32[32,512]{1,0:T(8,128)S(1)}, f32[32,512]{1,0:T(8,128)S(1)}, u32[]{:S(2)}, u32[]{:S(2)}) %collective-permute-start.1) | collective-permute-done | bytes 65568 | tf_op jit(solution)/shard_map/ppermute | solution.py:269
  40.0 1.5 %collective-permute-start.14 = (bf16[32,384]{1,0:T(8,128)(2,1)S(1)}, bf16[32,384]{1,0:T(8,128)(2,1)S(1)}, u32[]{:S(2)}, u32[]{:S(2)}) collective-permute-start(bf16[32,384]{1,0:T(8,128)(2,1)S(1)} %get-tuple-element.16), channel_id=1, source_target_pairs={{0,6},{1,7},{2,4},{3,5},{4,2},{5,3},{6,0},{7,1},{8,14},{9,15},{10,... | collective-permute-start | bytes 73736 | tf_op jit(solution)/shard_map/ppermute | solution.py:269
  41.8 1.7 %collective-permute-start.12 = (bf16[32,384]{1,0:T(8,128)(2,1)S(1)}, bf16[32,384]{1,0:T(8,128)(2,1)S(1)}, u32[]{:S(2)}, u32[]{:S(2)}) collective-permute-start(bf16[32,384]{1,0:T(8,128)(2,1)S(1)} %get-tuple-element.16), channel_id=1, source_target_pairs={{0,2},{1,3},{2,0},{3,1},{4,6},{5,7},{6,4},{7,5},{8,10},{9,11},{10,... | collective-permute-start | bytes 73736 | tf_op jit(solution)/shard_map/ppermute | solution.py:269
  43.5 1.5 %collective-permute-start.3 = (bf16[32,896]{1,0:T(8,128)(2,1)S(1)}, bf16[32,896]{1,0:T(8,128)(2,1)S(1)}, u32[]{:S(2)}, u32[]{:S(2)}) collective-permute-start(bf16[32,896]{1,0:T(8,128)(2,1)S(1)} %get-tuple-element.15), channel_id=1, source_target_pairs={{0,16},{1,17},{2,18},{3,19},{4,20},{5,21},{6,22},{7,23},{8,24},{9,... | collective-permute-start | bytes 172040 | tf_op jit(solution)/shard_map/ppermute | solution.py:269
  45.0 2.9 %collective-permute-start.2 = (bf16[32,896]{1,0:T(8,128)(2,1)S(1)}, bf16[32,896]{1,0:T(8,128)(2,1)S(1)}, u32[]{:S(2)}, u32[]{:S(2)}) collective-permute-start(bf16[32,896]{1,0:T(8,128)(2,1)S(1)} %get-tuple-element.15), channel_id=1, source_target_pairs={{0,8},{1,9},{2,10},{3,11},{4,12},{5,13},{6,14},{7,15},{8,0},{9,1},... | collective-permute-start | bytes 172040 | tf_op jit(solution)/shard_map/ppermute | solution.py:269
  48.0 2.2 %collective-permute-done.4 = bf16[32,896]{1,0:T(8,128)(2,1)S(1)} collective-permute-done((bf16[32,896]{1,0:T(8,128)(2,1)S(1)}, bf16[32,896]{1,0:T(8,128)(2,1)S(1)}, u32[]{:S(2)}, u32[]{:S(2)}) %collective-permute-start.4) | collective-permute-done | bytes 57376 | tf_op jit(solution)/shard_map/ppermute | solution.py:269
  50.2 1.3 %collective-permute-done.3 = bf16[32,896]{1,0:T(8,128)(2,1)S(1)} collective-permute-done((bf16[32,896]{1,0:T(8,128)(2,1)S(1)}, bf16[32,896]{1,0:T(8,128)(2,1)S(1)}, u32[]{:S(2)}, u32[]{:S(2)}) %collective-permute-start.3) | collective-permute-done | bytes 57376 | tf_op jit(solution)/shard_map/ppermute | solution.py:269
  51.6 2.5 %collective-permute-start.10 = (bf16[4,32,896]{2,1,0:T(8,128)(2,1)S(1)}, bf16[4,32,896]{2,1,0:T(8,128)(2,1)S(1)}, u32[]{:S(2)}, u32[]{:S(2)}) collective-permute-start(bf16[4,32,896]{2,1,0:T(8,128)(2,1)S(1)} %pad_maximum_fusion.rest_0_), channel_id=1, source_target_pairs={{0,6},{1,7},{2,4},{3,5},{4,2},{5,3},{6,0},{7,1},{8,14},{9,15},{10,... | collective-permute-start | bytes 688136 | tf_op jit(solution)/shard_map/ppermute | solution.py:269
  54.4 0.8 %collective-permute-start.6 = (bf16[4,32,896]{2,1,0:T(8,128)(2,1)S(1)}, bf16[4,32,896]{2,1,0:T(8,128)(2,1)S(1)}, u32[]{:S(2)}, u32[]{:S(2)}) collective-permute-start(bf16[4,32,896]{2,1,0:T(8,128)(2,1)S(1)} %pad_maximum_fusion.rest_0_), channel_id=1, source_target_pairs={{0,2},{1,3},{2,0},{3,1},{4,6},{5,7},{6,4},{7,5},{8,10},{9,11},{10,... | collective-permute-start | bytes 688136 | tf_op jit(solution)/shard_map/ppermute | solution.py:269
  55.2 0.8 %collective-permute-start.18 = (bf16[4,32,384]{2,1,0:T(8,128)(2,1)S(1)}, bf16[4,32,384]{2,1,0:T(8,128)(2,1)S(1)}, u32[]{:S(2)}, u32[]{:S(2)}) collective-permute-start(bf16[4,32,384]{2,1,0:T(8,128)(2,1)S(1)} %pad_maximum_fusion.1.rest_8_), channel_id=1, source_target_pairs={{0,16},{1,17},{2,18},{3,19},{4,20},{5,21},{6,22},{7,23},{8,24},{9,... | collective-permute-start | bytes 294920 | tf_op jit(solution)/shard_map/ppermute | solution.py:269
  56.0 1.6 %collective-permute-start.16 = (bf16[4,32,384]{2,1,0:T(8,128)(2,1)S(1)}, bf16[4,32,384]{2,1,0:T(8,128)(2,1)S(1)}, u32[]{:S(2)}, u32[]{:S(2)}) collective-permute-start(bf16[4,32,384]{2,1,0:T(8,128)(2,1)S(1)} %pad_maximum_fusion.1.rest_8_), channel_id=1, source_target_pairs={{0,8},{1,9},{2,10},{3,11},{4,12},{5,13},{6,14},{7,15},{8,0},{9,1},... | collective-permute-start | bytes 294920 | tf_op jit(solution)/shard_map/ppermute | solution.py:269
  57.6 4.1 %collective-permute-done.18.rest_12_ = bf16[4,32,384]{2,1,0:T(8,128)(2,1)S(1)} collective-permute-done((bf16[4,32,384]{2,1,0:T(8,128)(2,1)S(1)}, bf16[4,32,384]{2,1,0:T(8,128)(2,1)S(1)}, u32[]{:S(2)}, u32[]{:S(2)}) %collective-permute-start.18) | collective-permute-done | bytes 98336 | tf_op jit(solution)/shard_map/ppermute | solution.py:269
  61.7 0.5 collective-permute-start.21
  62.2 0.8 %collective-permute-done.15.rest_9_ = bf16[4,32,384]{2,1,0:T(8,128)(2,1)S(1)} collective-permute-done((bf16[4,32,384]{2,1,0:T(8,128)(2,1)S(1)}, bf16[4,32,384]{2,1,0:T(8,128)(2,1)S(1)}, u32[]{:S(2)}, u32[]{:S(2)}) %collective-permute-start.15) | collective-permute-done | bytes 98336 | tf_op jit(solution)/shard_map/ppermute | solution.py:269
  63.1 0.4 collective-permute-start.11
  64.2 1.4 %collective-permute-done.19.rest_13_ = bf16[4,32,384]{2,1,0:T(8,128)(2,1)S(1)} collective-permute-done((bf16[4,32,384]{2,1,0:T(8,128)(2,1)S(1)}, bf16[4,32,384]{2,1,0:T(8,128)(2,1)S(1)}, u32[]{:S(2)}, u32[]{:S(2)}) %collective-permute-start.19) | collective-permute-done | bytes 98336 | tf_op jit(solution)/shard_map/ppermute | solution.py:269
  65.9 1.0 %collective-permute-done.17.rest_11_ = bf16[4,32,384]{2,1,0:T(8,128)(2,1)S(1)} collective-permute-done((bf16[4,32,384]{2,1,0:T(8,128)(2,1)S(1)}, bf16[4,32,384]{2,1,0:T(8,128)(2,1)S(1)}, u32[]{:S(2)}, u32[]{:S(2)}) %collective-permute-start.17) | collective-permute-done | bytes 98336 | tf_op jit(solution)/shard_map/ppermute | solution.py:269
  66.9 5.8 %correlate.1 = f32[64,4,1001]{2,1,0:T(4,128)} custom-call(s32[1]{0:T(128)} %bitcast.place_ref, f32[8,4]{1,0:T(8,128)S(1)} %convert_element_type.3.flags_ref, s32[64,1]{1,0:T(8,128)S(1)} %copy.8.ids_ref, bf16[174080,128]{1,0:T(8,128)(2,1)} %constant.22.clone.table_ref, bf16[4,32,896]{2,1,0:T(8,128)(2,1)S(1)} %pad_maximum_fusion.rest_0_, ...), custom_call_target="tpu_custom_call" | custom-call | tf_op jit(solution)/shard_map/correlate/pallas_call | solution.py:242
  (36 shorter events, 2.1 us)
Async XLA Ops:
  0.0 22.5 %all-to-all-start = ((bf16[16,64,512]{2,1,0:T(8,128)(2,1)}), bf16[16,64,512]{2,1,0:T(8,128)(2,1)S(1)}, u32[]{:S(2)}, u32[]{:S(2)}) async-start(bf16[16,64,512]{2,1,0:T(8,128)(2,1)} %bitcast.14), calls=%async_computation | async-start | bytes 2097152 | tf_op jit(solution)/shard_map/all_to_all | solution.py:274
  22.5 43.3 %copy-start.1 = (s32[64]{0:T(128)S(1)}, s32[64]{0:T(128)}, u32[]{:S(2)}) copy-start(s32[64]{0:T(128)} %param.6) | copy-start | bytes 772
  27.5 12.3 %collective-permute-start = (f32[32,768]{1,0:T(8,128)S(1)}, f32[32,768]{1,0:T(8,128)S(1)}, u32[]{:S(2)}, u32[]{:S(2)}) collective-permute-start(f32[32,768]{1,0:T(8,128)S(1)} %get-tuple-element.12), channel_id=1, source_target_pairs={{0,16},{1,17},{2,18},{3,19},{4,20},{5,21},{6,22},{7,23},{8,24},{9,... | collective-permute-start | bytes 294920 | tf_op jit(solution)/shard_map/ppermute | solution.py:269
  33.9 5.9 %collective-permute-start.1 = (f32[32,512]{1,0:T(8,128)S(1)}, f32[32,512]{1,0:T(8,128)S(1)}, u32[]{:S(2)}, u32[]{:S(2)}) collective-permute-start(f32[32,512]{1,0:T(8,128)S(1)} %get-tuple-element.14), channel_id=1, source_target_pairs={{0,16},{1,17},{2,18},{3,19},{4,20},{5,21},{6,22},{7,23},{8,24},{9,... | collective-permute-start | bytes 196616 | tf_op jit(solution)/shard_map/ppermute | solution.py:269
  40.0 5.1 %collective-permute-start.14 = (bf16[32,384]{1,0:T(8,128)(2,1)S(1)}, bf16[32,384]{1,0:T(8,128)(2,1)S(1)}, u32[]{:S(2)}, u32[]{:S(2)}) collective-permute-start(bf16[32,384]{1,0:T(8,128)(2,1)S(1)} %get-tuple-element.16), channel_id=1, source_target_pairs={{0,6},{1,7},{2,4},{3,5},{4,2},{5,3},{6,0},{7,1},{8,14},{9,15},{10,... | collective-permute-start | bytes 73736 | tf_op jit(solution)/shard_map/ppermute | solution.py:269
  41.5 6.4 %collective-permute-start.13 = (bf16[32,384]{1,0:T(8,128)(2,1)S(1)}, bf16[32,384]{1,0:T(8,128)(2,1)S(1)}, u32[]{:S(2)}, u32[]{:S(2)}) collective-permute-start(bf16[32,384]{1,0:T(8,128)(2,1)S(1)} %get-tuple-element.16), channel_id=1, source_target_pairs={{0,4},{1,5},{2,6},{3,7},{4,0},{5,1},{6,2},{7,3},{8,12},{9,13},{10,... | collective-permute-start | bytes 73736 | tf_op jit(solution)/shard_map/ppermute | solution.py:269
  41.8 6.1 %collective-permute-start.12 = (bf16[32,384]{1,0:T(8,128)(2,1)S(1)}, bf16[32,384]{1,0:T(8,128)(2,1)S(1)}, u32[]{:S(2)}, u32[]{:S(2)}) collective-permute-start(bf16[32,384]{1,0:T(8,128)(2,1)S(1)} %get-tuple-element.16), channel_id=1, source_target_pairs={{0,2},{1,3},{2,0},{3,1},{4,6},{5,7},{6,4},{7,5},{8,10},{9,11},{10,... | collective-permute-start | bytes 73736 | tf_op jit(solution)/shard_map/ppermute | solution.py:269
  43.5 6.7 %collective-permute-start.4 = (bf16[32,896]{1,0:T(8,128)(2,1)S(1)}, bf16[32,896]{1,0:T(8,128)(2,1)S(1)}, u32[]{:S(2)}, u32[]{:S(2)}) collective-permute-start(bf16[32,896]{1,0:T(8,128)(2,1)S(1)} %get-tuple-element.15), channel_id=1, source_target_pairs={{0,24},{1,25},{2,26},{3,27},{4,28},{5,29},{6,30},{7,31},{8,16},{9,... | collective-permute-start | bytes 172040 | tf_op jit(solution)/shard_map/ppermute | solution.py:269
  43.5 8.0 %collective-permute-start.3 = (bf16[32,896]{1,0:T(8,128)(2,1)S(1)}, bf16[32,896]{1,0:T(8,128)(2,1)S(1)}, u32[]{:S(2)}, u32[]{:S(2)}) collective-permute-start(bf16[32,896]{1,0:T(8,128)(2,1)S(1)} %get-tuple-element.15), channel_id=1, source_target_pairs={{0,16},{1,17},{2,18},{3,19},{4,20},{5,21},{6,22},{7,23},{8,24},{9,... | collective-permute-start | bytes 172040 | tf_op jit(solution)/shard_map/ppermute | solution.py:269
  45.0 6.5 %collective-permute-start.2 = (bf16[32,896]{1,0:T(8,128)(2,1)S(1)}, bf16[32,896]{1,0:T(8,128)(2,1)S(1)}, u32[]{:S(2)}, u32[]{:S(2)}) collective-permute-start(bf16[32,896]{1,0:T(8,128)(2,1)S(1)} %get-tuple-element.15), channel_id=1, source_target_pairs={{0,8},{1,9},{2,10},{3,11},{4,12},{5,13},{6,14},{7,15},{8,0},{9,1},... | collective-permute-start | bytes 172040 | tf_op jit(solution)/shard_map/ppermute | solution.py:269
  47.9 8.0 %collective-permute-start.20 = (bf16[4,32,384]{2,1,0:T(8,128)(2,1)S(1)}, bf16[4,32,384]{2,1,0:T(8,128)(2,1)S(1)}, u32[]{:S(2)}, u32[]{:S(2)}) collective-permute-start(bf16[4,32,384]{2,1,0:T(8,128)(2,1)S(1)} %pad_maximum_fusion.1.rest_8_), channel_id=1, source_target_pairs={{0,24},{1,25},{2,26},{3,27},{4,28},{5,29},{6,30},{7,31},{8,16},{9,... | collective-permute-start | bytes 294920 | tf_op jit(solution)/shard_map/ppermute | solution.py:269
  51.6 11.5 %collective-permute-start.10 = (bf16[4,32,896]{2,1,0:T(8,128)(2,1)S(1)}, bf16[4,32,896]{2,1,0:T(8,128)(2,1)S(1)}, u32[]{:S(2)}, u32[]{:S(2)}) collective-permute-start(bf16[4,32,896]{2,1,0:T(8,128)(2,1)S(1)} %pad_maximum_fusion.rest_0_), channel_id=1, source_target_pairs={{0,6},{1,7},{2,4},{3,5},{4,2},{5,3},{6,0},{7,1},{8,14},{9,15},{10,... | collective-permute-start | bytes 688136 | tf_op jit(solution)/shard_map/ppermute | solution.py:269
  54.1 9.4 %collective-permute-start.8 = (bf16[4,32,896]{2,1,0:T(8,128)(2,1)S(1)}, bf16[4,32,896]{2,1,0:T(8,128)(2,1)S(1)}, u32[]{:S(2)}, u32[]{:S(2)}) collective-permute-start(bf16[4,32,896]{2,1,0:T(8,128)(2,1)S(1)} %pad_maximum_fusion.rest_0_), channel_id=1, source_target_pairs={{0,4},{1,5},{2,6},{3,7},{4,0},{5,1},{6,2},{7,3},{8,12},{9,13},{10,... | collective-permute-start | bytes 688136 | tf_op jit(solution)/shard_map/ppermute | solution.py:269
  54.4 9.3 %collective-permute-start.6 = (bf16[4,32,896]{2,1,0:T(8,128)(2,1)S(1)}, bf16[4,32,896]{2,1,0:T(8,128)(2,1)S(1)}, u32[]{:S(2)}, u32[]{:S(2)}) collective-permute-start(bf16[4,32,896]{2,1,0:T(8,128)(2,1)S(1)} %pad_maximum_fusion.rest_0_), channel_id=1, source_target_pairs={{0,2},{1,3},{2,0},{3,1},{4,6},{5,7},{6,4},{7,5},{8,10},{9,11},{10,... | collective-permute-start | bytes 688136 | tf_op jit(solution)/shard_map/ppermute | solution.py:269
  55.2 6.5 %collective-permute-start.18 = (bf16[4,32,384]{2,1,0:T(8,128)(2,1)S(1)}, bf16[4,32,384]{2,1,0:T(8,128)(2,1)S(1)}, u32[]{:S(2)}, u32[]{:S(2)}) collective-permute-start(bf16[4,32,384]{2,1,0:T(8,128)(2,1)S(1)} %pad_maximum_fusion.1.rest_8_), channel_id=1, source_target_pairs={{0,16},{1,17},{2,18},{3,19},{4,20},{5,21},{6,22},{7,23},{8,24},{9,... | collective-permute-start | bytes 294920 | tf_op jit(solution)/shard_map/ppermute | solution.py:269
  56.0 5.7 %collective-permute-start.16 = (bf16[4,32,384]{2,1,0:T(8,128)(2,1)S(1)}, bf16[4,32,384]{2,1,0:T(8,128)(2,1)S(1)}, u32[]{:S(2)}, u32[]{:S(2)}) collective-permute-start(bf16[4,32,384]{2,1,0:T(8,128)(2,1)S(1)} %pad_maximum_fusion.1.rest_8_), channel_id=1, source_target_pairs={{0,8},{1,9},{2,10},{3,11},{4,12},{5,13},{6,14},{7,15},{8,0},{9,1},... | collective-permute-start | bytes 294920 | tf_op jit(solution)/shard_map/ppermute | solution.py:269
  61.7 1.3 %collective-permute-start.15 = (bf16[4,32,384]{2,1,0:T(8,128)(2,1)S(1)}, bf16[4,32,384]{2,1,0:T(8,128)(2,1)S(1)}, u32[]{:S(2)}, u32[]{:S(2)}) collective-permute-start(bf16[4,32,384]{2,1,0:T(8,128)(2,1)S(1)} %pad_maximum_fusion.1.rest_8_), channel_id=1, source_target_pairs={{0,1},{1,0},{2,3},{3,2},{4,5},{5,4},{6,7},{7,6},{8,9},{9,8},{10,11... | collective-permute-start | bytes 294920 | tf_op jit(solution)/shard_map/ppermute | solution.py:269
  61.7 2.3 %collective-permute-start.21 = (bf16[4,32,384]{2,1,0:T(8,128)(2,1)S(1)}, bf16[4,32,384]{2,1,0:T(8,128)(2,1)S(1)}, u32[]{:S(2)}, u32[]{:S(2)}) collective-permute-start(bf16[4,32,384]{2,1,0:T(8,128)(2,1)S(1)} %collective-permute-done.20.rest_14_), channel_id=1, source_target_pairs={{0,1},{1,0},{2,3},{3,2},{4,5},{5,4},{6,7},{7,6},{8,9},{9,8},{10,11... | collective-permute-start | bytes 294920 | tf_op jit(solution)/shard_map/ppermute | solution.py:269
  63.0 3.9 %collective-permute-start.5 = (bf16[4,32,896]{2,1,0:T(8,128)(2,1)S(1)}, bf16[4,32,896]{2,1,0:T(8,128)(2,1)S(1)}, u32[]{:S(2)}, u32[]{:S(2)}) collective-permute-start(bf16[4,32,896]{2,1,0:T(8,128)(2,1)S(1)} %pad_maximum_fusion.rest_0_), channel_id=1, source_target_pairs={{0,1},{1,0},{2,3},{3,2},{4,5},{5,4},{6,7},{7,6},{8,9},{9,8},{10,11... | collective-permute-start | bytes 688136 | tf_op jit(solution)/shard_map/ppermute | solution.py:269
  63.1 3.8 %collective-permute-start.11 = (bf16[4,32,896]{2,1,0:T(8,128)(2,1)S(1)}, bf16[4,32,896]{2,1,0:T(8,128)(2,1)S(1)}, u32[]{:S(2)}, u32[]{:S(2)}) collective-permute-start(bf16[4,32,896]{2,1,0:T(8,128)(2,1)S(1)} %collective-permute-done.10.rest_6_), channel_id=1, source_target_pairs={{0,1},{1,0},{2,3},{3,2},{4,5},{5,4},{6,7},{7,6},{8,9},{9,8},{10,11... | collective-permute-start | bytes 688136 | tf_op jit(solution)/shard_map/ppermute | solution.py:269
  63.5 3.4 %collective-permute-start.9 = (bf16[4,32,896]{2,1,0:T(8,128)(2,1)S(1)}, bf16[4,32,896]{2,1,0:T(8,128)(2,1)S(1)}, u32[]{:S(2)}, u32[]{:S(2)}) collective-permute-start(bf16[4,32,896]{2,1,0:T(8,128)(2,1)S(1)} %collective-permute-done.8.rest_4_), channel_id=1, source_target_pairs={{0,1},{1,0},{2,3},{3,2},{4,5},{5,4},{6,7},{7,6},{8,9},{9,8},{10,11... | collective-permute-start | bytes 688136 | tf_op jit(solution)/shard_map/ppermute | solution.py:269
  63.7 3.3 %collective-permute-start.7 = (bf16[4,32,896]{2,1,0:T(8,128)(2,1)S(1)}, bf16[4,32,896]{2,1,0:T(8,128)(2,1)S(1)}, u32[]{:S(2)}, u32[]{:S(2)}) collective-permute-start(bf16[4,32,896]{2,1,0:T(8,128)(2,1)S(1)} %collective-permute-done.6.rest_2_), channel_id=1, source_target_pairs={{0,1},{1,0},{2,3},{3,2},{4,5},{5,4},{6,7},{7,6},{8,9},{9,8},{10,11... | collective-permute-start | bytes 688136 | tf_op jit(solution)/shard_map/ppermute | solution.py:269
  64.0 1.6 %collective-permute-start.19 = (bf16[4,32,384]{2,1,0:T(8,128)(2,1)S(1)}, bf16[4,32,384]{2,1,0:T(8,128)(2,1)S(1)}, u32[]{:S(2)}, u32[]{:S(2)}) collective-permute-start(bf16[4,32,384]{2,1,0:T(8,128)(2,1)S(1)} %collective-permute-done.18.rest_12_), channel_id=1, source_target_pairs={{0,1},{1,0},{2,3},{3,2},{4,5},{5,4},{6,7},{7,6},{8,9},{9,8},{10,11... | collective-permute-start | bytes 294920 | tf_op jit(solution)/shard_map/ppermute | solution.py:269
  65.6 1.3 %collective-permute-start.17 = (bf16[4,32,384]{2,1,0:T(8,128)(2,1)S(1)}, bf16[4,32,384]{2,1,0:T(8,128)(2,1)S(1)}, u32[]{:S(2)}, u32[]{:S(2)}) collective-permute-start(bf16[4,32,384]{2,1,0:T(8,128)(2,1)S(1)} %collective-permute-done.16.rest_10_), channel_id=1, source_target_pairs={{0,1},{1,0},{2,3},{3,2},{4,5},{5,4},{6,7},{7,6},{8,9},{9,8},{10,11... | collective-permute-start | bytes 294920 | tf_op jit(solution)/shard_map/ppermute | solution.py:269
  (1 other events, 11.8 us)

commit v4 on v1

v4 whole, which is shorter than its diff:
```python
import functools
import math

import jax
import jax.numpy as jnp
import ml_dtypes
import numpy as np
from jax import lax
from jax.experimental import pallas as pl
from jax.experimental.pallas import tpu as pltpu
from jax.sharding import PartitionSpec as P

BAND = 600
SOURCES = 64
HALF_LAG = 500

lowest_bin = 8
floor_share = 0.05
epsilon = 1e-06

PART = 640
WIDTH = 2 * PART
LAGS = 2 * HALF_LAG + 1
LAG_TILES = -(-LAGS // 128)
SHARES = 4
COLUMN_TILES = WIDTH // 128
FIRST_TILES = 6
FLAG_TILE = BAND // 128 * 128
FLAG_LANE = BAND - FLAG_TILE


def angles(phase, samples):
    step = np.float32(2.0 * math.pi / samples)
    return (phase.astype(np.float32) * step).astype(np.float64)


def cos_sin(samples):
    angle = angles(np.arange(samples), samples)
    return np.cos(angle).astype(np.float32), (-np.sin(angle)).astype(np.float32)


def lane_tiles(table):
    tiled = table.reshape(*table.shape[:-1], -1, 128)
    return np.ascontiguousarray(np.moveaxis(tiled, -2, -3))


@functools.lru_cache(maxsize=None)
def tables(samples, span):
    bins = lowest_bin + np.arange(BAND)
    cosine, sine = cos_sin(samples)
    phase = np.arange(samples)[:, None] * bins[None, :] % samples
    forward = np.zeros((samples, WIDTH), ml_dtypes.bfloat16)
    forward[:, :BAND] = cosine.astype(ml_dtypes.bfloat16)[phase]
    forward[:, PART : PART + BAND] = sine.astype(ml_dtypes.bfloat16)[phase]
    return lane_tiles(forward.reshape(-1, span, WIDTH)).reshape(-1, 128)


@functools.lru_cache(maxsize=None)
def inverse_table(samples):
    bins = lowest_bin + np.arange(BAND)
    cosine, sine = cos_sin(samples)
    factor = np.float32(1.0 / math.sqrt(BAND))
    phase = bins[:, None] * (np.arange(LAGS) - HALF_LAG)[None, :] % samples
    inverse = np.zeros((WIDTH, LAG_TILES * 128), ml_dtypes.bfloat16)
    inverse[:BAND, :LAGS] = (cosine * factor).astype(ml_dtypes.bfloat16)[phase]
    inverse[PART : PART + BAND, :LAGS] = (sine * factor).astype(ml_dtypes.bfloat16)[phase]
    return lane_tiles(inverse).reshape(-1, 128)


def chunk_device(chunk, members, segments):
    per_segment = members // segments
    segment, part = divmod(chunk, per_segment)
    return segment // 2 * 2 * per_segment + 2 * part + segment % 2


def transform_kernel(first, senders, share_ref, records_ref, table_ref, *rest):
    outs, (tiles_ref, sems) = rest[:-2], rest[-2:]
    members, rows, span = records_ref.shape
    lines = tiles_ref.shape[1]
    columns = lines // span
    copies = []
    for index, sender in enumerate(senders):
        start = ((share_ref[0] * members + sender) * COLUMN_TILES + first) * span
        source = table_ref.at[pl.ds(pl.multiple_of(start, span), lines)]
        copies.append(pltpu.make_async_copy(source, tiles_ref.at[index], sems.at[index]))
        copies[-1].start()
    total = jnp.zeros((rows, columns * 128), jnp.float32)
    for index in range(members):
        copies[index].wait()
        tiles = [tiles_ref[index, tile * span : (tile + 1) * span] for tile in range(columns)]
        total += jnp.dot(
            records_ref[index], jnp.concatenate(tiles, axis=1), preferred_element_type=jnp.float32
        )
    kept = rows // len(outs)
    for step, out in enumerate(outs):
        chosen = total[:kept]
        for owner in range(1, len(outs)):
            mine = (share_ref[0] ^ step) == owner
            chosen = jnp.where(mine, total[owner * kept : (owner + 1) * kept], chosen)
        out[...] = chosen


def transform(share, records, table, senders, first, last):
    members, rows, span = records.shape
    columns = last - first
    vmem = pl.BlockSpec(memory_space=pltpu.VMEM)
    shape = jax.ShapeDtypeStruct((rows // SHARES, columns * 128), jnp.float32)
    return pl.pallas_call(
        functools.partial(transform_kernel, first, senders),
        in_specs=[
            pl.BlockSpec(memory_space=pltpu.SMEM),
            vmem,
            pl.BlockSpec(memory_space=pltpu.HBM),
        ],
        out_specs=[vmem] * SHARES,
        out_shape=[shape] * SHARES,
        scratch_shapes=[
            pltpu.VMEM((members, columns * span, 128), jnp.bfloat16),
            pltpu.SemaphoreType.DMA((members,)),
        ],
        compiler_params=pltpu.CompilerParams(vmem_limit_bytes=32 * 2**20),
        cost_estimate=pl.CostEstimate(
            flops=2 * rows * members * span * columns * 128,
            bytes_accessed=2 * members * span * columns * 128,
            transcendentals=0,
        ),
        name="transform",
    )(share, records, table)


def whiten_kernel(flags_ref, *rest):
    parts, white_ref = rest[:-1], rest[-1]
    sums = []
    for first in range(0, len(parts), SHARES):
        sums.append(parts[first][...])
        for part in parts[first + 1 : first + SHARES]:
            sums[-1] += part[...]
    total = jnp.concatenate(sums, axis=1)
    real_part, imag_part = total[:, :PART], total[:, PART:]
    power = real_part * real_part + imag_part * imag_part
    level = jnp.sum(power, axis=1, keepdims=True) * (1.0 / BAND)
    factor = lax.rsqrt(power + floor_share * level + epsilon)
    white_ref[:, :PART] = (real_part * factor).astype(jnp.bfloat16)
    white_ref[:, PART:] = (imag_part * factor).astype(jnp.bfloat16)
    rows = total.shape[0]
    lane = lax.broadcasted_iota(jnp.int32, (rows, 128), 1)
    held = (lane >= FLAG_LANE) & (lane < FLAG_LANE + flags_ref.shape[1])
    tile = (real_part * factor)[:, FLAG_TILE : FLAG_TILE + 128]
    flags = jnp.concatenate(
        [
            jnp.zeros((1, FLAG_LANE), jnp.float32),
            flags_ref[...],
            jnp.zeros((1, 128 - FLAG_LANE - flags_ref.shape[1]), jnp.float32),
        ],
        axis=1,
    )
    white_ref[:, FLAG_TILE : FLAG_TILE + 128] = jnp.where(held, flags, tile).astype(jnp.bfloat16)


def whiten(flags, parts):
    return pl.pallas_call(
        whiten_kernel,
        out_shape=jax.ShapeDtypeStruct((parts[0].shape[0], WIDTH), jnp.bfloat16),
        compiler_params=pltpu.CompilerParams(vmem_limit_bytes=16 * 2**20),
        name="whiten",
    )(flags, *parts)


def correlate_kernel(shape, core, place_ref, flags_ref, ids_ref, *rest):
    segments, channels, devices, blocks = shape
    blocks, rest = rest[:blocks], rest[blocks:]
    if core:
        before_ref, table_ref, out_ref = rest[:3]
        held_ref, panel_ref, receivers_ref, inverse_ref, stacked_ref, sem = rest[3:]
        fetch = pltpu.make_async_copy(table_ref, inverse_ref, sem)
        fetch.start()
    else:
        out_ref, held_ref, panel_ref, receivers_ref = rest
    rows = held_ref.shape[1]
    members = devices // SHARES
    parts = members // segments
    ch_local = channels // devices
    ch_chip = 2 * ch_local
    place = place_ref[0]
    parity = place % 2 ^ core
    ids = ids_ref[...]
    sources = ids.shape[0]

    def position(device):
        member = device % members
        return (member // 2) * SHARES + device // members

    for index, block in enumerate(blocks):
        for line in range(block.shape[0]):
            device = place ^ (line * 8 + index * 2 + core)
            held_ref[position(device)] = block[line]

    tails = held_ref[:, :, FLAG_TILE : FLAG_TILE + 128].reshape(held_ref.shape[0] * rows, 128)
    column = lax.broadcasted_iota(jnp.int32, (sources, tails.shape[0]), 1)
    choice = (column == position(ids // ch_chip * 2 + parity) * rows).astype(jnp.bfloat16)
    tail = jnp.dot(choice, tails, preferred_element_type=jnp.float32)
    lane = lax.broadcasted_iota(jnp.int32, (sources, 128), 1)

    channel = lax.broadcasted_iota(jnp.int32, (sources, channels), 1)
    pick_sources = (channel == ids).astype(jnp.bfloat16)
    line = lax.broadcasted_iota(jnp.int32, (16, channels), 0)
    channel = lax.broadcasted_iota(jnp.int32, (16, channels), 1)
    pick_own = ((channel == place * ch_local + line) & (line < ch_local)).astype(jnp.bfloat16)
    pick = jnp.concatenate([pick_sources, pick_own], axis=0)

    counts = [jnp.zeros((sources, 1), jnp.float32) for _ in range(ch_local)]
    per_segment = channels // rows
    for g in range(segments // 2):
        segment = held_ref[g * per_segment : (g + 1) * per_segment].reshape(channels, WIDTH)
        picked = jnp.dot(pick, segment, preferred_element_type=jnp.float32)
        mine = lane == FLAG_LANE + g * ch_chip + ids % ch_chip
        weight = jnp.sum(jnp.where(mine, tail, 0.0), axis=1, keepdims=True)
        panel_ref[g] = picked[:sources] * weight
        receivers_ref[g] = picked[sources:]
        for c in range(ch_local):
            counts[c] += weight * flags_ref[2 * g + parity, c]

    shares = [None] * ch_local
    for start in [FLAG_TILE] + [start for start in range(0, PART, 128) if start != FLAG_TILE]:
        re = slice(start, start + 128)
        im = slice(PART + start, PART + start + 128)
        for c in range(ch_local):
            real_sum = jnp.zeros((sources, 128), jnp.float32)
            imag_sum = jnp.zeros((sources, 128), jnp.float32)
            for g in range(segments // 2):
                flag = flags_ref[2 * g + parity, c]
                rec_real = receivers_ref[g, c : c + 1, re] * flag
                rec_imag = receivers_ref[g, c : c + 1, im] * flag
                src_real, src_imag = panel_ref[g, :, re], panel_ref[g, :, im]
                real_sum += src_real * rec_real + src_imag * rec_imag
                imag_sum += src_imag * rec_real - src_real * rec_imag
            if start == FLAG_TILE:
                real_sum = jnp.where(lane == FLAG_LANE, counts[c], real_sum)
            if not core:
                out_ref[c, :, re] = real_sum
                out_ref[c, :, im] = imag_sum
                continue
            real_sum += before_ref[c, :, re]
            imag_sum += before_ref[c, :, im]
            if start == FLAG_TILE:
                total = real_sum[:, FLAG_LANE : FLAG_LANE + 1]
                shares[c] = 1.0 / jnp.maximum(total, 1.0)
            lines = pl.ds(c, sources, stride=ch_local)
            stacked_ref[start // 128, lines, :] = real_sum * shares[c]
            stacked_ref[(PART + start) // 128, lines, :] = imag_sum * shares[c]
    if core:
        fetch.wait()
        tiles = [inverse_ref[tile * WIDTH : (tile + 1) * WIDTH] for tile in range(LAG_TILES)]
        lags = jnp.dot(
            jnp.concatenate([stacked_ref[i] for i in range(COLUMN_TILES)], axis=1).astype(
                jnp.bfloat16
            ),
            jnp.concatenate(tiles, axis=1),
            preferred_element_type=jnp.float32,
        )
        out_ref[...] = lags.reshape(sources, ch_local, LAG_TILES * 128)[:, :, :LAGS]


def correlate(core, place, weights, ids, blocks, shape, before=None, table=None):
    segments, channels, devices = shape
    rows = blocks[0].shape[1]
    ch_local = channels // devices
    sources = ids.shape[0]
    smem = pl.BlockSpec(memory_space=pltpu.SMEM)
    vmem = pl.BlockSpec(memory_space=pltpu.VMEM)
    in_specs = [smem, smem, vmem] + [vmem] * len(blocks)
    scratch = [
        pltpu.VMEM((devices // 2, rows, WIDTH), jnp.bfloat16),
        pltpu.VMEM((segments // 2, sources, WIDTH), jnp.float32),
        pltpu.VMEM((segments // 2, 16, WIDTH), jnp.float32),
    ]
    if core:
        in_specs += [vmem, pl.BlockSpec(memory_space=pltpu.HBM)]
        scratch += [
            pltpu.VMEM(table.shape, jnp.bfloat16),
            pltpu.VMEM((COLUMN_TILES, sources * ch_local, 128), jnp.float32),
            pltpu.SemaphoreType.DMA,
        ]
    out = (sources, ch_local, LAGS) if core else (ch_local, sources, WIDTH)
    return pl.pallas_call(
        functools.partial(correlate_kernel, (*shape, len(blocks)), core),
        in_specs=in_specs,
        out_specs=vmem,
        out_shape=jax.ShapeDtypeStruct(out, jnp.float32),
        scratch_shapes=scratch,
        compiler_params=pltpu.CompilerParams(vmem_limit_bytes=32 * 2**20),
        cost_estimate=pl.CostEstimate(
            flops=sources * channels * WIDTH * segments,
            bytes_accessed=2 * (segments // 2) * channels * WIDTH,
            transcendentals=0,
        ),
        name="correlate",
    )(place, weights, ids, *blocks, *([before, table] if core else []))


def per_device(records, valid_flags, source_ids):
    segments, channels, span = records.shape
    devices = lax.axis_size("chan")
    members = devices // SHARES
    samples = span * devices
    place = lax.axis_index("chan")
    weights = valid_flags.astype(jnp.float32)

    def exchange(block, bits):
        return lax.ppermute(block, "chan", [(i, i ^ bits) for i in range(devices)])

    parity = place % 2
    partner = exchange(weights, 1)
    chip = jnp.where(
        parity == 0,
        jnp.concatenate([weights, partner], axis=1),
        jnp.concatenate([partner, weights], axis=1),
    )
    chip = chip.reshape(segments // 2, 2, -1)
    flags = lax.dynamic_index_in_dim(chip, parity, 1, keepdims=False).reshape(1, -1)

    share = (place // members).reshape(1)
    senders = [chunk_device(chunk, members, segments) for chunk in range(members)]
    groups = [[first + sender for sender in senders] for first in range(0, devices, members)]
    grouped = records.reshape(members, segments * channels // members, span)
    regrouped = lax.all_to_all(
        grouped, "chan", split_axis=0, concat_axis=0, axis_index_groups=groups, tiled=True
    )
    parts = []
    for first, last in ((0, FIRST_TILES), (FIRST_TILES, COLUMN_TILES)):
        sums = transform(share, regrouped, tables(samples, span), senders, first, last)
        parts += [sums[0]] + [exchange(sums[k], k * members) for k in range(1, SHARES)]
    white = whiten(flags, parts)

    far = devices // 8
    line = jnp.stack([white] + [exchange(white, 8 * k) for k in range(1, far)])
    plane = [line] + [exchange(line, 2 * k) for k in range(1, 4)]
    swapped = [exchange(block, 1) for block in plane]
    ids = source_ids.reshape(-1, 1)
    common = place.reshape(1), weights, ids
    shape = segments, channels, devices
    before = correlate(0, *common, plane, shape)
    inverse = inverse_table(samples)
    return correlate(1, *common, swapped, shape, before, inverse)


def solution(mesh):
    return jax.shard_map(
        per_device,
        mesh=mesh,
        in_specs=(P("group", None, "chan"), P("group", "chan"), P("group")),
        out_specs=P("group", "chan", None),
        check_vma=False,
    )
```

time: 73.4 us -> 81.6 us (1.11)
  starting transfers between devices: 17.9 us -> 23.6 us
  waiting for transfers between devices: 40.3 us -> 42.1 us
    ppermute x12 -> x17, starting transfers between devices: 11.6 us -> 18.5 us  [exchange(): return lax.ppermute(block, 'chan', [(i, i ^ bits) for i in range(devices)])]
    ppermute x12 -> x17, waiting for transfers between devices: 24.2 us -> 26.7 us  [exchange(): return lax.ppermute(block, 'chan', [(i, i ^ bits) for i in range(devices)])]
    all_to_all x1, starting transfers between devices: 6.29 us -> 5.17 us  [per_device(): lax.all_to_all(grouped, 'chan', split_axis=0, concat_axis=0, axis_index_g...]
    pallas_call x3 -> x4, Pallas kernels: 14.5 us -> 14.3 us  [the longest x2 7.36 us: correlate(): pl.pallas_call(functools.partial(correlate_kernel, (*shape, len(blocks)),...]
  transfers between devices with their start and end apart: 13 -> 18, of which waited for: 8 -> 7; matrix products, arithmetic and copies ran while one was open for 0% -> 0% of each run, Pallas kernels for 5% -> 8%
where the time goes in v4:
time: 81.6 us; the launch traced here: 80.7 us
  waiting for transfers between devices  42.1 us (52%)
  starting transfers between devices  23.6 us (29%)
  Pallas kernels  14.4 us (18%)
    ppermute x17, waiting for transfers between devices, exchange(): return lax.ppermute(block, 'chan', [(i, i ^ bits) for i in range(devices)])  26.7 us
    ppermute x17, starting transfers between devices, exchange(): return lax.ppermute(block, 'chan', [(i, i ^ bits) for i in range(devices)])  18.5 us
    all_to_all x1, waiting for transfers between devices, per_device(): lax.all_to_all(grouped, 'chan', split_axis=0, concat_axis=0, axis_index_g...  15.4 us
    pallas_call x2, Pallas kernels, correlate(): pl.pallas_call(functools.partial(correlate_kernel, (*shape, len(blocks)),...  7.36 us
    pallas_call x2, Pallas kernels, transform(): pl.pallas_call(functools.partial(transform_kernel, first, senders), in_sp...  6.9 us
    all_to_all x1, starting transfers between devices, per_device(): lax.all_to_all(grouped, 'chan', split_axis=0, concat_axis=0, axis_index_g...  5.17 us
  transfers between devices with their start and end apart: 18, of which 7 were waited for; matrix products, arithmetic and copies ran while one was open for 0% of the time, Pallas kernels for 8%

profile of v4, /device:TPU:0, one launch (start us, length us, event | category | flops | bytes accessed | tf_op | source)
XLA Modules:
  0.0 80.7 jit_solution(11751127731989813364)
XLA Ops:
  0.0 5.2 %all-to-all-start = ((bf16[8,128,512]{2,1,0:T(8,128)(2,1)}), bf16[8,128,512]{2,1,0:T(8,128)(2,1)S(1)}, u32[]{:S(2)}, u32[]{:S(2)}) async-start(bf16[8,128,512]{2,1,0:T(8,128)(2,1)} %param.5), calls=%async_computation | async-start | bytes 2097152 | tf_op jit(solution)/shard_map/all_to_all | solution.py:326
  5.2 15.4 %all-to-all-done.records_ref = bf16[8,128,512]{2,1,0:T(8,128)(2,1)S(1)} async-done(((bf16[8,128,512]{2,1,0:T(8,128)(2,1)}), bf16[8,128,512]{2,1,0:T(8,128)(2,1)S(1)}, u32[]{:S(2)}, u32[]{:S(2)}) %all-to-all-start) | async-done | bytes 1048608 | tf_op jit(solution)/shard_map/all_to_all | solution.py:326
  20.6 3.1 %transform.3 = (f32[32,512]{1,0:T(8,128)S(1)}, f32[32,512]{1,0:T(8,128)S(1)}, f32[32,512]{1,0:T(8,128)}, f32[32,512]{1,0:T(8,128)S(1)}) custom-call(s32[1]{0:T(128)} %bitcast.4.share_ref, bf16[8,128,512]{2,1,0:T(8,128)(2,1)S(1)} %all-to-all-done.records_ref, bf16[163840,128]{1,0:T(8,128)(2,1)} %constant.40.clone.table_ref), custom_call_target="tpu_custom_call" | custom-call | flops 536870912 | bytes 4194304 | tf_op jit(solution)/shard_map/transform/pallas_call | solution.py:108
  23.7 1.6 %collective-permute-start.4 = (f32[32,512]{1,0:T(8,128)S(1)}, f32[32,512]{1,0:T(8,128)S(1)}, u32[]{:S(2)}, u32[]{:S(2)}) collective-permute-start(f32[32,512]{1,0:T(8,128)S(1)} %get-tuple-element.18), channel_id=1, source_target_pairs={{0,8},{1,9},{2,10},{3,11},{4,12},{5,13},{6,14},{7,15},{8,0},{9,1},... | collective-permute-start | bytes 196616 | tf_op jit(solution)/shard_map/ppermute | solution.py:310
  25.3 3.8 %transform.2 = (f32[32,768]{1,0:T(8,128)S(1)}, f32[32,768]{1,0:T(8,128)}, f32[32,768]{1,0:T(8,128)S(1)}, f32[32,768]{1,0:T(8,128)S(1)}) custom-call(s32[1]{0:T(128)} %bitcast.4.share_ref, bf16[8,128,512]{2,1,0:T(8,128)(2,1)S(1)} %all-to-all-done.records_ref, bf16[163840,128]{1,0:T(8,128)(2,1)} %constant.40.clone.table_ref), custom_call_target="tpu_custom_call" | custom-call | flops 805306368 | bytes 6291456 | tf_op jit(solution)/shard_map/transform/pallas_call | solution.py:108
  29.2 0.5 collective-permute-start.1
  29.7 2.6 %collective-permute-start.2 = (f32[32,768]{1,0:T(8,128)S(1)}, f32[32,768]{1,0:T(8,128)S(1)}, u32[]{:S(2)}, u32[]{:S(2)}) collective-permute-start(f32[32,768]{1,0:T(8,128)S(1)} %get-tuple-element.15), channel_id=1, source_target_pairs={{0,16},{1,17},{2,18},{3,19},{4,20},{5,21},{6,22},{7,23},{8,24},{9,... | collective-permute-start | bytes 294920 | tf_op jit(solution)/shard_map/ppermute | solution.py:310
  32.3 1.4 %collective-permute-start.3 = (f32[32,768]{1,0:T(8,128)S(1)}, f32[32,768]{1,0:T(8,128)S(1)}, u32[]{:S(2)}, u32[]{:S(2)}) collective-permute-start(f32[32,768]{1,0:T(8,128)S(1)} %get-tuple-element.16), channel_id=1, source_target_pairs={{0,24},{1,25},{2,26},{3,27},{4,28},{5,29},{6,30},{7,31},{8,16},{9,... | collective-permute-start | bytes 294920 | tf_op jit(solution)/shard_map/ppermute | solution.py:310
  33.7 1.2 %collective-permute-done = f32[8,4]{1,0:T(8,128)S(1)} collective-permute-done((f32[8,4]{1,0:T(8,128)S(1)}, f32[8,4]{1,0:T(8,128)S(1)}, u32[]{:S(2)}, u32[]{:S(2)}) %collective-permute-start) | collective-permute-done | bytes 160 | tf_op jit(solution)/shard_map/ppermute | solution.py:310
  34.9 1.7 %collective-permute-start.5 = (f32[32,512]{1,0:T(8,128)}, f32[32,512]{1,0:T(8,128)S(1)}, u32[]{:S(2)}, u32[]{:S(2)}) collective-permute-start(f32[32,512]{1,0:T(8,128)} %get-tuple-element.19), channel_id=1, source_target_pairs={{0,16},{1,17},{2,18},{3,19},{4,20},{5,21},{6,22},{7,23},{8,24},{9,... | collective-permute-start | bytes 196616 | tf_op jit(solution)/shard_map/ppermute | solution.py:310
  36.6 0.9 %collective-permute-start.6 = (f32[32,512]{1,0:T(8,128)S(1)}, f32[32,512]{1,0:T(8,128)S(1)}, u32[]{:S(2)}, u32[]{:S(2)}) collective-permute-start(f32[32,512]{1,0:T(8,128)S(1)} %get-tuple-element.20), channel_id=1, source_target_pairs={{0,24},{1,25},{2,26},{3,27},{4,28},{5,29},{6,30},{7,31},{8,16},{9,... | collective-permute-start | bytes 196616 | tf_op jit(solution)/shard_map/ppermute | solution.py:310
  37.7 6.3 %collective-permute-done.5.rest_6_ = f32[32,512]{1,0:T(8,128)S(1)} collective-permute-done((f32[32,512]{1,0:T(8,128)}, f32[32,512]{1,0:T(8,128)S(1)}, u32[]{:S(2)}, u32[]{:S(2)}) %collective-permute-start.5) | collective-permute-done | bytes 65568 | tf_op jit(solution)/shard_map/ppermute | solution.py:310
  44.1 1.6 %collective-permute-start.7 = (bf16[32,1280]{1,0:T(8,128)(2,1)S(1)}, bf16[32,1280]{1,0:T(8,128)(2,1)S(1)}, u32[]{:S(2)}, u32[]{:S(2)}) collective-permute-start(bf16[32,1280]{1,0:T(8,128)(2,1)S(1)} %whiten.1), channel_id=1, source_target_pairs={{0,8},{1,9},{2,10},{3,11},{4,12},{5,13},{6,14},{7,15},{8,0},{9,1},... | collective-permute-start | bytes 245768 | tf_op jit(solution)/shard_map/ppermute | solution.py:310
  45.7 1.7 %collective-permute-start.8 = (bf16[32,1280]{1,0:T(8,128)(2,1)S(1)}, bf16[32,1280]{1,0:T(8,128)(2,1)S(1)}, u32[]{:S(2)}, u32[]{:S(2)}) collective-permute-start(bf16[32,1280]{1,0:T(8,128)(2,1)S(1)} %whiten.1), channel_id=1, source_target_pairs={{0,16},{1,17},{2,18},{3,19},{4,20},{5,21},{6,22},{7,23},{8,24},{9,... | collective-permute-start | bytes 245768 | tf_op jit(solution)/shard_map/ppermute | solution.py:310
  47.4 1.2 %collective-permute-start.9 = (bf16[32,1280]{1,0:T(8,128)(2,1)S(1)}, bf16[32,1280]{1,0:T(8,128)(2,1)S(1)}, u32[]{:S(2)}, u32[]{:S(2)}) collective-permute-start(bf16[32,1280]{1,0:T(8,128)(2,1)S(1)} %whiten.1), channel_id=1, source_target_pairs={{0,24},{1,25},{2,26},{3,27},{4,28},{5,29},{6,30},{7,31},{8,16},{9,... | collective-permute-start | bytes 245768 | tf_op jit(solution)/shard_map/ppermute | solution.py:310
  48.6 6.0 %collective-permute-done.8 = bf16[32,1280]{1,0:T(8,128)(2,1)S(1)} collective-permute-done((bf16[32,1280]{1,0:T(8,128)(2,1)S(1)}, bf16[32,1280]{1,0:T(8,128)(2,1)S(1)}, u32[]{:S(2)}, u32[]{:S(2)}) %collective-permute-start.8) | collective-permute-done | bytes 81952 | tf_op jit(solution)/shard_map/ppermute | solution.py:310
  54.7 3.3 %collective-permute-start.11 = (bf16[4,32,1280]{2,1,0:T(8,128)(2,1)S(1)}, bf16[4,32,1280]{2,1,0:T(8,128)(2,1)}, u32[]{:S(2)}, u32[]{:S(2)}) collective-permute-start(bf16[4,32,1280]{2,1,0:T(8,128)(2,1)S(1)} %pad_maximum_fusion.rest_0_), channel_id=1, source_target_pairs={{0,2},{1,3},{2,0},{3,1},{4,6},{5,7},{6,4},{7,5},{8,10},{9,11},{10,... | collective-permute-start | bytes 983048 | tf_op jit(solution)/shard_map/ppermute | solution.py:310
  58.0 0.3 collective-permute-start.13
  58.3 1.3 %collective-permute-start.15 = (bf16[4,32,1280]{2,1,0:T(8,128)(2,1)S(1)}, bf16[4,32,1280]{2,1,0:T(8,128)(2,1)}, u32[]{:S(2)}, u32[]{:S(2)}) collective-permute-start(bf16[4,32,1280]{2,1,0:T(8,128)(2,1)S(1)} %pad_maximum_fusion.rest_0_), channel_id=1, source_target_pairs={{0,6},{1,7},{2,4},{3,5},{4,2},{5,3},{6,0},{7,1},{8,14},{9,15},{10,... | collective-permute-start | bytes 983048 | tf_op jit(solution)/shard_map/ppermute | solution.py:310
  59.6 7.2 %collective-permute-done.11.rest_1_ = bf16[4,32,1280]{2,1,0:T(8,128)(2,1)} collective-permute-done((bf16[4,32,1280]{2,1,0:T(8,128)(2,1)S(1)}, bf16[4,32,1280]{2,1,0:T(8,128)(2,1)}, u32[]{:S(2)}, u32[]{:S(2)}) %collective-permute-start.11) | collective-permute-done | bytes 327712 | tf_op jit(solution)/shard_map/ppermute | solution.py:310
  66.7 5.9 %collective-permute-done.13.rest_2_ = bf16[4,32,1280]{2,1,0:T(8,128)(2,1)} collective-permute-done((bf16[4,32,1280]{2,1,0:T(8,128)(2,1)S(1)}, bf16[4,32,1280]{2,1,0:T(8,128)(2,1)}, u32[]{:S(2)}, u32[]{:S(2)}) %collective-permute-start.13) | collective-permute-done | bytes 327712 | tf_op jit(solution)/shard_map/ppermute | solution.py:310
  72.7 0.5 collective-permute-start.16
  73.3 2.6 %correlate.2.rest_4_ = f32[4,64,1280]{2,1,0:T(8,128)S(1)} custom-call(s32[1]{0:T(128)} %bitcast.place_ref, f32[8,4]{1,0:T(8,128)S(1)} %convert_element_type.3.flags_ref, s32[64,1]{1,0:T(8,128)S(1)} %copy.8.ids_ref, bf16[4,32,1280]{2,1,0:T(8,128)(2,1)S(1)} %pad_maximum_fusion.rest_0_, bf16[4,32,1280]{2,1,0:T(8,128)(2,1)} %collective-permute-done.11.rest_1_, ...), custom_call_target="tpu_custom_call" | custom-call | flops 83886080 | bytes 1310720 | tf_op jit(solution)/shard_map/correlate/pallas_call | solution.py:285
  76.0 4.7 %correlate.3 = f32[64,4,1001]{2,1,0:T(4,128)} custom-call(s32[1]{0:T(128)} %bitcast.place_ref, f32[8,4]{1,0:T(8,128)S(1)} %convert_element_type.3.flags_ref, s32[64,1]{1,0:T(8,128)S(1)} %copy.8.ids_ref, bf16[4,32,1280]{2,1,0:T(8,128)(2,1)S(1)} %collective-permute-done.10.rest_0_, bf16[4,32,1280]{2,1,0:T(8,128)(2,1)} %collective-permute-done.12.rest_1_, ...), custom_call_target="tpu_custom_call" | custom-call | flops 83886080 | bytes 1310720 | tf_op jit(solution)/shard_map/correlate/pallas_call | solution.py:285
  (29 shorter events, 0.7 us)
Async XLA Ops:
  0.0 20.6 %all-to-all-start = ((bf16[8,128,512]{2,1,0:T(8,128)(2,1)}), bf16[8,128,512]{2,1,0:T(8,128)(2,1)S(1)}, u32[]{:S(2)}, u32[]{:S(2)}) async-start(bf16[8,128,512]{2,1,0:T(8,128)(2,1)} %param.5), calls=%async_computation | async-start | bytes 2097152 | tf_op jit(solution)/shard_map/all_to_all | solution.py:326
  23.7 10.0 %copy-start.1 = (s32[8,4]{0,1:T(4,128)S(1)}, s32[8,4]{0,1:T(4,128)}, u32[]{:S(2)}) copy-start(s32[8,4]{0,1:T(4,128)} %param.6) | copy-start | bytes 388
  23.7 49.5 %copy-start.2 = (s32[64]{0:T(128)S(1)}, s32[64]{0:T(128)}, u32[]{:S(2)}) copy-start(s32[64]{0:T(128)} %param.7) | copy-start | bytes 772
  23.7 12.9 %collective-permute-start.4 = (f32[32,512]{1,0:T(8,128)S(1)}, f32[32,512]{1,0:T(8,128)S(1)}, u32[]{:S(2)}, u32[]{:S(2)}) collective-permute-start(f32[32,512]{1,0:T(8,128)S(1)} %get-tuple-element.18), channel_id=1, source_target_pairs={{0,8},{1,9},{2,10},{3,11},{4,12},{5,13},{6,14},{7,15},{8,0},{9,1},... | collective-permute-start | bytes 196616 | tf_op jit(solution)/shard_map/ppermute | solution.py:310
  29.2 46.8 %copy-start = (bf16[10240,128]{1,0:T(8,128)(2,1)S(1)}, bf16[10240,128]{1,0:T(8,128)(2,1)}, u32[]{:S(2)}) copy-start(bf16[10240,128]{1,0:T(8,128)(2,1)} %constant.41.clone.rest_5_) | copy-start | bytes 7864324
  29.2 14.8 %collective-permute-start.1 = (f32[32,768]{1,0:T(8,128)}, f32[32,768]{1,0:T(8,128)S(1)}, u32[]{:S(2)}, u32[]{:S(2)}) collective-permute-start(f32[32,768]{1,0:T(8,128)} %get-tuple-element.14), channel_id=1, source_target_pairs={{0,8},{1,9},{2,10},{3,11},{4,12},{5,13},{6,14},{7,15},{8,0},{9,1},... | collective-permute-start | bytes 294920 | tf_op jit(solution)/shard_map/ppermute | solution.py:310
  29.7 14.3 %collective-permute-start.2 = (f32[32,768]{1,0:T(8,128)S(1)}, f32[32,768]{1,0:T(8,128)S(1)}, u32[]{:S(2)}, u32[]{:S(2)}) collective-permute-start(f32[32,768]{1,0:T(8,128)S(1)} %get-tuple-element.15), channel_id=1, source_target_pairs={{0,16},{1,17},{2,18},{3,19},{4,20},{5,21},{6,22},{7,23},{8,24},{9,... | collective-permute-start | bytes 294920 | tf_op jit(solution)/shard_map/ppermute | solution.py:310
  32.3 11.7 %collective-permute-start.3 = (f32[32,768]{1,0:T(8,128)S(1)}, f32[32,768]{1,0:T(8,128)S(1)}, u32[]{:S(2)}, u32[]{:S(2)}) collective-permute-start(f32[32,768]{1,0:T(8,128)S(1)} %get-tuple-element.16), channel_id=1, source_target_pairs={{0,24},{1,25},{2,26},{3,27},{4,28},{5,29},{6,30},{7,31},{8,16},{9,... | collective-permute-start | bytes 294920 | tf_op jit(solution)/shard_map/ppermute | solution.py:310
  33.7 1.2 %collective-permute-start = (f32[8,4]{1,0:T(8,128)S(1)}, f32[8,4]{1,0:T(8,128)S(1)}, u32[]{:S(2)}, u32[]{:S(2)}) collective-permute-start(f32[8,4]{1,0:T(8,128)S(1)} %convert_element_type.3.flags_ref), channel_id=1, source_target_pairs={{0,1},{1,0},{2,3},{3,2},{4,5},{5,4},{6,7},{7,6},{8,9},{9,8},{10,11... | collective-permute-start | bytes 392 | tf_op jit(solution)/shard_map/ppermute | solution.py:310
  34.9 9.1 %collective-permute-start.5 = (f32[32,512]{1,0:T(8,128)}, f32[32,512]{1,0:T(8,128)S(1)}, u32[]{:S(2)}, u32[]{:S(2)}) collective-permute-start(f32[32,512]{1,0:T(8,128)} %get-tuple-element.19), channel_id=1, source_target_pairs={{0,16},{1,17},{2,18},{3,19},{4,20},{5,21},{6,22},{7,23},{8,24},{9,... | collective-permute-start | bytes 196616 | tf_op jit(solution)/shard_map/ppermute | solution.py:310
  36.6 7.4 %collective-permute-start.6 = (f32[32,512]{1,0:T(8,128)S(1)}, f32[32,512]{1,0:T(8,128)S(1)}, u32[]{:S(2)}, u32[]{:S(2)}) collective-permute-start(f32[32,512]{1,0:T(8,128)S(1)} %get-tuple-element.20), channel_id=1, source_target_pairs={{0,24},{1,25},{2,26},{3,27},{4,28},{5,29},{6,30},{7,31},{8,16},{9,... | collective-permute-start | bytes 196616 | tf_op jit(solution)/shard_map/ppermute | solution.py:310
  44.1 4.5 %collective-permute-start.7 = (bf16[32,1280]{1,0:T(8,128)(2,1)S(1)}, bf16[32,1280]{1,0:T(8,128)(2,1)S(1)}, u32[]{:S(2)}, u32[]{:S(2)}) collective-permute-start(bf16[32,1280]{1,0:T(8,128)(2,1)S(1)} %whiten.1), channel_id=1, source_target_pairs={{0,8},{1,9},{2,10},{3,11},{4,12},{5,13},{6,14},{7,15},{8,0},{9,1},... | collective-permute-start | bytes 245768 | tf_op jit(solution)/shard_map/ppermute | solution.py:310
  45.7 9.0 %collective-permute-start.8 = (bf16[32,1280]{1,0:T(8,128)(2,1)S(1)}, bf16[32,1280]{1,0:T(8,128)(2,1)S(1)}, u32[]{:S(2)}, u32[]{:S(2)}) collective-permute-start(bf16[32,1280]{1,0:T(8,128)(2,1)S(1)} %whiten.1), channel_id=1, source_target_pairs={{0,16},{1,17},{2,18},{3,19},{4,20},{5,21},{6,22},{7,23},{8,24},{9,... | collective-permute-start | bytes 245768 | tf_op jit(solution)/shard_map/ppermute | solution.py:310
  47.4 7.3 %collective-permute-start.9 = (bf16[32,1280]{1,0:T(8,128)(2,1)S(1)}, bf16[32,1280]{1,0:T(8,128)(2,1)S(1)}, u32[]{:S(2)}, u32[]{:S(2)}) collective-permute-start(bf16[32,1280]{1,0:T(8,128)(2,1)S(1)} %whiten.1), channel_id=1, source_target_pairs={{0,24},{1,25},{2,26},{3,27},{4,28},{5,29},{6,30},{7,31},{8,16},{9,... | collective-permute-start | bytes 245768 | tf_op jit(solution)/shard_map/ppermute | solution.py:310
  54.7 12.0 %collective-permute-start.11 = (bf16[4,32,1280]{2,1,0:T(8,128)(2,1)S(1)}, bf16[4,32,1280]{2,1,0:T(8,128)(2,1)}, u32[]{:S(2)}, u32[]{:S(2)}) collective-permute-start(bf16[4,32,1280]{2,1,0:T(8,128)(2,1)S(1)} %pad_maximum_fusion.rest_0_), channel_id=1, source_target_pairs={{0,2},{1,3},{2,0},{3,1},{4,6},{5,7},{6,4},{7,5},{8,10},{9,11},{10,... | collective-permute-start | bytes 983048 | tf_op jit(solution)/shard_map/ppermute | solution.py:310
  58.0 14.7 %collective-permute-start.13 = (bf16[4,32,1280]{2,1,0:T(8,128)(2,1)S(1)}, bf16[4,32,1280]{2,1,0:T(8,128)(2,1)}, u32[]{:S(2)}, u32[]{:S(2)}) collective-permute-start(bf16[4,32,1280]{2,1,0:T(8,128)(2,1)S(1)} %pad_maximum_fusion.rest_0_), channel_id=1, source_target_pairs={{0,4},{1,5},{2,6},{3,7},{4,0},{5,1},{6,2},{7,3},{8,12},{9,13},{10,... | collective-permute-start | bytes 983048 | tf_op jit(solution)/shard_map/ppermute | solution.py:310
  58.3 14.4 %collective-permute-start.15 = (bf16[4,32,1280]{2,1,0:T(8,128)(2,1)S(1)}, bf16[4,32,1280]{2,1,0:T(8,128)(2,1)}, u32[]{:S(2)}, u32[]{:S(2)}) collective-permute-start(bf16[4,32,1280]{2,1,0:T(8,128)(2,1)S(1)} %pad_maximum_fusion.rest_0_), channel_id=1, source_target_pairs={{0,6},{1,7},{2,4},{3,5},{4,2},{5,3},{6,0},{7,1},{8,14},{9,15},{10,... | collective-permute-start | bytes 983048 | tf_op jit(solution)/shard_map/ppermute | solution.py:310
  59.5 16.4 %collective-permute-start.10 = (bf16[4,32,1280]{2,1,0:T(8,128)(2,1)S(1)}, bf16[4,32,1280]{2,1,0:T(8,128)(2,1)S(1)}, u32[]{:S(2)}, u32[]{:S(2)}) collective-permute-start(bf16[4,32,1280]{2,1,0:T(8,128)(2,1)S(1)} %pad_maximum_fusion.rest_0_), channel_id=1, source_target_pairs={{0,1},{1,0},{2,3},{3,2},{4,5},{5,4},{6,7},{7,6},{8,9},{9,8},{10,11... | collective-permute-start | bytes 983048 | tf_op jit(solution)/shard_map/ppermute | solution.py:310
  66.7 9.2 %collective-permute-start.12 = (bf16[4,32,1280]{2,1,0:T(8,128)(2,1)}, bf16[4,32,1280]{2,1,0:T(8,128)(2,1)}, u32[]{:S(2)}, u32[]{:S(2)}) collective-permute-start(bf16[4,32,1280]{2,1,0:T(8,128)(2,1)} %collective-permute-done.11.rest_1_), channel_id=1, source_target_pairs={{0,1},{1,0},{2,3},{3,2},{4,5},{5,4},{6,7},{7,6},{8,9},{9,8},{10,11... | collective-permute-start | bytes 983048 | tf_op jit(solution)/shard_map/ppermute | solution.py:310
  72.7 3.3 %collective-permute-start.14 = (bf16[4,32,1280]{2,1,0:T(8,128)(2,1)}, bf16[4,32,1280]{2,1,0:T(8,128)(2,1)}, u32[]{:S(2)}, u32[]{:S(2)}) collective-permute-start(bf16[4,32,1280]{2,1,0:T(8,128)(2,1)} %collective-permute-done.13.rest_2_), channel_id=1, source_target_pairs={{0,1},{1,0},{2,3},{3,2},{4,5},{5,4},{6,7},{7,6},{8,9},{9,8},{10,11... | collective-permute-start | bytes 983048 | tf_op jit(solution)/shard_map/ppermute | solution.py:310
  72.7 3.3 %collective-permute-start.16 = (bf16[4,32,1280]{2,1,0:T(8,128)(2,1)}, bf16[4,32,1280]{2,1,0:T(8,128)(2,1)}, u32[]{:S(2)}, u32[]{:S(2)}) collective-permute-start(bf16[4,32,1280]{2,1,0:T(8,128)(2,1)} %collective-permute-done.15.rest_3_), channel_id=1, source_target_pairs={{0,1},{1,0},{2,3},{3,2},{4,5},{5,4},{6,7},{7,6},{8,9},{9,8},{10,11... | collective-permute-start | bytes 983048 | tf_op jit(solution)/shard_map/ppermute | solution.py:310

commit v5 on v4

--- a/solution.py
+++ b/solution.py
@@ -22,7 +22,7 @@
 WIDTH = 2 * PART
 LAGS = 2 * HALF_LAG + 1
 LAG_TILES = -(-LAGS // 128)
-SHARES = 4
+SHARES = 2
 COLUMN_TILES = WIDTH // 128
 FIRST_TILES = 6
 FLAG_TILE = BAND // 128 * 128
@@ -67,20 +67,20 @@
     return lane_tiles(inverse).reshape(-1, 128)
 
 
-def chunk_device(chunk, members, segments):
-    per_segment = members // segments
-    segment, part = divmod(chunk, per_segment)
-    return segment // 2 * 2 * per_segment + 2 * part + segment % 2
-
-
-def transform_kernel(first, senders, share_ref, records_ref, table_ref, *rest):
+def balanced_steps(chips):
+    pairs = [step for low in range(1, chips // 2) for step in (low, low ^ (chips - 1))]
+    return pairs + [chips - 1]
+
+
+def transform_kernel(first, place_ref, table_ref, *rest):
+    records, rest = rest[: -SHARES - 2], rest[-SHARES - 2 :]
     outs, (tiles_ref, sems) = rest[:-2], rest[-2:]
-    members, rows, span = records_ref.shape
-    lines = tiles_ref.shape[1]
+    _, rows, span = records[0].shape
+    members, lines, _ = tiles_ref.shape
     columns = lines // span
     copies = []
-    for index, sender in enumerate(senders):
-        start = ((share_ref[0] * members + sender) * COLUMN_TILES + first) * span
+    for index in range(members):
+        start = ((place_ref[0] ^ index) * COLUMN_TILES + first) * span
         source = table_ref.at[pl.ds(pl.multiple_of(start, span), lines)]
         copies.append(pltpu.make_async_copy(source, tiles_ref.at[index], sems.at[index]))
         copies[-1].start()
@@ -89,29 +89,32 @@
         copies[index].wait()
         tiles = [tiles_ref[index, tile * span : (tile + 1) * span] for tile in range(columns)]
         total += jnp.dot(
-            records_ref[index], jnp.concatenate(tiles, axis=1), preferred_element_type=jnp.float32
+            records[index // 2][index % 2],
+            jnp.concatenate(tiles, axis=1),
+            preferred_element_type=jnp.float32,
         )
     kept = rows // len(outs)
     for step, out in enumerate(outs):
         chosen = total[:kept]
         for owner in range(1, len(outs)):
-            mine = (share_ref[0] ^ step) == owner
+            mine = (place_ref[0] // members ^ step) == owner
             chosen = jnp.where(mine, total[owner * kept : (owner + 1) * kept], chosen)
         out[...] = chosen
 
 
-def transform(share, records, table, senders, first, last):
-    members, rows, span = records.shape
+def transform(place, table, records, first, last):
+    _, rows, span = records[0].shape
+    members = 2 * len(records)
     columns = last - first
     vmem = pl.BlockSpec(memory_space=pltpu.VMEM)
     shape = jax.ShapeDtypeStruct((rows // SHARES, columns * 128), jnp.float32)
     return pl.pallas_call(
-        functools.partial(transform_kernel, first, senders),
+        functools.partial(transform_kernel, first),
         in_specs=[
             pl.BlockSpec(memory_space=pltpu.SMEM),
-            vmem,
             pl.BlockSpec(memory_space=pltpu.HBM),
-        ],
+        ]
+        + [vmem] * len(records),
         out_specs=[vmem] * SHARES,
         out_shape=[shape] * SHARES,
         scratch_shapes=[
@@ -125,7 +128,7 @@
             transcendentals=0,
         ),
         name="transform",
-    )(share, records, table)
+    )(place, table, *records)
 
 
 def whiten_kernel(flags_ref, *rest):
@@ -319,16 +322,23 @@
     chip = chip.reshape(segments // 2, 2, -1)
     flags = lax.dynamic_index_in_dim(chip, parity, 1, keepdims=False).reshape(1, -1)
 
-    share = (place // members).reshape(1)
-    senders = [chunk_device(chunk, members, segments) for chunk in range(members)]
-    groups = [[first + sender for sender in senders] for first in range(0, devices, members)]
-    grouped = records.reshape(members, segments * channels // members, span)
-    regrouped = lax.all_to_all(
-        grouped, "chan", split_axis=0, concat_axis=0, axis_index_groups=groups, tiled=True
+    chips = members // 2
+    grouped = records.reshape(segments // 2, 2, -1, span)
+    kept, handed = (
+        lax.dynamic_index_in_dim(grouped, side, 1, keepdims=False).reshape(chips, -1, span)
+        for side in (parity, 1 - parity)
     )
+    pair = kept, exchange(handed, 1)
+    chip_place = place % members // 2
+    arrived = {}
+    for step in [0] + balanced_steps(chips):
+        block = jnp.stack([lax.dynamic_index_in_dim(p, chip_place ^ step, 0, False) for p in pair])
+        arrived[step] = exchange(block, 2 * step) if step else block
+    blocks = [arrived[step] for step in range(chips)]
+    me = place.reshape(1)
     parts = []
     for first, last in ((0, FIRST_TILES), (FIRST_TILES, COLUMN_TILES)):
-        sums = transform(share, regrouped, tables(samples, span), senders, first, last)
+        sums = transform(me, tables(samples, span), blocks, first, last)
         parts += [sums[0]] + [exchange(sums[k], k * members) for k in range(1, SHARES)]
     white = whiten(flags, parts)
 
@@ -337,7 +347,7 @@
     plane = [line] + [exchange(line, 2 * k) for k in range(1, 4)]
     swapped = [exchange(block, 1) for block in plane]
     ids = source_ids.reshape(-1, 1)
-    common = place.reshape(1), weights, ids
+    common = me, weights, ids
     shape = segments, channels, devices
     before = correlate(0, *common, plane, shape)
     inverse = inverse_table(samples)

time: 81.6 us -> 69.6 us (0.85)
  waiting for transfers between devices: 42.1 us -> 26.9 us
  Pallas kernels: 14.4 us -> 16.2 us
  local copies, waits for them, and re-layouts: 0.28 us -> 1.65 us
    all_to_all x1 -> x0, waiting for transfers between devices: 15.4 us -> none  [per_device(): lax.all_to_all(grouped, 'chan', split_axis=0, concat_axis=0, axis_index_g...]
    ppermute x17 -> x21, starting transfers between devices: 18.5 us -> 24.3 us  [exchange(): return lax.ppermute(block, 'chan', [(i, i ^ bits) for i in range(devices)])]
    all_to_all x1 -> x0, starting transfers between devices: 5.17 us -> none  [per_device(): lax.all_to_all(grouped, 'chan', split_axis=0, concat_axis=0, axis_index_g...]
    pallas_call x2, Pallas kernels: 6.9 us -> 8.73 us  [transform(): pl.pallas_call(functools.partial(transform_kernel, first), in_specs=[pl.B...]
    dynamic_slice x0 -> x3, local copies, waits for them, and re-layouts: none -> 1.37 us  [the longest x1 1.3 us: per_device(): lax.dynamic_index_in_dim(grouped, side, 1, keepdims=False)]
    ppermute x17 -> x21, waiting for transfers between devices: 26.7 us -> 26.9 us  [exchange(): return lax.ppermute(block, 'chan', [(i, i ^ bits) for i in range(devices)])]
  transfers between devices with their start and end apart: 18 -> 21, of which waited for: 7 -> 12; matrix products, arithmetic and copies ran while one was open for 0% -> 1% of each run, Pallas kernels for 8% -> 9%
where the time goes in v5:
time: 69.6 us; the launch traced here: 69.4 us
  waiting for transfers between devices  26.9 us (39%)
  starting transfers between devices  24.3 us (35%)
  Pallas kernels  16.2 us (23%)
  local copies, waits for them, and re-layouts  1.65 us (2%)
    ppermute x21, waiting for transfers between devices, exchange(): return lax.ppermute(block, 'chan', [(i, i ^ bits) for i in range(devices)])  26.9 us
    ppermute x21, starting transfers between devices, exchange(): return lax.ppermute(block, 'chan', [(i, i ^ bits) for i in range(devices)])  24.3 us
    pallas_call x2, Pallas kernels, transform(): pl.pallas_call(functools.partial(transform_kernel, first), in_specs=[pl.B...  8.73 us
    pallas_call x2, Pallas kernels, correlate(): pl.pallas_call(functools.partial(correlate_kernel, (*shape, len(blocks)),...  7.37 us
  transfers between devices with their start and end apart: 21, of which 12 were waited for; matrix products, arithmetic and copies ran while one was open for 1% of the time, Pallas kernels for 9%

profile of v5, /device:TPU:0, one launch (start us, length us, event | category | flops | bytes accessed | tf_op | source)
XLA Modules:
  0.0 69.4 jit_solution(479999260362891803)
XLA Ops:
  0.0 1.3 %constant_dynamic-slice_fusion.20 = (bf16[4,1,128,512]{3,2,1,0:T(8,128)(2,1)S(1)}, bf16[4,1,128,512]{3,2,1,0:T(8,128)(2,1)S(1)}) fusion(bf16[4,2,128,512]{3,2,1,0:T(8,128)(2,1)} %bitcast.18, s32[]{:T(128)S(6)} %select_n.69, s32[]{:T(128)S(6)} %select_n.73), kind=kLoop, calls=%fused_computation.29 | loop fusion | bytes 2097160 | tf_op jit(solution)/shard_map/jit(dynamic_index_in_dim)/dynamic_slice | solution.py:328
  1.9 1.5 %collective-permute-done.1 = bf16[8,64,512]{2,1,0:T(8,128)(2,1)S(1)} collective-permute-done((bf16[8,64,512]{2,1,0:T(8,128)(2,1)S(1)}, bf16[8,64,512]{2,1,0:T(8,128)(2,1)S(1)}, u32[]{:S(2)}, u32[]{:S(2)}) %collective-permute-start.1) | collective-permute-done | bytes 524320 | tf_op jit(solution)/shard_map/ppermute | solution.py:313
  3.4 4.9 %collective-permute-start.8 = (bf16[2,64,512]{2,1,0:T(8,128)(2,1)S(1)}, bf16[2,64,512]{2,1,0:T(8,128)(2,1)S(1)}, u32[]{:S(2)}, u32[]{:S(2)}) collective-permute-start(bf16[2,64,512]{2,1,0:T(8,128)(2,1)S(1)} %pad_maximum_fusion.8), channel_id=1, source_target_pairs={{0,14},{1,15},{2,12},{3,13},{4,10},{5,11},{6,8},{7,9},{8,6},{9,7},... | collective-permute-start | bytes 393224 | tf_op jit(solution)/shard_map/ppermute | solution.py:313
  8.8 1.6 %collective-permute-start.6 = (bf16[2,64,512]{2,1,0:T(8,128)(2,1)S(1)}, bf16[2,64,512]{2,1,0:T(8,128)(2,1)S(1)}, u32[]{:S(2)}, u32[]{:S(2)}) collective-permute-start(bf16[2,64,512]{2,1,0:T(8,128)(2,1)S(1)} %pad_maximum_fusion.6), channel_id=1, source_target_pairs={{0,10},{1,11},{2,8},{3,9},{4,14},{5,15},{6,12},{7,13},{8,2},{9,3},... | collective-permute-start | bytes 393224 | tf_op jit(solution)/shard_map/ppermute | solution.py:313
  10.6 2.9 %collective-permute-start.4 = (bf16[2,64,512]{2,1,0:T(8,128)(2,1)S(1)}, bf16[2,64,512]{2,1,0:T(8,128)(2,1)S(1)}, u32[]{:S(2)}, u32[]{:S(2)}) collective-permute-start(bf16[2,64,512]{2,1,0:T(8,128)(2,1)S(1)} %pad_maximum_fusion.4), channel_id=1, source_target_pairs={{0,6},{1,7},{2,4},{3,5},{4,2},{5,3},{6,0},{7,1},{8,14},{9,15},{10,... | collective-permute-start | bytes 393224 | tf_op jit(solution)/shard_map/ppermute | solution.py:313
  14.5 2.2 %collective-permute-done.7.rest_6_ = bf16[2,64,512]{2,1,0:T(8,128)(2,1)S(1)} collective-permute-done((bf16[2,64,512]{2,1,0:T(8,128)(2,1)S(1)}, bf16[2,64,512]{2,1,0:T(8,128)(2,1)S(1)}, u32[]{:S(2)}, u32[]{:S(2)}) %collective-permute-start.7) | collective-permute-done | bytes 131104 | tf_op jit(solution)/shard_map/ppermute | solution.py:313
  16.7 1.2 %collective-permute-start.2 = (bf16[2,64,512]{2,1,0:T(8,128)(2,1)S(1)}, bf16[2,64,512]{2,1,0:T(8,128)(2,1)S(1)}, u32[]{:S(2)}, u32[]{:S(2)}) collective-permute-start(bf16[2,64,512]{2,1,0:T(8,128)(2,1)S(1)} %pad_maximum_fusion.2), channel_id=1, source_target_pairs={{0,2},{1,3},{2,0},{3,1},{4,6},{5,7},{6,4},{7,5},{8,10},{9,11},{10,... | collective-permute-start | bytes 393224 | tf_op jit(solution)/shard_map/ppermute | solution.py:313
  17.9 1.3 %collective-permute-done.6.rest_5_ = bf16[2,64,512]{2,1,0:T(8,128)(2,1)S(1)} collective-permute-done((bf16[2,64,512]{2,1,0:T(8,128)(2,1)S(1)}, bf16[2,64,512]{2,1,0:T(8,128)(2,1)S(1)}, u32[]{:S(2)}, u32[]{:S(2)}) %collective-permute-start.6) | collective-permute-done | bytes 131104 | tf_op jit(solution)/shard_map/ppermute | solution.py:313
  19.2 1.5 %collective-permute-done.5.rest_4_ = bf16[2,64,512]{2,1,0:T(8,128)(2,1)S(1)} collective-permute-done((bf16[2,64,512]{2,1,0:T(8,128)(2,1)S(1)}, bf16[2,64,512]{2,1,0:T(8,128)(2,1)S(1)}, u32[]{:S(2)}, u32[]{:S(2)}) %collective-permute-start.5) | collective-permute-done | bytes 131104 | tf_op jit(solution)/shard_map/ppermute | solution.py:313
  20.7 1.5 %collective-permute-done.2.rest_1_ = bf16[2,64,512]{2,1,0:T(8,128)(2,1)S(1)} collective-permute-done((bf16[2,64,512]{2,1,0:T(8,128)(2,1)S(1)}, bf16[2,64,512]{2,1,0:T(8,128)(2,1)S(1)}, u32[]{:S(2)}, u32[]{:S(2)}) %collective-permute-start.2) | collective-permute-done | bytes 131104 | tf_op jit(solution)/shard_map/ppermute | solution.py:313
  22.2 5.0 %transform.2 = (f32[32,768]{1,0:T(8,128)S(1)}, f32[32,768]{1,0:T(8,128)S(1)}) custom-call(s32[1]{0:T(128)} %bitcast.place_ref, bf16[163840,128]{1,0:T(8,128)(2,1)} %constant.100.clone.table_ref, bf16[2,64,512]{2,1,0:T(8,128)(2,1)S(1)} %pad_maximum_fusion.1.rest_0_, bf16[2,64,512]{2,1,0:T(8,128)(2,1)S(1)} %collective-permute-done.2.rest_1_, ...), custom_call_target="tpu_custom_call" | custom-call | flops 805306368 | bytes 12582912 | tf_op jit(solution)/shard_map/transform/pallas_call | solution.py:111
  27.2 2.7 %collective-permute-start.9 = (f32[32,768]{1,0:T(8,128)S(1)}, f32[32,768]{1,0:T(8,128)S(1)}, u32[]{:S(2)}, u32[]{:S(2)}) collective-permute-start(f32[32,768]{1,0:T(8,128)S(1)} %get-tuple-element.10), channel_id=1, source_target_pairs={{0,16},{1,17},{2,18},{3,19},{4,20},{5,21},{6,22},{7,23},{8,24},{9,... | collective-permute-start | bytes 294920 | tf_op jit(solution)/shard_map/ppermute | solution.py:313
  29.9 3.7 %transform.3 = (f32[32,512]{1,0:T(8,128)S(1)}, f32[32,512]{1,0:T(8,128)S(1)}) custom-call(s32[1]{0:T(128)} %bitcast.place_ref, bf16[163840,128]{1,0:T(8,128)(2,1)} %constant.100.clone.table_ref, bf16[2,64,512]{2,1,0:T(8,128)(2,1)S(1)} %pad_maximum_fusion.1.rest_0_, bf16[2,64,512]{2,1,0:T(8,128)(2,1)S(1)} %collective-permute-done.2.rest_1_, ...), custom_call_target="tpu_custom_call" | custom-call | flops 536870912 | bytes 8388608 | tf_op jit(solution)/shard_map/transform/pallas_call | solution.py:111
  35.5 3.4 %collective-permute-done.10.rest_3_ = f32[32,512]{1,0:T(8,128)S(1)} collective-permute-done((f32[32,512]{1,0:T(8,128)S(1)}, f32[32,512]{1,0:T(8,128)S(1)}, u32[]{:S(2)}, u32[]{:S(2)}) %collective-permute-start.10) | collective-permute-done | bytes 65568 | tf_op jit(solution)/shard_map/ppermute | solution.py:313
  39.0 2.0 %collective-permute-start.13 = (bf16[32,1280]{1,0:T(8,128)(2,1)S(1)}, bf16[32,1280]{1,0:T(8,128)(2,1)S(1)}, u32[]{:S(2)}, u32[]{:S(2)}) collective-permute-start(bf16[32,1280]{1,0:T(8,128)(2,1)S(1)} %whiten.1), channel_id=1, source_target_pairs={{0,24},{1,25},{2,26},{3,27},{4,28},{5,29},{6,30},{7,31},{8,16},{9,... | collective-permute-start | bytes 245768 | tf_op jit(solution)/shard_map/ppermute | solution.py:313
  41.0 2.4 %collective-permute-start.12 = (bf16[32,1280]{1,0:T(8,128)(2,1)S(1)}, bf16[32,1280]{1,0:T(8,128)(2,1)S(1)}, u32[]{:S(2)}, u32[]{:S(2)}) collective-permute-start(bf16[32,1280]{1,0:T(8,128)(2,1)S(1)} %whiten.1), channel_id=1, source_target_pairs={{0,16},{1,17},{2,18},{3,19},{4,20},{5,21},{6,22},{7,23},{8,24},{9,... | collective-permute-start | bytes 245768 | tf_op jit(solution)/shard_map/ppermute | solution.py:313
  43.4 2.3 %collective-permute-done.13 = bf16[32,1280]{1,0:T(8,128)(2,1)S(1)} collective-permute-done((bf16[32,1280]{1,0:T(8,128)(2,1)S(1)}, bf16[32,1280]{1,0:T(8,128)(2,1)S(1)}, u32[]{:S(2)}, u32[]{:S(2)}) %collective-permute-start.13) | collective-permute-done | bytes 81952 | tf_op jit(solution)/shard_map/ppermute | solution.py:313
  46.3 1.7 %collective-permute-done.12 = bf16[32,1280]{1,0:T(8,128)(2,1)S(1)} collective-permute-done((bf16[32,1280]{1,0:T(8,128)(2,1)S(1)}, bf16[32,1280]{1,0:T(8,128)(2,1)S(1)}, u32[]{:S(2)}, u32[]{:S(2)}) %collective-permute-start.12) | collective-permute-done | bytes 81952 | tf_op jit(solution)/shard_map/ppermute | solution.py:313
  48.1 1.5 %collective-permute-start.15 = (bf16[4,32,1280]{2,1,0:T(8,128)(2,1)S(1)}, bf16[4,32,1280]{2,1,0:T(8,128)(2,1)}, u32[]{:S(2)}, u32[]{:S(2)}) collective-permute-start(bf16[4,32,1280]{2,1,0:T(8,128)(2,1)S(1)} %pad_maximum_fusion.rest_0_), channel_id=1, source_target_pairs={{0,2},{1,3},{2,0},{3,1},{4,6},{5,7},{6,4},{7,5},{8,10},{9,11},{10,... | collective-permute-start | bytes 983048 | tf_op jit(solution)/shard_map/ppermute | solution.py:313
  50.2 1.4 %collective-permute-start.19 = (bf16[4,32,1280]{2,1,0:T(8,128)(2,1)S(1)}, bf16[4,32,1280]{2,1,0:T(8,128)(2,1)}, u32[]{:S(2)}, u32[]{:S(2)}) collective-permute-start(bf16[4,32,1280]{2,1,0:T(8,128)(2,1)S(1)} %pad_maximum_fusion.rest_0_), channel_id=1, source_target_pairs={{0,6},{1,7},{2,4},{3,5},{4,2},{5,3},{6,0},{7,1},{8,14},{9,15},{10,... | collective-permute-start | bytes 983048 | tf_op jit(solution)/shard_map/ppermute | solution.py:313
  51.6 5.5 %collective-permute-done.15.rest_1_ = bf16[4,32,1280]{2,1,0:T(8,128)(2,1)} collective-permute-done((bf16[4,32,1280]{2,1,0:T(8,128)(2,1)S(1)}, bf16[4,32,1280]{2,1,0:T(8,128)(2,1)}, u32[]{:S(2)}, u32[]{:S(2)}) %collective-permute-start.15) | collective-permute-done | bytes 327712 | tf_op jit(solution)/shard_map/ppermute | solution.py:313
  57.1 4.3 %collective-permute-done.17.rest_2_ = bf16[4,32,1280]{2,1,0:T(8,128)(2,1)} collective-permute-done((bf16[4,32,1280]{2,1,0:T(8,128)(2,1)S(1)}, bf16[4,32,1280]{2,1,0:T(8,128)(2,1)}, u32[]{:S(2)}, u32[]{:S(2)}) %collective-permute-start.17) | collective-permute-done | bytes 327712 | tf_op jit(solution)/shard_map/ppermute | solution.py:313
  62.0 2.6 %correlate.2.rest_4_ = f32[4,64,1280]{2,1,0:T(8,128)S(1)} custom-call(s32[1]{0:T(128)} %bitcast.place_ref, f32[8,4]{1,0:T(8,128)S(1)} %convert_element_type.3.flags_ref, s32[64,1]{1,0:T(8,128)S(1)} %copy.10.ids_ref, bf16[4,32,1280]{2,1,0:T(8,128)(2,1)S(1)} %pad_maximum_fusion.rest_0_, bf16[4,32,1280]{2,1,0:T(8,128)(2,1)} %collective-permute-done.15.rest_1_, ...), custom_call_target="tpu_custom_call" | custom-call | flops 83886080 | bytes 1310720 | tf_op jit(solution)/shard_map/correlate/pallas_call | solution.py:288
  64.7 4.8 %correlate.3 = f32[64,4,1001]{2,1,0:T(4,128)} custom-call(s32[1]{0:T(128)} %bitcast.place_ref, f32[8,4]{1,0:T(8,128)S(1)} %convert_element_type.3.flags_ref, s32[64,1]{1,0:T(8,128)S(1)} %copy.10.ids_ref, bf16[4,32,1280]{2,1,0:T(8,128)(2,1)S(1)} %collective-permute-done.14.rest_0_, bf16[4,32,1280]{2,1,0:T(8,128)(2,1)} %collective-permute-done.16.rest_1_, ...), custom_call_target="tpu_custom_call" | custom-call | flops 83886080 | bytes 1310720 | tf_op jit(solution)/shard_map/correlate/pallas_call | solution.py:288
  (46 shorter events, 6.2 us)
Async XLA Ops:
  1.3 2.1 %collective-permute-start.1 = (bf16[8,64,512]{2,1,0:T(8,128)(2,1)S(1)}, bf16[8,64,512]{2,1,0:T(8,128)(2,1)S(1)}, u32[]{:S(2)}, u32[]{:S(2)}) collective-permute-start(bf16[8,64,512]{2,1,0:T(8,128)(2,1)S(1)} %bitcast.19), channel_id=1, source_target_pairs={{0,1},{1,0},{2,3},{3,2},{4,5},{5,4},{6,7},{7,6},{8,9},{9,8},{10,11... | collective-permute-start | bytes 1572872 | tf_op jit(solution)/shard_map/ppermute | solution.py:313
  3.4 10.1 %collective-permute-start.8 = (bf16[2,64,512]{2,1,0:T(8,128)(2,1)S(1)}, bf16[2,64,512]{2,1,0:T(8,128)(2,1)S(1)}, u32[]{:S(2)}, u32[]{:S(2)}) collective-permute-start(bf16[2,64,512]{2,1,0:T(8,128)(2,1)S(1)} %pad_maximum_fusion.8), channel_id=1, source_target_pairs={{0,14},{1,15},{2,12},{3,13},{4,10},{5,11},{6,8},{7,9},{8,6},{9,7},... | collective-permute-start | bytes 393224 | tf_op jit(solution)/shard_map/ppermute | solution.py:313
  8.3 8.4 %collective-permute-start.7 = (bf16[2,64,512]{2,1,0:T(8,128)(2,1)S(1)}, bf16[2,64,512]{2,1,0:T(8,128)(2,1)S(1)}, u32[]{:S(2)}, u32[]{:S(2)}) collective-permute-start(bf16[2,64,512]{2,1,0:T(8,128)(2,1)S(1)} %pad_maximum_fusion.7), channel_id=1, source_target_pairs={{0,12},{1,13},{2,14},{3,15},{4,8},{5,9},{6,10},{7,11},{8,4},{9,5},... | collective-permute-start | bytes 393224 | tf_op jit(solution)/shard_map/ppermute | solution.py:313
  8.8 10.4 %collective-permute-start.6 = (bf16[2,64,512]{2,1,0:T(8,128)(2,1)S(1)}, bf16[2,64,512]{2,1,0:T(8,128)(2,1)S(1)}, u32[]{:S(2)}, u32[]{:S(2)}) collective-permute-start(bf16[2,64,512]{2,1,0:T(8,128)(2,1)S(1)} %pad_maximum_fusion.6), channel_id=1, source_target_pairs={{0,10},{1,11},{2,8},{3,9},{4,14},{5,15},{6,12},{7,13},{8,2},{9,3},... | collective-permute-start | bytes 393224 | tf_op jit(solution)/shard_map/ppermute | solution.py:313
  10.4 10.3 %collective-permute-start.5 = (bf16[2,64,512]{2,1,0:T(8,128)(2,1)S(1)}, bf16[2,64,512]{2,1,0:T(8,128)(2,1)S(1)}, u32[]{:S(2)}, u32[]{:S(2)}) collective-permute-start(bf16[2,64,512]{2,1,0:T(8,128)(2,1)S(1)} %pad_maximum_fusion.5), channel_id=1, source_target_pairs={{0,8},{1,9},{2,10},{3,11},{4,12},{5,13},{6,14},{7,15},{8,0},{9,1},... | collective-permute-start | bytes 393224 | tf_op jit(solution)/shard_map/ppermute | solution.py:313
  10.6 10.1 %collective-permute-start.4 = (bf16[2,64,512]{2,1,0:T(8,128)(2,1)S(1)}, bf16[2,64,512]{2,1,0:T(8,128)(2,1)S(1)}, u32[]{:S(2)}, u32[]{:S(2)}) collective-permute-start(bf16[2,64,512]{2,1,0:T(8,128)(2,1)S(1)} %pad_maximum_fusion.4), channel_id=1, source_target_pairs={{0,6},{1,7},{2,4},{3,5},{4,2},{5,3},{6,0},{7,1},{8,14},{9,15},{10,... | collective-permute-start | bytes 393224 | tf_op jit(solution)/shard_map/ppermute | solution.py:313
  13.5 7.2 %collective-permute-start.3 = (bf16[2,64,512]{2,1,0:T(8,128)(2,1)S(1)}, bf16[2,64,512]{2,1,0:T(8,128)(2,1)S(1)}, u32[]{:S(2)}, u32[]{:S(2)}) collective-permute-start(bf16[2,64,512]{2,1,0:T(8,128)(2,1)S(1)} %pad_maximum_fusion.3), channel_id=1, source_target_pairs={{0,4},{1,5},{2,6},{3,7},{4,0},{5,1},{6,2},{7,3},{8,12},{9,13},{10,... | collective-permute-start | bytes 393224 | tf_op jit(solution)/shard_map/ppermute | solution.py:313
  16.7 5.5 %collective-permute-start.2 = (bf16[2,64,512]{2,1,0:T(8,128)(2,1)S(1)}, bf16[2,64,512]{2,1,0:T(8,128)(2,1)S(1)}, u32[]{:S(2)}, u32[]{:S(2)}) collective-permute-start(bf16[2,64,512]{2,1,0:T(8,128)(2,1)S(1)} %pad_maximum_fusion.2), channel_id=1, source_target_pairs={{0,2},{1,3},{2,0},{3,1},{4,6},{5,7},{6,4},{7,5},{8,10},{9,11},{10,... | collective-permute-start | bytes 393224 | tf_op jit(solution)/shard_map/ppermute | solution.py:313
  27.2 6.8 %copy-start.1 = (s32[8,4]{0,1:T(4,128)S(1)}, s32[8,4]{0,1:T(4,128)}, u32[]{:S(2)}) copy-start(s32[8,4]{0,1:T(4,128)} %param.6) | copy-start | bytes 388
  27.2 34.7 %copy-start.2 = (s32[64]{0:T(128)S(1)}, s32[64]{0:T(128)}, u32[]{:S(2)}) copy-start(s32[64]{0:T(128)} %param.7) | copy-start | bytes 772
  27.2 11.6 %collective-permute-start.9 = (f32[32,768]{1,0:T(8,128)S(1)}, f32[32,768]{1,0:T(8,128)S(1)}, u32[]{:S(2)}, u32[]{:S(2)}) collective-permute-start(f32[32,768]{1,0:T(8,128)S(1)} %get-tuple-element.10), channel_id=1, source_target_pairs={{0,16},{1,17},{2,18},{3,19},{4,20},{5,21},{6,22},{7,23},{8,24},{9,... | collective-permute-start | bytes 294920 | tf_op jit(solution)/shard_map/ppermute | solution.py:313
  33.6 31.0 %copy-start = (bf16[10240,128]{1,0:T(8,128)(2,1)S(1)}, bf16[10240,128]{1,0:T(8,128)(2,1)}, u32[]{:S(2)}) copy-start(bf16[10240,128]{1,0:T(8,128)(2,1)} %constant.101.clone.rest_5_) | copy-start | bytes 7864324
  33.6 5.2 %collective-permute-start.10 = (f32[32,512]{1,0:T(8,128)S(1)}, f32[32,512]{1,0:T(8,128)S(1)}, u32[]{:S(2)}, u32[]{:S(2)}) collective-permute-start(f32[32,512]{1,0:T(8,128)S(1)} %get-tuple-element.12), channel_id=1, source_target_pairs={{0,16},{1,17},{2,18},{3,19},{4,20},{5,21},{6,22},{7,23},{8,24},{9,... | collective-permute-start | bytes 196616 | tf_op jit(solution)/shard_map/ppermute | solution.py:313
  34.1 1.2 %collective-permute-start = (f32[8,4]{1,0:T(8,128)S(1)}, f32[8,4]{1,0:T(8,128)S(1)}, u32[]{:S(2)}, u32[]{:S(2)}) collective-permute-start(f32[8,4]{1,0:T(8,128)S(1)} %convert_element_type.3.flags_ref), channel_id=1, source_target_pairs={{0,1},{1,0},{2,3},{3,2},{4,5},{5,4},{6,7},{7,6},{8,9},{9,8},{10,11... | collective-permute-start | bytes 392 | tf_op jit(solution)/shard_map/ppermute | solution.py:313
  39.0 6.8 %collective-permute-start.13 = (bf16[32,1280]{1,0:T(8,128)(2,1)S(1)}, bf16[32,1280]{1,0:T(8,128)(2,1)S(1)}, u32[]{:S(2)}, u32[]{:S(2)}) collective-permute-start(bf16[32,1280]{1,0:T(8,128)(2,1)S(1)} %whiten.1), channel_id=1, source_target_pairs={{0,24},{1,25},{2,26},{3,27},{4,28},{5,29},{6,30},{7,31},{8,16},{9,... | collective-permute-start | bytes 245768 | tf_op jit(solution)/shard_map/ppermute | solution.py:313
  41.0 5.3 %collective-permute-start.11 = (bf16[32,1280]{1,0:T(8,128)(2,1)S(1)}, bf16[32,1280]{1,0:T(8,128)(2,1)S(1)}, u32[]{:S(2)}, u32[]{:S(2)}) collective-permute-start(bf16[32,1280]{1,0:T(8,128)(2,1)S(1)} %whiten.1), channel_id=1, source_target_pairs={{0,8},{1,9},{2,10},{3,11},{4,12},{5,13},{6,14},{7,15},{8,0},{9,1},... | collective-permute-start | bytes 245768 | tf_op jit(solution)/shard_map/ppermute | solution.py:313
  41.0 7.0 %collective-permute-start.12 = (bf16[32,1280]{1,0:T(8,128)(2,1)S(1)}, bf16[32,1280]{1,0:T(8,128)(2,1)S(1)}, u32[]{:S(2)}, u32[]{:S(2)}) collective-permute-start(bf16[32,1280]{1,0:T(8,128)(2,1)S(1)} %whiten.1), channel_id=1, source_target_pairs={{0,16},{1,17},{2,18},{3,19},{4,20},{5,21},{6,22},{7,23},{8,24},{9,... | collective-permute-start | bytes 245768 | tf_op jit(solution)/shard_map/ppermute | solution.py:313
  48.1 9.0 %collective-permute-start.15 = (bf16[4,32,1280]{2,1,0:T(8,128)(2,1)S(1)}, bf16[4,32,1280]{2,1,0:T(8,128)(2,1)}, u32[]{:S(2)}, u32[]{:S(2)}) collective-permute-start(bf16[4,32,1280]{2,1,0:T(8,128)(2,1)S(1)} %pad_maximum_fusion.rest_0_), channel_id=1, source_target_pairs={{0,2},{1,3},{2,0},{3,1},{4,6},{5,7},{6,4},{7,5},{8,10},{9,11},{10,... | collective-permute-start | bytes 983048 | tf_op jit(solution)/shard_map/ppermute | solution.py:313
  49.5 11.8 %collective-permute-start.17 = (bf16[4,32,1280]{2,1,0:T(8,128)(2,1)S(1)}, bf16[4,32,1280]{2,1,0:T(8,128)(2,1)}, u32[]{:S(2)}, u32[]{:S(2)}) collective-permute-start(bf16[4,32,1280]{2,1,0:T(8,128)(2,1)S(1)} %pad_maximum_fusion.rest_0_), channel_id=1, source_target_pairs={{0,4},{1,5},{2,6},{3,7},{4,0},{5,1},{6,2},{7,3},{8,12},{9,13},{10,... | collective-permute-start | bytes 983048 | tf_op jit(solution)/shard_map/ppermute | solution.py:313
  50.2 11.2 %collective-permute-start.19 = (bf16[4,32,1280]{2,1,0:T(8,128)(2,1)S(1)}, bf16[4,32,1280]{2,1,0:T(8,128)(2,1)}, u32[]{:S(2)}, u32[]{:S(2)}) collective-permute-start(bf16[4,32,1280]{2,1,0:T(8,128)(2,1)S(1)} %pad_maximum_fusion.rest_0_), channel_id=1, source_target_pairs={{0,6},{1,7},{2,4},{3,5},{4,2},{5,3},{6,0},{7,1},{8,14},{9,15},{10,... | collective-permute-start | bytes 983048 | tf_op jit(solution)/shard_map/ppermute | solution.py:313
  51.6 13.0 %collective-permute-start.14 = (bf16[4,32,1280]{2,1,0:T(8,128)(2,1)S(1)}, bf16[4,32,1280]{2,1,0:T(8,128)(2,1)S(1)}, u32[]{:S(2)}, u32[]{:S(2)}) collective-permute-start(bf16[4,32,1280]{2,1,0:T(8,128)(2,1)S(1)} %pad_maximum_fusion.rest_0_), channel_id=1, source_target_pairs={{0,1},{1,0},{2,3},{3,2},{4,5},{5,4},{6,7},{7,6},{8,9},{9,8},{10,11... | collective-permute-start | bytes 983048 | tf_op jit(solution)/shard_map/ppermute | solution.py:313
  57.1 7.5 %collective-permute-start.16 = (bf16[4,32,1280]{2,1,0:T(8,128)(2,1)}, bf16[4,32,1280]{2,1,0:T(8,128)(2,1)}, u32[]{:S(2)}, u32[]{:S(2)}) collective-permute-start(bf16[4,32,1280]{2,1,0:T(8,128)(2,1)} %collective-permute-done.15.rest_1_), channel_id=1, source_target_pairs={{0,1},{1,0},{2,3},{3,2},{4,5},{5,4},{6,7},{7,6},{8,9},{9,8},{10,11... | collective-permute-start | bytes 983048 | tf_op jit(solution)/shard_map/ppermute | solution.py:313
  61.4 3.3 %collective-permute-start.18 = (bf16[4,32,1280]{2,1,0:T(8,128)(2,1)}, bf16[4,32,1280]{2,1,0:T(8,128)(2,1)}, u32[]{:S(2)}, u32[]{:S(2)}) collective-permute-start(bf16[4,32,1280]{2,1,0:T(8,128)(2,1)} %collective-permute-done.17.rest_2_), channel_id=1, source_target_pairs={{0,1},{1,0},{2,3},{3,2},{4,5},{5,4},{6,7},{7,6},{8,9},{9,8},{10,11... | collective-permute-start | bytes 983048 | tf_op jit(solution)/shard_map/ppermute | solution.py:313
  61.4 3.3 %collective-permute-start.20 = (bf16[4,32,1280]{2,1,0:T(8,128)(2,1)}, bf16[4,32,1280]{2,1,0:T(8,128)(2,1)}, u32[]{:S(2)}, u32[]{:S(2)}) collective-permute-start(bf16[4,32,1280]{2,1,0:T(8,128)(2,1)} %collective-permute-done.19.rest_3_), channel_id=1, source_target_pairs={{0,1},{1,0},{2,3},{3,2},{4,5},{5,4},{6,7},{7,6},{8,9},{9,8},{10,11... | collective-permute-start | bytes 983048 | tf_op jit(solution)/shard_map/ppermute | solution.py:313

commit v6 on v5

--- a/solution.py
+++ b/solution.py
@@ -68,24 +68,32 @@
 
 
 def balanced_steps(chips):
-    pairs = [step for low in range(1, chips // 2) for step in (low, low ^ (chips - 1))]
-    return pairs + [chips - 1]
-
-
-def transform_kernel(first, place_ref, table_ref, *rest):
-    records, rest = rest[: -SHARES - 2], rest[-SHARES - 2 :]
+    steps = [chips - 1]
+    for low in range(1, chips // 2):
+        steps += [low, low ^ (chips - 1)]
+    return steps
+
+
+def transform_kernel(steps, first, started, place_ref, table_ref, *rest):
+    records, rest = rest[: len(steps)], rest[len(steps) :]
+    if started:
+        before_ref, rest = rest[0], rest[1:]
     outs, (tiles_ref, sems) = rest[:-2], rest[-2:]
     _, rows, span = records[0].shape
-    members, lines, _ = tiles_ref.shape
+    blocks, lines, _ = tiles_ref.shape
     columns = lines // span
     copies = []
-    for index in range(members):
-        start = ((place_ref[0] ^ index) * COLUMN_TILES + first) * span
+    for index in range(blocks):
+        sender = place_ref[0] ^ (2 * steps[index // 2] + index % 2)
+        start = (sender * COLUMN_TILES + first) * span
         source = table_ref.at[pl.ds(pl.multiple_of(start, span), lines)]
         copies.append(pltpu.make_async_copy(source, tiles_ref.at[index], sems.at[index]))
         copies[-1].start()
-    total = jnp.zeros((rows, columns * 128), jnp.float32)
-    for index in range(members):
+    if started:
+        total = before_ref[:, first * 128 : (first + columns) * 128]
+    else:
+        total = jnp.zeros((rows, columns * 128), jnp.float32)
+    for index in range(blocks):
         copies[index].wait()
         tiles = [tiles_ref[index, tile * span : (tile + 1) * span] for tile in range(columns)]
         total += jnp.dot(
@@ -93,42 +101,44 @@
             jnp.concatenate(tiles, axis=1),
             preferred_element_type=jnp.float32,
         )
-    kept = rows // len(outs)
-    for step, out in enumerate(outs):
-        chosen = total[:kept]
-        for owner in range(1, len(outs)):
-            mine = (place_ref[0] // members ^ step) == owner
-            chosen = jnp.where(mine, total[owner * kept : (owner + 1) * kept], chosen)
-        out[...] = chosen
-
-
-def transform(place, table, records, first, last):
+    if len(outs) == 1:
+        outs[0][...] = total
+    else:
+        kept = rows // 2
+        mine = place_ref[0] < table_ref.shape[0] // (2 * COLUMN_TILES * span)
+        outs[0][...] = jnp.where(mine, total[:kept], total[kept:])
+        outs[1][...] = jnp.where(mine, total[kept:], total[:kept])
+
+
+def transform(place, table, arrived, steps, first, last, before=None):
+    records = [arrived[step] for step in steps]
     _, rows, span = records[0].shape
-    members = 2 * len(records)
     columns = last - first
+    blocks = 2 * len(steps)
     vmem = pl.BlockSpec(memory_space=pltpu.VMEM)
-    shape = jax.ShapeDtypeStruct((rows // SHARES, columns * 128), jnp.float32)
+    started = before is not None
+    outs = 2 if started else 1
     return pl.pallas_call(
-        functools.partial(transform_kernel, first),
+        functools.partial(transform_kernel, steps, first, started),
         in_specs=[
             pl.BlockSpec(memory_space=pltpu.SMEM),
             pl.BlockSpec(memory_space=pltpu.HBM),
         ]
-        + [vmem] * len(records),
-        out_specs=[vmem] * SHARES,
-        out_shape=[shape] * SHARES,
+        + [vmem] * (len(records) + started),
+        out_specs=[vmem] * outs,
+        out_shape=[jax.ShapeDtypeStruct((rows // outs, columns * 128), jnp.float32)] * outs,
         scratch_shapes=[
-            pltpu.VMEM((members, columns * span, 128), jnp.bfloat16),
-            pltpu.SemaphoreType.DMA((members,)),
+            pltpu.VMEM((blocks, columns * span, 128), jnp.bfloat16),
+            pltpu.SemaphoreType.DMA((blocks,)),
         ],
-        compiler_params=pltpu.CompilerParams(vmem_limit_bytes=32 * 2**20),
+        compiler_params=pltpu.CompilerParams(vmem_limit_bytes=24 * 2**20),
         cost_estimate=pl.CostEstimate(
-            flops=2 * rows * members * span * columns * 128,
-            bytes_accessed=2 * members * span * columns * 128,
+            flops=2 * rows * blocks * span * columns * 128,
+            bytes_accessed=2 * blocks * span * columns * 128,
             transcendentals=0,
         ),
         name="transform",
-    )(place, table, *records)
+    )(place, table, *records, *([before] if started else []))
 
 
 def whiten_kernel(flags_ref, *rest):
@@ -330,16 +340,19 @@
     )
     pair = kept, exchange(handed, 1)
     chip_place = place % members // 2
+    steps = [0] + balanced_steps(chips)
     arrived = {}
-    for step in [0] + balanced_steps(chips):
+    for step in steps:
         block = jnp.stack([lax.dynamic_index_in_dim(p, chip_place ^ step, 0, False) for p in pair])
         arrived[step] = exchange(block, 2 * step) if step else block
-    blocks = [arrived[step] for step in range(chips)]
     me = place.reshape(1)
+    table = tables(samples, span)
+    early, late = steps[: chips // 2], steps[chips // 2 :]
+    before = transform(me, table, arrived, early, 0, COLUMN_TILES)[0]
     parts = []
     for first, last in ((0, FIRST_TILES), (FIRST_TILES, COLUMN_TILES)):
-        sums = transform(me, tables(samples, span), blocks, first, last)
-        parts += [sums[0]] + [exchange(sums[k], k * members) for k in range(1, SHARES)]
+        own, other = transform(me, table, arrived, late, first, last, before)
+        parts += [own, exchange(other, members)]
     white = whiten(flags, parts)
 
     far = devices // 8

time: 69.6 us -> 69.1 us (level)
  starting transfers between devices: 24.3 us -> 22.9 us
  Pallas kernels: 16.2 us -> 17.5 us
    ppermute x21, starting transfers between devices: 24.3 us -> 22.9 us  [exchange(): return lax.ppermute(block, 'chan', [(i, i ^ bits) for i in range(devices)])]
    pallas_call x2 -> x3, Pallas kernels: 8.73 us -> 10 us  [transform(): pl.pallas_call(functools.partial(transform_kernel, steps, first, started)...]
  transfers between devices with their start and end apart: 21 -> 21, of which waited for: 12 -> 11; matrix products, arithmetic and copies ran while one was open for 1% -> 1% of each run, Pallas kernels for 9% -> 14%
where the time goes in v6:
time: 69.1 us; the launch traced here: 68.9 us
  waiting for transfers between devices  26.4 us (38%)
  starting transfers between devices  22.9 us (33%)
  Pallas kernels  17.5 us (25%)
  local copies, waits for them, and re-layouts  1.65 us (2%)
    ppermute x21, waiting for transfers between devices, exchange(): return lax.ppermute(block, 'chan', [(i, i ^ bits) for i in range(devices)])  26.4 us
    ppermute x21, starting transfers between devices, exchange(): return lax.ppermute(block, 'chan', [(i, i ^ bits) for i in range(devices)])  22.9 us
    pallas_call x3, Pallas kernels, transform(): pl.pallas_call(functools.partial(transform_kernel, steps, first, started)...  10 us
    pallas_call x2, Pallas kernels, correlate(): pl.pallas_call(functools.partial(correlate_kernel, (*shape, len(blocks)),...  7.38 us
  transfers between devices with their start and end apart: 21, of which 11 were waited for; matrix products, arithmetic and copies ran while one was open for 1% of the time, Pallas kernels for 14%

profile of v6, /device:TPU:0, one launch (start us, length us, event | category | flops | bytes accessed | tf_op | source)
XLA Modules:
  0.0 68.9 jit_solution(10416316784145963974)
XLA Ops:
  0.0 1.3 %constant_dynamic-slice_fusion.20 = (bf16[4,1,128,512]{3,2,1,0:T(8,128)(2,1)S(1)}, bf16[4,1,128,512]{3,2,1,0:T(8,128)(2,1)S(1)}) fusion(bf16[4,2,128,512]{3,2,1,0:T(8,128)(2,1)} %bitcast.18, s32[]{:T(128)S(6)} %select_n.69, s32[]{:T(128)S(6)} %select_n.73), kind=kLoop, calls=%fused_computation.29 | loop fusion | bytes 2097160 | tf_op jit(solution)/shard_map/jit(dynamic_index_in_dim)/dynamic_slice | solution.py:338
  1.9 1.5 %collective-permute-done.1 = bf16[8,64,512]{2,1,0:T(8,128)(2,1)S(1)} collective-permute-done((bf16[8,64,512]{2,1,0:T(8,128)(2,1)S(1)}, bf16[8,64,512]{2,1,0:T(8,128)(2,1)S(1)}, u32[]{:S(2)}, u32[]{:S(2)}) %collective-permute-start.1) | collective-permute-done | bytes 524320 | tf_op jit(solution)/shard_map/ppermute | solution.py:323
  3.4 4.0 %collective-permute-start.8 = (bf16[2,64,512]{2,1,0:T(8,128)(2,1)S(1)}, bf16[2,64,512]{2,1,0:T(8,128)(2,1)S(1)}, u32[]{:S(2)}, u32[]{:S(2)}) collective-permute-start(bf16[2,64,512]{2,1,0:T(8,128)(2,1)S(1)} %pad_maximum_fusion.8), channel_id=1, source_target_pairs={{0,12},{1,13},{2,14},{3,15},{4,8},{5,9},{6,10},{7,11},{8,4},{9,5},... | collective-permute-start | bytes 393224 | tf_op jit(solution)/shard_map/ppermute | solution.py:323
  7.4 1.6 %collective-permute-start.7 = (bf16[2,64,512]{2,1,0:T(8,128)(2,1)S(1)}, bf16[2,64,512]{2,1,0:T(8,128)(2,1)S(1)}, u32[]{:S(2)}, u32[]{:S(2)}) collective-permute-start(bf16[2,64,512]{2,1,0:T(8,128)(2,1)S(1)} %pad_maximum_fusion.7), channel_id=1, source_target_pairs={{0,2},{1,3},{2,0},{3,1},{4,6},{5,7},{6,4},{7,5},{8,10},{9,11},{10,... | collective-permute-start | bytes 393224 | tf_op jit(solution)/shard_map/ppermute | solution.py:323
  9.1 2.0 %collective-permute-start.5 = (bf16[2,64,512]{2,1,0:T(8,128)(2,1)S(1)}, bf16[2,64,512]{2,1,0:T(8,128)(2,1)S(1)}, u32[]{:S(2)}, u32[]{:S(2)}) collective-permute-start(bf16[2,64,512]{2,1,0:T(8,128)(2,1)S(1)} %pad_maximum_fusion.4), channel_id=1, source_target_pairs={{0,8},{1,9},{2,10},{3,11},{4,12},{5,13},{6,14},{7,15},{8,0},{9,1},... | collective-permute-start | bytes 393224 | tf_op jit(solution)/shard_map/ppermute | solution.py:323
  11.1 2.5 %collective-permute-start.4 = (bf16[2,64,512]{2,1,0:T(8,128)(2,1)S(1)}, bf16[2,64,512]{2,1,0:T(8,128)(2,1)S(1)}, u32[]{:S(2)}, u32[]{:S(2)}) collective-permute-start(bf16[2,64,512]{2,1,0:T(8,128)(2,1)S(1)} %pad_maximum_fusion.3), channel_id=1, source_target_pairs={{0,6},{1,7},{2,4},{3,5},{4,2},{5,3},{6,0},{7,1},{8,14},{9,15},{10,... | collective-permute-start | bytes 393224 | tf_op jit(solution)/shard_map/ppermute | solution.py:323
  14.1 1.5 %collective-permute-done.7.rest_2_ = bf16[2,64,512]{2,1,0:T(8,128)(2,1)S(1)} collective-permute-done((bf16[2,64,512]{2,1,0:T(8,128)(2,1)S(1)}, bf16[2,64,512]{2,1,0:T(8,128)(2,1)S(1)}, u32[]{:S(2)}, u32[]{:S(2)}) %collective-permute-start.7) | collective-permute-done | bytes 131104 | tf_op jit(solution)/shard_map/ppermute | solution.py:323
  16.2 1.2 %collective-permute-done.6.rest_1_ = bf16[2,64,512]{2,1,0:T(8,128)(2,1)S(1)} collective-permute-done((bf16[2,64,512]{2,1,0:T(8,128)(2,1)S(1)}, bf16[2,64,512]{2,1,0:T(8,128)(2,1)S(1)}, u32[]{:S(2)}, u32[]{:S(2)}) %collective-permute-start.6) | collective-permute-done | bytes 131104 | tf_op jit(solution)/shard_map/ppermute | solution.py:323
  17.3 4.5 %transform.3.rest_4_ = f32[64,1280]{1,0:T(8,128)S(1)} custom-call(s32[1]{0:T(128)} %bitcast.place_ref, bf16[163840,128]{1,0:T(8,128)(2,1)} %constant.100.clone.table_ref, bf16[2,64,512]{2,1,0:T(8,128)(2,1)S(1)} %pad_maximum_fusion.5.rest_0_, bf16[2,64,512]{2,1,0:T(8,128)(2,1)S(1)} %collective-permute-done.6.rest_1_, ...), custom_call_target="tpu_custom_call" | custom-call | flops 671088640 | bytes 10485760 | tf_op jit(solution)/shard_map/transform/pallas_call | solution.py:121
  21.8 3.1 %transform.4 = (f32[32,768]{1,0:T(8,128)S(1)}, f32[32,768]{1,0:T(8,128)S(1)}) custom-call(s32[1]{0:T(128)} %bitcast.place_ref, bf16[163840,128]{1,0:T(8,128)(2,1)} %constant.100.clone.table_ref, bf16[2,64,512]{2,1,0:T(8,128)(2,1)S(1)} %collective-permute-done.2.rest_0_, bf16[2,64,512]{2,1,0:T(8,128)(2,1)S(1)} %collective-permute-done.3.rest_1_, ...), custom_call_target="tpu_custom_call" | custom-call | flops 402653184 | bytes 6291456 | tf_op jit(solution)/shard_map/transform/pallas_call | solution.py:121
  25.0 2.6 %collective-permute-start.9 = (f32[32,768]{1,0:T(8,128)S(1)}, f32[32,768]{1,0:T(8,128)S(1)}, u32[]{:S(2)}, u32[]{:S(2)}) collective-permute-start(f32[32,768]{1,0:T(8,128)S(1)} %get-tuple-element.10), channel_id=1, source_target_pairs={{0,16},{1,17},{2,18},{3,19},{4,20},{5,21},{6,22},{7,23},{8,24},{9,... | collective-permute-start | bytes 294920 | tf_op jit(solution)/shard_map/ppermute | solution.py:323
  27.6 2.4 %transform.5 = (f32[32,512]{1,0:T(8,128)S(1)}, f32[32,512]{1,0:T(8,128)S(1)}) custom-call(s32[1]{0:T(128)} %bitcast.place_ref, bf16[163840,128]{1,0:T(8,128)(2,1)} %constant.100.clone.table_ref, bf16[2,64,512]{2,1,0:T(8,128)(2,1)S(1)} %collective-permute-done.2.rest_0_, bf16[2,64,512]{2,1,0:T(8,128)(2,1)S(1)} %collective-permute-done.3.rest_1_, ...), custom_call_target="tpu_custom_call" | custom-call | flops 268435456 | bytes 4194304 | tf_op jit(solution)/shard_map/transform/pallas_call | solution.py:121
  30.6 1.2 %collective-permute-done = f32[8,4]{1,0:T(8,128)S(1)} collective-permute-done((f32[8,4]{1,0:T(8,128)S(1)}, f32[8,4]{1,0:T(8,128)S(1)}, u32[]{:S(2)}, u32[]{:S(2)}) %collective-permute-start) | collective-permute-done | bytes 160 | tf_op jit(solution)/shard_map/ppermute | solution.py:323
  32.0 4.0 %collective-permute-done.10.rest_3_ = f32[32,512]{1,0:T(8,128)S(1)} collective-permute-done((f32[32,512]{1,0:T(8,128)S(1)}, f32[32,512]{1,0:T(8,128)S(1)}, u32[]{:S(2)}, u32[]{:S(2)}) %collective-permute-start.10) | collective-permute-done | bytes 65568 | tf_op jit(solution)/shard_map/ppermute | solution.py:323
  36.1 1.7 %collective-permute-start.13 = (bf16[32,1280]{1,0:T(8,128)(2,1)S(1)}, bf16[32,1280]{1,0:T(8,128)(2,1)S(1)}, u32[]{:S(2)}, u32[]{:S(2)}) collective-permute-start(bf16[32,1280]{1,0:T(8,128)(2,1)S(1)} %whiten.1), channel_id=1, source_target_pairs={{0,24},{1,25},{2,26},{3,27},{4,28},{5,29},{6,30},{7,31},{8,16},{9,... | collective-permute-start | bytes 245768 | tf_op jit(solution)/shard_map/ppermute | solution.py:323
  37.8 2.8 %collective-permute-start.12 = (bf16[32,1280]{1,0:T(8,128)(2,1)S(1)}, bf16[32,1280]{1,0:T(8,128)(2,1)S(1)}, u32[]{:S(2)}, u32[]{:S(2)}) collective-permute-start(bf16[32,1280]{1,0:T(8,128)(2,1)S(1)} %whiten.1), channel_id=1, source_target_pairs={{0,16},{1,17},{2,18},{3,19},{4,20},{5,21},{6,22},{7,23},{8,24},{9,... | collective-permute-start | bytes 245768 | tf_op jit(solution)/shard_map/ppermute | solution.py:323
  40.6 2.6 %collective-permute-done.13 = bf16[32,1280]{1,0:T(8,128)(2,1)S(1)} collective-permute-done((bf16[32,1280]{1,0:T(8,128)(2,1)S(1)}, bf16[32,1280]{1,0:T(8,128)(2,1)S(1)}, u32[]{:S(2)}, u32[]{:S(2)}) %collective-permute-start.13) | collective-permute-done | bytes 81952 | tf_op jit(solution)/shard_map/ppermute | solution.py:323
  44.9 1.7 %collective-permute-start.17 = (bf16[4,32,1280]{2,1,0:T(8,128)(2,1)S(1)}, bf16[4,32,1280]{2,1,0:T(8,128)(2,1)}, u32[]{:S(2)}, u32[]{:S(2)}) collective-permute-start(bf16[4,32,1280]{2,1,0:T(8,128)(2,1)S(1)} %pad_maximum_fusion.rest_0_), channel_id=1, source_target_pairs={{0,4},{1,5},{2,6},{3,7},{4,0},{5,1},{6,2},{7,3},{8,12},{9,13},{10,... | collective-permute-start | bytes 983048 | tf_op jit(solution)/shard_map/ppermute | solution.py:323
  46.6 1.4 %collective-permute-start.19 = (bf16[4,32,1280]{2,1,0:T(8,128)(2,1)S(1)}, bf16[4,32,1280]{2,1,0:T(8,128)(2,1)}, u32[]{:S(2)}, u32[]{:S(2)}) collective-permute-start(bf16[4,32,1280]{2,1,0:T(8,128)(2,1)S(1)} %pad_maximum_fusion.rest_0_), channel_id=1, source_target_pairs={{0,6},{1,7},{2,4},{3,5},{4,2},{5,3},{6,0},{7,1},{8,14},{9,15},{10,... | collective-permute-start | bytes 983048 | tf_op jit(solution)/shard_map/ppermute | solution.py:323
  48.0 6.8 %collective-permute-done.15.rest_1_ = bf16[4,32,1280]{2,1,0:T(8,128)(2,1)} collective-permute-done((bf16[4,32,1280]{2,1,0:T(8,128)(2,1)S(1)}, bf16[4,32,1280]{2,1,0:T(8,128)(2,1)}, u32[]{:S(2)}, u32[]{:S(2)}) %collective-permute-start.15) | collective-permute-done | bytes 327712 | tf_op jit(solution)/shard_map/ppermute | solution.py:323
  54.8 4.7 %collective-permute-done.17.rest_2_ = bf16[4,32,1280]{2,1,0:T(8,128)(2,1)} collective-permute-done((bf16[4,32,1280]{2,1,0:T(8,128)(2,1)S(1)}, bf16[4,32,1280]{2,1,0:T(8,128)(2,1)}, u32[]{:S(2)}, u32[]{:S(2)}) %collective-permute-start.17) | collective-permute-done | bytes 327712 | tf_op jit(solution)/shard_map/ppermute | solution.py:323
  59.4 1.9 %collective-permute-done.19.rest_3_ = bf16[4,32,1280]{2,1,0:T(8,128)(2,1)} collective-permute-done((bf16[4,32,1280]{2,1,0:T(8,128)(2,1)S(1)}, bf16[4,32,1280]{2,1,0:T(8,128)(2,1)}, u32[]{:S(2)}, u32[]{:S(2)}) %collective-permute-start.19) | collective-permute-done | bytes 327712 | tf_op jit(solution)/shard_map/ppermute | solution.py:323
  61.5 2.6 %correlate.2.rest_4_ = f32[4,64,1280]{2,1,0:T(8,128)S(1)} custom-call(s32[1]{0:T(128)} %bitcast.place_ref, f32[8,4]{1,0:T(8,128)S(1)} %convert_element_type.3.flags_ref, s32[64,1]{1,0:T(8,128)S(1)} %copy.10.ids_ref, bf16[4,32,1280]{2,1,0:T(8,128)(2,1)S(1)} %pad_maximum_fusion.rest_0_, bf16[4,32,1280]{2,1,0:T(8,128)(2,1)} %collective-permute-done.15.rest_1_, ...), custom_call_target="tpu_custom_call" | custom-call | flops 83886080 | bytes 1310720 | tf_op jit(solution)/shard_map/correlate/pallas_call | solution.py:298
  64.1 4.8 %correlate.3 = f32[64,4,1001]{2,1,0:T(4,128)} custom-call(s32[1]{0:T(128)} %bitcast.place_ref, f32[8,4]{1,0:T(8,128)S(1)} %convert_element_type.3.flags_ref, s32[64,1]{1,0:T(8,128)S(1)} %copy.10.ids_ref, bf16[4,32,1280]{2,1,0:T(8,128)(2,1)S(1)} %collective-permute-done.14.rest_0_, bf16[4,32,1280]{2,1,0:T(8,128)(2,1)} %collective-permute-done.16.rest_1_, ...), custom_call_target="tpu_custom_call" | custom-call | flops 83886080 | bytes 1310720 | tf_op jit(solution)/shard_map/correlate/pallas_call | solution.py:298
  (47 shorter events, 4.5 us)
Async XLA Ops:
  1.3 2.1 %collective-permute-start.1 = (bf16[8,64,512]{2,1,0:T(8,128)(2,1)S(1)}, bf16[8,64,512]{2,1,0:T(8,128)(2,1)S(1)}, u32[]{:S(2)}, u32[]{:S(2)}) collective-permute-start(bf16[8,64,512]{2,1,0:T(8,128)(2,1)S(1)} %bitcast.19), channel_id=1, source_target_pairs={{0,1},{1,0},{2,3},{3,2},{4,5},{5,4},{6,7},{7,6},{8,9},{9,8},{10,11... | collective-permute-start | bytes 1572872 | tf_op jit(solution)/shard_map/ppermute | solution.py:323
  3.4 10.2 %collective-permute-start.8 = (bf16[2,64,512]{2,1,0:T(8,128)(2,1)S(1)}, bf16[2,64,512]{2,1,0:T(8,128)(2,1)S(1)}, u32[]{:S(2)}, u32[]{:S(2)}) collective-permute-start(bf16[2,64,512]{2,1,0:T(8,128)(2,1)S(1)} %pad_maximum_fusion.8), channel_id=1, source_target_pairs={{0,12},{1,13},{2,14},{3,15},{4,8},{5,9},{6,10},{7,11},{8,4},{9,5},... | collective-permute-start | bytes 393224 | tf_op jit(solution)/shard_map/ppermute | solution.py:323
  7.4 8.2 %collective-permute-start.7 = (bf16[2,64,512]{2,1,0:T(8,128)(2,1)S(1)}, bf16[2,64,512]{2,1,0:T(8,128)(2,1)S(1)}, u32[]{:S(2)}, u32[]{:S(2)}) collective-permute-start(bf16[2,64,512]{2,1,0:T(8,128)(2,1)S(1)} %pad_maximum_fusion.7), channel_id=1, source_target_pairs={{0,2},{1,3},{2,0},{3,1},{4,6},{5,7},{6,4},{7,5},{8,10},{9,11},{10,... | collective-permute-start | bytes 393224 | tf_op jit(solution)/shard_map/ppermute | solution.py:323
  9.0 8.3 %collective-permute-start.6 = (bf16[2,64,512]{2,1,0:T(8,128)(2,1)S(1)}, bf16[2,64,512]{2,1,0:T(8,128)(2,1)S(1)}, u32[]{:S(2)}, u32[]{:S(2)}) collective-permute-start(bf16[2,64,512]{2,1,0:T(8,128)(2,1)S(1)} %pad_maximum_fusion.6), channel_id=1, source_target_pairs={{0,14},{1,15},{2,12},{3,13},{4,10},{5,11},{6,8},{7,9},{8,6},{9,7},... | collective-permute-start | bytes 393224 | tf_op jit(solution)/shard_map/ppermute | solution.py:323
  9.1 12.7 %collective-permute-start.5 = (bf16[2,64,512]{2,1,0:T(8,128)(2,1)S(1)}, bf16[2,64,512]{2,1,0:T(8,128)(2,1)S(1)}, u32[]{:S(2)}, u32[]{:S(2)}) collective-permute-start(bf16[2,64,512]{2,1,0:T(8,128)(2,1)S(1)} %pad_maximum_fusion.4), channel_id=1, source_target_pairs={{0,8},{1,9},{2,10},{3,11},{4,12},{5,13},{6,14},{7,15},{8,0},{9,1},... | collective-permute-start | bytes 393224 | tf_op jit(solution)/shard_map/ppermute | solution.py:323
  11.1 10.7 %collective-permute-start.4 = (bf16[2,64,512]{2,1,0:T(8,128)(2,1)S(1)}, bf16[2,64,512]{2,1,0:T(8,128)(2,1)S(1)}, u32[]{:S(2)}, u32[]{:S(2)}) collective-permute-start(bf16[2,64,512]{2,1,0:T(8,128)(2,1)S(1)} %pad_maximum_fusion.3), channel_id=1, source_target_pairs={{0,6},{1,7},{2,4},{3,5},{4,2},{5,3},{6,0},{7,1},{8,14},{9,15},{10,... | collective-permute-start | bytes 393224 | tf_op jit(solution)/shard_map/ppermute | solution.py:323
  13.7 8.2 %collective-permute-start.3 = (bf16[2,64,512]{2,1,0:T(8,128)(2,1)S(1)}, bf16[2,64,512]{2,1,0:T(8,128)(2,1)S(1)}, u32[]{:S(2)}, u32[]{:S(2)}) collective-permute-start(bf16[2,64,512]{2,1,0:T(8,128)(2,1)S(1)} %pad_maximum_fusion.2), channel_id=1, source_target_pairs={{0,10},{1,11},{2,8},{3,9},{4,14},{5,15},{6,12},{7,13},{8,2},{9,3},... | collective-permute-start | bytes 393224 | tf_op jit(solution)/shard_map/ppermute | solution.py:323
  15.7 6.2 %collective-permute-start.2 = (bf16[2,64,512]{2,1,0:T(8,128)(2,1)S(1)}, bf16[2,64,512]{2,1,0:T(8,128)(2,1)S(1)}, u32[]{:S(2)}, u32[]{:S(2)}) collective-permute-start(bf16[2,64,512]{2,1,0:T(8,128)(2,1)S(1)} %pad_maximum_fusion.1), channel_id=1, source_target_pairs={{0,4},{1,5},{2,6},{3,7},{4,0},{5,1},{6,2},{7,3},{8,12},{9,13},{10,... | collective-permute-start | bytes 393224 | tf_op jit(solution)/shard_map/ppermute | solution.py:323
  25.0 5.5 %copy-start.1 = (s32[8,4]{0,1:T(4,128)S(1)}, s32[8,4]{0,1:T(4,128)}, u32[]{:S(2)}) copy-start(s32[8,4]{0,1:T(4,128)} %param.6) | copy-start | bytes 388
  25.0 36.4 %copy-start.2 = (s32[64]{0:T(128)S(1)}, s32[64]{0:T(128)}, u32[]{:S(2)}) copy-start(s32[64]{0:T(128)} %param.7) | copy-start | bytes 772
  25.0 11.0 %collective-permute-start.9 = (f32[32,768]{1,0:T(8,128)S(1)}, f32[32,768]{1,0:T(8,128)S(1)}, u32[]{:S(2)}, u32[]{:S(2)}) collective-permute-start(f32[32,768]{1,0:T(8,128)S(1)} %get-tuple-element.10), channel_id=1, source_target_pairs={{0,16},{1,17},{2,18},{3,19},{4,20},{5,21},{6,22},{7,23},{8,24},{9,... | collective-permute-start | bytes 294920 | tf_op jit(solution)/shard_map/ppermute | solution.py:323
  30.1 34.1 %copy-start = (bf16[10240,128]{1,0:T(8,128)(2,1)S(1)}, bf16[10240,128]{1,0:T(8,128)(2,1)}, u32[]{:S(2)}) copy-start(bf16[10240,128]{1,0:T(8,128)(2,1)} %constant.101.clone.rest_5_) | copy-start | bytes 7864324
  30.1 5.9 %collective-permute-start.10 = (f32[32,512]{1,0:T(8,128)S(1)}, f32[32,512]{1,0:T(8,128)S(1)}, u32[]{:S(2)}, u32[]{:S(2)}) collective-permute-start(f32[32,512]{1,0:T(8,128)S(1)} %get-tuple-element.12), channel_id=1, source_target_pairs={{0,16},{1,17},{2,18},{3,19},{4,20},{5,21},{6,22},{7,23},{8,24},{9,... | collective-permute-start | bytes 196616 | tf_op jit(solution)/shard_map/ppermute | solution.py:323
  30.6 1.2 %collective-permute-start = (f32[8,4]{1,0:T(8,128)S(1)}, f32[8,4]{1,0:T(8,128)S(1)}, u32[]{:S(2)}, u32[]{:S(2)}) collective-permute-start(f32[8,4]{1,0:T(8,128)S(1)} %convert_element_type.3.flags_ref), channel_id=1, source_target_pairs={{0,1},{1,0},{2,3},{3,2},{4,5},{5,4},{6,7},{7,6},{8,9},{9,8},{10,11... | collective-permute-start | bytes 392 | tf_op jit(solution)/shard_map/ppermute | solution.py:323
  36.1 7.1 %collective-permute-start.13 = (bf16[32,1280]{1,0:T(8,128)(2,1)S(1)}, bf16[32,1280]{1,0:T(8,128)(2,1)S(1)}, u32[]{:S(2)}, u32[]{:S(2)}) collective-permute-start(bf16[32,1280]{1,0:T(8,128)(2,1)S(1)} %whiten.1), channel_id=1, source_target_pairs={{0,24},{1,25},{2,26},{3,27},{4,28},{5,29},{6,30},{7,31},{8,16},{9,... | collective-permute-start | bytes 245768 | tf_op jit(solution)/shard_map/ppermute | solution.py:323
  37.8 5.6 %collective-permute-start.11 = (bf16[32,1280]{1,0:T(8,128)(2,1)S(1)}, bf16[32,1280]{1,0:T(8,128)(2,1)S(1)}, u32[]{:S(2)}, u32[]{:S(2)}) collective-permute-start(bf16[32,1280]{1,0:T(8,128)(2,1)S(1)} %whiten.1), channel_id=1, source_target_pairs={{0,8},{1,9},{2,10},{3,11},{4,12},{5,13},{6,14},{7,15},{8,0},{9,1},... | collective-permute-start | bytes 245768 | tf_op jit(solution)/shard_map/ppermute | solution.py:323
  37.8 6.4 %collective-permute-start.12 = (bf16[32,1280]{1,0:T(8,128)(2,1)S(1)}, bf16[32,1280]{1,0:T(8,128)(2,1)S(1)}, u32[]{:S(2)}, u32[]{:S(2)}) collective-permute-start(bf16[32,1280]{1,0:T(8,128)(2,1)S(1)} %whiten.1), channel_id=1, source_target_pairs={{0,16},{1,17},{2,18},{3,19},{4,20},{5,21},{6,22},{7,23},{8,24},{9,... | collective-permute-start | bytes 245768 | tf_op jit(solution)/shard_map/ppermute | solution.py:323
  44.2 10.5 %collective-permute-start.15 = (bf16[4,32,1280]{2,1,0:T(8,128)(2,1)S(1)}, bf16[4,32,1280]{2,1,0:T(8,128)(2,1)}, u32[]{:S(2)}, u32[]{:S(2)}) collective-permute-start(bf16[4,32,1280]{2,1,0:T(8,128)(2,1)S(1)} %pad_maximum_fusion.rest_0_), channel_id=1, source_target_pairs={{0,2},{1,3},{2,0},{3,1},{4,6},{5,7},{6,4},{7,5},{8,10},{9,11},{10,... | collective-permute-start | bytes 983048 | tf_op jit(solution)/shard_map/ppermute | solution.py:323
  44.9 14.5 %collective-permute-start.17 = (bf16[4,32,1280]{2,1,0:T(8,128)(2,1)S(1)}, bf16[4,32,1280]{2,1,0:T(8,128)(2,1)}, u32[]{:S(2)}, u32[]{:S(2)}) collective-permute-start(bf16[4,32,1280]{2,1,0:T(8,128)(2,1)S(1)} %pad_maximum_fusion.rest_0_), channel_id=1, source_target_pairs={{0,4},{1,5},{2,6},{3,7},{4,0},{5,1},{6,2},{7,3},{8,12},{9,13},{10,... | collective-permute-start | bytes 983048 | tf_op jit(solution)/shard_map/ppermute | solution.py:323
  46.6 14.8 %collective-permute-start.19 = (bf16[4,32,1280]{2,1,0:T(8,128)(2,1)S(1)}, bf16[4,32,1280]{2,1,0:T(8,128)(2,1)}, u32[]{:S(2)}, u32[]{:S(2)}) collective-permute-start(bf16[4,32,1280]{2,1,0:T(8,128)(2,1)S(1)} %pad_maximum_fusion.rest_0_), channel_id=1, source_target_pairs={{0,6},{1,7},{2,4},{3,5},{4,2},{5,3},{6,0},{7,1},{8,14},{9,15},{10,... | collective-permute-start | bytes 983048 | tf_op jit(solution)/shard_map/ppermute | solution.py:323
  48.0 16.1 %collective-permute-start.14 = (bf16[4,32,1280]{2,1,0:T(8,128)(2,1)S(1)}, bf16[4,32,1280]{2,1,0:T(8,128)(2,1)S(1)}, u32[]{:S(2)}, u32[]{:S(2)}) collective-permute-start(bf16[4,32,1280]{2,1,0:T(8,128)(2,1)S(1)} %pad_maximum_fusion.rest_0_), channel_id=1, source_target_pairs={{0,1},{1,0},{2,3},{3,2},{4,5},{5,4},{6,7},{7,6},{8,9},{9,8},{10,11... | collective-permute-start | bytes 983048 | tf_op jit(solution)/shard_map/ppermute | solution.py:323
  54.8 9.4 %collective-permute-start.16 = (bf16[4,32,1280]{2,1,0:T(8,128)(2,1)}, bf16[4,32,1280]{2,1,0:T(8,128)(2,1)}, u32[]{:S(2)}, u32[]{:S(2)}) collective-permute-start(bf16[4,32,1280]{2,1,0:T(8,128)(2,1)} %collective-permute-done.15.rest_1_), channel_id=1, source_target_pairs={{0,1},{1,0},{2,3},{3,2},{4,5},{5,4},{6,7},{7,6},{8,9},{9,8},{10,11... | collective-permute-start | bytes 983048 | tf_op jit(solution)/shard_map/ppermute | solution.py:323
  59.4 4.7 %collective-permute-start.18 = (bf16[4,32,1280]{2,1,0:T(8,128)(2,1)}, bf16[4,32,1280]{2,1,0:T(8,128)(2,1)}, u32[]{:S(2)}, u32[]{:S(2)}) collective-permute-start(bf16[4,32,1280]{2,1,0:T(8,128)(2,1)} %collective-permute-done.17.rest_2_), channel_id=1, source_target_pairs={{0,1},{1,0},{2,3},{3,2},{4,5},{5,4},{6,7},{7,6},{8,9},{9,8},{10,11... | collective-permute-start | bytes 983048 | tf_op jit(solution)/shard_map/ppermute | solution.py:323
  61.4 2.8 %collective-permute-start.20 = (bf16[4,32,1280]{2,1,0:T(8,128)(2,1)}, bf16[4,32,1280]{2,1,0:T(8,128)(2,1)}, u32[]{:S(2)}, u32[]{:S(2)}) collective-permute-start(bf16[4,32,1280]{2,1,0:T(8,128)(2,1)} %collective-permute-done.19.rest_3_), channel_id=1, source_target_pairs={{0,1},{1,0},{2,3},{3,2},{4,5},{5,4},{6,7},{7,6},{8,9},{9,8},{10,11... | collective-permute-start | bytes 983048 | tf_op jit(solution)/shard_map/ppermute | solution.py:323

commit v7 on v6

--- a/solution.py
+++ b/solution.py
@@ -179,9 +179,9 @@
     )(flags, *parts)
 
 
-def correlate_kernel(shape, core, place_ref, flags_ref, ids_ref, *rest):
-    segments, channels, devices, blocks = shape
-    blocks, rest = rest[:blocks], rest[blocks:]
+def correlate_kernel(shape, core, steps, place_ref, flags_ref, ids_ref, *rest):
+    segments, channels, devices = shape
+    blocks, rest = rest[: len(steps)], rest[len(steps) :]
     if core:
         before_ref, table_ref, out_ref = rest[:3]
         held_ref, panel_ref, receivers_ref, inverse_ref, stacked_ref, sem = rest[3:]
@@ -203,9 +203,10 @@
         member = device % members
         return (member // 2) * SHARES + device // members
 
-    for index, block in enumerate(blocks):
-        for line in range(block.shape[0]):
-            device = place ^ (line * 8 + index * 2 + core)
+    for step, block in zip(steps, blocks):
+        far = block.shape[0]
+        for line in range(far):
+            device = place ^ ((line + far // 2) % far * 8 + step + core)
             held_ref[position(device)] = block[line]
 
     tails = held_ref[:, :, FLAG_TILE : FLAG_TILE + 128].reshape(held_ref.shape[0] * rows, 128)
@@ -274,7 +275,7 @@
         out_ref[...] = lags.reshape(sources, ch_local, LAG_TILES * 128)[:, :, :LAGS]
 
 
-def correlate(core, place, weights, ids, blocks, shape, before=None, table=None):
+def correlate(core, place, weights, ids, steps, blocks, shape, before=None, table=None):
     segments, channels, devices = shape
     rows = blocks[0].shape[1]
     ch_local = channels // devices
@@ -296,12 +297,12 @@
         ]
     out = (sources, ch_local, LAGS) if core else (ch_local, sources, WIDTH)
     return pl.pallas_call(
-        functools.partial(correlate_kernel, (*shape, len(blocks)), core),
+        functools.partial(correlate_kernel, shape, core, steps),
         in_specs=in_specs,
         out_specs=vmem,
         out_shape=jax.ShapeDtypeStruct(out, jnp.float32),
         scratch_shapes=scratch,
-        compiler_params=pltpu.CompilerParams(vmem_limit_bytes=32 * 2**20),
+        compiler_params=pltpu.CompilerParams(vmem_limit_bytes=16 * 2**20),
         cost_estimate=pl.CostEstimate(
             flops=sources * channels * WIDTH * segments,
             bytes_accessed=2 * (segments // 2) * channels * WIDTH,
@@ -356,15 +357,19 @@
     white = whiten(flags, parts)
 
     far = devices // 8
-    line = jnp.stack([white] + [exchange(white, 8 * k) for k in range(1, far)])
-    plane = [line] + [exchange(line, 2 * k) for k in range(1, 4)]
-    swapped = [exchange(block, 1) for block in plane]
+    line = [white] + [exchange(white, 8 * k) for k in range(1, far)]
+    halves = [jnp.stack(line[far // 2 :]), jnp.stack(line[: far // 2])]
+    steps = [2 * near for near in range(4)]
+    blocks = [
+        jnp.concatenate([exchange(half, step) if step else half for half in halves])
+        for step in steps
+    ]
+    swapped = [exchange(block, 1) for block in blocks]
     ids = source_ids.reshape(-1, 1)
     common = me, weights, ids
     shape = segments, channels, devices
-    before = correlate(0, *common, plane, shape)
-    inverse = inverse_table(samples)
-    return correlate(1, *common, swapped, shape, before, inverse)
+    before = correlate(0, *common, steps, blocks, shape)
+    return correlate(1, *common, steps, swapped, shape, before, inverse_table(samples))
 
 
 def solution(mesh):

time: 69.1 us -> 67.2 us (0.973)
  waiting for transfers between devices: 26.4 us -> 14.3 us
  starting transfers between devices: 22.9 us -> 30.3 us
  local copies, waits for them, and re-layouts: 1.65 us -> 4.36 us
    ppermute x21 -> x24, waiting for transfers between devices: 26.4 us -> 14.3 us  [exchange(): return lax.ppermute(block, 'chan', [(i, i ^ bits) for i in range(devices)])]
    ppermute x21 -> x24, starting transfers between devices: 22.9 us -> 30.3 us  [exchange(): return lax.ppermute(block, 'chan', [(i, i ^ bits) for i in range(devices)])]
    concatenate x0 -> x3, local copies, waits for them, and re-layouts: none -> 1.36 us  [per_device(): jnp.concatenate([exchange(half, step) if step else half for half in halves])]
    unnamed x7 -> x10, local copies, waits for them, and re-layouts: 0.1 us -> 1.45 us
  transfers between devices with their start and end apart: 21 -> 24, of which waited for: 11 -> 9; matrix products, arithmetic and copies ran while one was open for 1% -> 5% of each run, Pallas kernels for 14% -> 14%
where the time goes in v7:
time: 67.2 us; the launch traced here: 67 us
  starting transfers between devices  30.3 us (45%)
  Pallas kernels  17.5 us (26%)
  waiting for transfers between devices  14.3 us (21%)
  local copies, waits for them, and re-layouts  4.36 us (6%)
    ppermute x24, starting transfers between devices, exchange(): return lax.ppermute(block, 'chan', [(i, i ^ bits) for i in range(devices)])  30.3 us
    ppermute x24, waiting for transfers between devices, exchange(): return lax.ppermute(block, 'chan', [(i, i ^ bits) for i in range(devices)])  14.3 us
    pallas_call x3, Pallas kernels, transform(): pl.pallas_call(functools.partial(transform_kernel, steps, first, started)...  10 us
    pallas_call x2, Pallas kernels, correlate(): pl.pallas_call(functools.partial(correlate_kernel, shape, core, steps), i...  7.38 us
    unnamed x10, local copies, waits for them, and re-layouts  1.45 us
    concatenate x3, local copies, waits for them, and re-layouts, per_device(): jnp.concatenate([exchange(half, step) if step else half for half in halves])  1.36 us
  transfers between devices with their start and end apart: 24, of which 9 were waited for; matrix products, arithmetic and copies ran while one was open for 5% of the time, Pallas kernels for 14%

profile of v7, /device:TPU:0, one launch (start us, length us, event | category | flops | bytes accessed | tf_op | source)
XLA Modules:
  0.0 67.0 jit_solution(667101851329572062)
XLA Ops:
  0.0 1.3 %constant_dynamic-slice_fusion.20 = (bf16[4,1,128,512]{3,2,1,0:T(8,128)(2,1)S(1)}, bf16[4,1,128,512]{3,2,1,0:T(8,128)(2,1)S(1)}) fusion(bf16[4,2,128,512]{3,2,1,0:T(8,128)(2,1)} %bitcast.19, s32[]{:T(128)S(6)} %select_n.69, s32[]{:T(128)S(6)} %select_n.73), kind=kLoop, calls=%fused_computation.37 | loop fusion | bytes 2097160 | tf_op jit(solution)/shard_map/jit(dynamic_index_in_dim)/dynamic_slice | solution.py:339
  1.9 1.5 %collective-permute-done.1 = bf16[8,64,512]{2,1,0:T(8,128)(2,1)S(1)} collective-permute-done((bf16[8,64,512]{2,1,0:T(8,128)(2,1)S(1)}, bf16[8,64,512]{2,1,0:T(8,128)(2,1)S(1)}, u32[]{:S(2)}, u32[]{:S(2)}) %collective-permute-start.1) | collective-permute-done | bytes 524320 | tf_op jit(solution)/shard_map/ppermute | solution.py:324
  3.4 4.0 %collective-permute-start.8 = (bf16[2,64,512]{2,1,0:T(8,128)(2,1)S(1)}, bf16[2,64,512]{2,1,0:T(8,128)(2,1)S(1)}, u32[]{:S(2)}, u32[]{:S(2)}) collective-permute-start(bf16[2,64,512]{2,1,0:T(8,128)(2,1)S(1)} %pad_maximum_fusion.10), channel_id=1, source_target_pairs={{0,12},{1,13},{2,14},{3,15},{4,8},{5,9},{6,10},{7,11},{8,4},{9,5},... | collective-permute-start | bytes 393224 | tf_op jit(solution)/shard_map/ppermute | solution.py:324
  7.4 1.6 %collective-permute-start.7 = (bf16[2,64,512]{2,1,0:T(8,128)(2,1)S(1)}, bf16[2,64,512]{2,1,0:T(8,128)(2,1)S(1)}, u32[]{:S(2)}, u32[]{:S(2)}) collective-permute-start(bf16[2,64,512]{2,1,0:T(8,128)(2,1)S(1)} %pad_maximum_fusion.9), channel_id=1, source_target_pairs={{0,2},{1,3},{2,0},{3,1},{4,6},{5,7},{6,4},{7,5},{8,10},{9,11},{10,... | collective-permute-start | bytes 393224 | tf_op jit(solution)/shard_map/ppermute | solution.py:324
  9.1 2.0 %collective-permute-start.5 = (bf16[2,64,512]{2,1,0:T(8,128)(2,1)S(1)}, bf16[2,64,512]{2,1,0:T(8,128)(2,1)S(1)}, u32[]{:S(2)}, u32[]{:S(2)}) collective-permute-start(bf16[2,64,512]{2,1,0:T(8,128)(2,1)S(1)} %pad_maximum_fusion.6), channel_id=1, source_target_pairs={{0,8},{1,9},{2,10},{3,11},{4,12},{5,13},{6,14},{7,15},{8,0},{9,1},... | collective-permute-start | bytes 393224 | tf_op jit(solution)/shard_map/ppermute | solution.py:324
  11.1 2.5 %collective-permute-start.4 = (bf16[2,64,512]{2,1,0:T(8,128)(2,1)S(1)}, bf16[2,64,512]{2,1,0:T(8,128)(2,1)S(1)}, u32[]{:S(2)}, u32[]{:S(2)}) collective-permute-start(bf16[2,64,512]{2,1,0:T(8,128)(2,1)S(1)} %pad_maximum_fusion.5), channel_id=1, source_target_pairs={{0,6},{1,7},{2,4},{3,5},{4,2},{5,3},{6,0},{7,1},{8,14},{9,15},{10,... | collective-permute-start | bytes 393224 | tf_op jit(solution)/shard_map/ppermute | solution.py:324
  14.1 1.5 %collective-permute-done.7.rest_2_ = bf16[2,64,512]{2,1,0:T(8,128)(2,1)S(1)} collective-permute-done((bf16[2,64,512]{2,1,0:T(8,128)(2,1)S(1)}, bf16[2,64,512]{2,1,0:T(8,128)(2,1)S(1)}, u32[]{:S(2)}, u32[]{:S(2)}) %collective-permute-start.7) | collective-permute-done | bytes 131104 | tf_op jit(solution)/shard_map/ppermute | solution.py:324
  16.2 1.2 %collective-permute-done.6.rest_1_ = bf16[2,64,512]{2,1,0:T(8,128)(2,1)S(1)} collective-permute-done((bf16[2,64,512]{2,1,0:T(8,128)(2,1)S(1)}, bf16[2,64,512]{2,1,0:T(8,128)(2,1)S(1)}, u32[]{:S(2)}, u32[]{:S(2)}) %collective-permute-start.6) | collective-permute-done | bytes 131104 | tf_op jit(solution)/shard_map/ppermute | solution.py:324
  17.3 4.4 %transform.3.rest_4_ = f32[64,1280]{1,0:T(8,128)S(1)} custom-call(s32[1]{0:T(128)} %bitcast.place_ref, bf16[163840,128]{1,0:T(8,128)(2,1)} %constant.100.clone.table_ref, bf16[2,64,512]{2,1,0:T(8,128)(2,1)S(1)} %pad_maximum_fusion.7.rest_0_, bf16[2,64,512]{2,1,0:T(8,128)(2,1)S(1)} %collective-permute-done.6.rest_1_, ...), custom_call_target="tpu_custom_call" | custom-call | flops 671088640 | bytes 10485760 | tf_op jit(solution)/shard_map/transform/pallas_call | solution.py:121
  21.8 3.1 %transform.4 = (f32[32,768]{1,0:T(8,128)S(1)}, f32[32,768]{1,0:T(8,128)S(1)}) custom-call(s32[1]{0:T(128)} %bitcast.place_ref, bf16[163840,128]{1,0:T(8,128)(2,1)} %constant.100.clone.table_ref, bf16[2,64,512]{2,1,0:T(8,128)(2,1)S(1)} %collective-permute-done.2.rest_0_, bf16[2,64,512]{2,1,0:T(8,128)(2,1)S(1)} %collective-permute-done.3.rest_1_, ...), custom_call_target="tpu_custom_call" | custom-call | flops 402653184 | bytes 6291456 | tf_op jit(solution)/shard_map/transform/pallas_call | solution.py:121
  25.0 2.7 %collective-permute-start.9 = (f32[32,768]{1,0:T(8,128)S(1)}, f32[32,768]{1,0:T(8,128)S(1)}, u32[]{:S(2)}, u32[]{:S(2)}) collective-permute-start(f32[32,768]{1,0:T(8,128)S(1)} %get-tuple-element.10), channel_id=1, source_target_pairs={{0,16},{1,17},{2,18},{3,19},{4,20},{5,21},{6,22},{7,23},{8,24},{9,... | collective-permute-start | bytes 294920 | tf_op jit(solution)/shard_map/ppermute | solution.py:324
  27.6 2.4 %transform.5 = (f32[32,512]{1,0:T(8,128)S(1)}, f32[32,512]{1,0:T(8,128)S(1)}) custom-call(s32[1]{0:T(128)} %bitcast.place_ref, bf16[163840,128]{1,0:T(8,128)(2,1)} %constant.100.clone.table_ref, bf16[2,64,512]{2,1,0:T(8,128)(2,1)S(1)} %collective-permute-done.2.rest_0_, bf16[2,64,512]{2,1,0:T(8,128)(2,1)S(1)} %collective-permute-done.3.rest_1_, ...), custom_call_target="tpu_custom_call" | custom-call | flops 268435456 | bytes 4194304 | tf_op jit(solution)/shard_map/transform/pallas_call | solution.py:121
  30.6 1.2 %collective-permute-done = f32[8,4]{1,0:T(8,128)S(1)} collective-permute-done((f32[8,4]{1,0:T(8,128)S(1)}, f32[8,4]{1,0:T(8,128)S(1)}, u32[]{:S(2)}, u32[]{:S(2)}) %collective-permute-start) | collective-permute-done | bytes 160 | tf_op jit(solution)/shard_map/ppermute | solution.py:324
  31.9 4.2 %collective-permute-done.10.rest_3_ = f32[32,512]{1,0:T(8,128)S(1)} collective-permute-done((f32[32,512]{1,0:T(8,128)S(1)}, f32[32,512]{1,0:T(8,128)S(1)}, u32[]{:S(2)}, u32[]{:S(2)}) %collective-permute-start.10) | collective-permute-done | bytes 65568 | tf_op jit(solution)/shard_map/ppermute | solution.py:324
  36.3 2.0 %collective-permute-start.11 = (bf16[32,1280]{1,0:T(8,128)(2,1)S(1)}, bf16[32,1280]{1,0:T(8,128)(2,1)S(1)}, u32[]{:S(2)}, u32[]{:S(2)}) collective-permute-start(bf16[32,1280]{1,0:T(8,128)(2,1)S(1)} %whiten.1), channel_id=1, source_target_pairs={{0,16},{1,17},{2,18},{3,19},{4,20},{5,21},{6,22},{7,23},{8,24},{9,... | collective-permute-start | bytes 245768 | tf_op jit(solution)/shard_map/ppermute | solution.py:324
  38.3 2.3 %collective-permute-start.12 = (bf16[32,1280]{1,0:T(8,128)(2,1)S(1)}, bf16[32,1280]{1,0:T(8,128)(2,1)S(1)}, u32[]{:S(2)}, u32[]{:S(2)}) collective-permute-start(bf16[32,1280]{1,0:T(8,128)(2,1)S(1)} %whiten.1), channel_id=1, source_target_pairs={{0,24},{1,25},{2,26},{3,27},{4,28},{5,29},{6,30},{7,31},{8,16},{9,... | collective-permute-start | bytes 245768 | tf_op jit(solution)/shard_map/ppermute | solution.py:324
  40.7 2.1 %collective-permute-start.22 = (bf16[2,32,1280]{2,1,0:T(8,128)(2,1)S(1)}, bf16[2,32,1280]{2,1,0:T(8,128)(2,1)S(1)}, u32[]{:S(2)}, u32[]{:S(2)}) collective-permute-start(bf16[2,32,1280]{2,1,0:T(8,128)(2,1)S(1)} %pad_maximum_fusion.2), channel_id=1, source_target_pairs={{0,6},{1,7},{2,4},{3,5},{4,2},{5,3},{6,0},{7,1},{8,14},{9,15},{10,... | collective-permute-start | bytes 491528 | tf_op jit(solution)/shard_map/ppermute | solution.py:324
  42.8 2.6 %collective-permute-start.19 = (bf16[2,32,1280]{2,1,0:T(8,128)(2,1)S(1)}, bf16[2,32,1280]{2,1,0:T(8,128)(2,1)S(1)}, u32[]{:S(2)}, u32[]{:S(2)}) collective-permute-start(bf16[2,32,1280]{2,1,0:T(8,128)(2,1)S(1)} %pad_maximum_fusion.2), channel_id=1, source_target_pairs={{0,4},{1,5},{2,6},{3,7},{4,0},{5,1},{6,2},{7,3},{8,12},{9,13},{10,... | collective-permute-start | bytes 491528 | tf_op jit(solution)/shard_map/ppermute | solution.py:324
  45.5 0.9 %collective-permute-start.21 = (bf16[2,32,1280]{2,1,0:T(8,128)(2,1)S(1)}, bf16[2,32,1280]{2,1,0:T(8,128)(2,1)S(1)}, u32[]{:S(2)}, u32[]{:S(2)}) collective-permute-start(bf16[2,32,1280]{2,1,0:T(8,128)(2,1)S(1)} %pad_maximum_fusion.1), channel_id=1, source_target_pairs={{0,6},{1,7},{2,4},{3,5},{4,2},{5,3},{6,0},{7,1},{8,14},{9,15},{10,... | collective-permute-start | bytes 491528 | tf_op jit(solution)/shard_map/ppermute | solution.py:324
  47.1 2.0 %collective-permute-start.16 = (bf16[2,32,1280]{2,1,0:T(8,128)(2,1)S(1)}, bf16[2,32,1280]{2,1,0:T(8,128)(2,1)S(1)}, u32[]{:S(2)}, u32[]{:S(2)}) collective-permute-start(bf16[2,32,1280]{2,1,0:T(8,128)(2,1)S(1)} %pad_maximum_fusion.2), channel_id=1, source_target_pairs={{0,2},{1,3},{2,0},{3,1},{4,6},{5,7},{6,4},{7,5},{8,10},{9,11},{10,... | collective-permute-start | bytes 491528 | tf_op jit(solution)/shard_map/ppermute | solution.py:324
  49.1 3.3 %collective-permute-done.21 = bf16[2,32,1280]{2,1,0:T(8,128)(2,1)S(1)} collective-permute-done((bf16[2,32,1280]{2,1,0:T(8,128)(2,1)S(1)}, bf16[2,32,1280]{2,1,0:T(8,128)(2,1)S(1)}, u32[]{:S(2)}, u32[]{:S(2)}) %collective-permute-start.21) | collective-permute-done | bytes 163872 | tf_op jit(solution)/shard_map/ppermute | solution.py:324
  52.4 2.4 %collective-permute-start.15 = (bf16[2,32,1280]{2,1,0:T(8,128)(2,1)S(1)}, bf16[2,32,1280]{2,1,0:T(8,128)(2,1)S(1)}, u32[]{:S(2)}, u32[]{:S(2)}) collective-permute-start(bf16[2,32,1280]{2,1,0:T(8,128)(2,1)S(1)} %pad_maximum_fusion.1), channel_id=1, source_target_pairs={{0,2},{1,3},{2,0},{3,1},{4,6},{5,7},{6,4},{7,5},{8,10},{9,11},{10,... | collective-permute-start | bytes 491528 | tf_op jit(solution)/shard_map/ppermute | solution.py:324
  59.6 2.5 %correlate.2.rest_4_ = f32[4,64,1280]{2,1,0:T(8,128)S(1)} custom-call(s32[1]{0:T(128)} %bitcast.place_ref, f32[8,4]{1,0:T(8,128)S(1)} %convert_element_type.3.flags_ref, s32[64,1]{1,0:T(8,128)S(1)} %copy.10.ids_ref, bf16[4,32,1280]{2,1,0:T(8,128)(2,1)S(1)} %pad_maximum_fusion.rest_0_, bf16[4,32,1280]{2,1,0:T(8,128)(2,1)} %constant_dynamic-update-slice_fusion.rest_1_, ...), custom_call_target="tpu_custom_call" | custom-call | flops 83886080 | bytes 1310720 | tf_op jit(solution)/shard_map/correlate/pallas_call | solution.py:299
  62.1 4.9 %correlate.3 = f32[64,4,1001]{2,1,0:T(4,128)} custom-call(s32[1]{0:T(128)} %bitcast.place_ref, f32[8,4]{1,0:T(8,128)S(1)} %convert_element_type.3.flags_ref, s32[64,1]{1,0:T(8,128)S(1)} %copy.10.ids_ref, bf16[4,32,1280]{2,1,0:T(8,128)(2,1)} %collective-permute-done.14.rest_0_, bf16[4,32,1280]{2,1,0:T(8,128)(2,1)} %collective-permute-done.17.rest_1_, ...), custom_call_target="tpu_custom_call" | custom-call | flops 83886080 | bytes 1310720 | tf_op jit(solution)/shard_map/correlate/pallas_call | solution.py:299
  (61 shorter events, 8.2 us)
Async XLA Ops:
  1.3 2.1 %collective-permute-start.1 = (bf16[8,64,512]{2,1,0:T(8,128)(2,1)S(1)}, bf16[8,64,512]{2,1,0:T(8,128)(2,1)S(1)}, u32[]{:S(2)}, u32[]{:S(2)}) collective-permute-start(bf16[8,64,512]{2,1,0:T(8,128)(2,1)S(1)} %bitcast.20), channel_id=1, source_target_pairs={{0,1},{1,0},{2,3},{3,2},{4,5},{5,4},{6,7},{7,6},{8,9},{9,8},{10,11... | collective-permute-start | bytes 1572872 | tf_op jit(solution)/shard_map/ppermute | solution.py:324
  3.4 10.2 %collective-permute-start.8 = (bf16[2,64,512]{2,1,0:T(8,128)(2,1)S(1)}, bf16[2,64,512]{2,1,0:T(8,128)(2,1)S(1)}, u32[]{:S(2)}, u32[]{:S(2)}) collective-permute-start(bf16[2,64,512]{2,1,0:T(8,128)(2,1)S(1)} %pad_maximum_fusion.10), channel_id=1, source_target_pairs={{0,12},{1,13},{2,14},{3,15},{4,8},{5,9},{6,10},{7,11},{8,4},{9,5},... | collective-permute-start | bytes 393224 | tf_op jit(solution)/shard_map/ppermute | solution.py:324
  7.4 8.2 %collective-permute-start.7 = (bf16[2,64,512]{2,1,0:T(8,128)(2,1)S(1)}, bf16[2,64,512]{2,1,0:T(8,128)(2,1)S(1)}, u32[]{:S(2)}, u32[]{:S(2)}) collective-permute-start(bf16[2,64,512]{2,1,0:T(8,128)(2,1)S(1)} %pad_maximum_fusion.9), channel_id=1, source_target_pairs={{0,2},{1,3},{2,0},{3,1},{4,6},{5,7},{6,4},{7,5},{8,10},{9,11},{10,... | collective-permute-start | bytes 393224 | tf_op jit(solution)/shard_map/ppermute | solution.py:324
  9.0 8.3 %collective-permute-start.6 = (bf16[2,64,512]{2,1,0:T(8,128)(2,1)S(1)}, bf16[2,64,512]{2,1,0:T(8,128)(2,1)S(1)}, u32[]{:S(2)}, u32[]{:S(2)}) collective-permute-start(bf16[2,64,512]{2,1,0:T(8,128)(2,1)S(1)} %pad_maximum_fusion.8), channel_id=1, source_target_pairs={{0,14},{1,15},{2,12},{3,13},{4,10},{5,11},{6,8},{7,9},{8,6},{9,7},... | collective-permute-start | bytes 393224 | tf_op jit(solution)/shard_map/ppermute | solution.py:324
  9.1 12.7 %collective-permute-start.5 = (bf16[2,64,512]{2,1,0:T(8,128)(2,1)S(1)}, bf16[2,64,512]{2,1,0:T(8,128)(2,1)S(1)}, u32[]{:S(2)}, u32[]{:S(2)}) collective-permute-start(bf16[2,64,512]{2,1,0:T(8,128)(2,1)S(1)} %pad_maximum_fusion.6), channel_id=1, source_target_pairs={{0,8},{1,9},{2,10},{3,11},{4,12},{5,13},{6,14},{7,15},{8,0},{9,1},... | collective-permute-start | bytes 393224 | tf_op jit(solution)/shard_map/ppermute | solution.py:324
  11.1 10.7 %collective-permute-start.4 = (bf16[2,64,512]{2,1,0:T(8,128)(2,1)S(1)}, bf16[2,64,512]{2,1,0:T(8,128)(2,1)S(1)}, u32[]{:S(2)}, u32[]{:S(2)}) collective-permute-start(bf16[2,64,512]{2,1,0:T(8,128)(2,1)S(1)} %pad_maximum_fusion.5), channel_id=1, source_target_pairs={{0,6},{1,7},{2,4},{3,5},{4,2},{5,3},{6,0},{7,1},{8,14},{9,15},{10,... | collective-permute-start | bytes 393224 | tf_op jit(solution)/shard_map/ppermute | solution.py:324
  13.7 8.1 %collective-permute-start.3 = (bf16[2,64,512]{2,1,0:T(8,128)(2,1)S(1)}, bf16[2,64,512]{2,1,0:T(8,128)(2,1)S(1)}, u32[]{:S(2)}, u32[]{:S(2)}) collective-permute-start(bf16[2,64,512]{2,1,0:T(8,128)(2,1)S(1)} %pad_maximum_fusion.4), channel_id=1, source_target_pairs={{0,10},{1,11},{2,8},{3,9},{4,14},{5,15},{6,12},{7,13},{8,2},{9,3},... | collective-permute-start | bytes 393224 | tf_op jit(solution)/shard_map/ppermute | solution.py:324
  15.7 6.1 %collective-permute-start.2 = (bf16[2,64,512]{2,1,0:T(8,128)(2,1)S(1)}, bf16[2,64,512]{2,1,0:T(8,128)(2,1)S(1)}, u32[]{:S(2)}, u32[]{:S(2)}) collective-permute-start(bf16[2,64,512]{2,1,0:T(8,128)(2,1)S(1)} %pad_maximum_fusion.3), channel_id=1, source_target_pairs={{0,4},{1,5},{2,6},{3,7},{4,0},{5,1},{6,2},{7,3},{8,12},{9,13},{10,... | collective-permute-start | bytes 393224 | tf_op jit(solution)/shard_map/ppermute | solution.py:324
  25.0 11.1 %collective-permute-start.9 = (f32[32,768]{1,0:T(8,128)S(1)}, f32[32,768]{1,0:T(8,128)S(1)}, u32[]{:S(2)}, u32[]{:S(2)}) collective-permute-start(f32[32,768]{1,0:T(8,128)S(1)} %get-tuple-element.10), channel_id=1, source_target_pairs={{0,16},{1,17},{2,18},{3,19},{4,20},{5,21},{6,22},{7,23},{8,24},{9,... | collective-permute-start | bytes 294920 | tf_op jit(solution)/shard_map/ppermute | solution.py:324
  30.1 6.0 %collective-permute-start.10 = (f32[32,512]{1,0:T(8,128)S(1)}, f32[32,512]{1,0:T(8,128)S(1)}, u32[]{:S(2)}, u32[]{:S(2)}) collective-permute-start(f32[32,512]{1,0:T(8,128)S(1)} %get-tuple-element.12), channel_id=1, source_target_pairs={{0,16},{1,17},{2,18},{3,19},{4,20},{5,21},{6,22},{7,23},{8,24},{9,... | collective-permute-start | bytes 196616 | tf_op jit(solution)/shard_map/ppermute | solution.py:324
  30.6 1.2 %collective-permute-start = (f32[8,4]{1,0:T(8,128)S(1)}, f32[8,4]{1,0:T(8,128)S(1)}, u32[]{:S(2)}, u32[]{:S(2)}) collective-permute-start(f32[8,4]{1,0:T(8,128)S(1)} %convert_element_type.3.flags_ref), channel_id=1, source_target_pairs={{0,1},{1,0},{2,3},{3,2},{4,5},{5,4},{6,7},{7,6},{8,9},{9,8},{10,11... | collective-permute-start | bytes 392 | tf_op jit(solution)/shard_map/ppermute | solution.py:324
  36.2 4.5 %collective-permute-start.13 = (bf16[32,1280]{1,0:T(8,128)(2,1)S(1)}, bf16[32,1280]{1,0:T(8,128)(2,1)S(1)}, u32[]{:S(2)}, u32[]{:S(2)}) collective-permute-start(bf16[32,1280]{1,0:T(8,128)(2,1)S(1)} %whiten.1), channel_id=1, source_target_pairs={{0,8},{1,9},{2,10},{3,11},{4,12},{5,13},{6,14},{7,15},{8,0},{9,1},... | collective-permute-start | bytes 245768 | tf_op jit(solution)/shard_map/ppermute | solution.py:324
  36.3 9.2 %collective-permute-start.11 = (bf16[32,1280]{1,0:T(8,128)(2,1)S(1)}, bf16[32,1280]{1,0:T(8,128)(2,1)S(1)}, u32[]{:S(2)}, u32[]{:S(2)}) collective-permute-start(bf16[32,1280]{1,0:T(8,128)(2,1)S(1)} %whiten.1), channel_id=1, source_target_pairs={{0,16},{1,17},{2,18},{3,19},{4,20},{5,21},{6,22},{7,23},{8,24},{9,... | collective-permute-start | bytes 245768 | tf_op jit(solution)/shard_map/ppermute | solution.py:324
  38.3 7.1 %collective-permute-start.12 = (bf16[32,1280]{1,0:T(8,128)(2,1)S(1)}, bf16[32,1280]{1,0:T(8,128)(2,1)S(1)}, u32[]{:S(2)}, u32[]{:S(2)}) collective-permute-start(bf16[32,1280]{1,0:T(8,128)(2,1)S(1)} %whiten.1), channel_id=1, source_target_pairs={{0,24},{1,25},{2,26},{3,27},{4,28},{5,29},{6,30},{7,31},{8,16},{9,... | collective-permute-start | bytes 245768 | tf_op jit(solution)/shard_map/ppermute | solution.py:324
  40.7 14.1 %collective-permute-start.22 = (bf16[2,32,1280]{2,1,0:T(8,128)(2,1)S(1)}, bf16[2,32,1280]{2,1,0:T(8,128)(2,1)S(1)}, u32[]{:S(2)}, u32[]{:S(2)}) collective-permute-start(bf16[2,32,1280]{2,1,0:T(8,128)(2,1)S(1)} %pad_maximum_fusion.2), channel_id=1, source_target_pairs={{0,6},{1,7},{2,4},{3,5},{4,2},{5,3},{6,0},{7,1},{8,14},{9,15},{10,... | collective-permute-start | bytes 491528 | tf_op jit(solution)/shard_map/ppermute | solution.py:324
  42.8 13.6 %collective-permute-start.19 = (bf16[2,32,1280]{2,1,0:T(8,128)(2,1)S(1)}, bf16[2,32,1280]{2,1,0:T(8,128)(2,1)S(1)}, u32[]{:S(2)}, u32[]{:S(2)}) collective-permute-start(bf16[2,32,1280]{2,1,0:T(8,128)(2,1)S(1)} %pad_maximum_fusion.2), channel_id=1, source_target_pairs={{0,4},{1,5},{2,6},{3,7},{4,0},{5,1},{6,2},{7,3},{8,12},{9,13},{10,... | collective-permute-start | bytes 491528 | tf_op jit(solution)/shard_map/ppermute | solution.py:324
  45.5 7.0 %collective-permute-start.21 = (bf16[2,32,1280]{2,1,0:T(8,128)(2,1)S(1)}, bf16[2,32,1280]{2,1,0:T(8,128)(2,1)S(1)}, u32[]{:S(2)}, u32[]{:S(2)}) collective-permute-start(bf16[2,32,1280]{2,1,0:T(8,128)(2,1)S(1)} %pad_maximum_fusion.1), channel_id=1, source_target_pairs={{0,6},{1,7},{2,4},{3,5},{4,2},{5,3},{6,0},{7,1},{8,14},{9,15},{10,... | collective-permute-start | bytes 491528 | tf_op jit(solution)/shard_map/ppermute | solution.py:324
  46.4 9.4 %collective-permute-start.18 = (bf16[2,32,1280]{2,1,0:T(8,128)(2,1)S(1)}, bf16[2,32,1280]{2,1,0:T(8,128)(2,1)S(1)}, u32[]{:S(2)}, u32[]{:S(2)}) collective-permute-start(bf16[2,32,1280]{2,1,0:T(8,128)(2,1)S(1)} %pad_maximum_fusion.1), channel_id=1, source_target_pairs={{0,4},{1,5},{2,6},{3,7},{4,0},{5,1},{6,2},{7,3},{8,12},{9,13},{10,... | collective-permute-start | bytes 491528 | tf_op jit(solution)/shard_map/ppermute | solution.py:324
  47.1 11.7 %collective-permute-start.16 = (bf16[2,32,1280]{2,1,0:T(8,128)(2,1)S(1)}, bf16[2,32,1280]{2,1,0:T(8,128)(2,1)S(1)}, u32[]{:S(2)}, u32[]{:S(2)}) collective-permute-start(bf16[2,32,1280]{2,1,0:T(8,128)(2,1)S(1)} %pad_maximum_fusion.2), channel_id=1, source_target_pairs={{0,2},{1,3},{2,0},{3,1},{4,6},{5,7},{6,4},{7,5},{8,10},{9,11},{10,... | collective-permute-start | bytes 491528 | tf_op jit(solution)/shard_map/ppermute | solution.py:324
  52.4 5.7 %collective-permute-start.15 = (bf16[2,32,1280]{2,1,0:T(8,128)(2,1)S(1)}, bf16[2,32,1280]{2,1,0:T(8,128)(2,1)S(1)}, u32[]{:S(2)}, u32[]{:S(2)}) collective-permute-start(bf16[2,32,1280]{2,1,0:T(8,128)(2,1)S(1)} %pad_maximum_fusion.1), channel_id=1, source_target_pairs={{0,2},{1,3},{2,0},{3,1},{4,6},{5,7},{6,4},{7,5},{8,10},{9,11},{10,... | collective-permute-start | bytes 491528 | tf_op jit(solution)/shard_map/ppermute | solution.py:324
  54.8 7.3 %collective-permute-start.14 = (bf16[4,32,1280]{2,1,0:T(8,128)(2,1)S(1)}, bf16[4,32,1280]{2,1,0:T(8,128)(2,1)}, u32[]{:S(2)}, u32[]{:S(2)}) collective-permute-start(bf16[4,32,1280]{2,1,0:T(8,128)(2,1)S(1)} %pad_maximum_fusion.rest_0_), channel_id=1, source_target_pairs={{0,1},{1,0},{2,3},{3,2},{4,5},{5,4},{6,7},{7,6},{8,9},{9,8},{10,11... | collective-permute-start | bytes 983048 | tf_op jit(solution)/shard_map/ppermute | solution.py:324
  55.8 6.3 %collective-permute-start.23 = (bf16[4,32,1280]{2,1,0:T(8,128)(2,1)S(1)}, bf16[4,32,1280]{2,1,0:T(8,128)(2,1)}, u32[]{:S(2)}, u32[]{:S(2)}) collective-permute-start(bf16[4,32,1280]{2,1,0:T(8,128)(2,1)S(1)} %constant_dynamic-update-slice_fusion.4.rest_3_), channel_id=1, source_target_pairs={{0,1},{1,0},{2,3},{3,2},{4,5},{5,4},{6,7},{7,6},{8,9},{9,8},{10,11... | collective-permute-start | bytes 983048 | tf_op jit(solution)/shard_map/ppermute | solution.py:324
  57.1 5.0 %collective-permute-start.20 = (bf16[4,32,1280]{2,1,0:T(8,128)(2,1)}, bf16[4,32,1280]{2,1,0:T(8,128)(2,1)}, u32[]{:S(2)}, u32[]{:S(2)}) collective-permute-start(bf16[4,32,1280]{2,1,0:T(8,128)(2,1)} %constant_dynamic-update-slice_fusion.2.rest_2_), channel_id=1, source_target_pairs={{0,1},{1,0},{2,3},{3,2},{4,5},{5,4},{6,7},{7,6},{8,9},{9,8},{10,11... | collective-permute-start | bytes 983048 | tf_op jit(solution)/shard_map/ppermute | solution.py:324
  59.5 2.7 %collective-permute-start.17 = (bf16[4,32,1280]{2,1,0:T(8,128)(2,1)}, bf16[4,32,1280]{2,1,0:T(8,128)(2,1)}, u32[]{:S(2)}, u32[]{:S(2)}) collective-permute-start(bf16[4,32,1280]{2,1,0:T(8,128)(2,1)} %constant_dynamic-update-slice_fusion.rest_1_), channel_id=1, source_target_pairs={{0,1},{1,0},{2,3},{3,2},{4,5},{5,4},{6,7},{7,6},{8,9},{9,8},{10,11... | collective-permute-start | bytes 983048 | tf_op jit(solution)/shard_map/ppermute | solution.py:324
  (3 other events, 51.6 us)

commit v8 on v7

--- a/solution.py
+++ b/solution.py
@@ -177,6 +177,22 @@
         compiler_params=pltpu.CompilerParams(vmem_limit_bytes=16 * 2**20),
         name="whiten",
     )(flags, *parts)
+
+
+def join_kernel(first_ref, second_ref, out_ref):
+    half = first_ref.shape[0]
+    out_ref[:half] = first_ref[...]
+    out_ref[half:] = second_ref[...]
+
+
+def join(first, second):
+    half, rows, columns = first.shape
+    return pl.pallas_call(
+        join_kernel,
+        out_shape=jax.ShapeDtypeStruct((2 * half, rows, columns), first.dtype),
+        compiler_params=pltpu.CompilerParams(vmem_limit_bytes=16 * 2**20),
+        name="join",
+    )(first, second)
 
 
 def correlate_kernel(shape, core, steps, place_ref, flags_ref, ids_ref, *rest):
@@ -360,10 +376,10 @@
     line = [white] + [exchange(white, 8 * k) for k in range(1, far)]
     halves = [jnp.stack(line[far // 2 :]), jnp.stack(line[: far // 2])]
     steps = [2 * near for near in range(4)]
-    blocks = [
-        jnp.concatenate([exchange(half, step) if step else half for half in halves])
-        for step in steps
-    ]
+    blocks = []
+    for step in steps:
+        came = [exchange(half, step) if step else half for half in halves]
+        blocks.append(join(*came))
     swapped = [exchange(block, 1) for block in blocks]
     ids = source_ids.reshape(-1, 1)
     common = me, weights, ids

time: 67.2 us -> 67.3 us (level)
  waiting for transfers between devices: 14.3 us -> 17.7 us
  local copies, waits for them, and re-layouts: 4.36 us -> 1.65 us
  starting transfers between devices: 30.3 us -> 28.2 us
  Pallas kernels: 17.5 us -> 19 us
    ppermute x24, waiting for transfers between devices: 14.3 us -> 17.7 us  [exchange(): return lax.ppermute(block, 'chan', [(i, i ^ bits) for i in range(devices)])]
    ppermute x24, starting transfers between devices: 30.3 us -> 28.2 us  [exchange(): return lax.ppermute(block, 'chan', [(i, i ^ bits) for i in range(devices)])]
    pallas_call x0 -> x4, Pallas kernels: none -> 1.54 us  [join(): pl.pallas_call(join_kernel, out_shape=jax.ShapeDtypeStruct((2 * half, row...]
    concatenate x3 -> x0, local copies, waits for them, and re-layouts: 1.36 us -> none  [per_device(): jnp.concatenate([exchange(half, step) if step else half for half in halves])]
    unnamed x10 -> x7, local copies, waits for them, and re-layouts: 1.45 us -> 0.1 us
  transfers between devices with their start and end apart: 24 -> 24, of which waited for: 9 -> 10; matrix products, arithmetic and copies ran while one was open for 5% -> 1% of each run, Pallas kernels for 14% -> 16%
where the time goes in v8:
time: 67.3 us; the launch traced here: 67.1 us
  starting transfers between devices  28.2 us (42%)
  Pallas kernels  19 us (28%)
  waiting for transfers between devices  17.7 us (26%)
  local copies, waits for them, and re-layouts  1.65 us (2%)
    ppermute x24, starting transfers between devices, exchange(): return lax.ppermute(block, 'chan', [(i, i ^ bits) for i in range(devices)])  28.2 us
    ppermute x24, waiting for transfers between devices, exchange(): return lax.ppermute(block, 'chan', [(i, i ^ bits) for i in range(devices)])  17.7 us
    pallas_call x3, Pallas kernels, transform(): pl.pallas_call(functools.partial(transform_kernel, steps, first, started)...  10 us
    pallas_call x2, Pallas kernels, correlate(): pl.pallas_call(functools.partial(correlate_kernel, shape, core, steps), i...  7.39 us
    pallas_call x4, Pallas kernels, join(): pl.pallas_call(join_kernel, out_shape=jax.ShapeDtypeStruct((2 * half, row...  1.54 us
  transfers between devices with their start and end apart: 24, of which 10 were waited for; matrix products, arithmetic and copies ran while one was open for 1% of the time, Pallas kernels for 16%

profile of v8, /device:TPU:0, one launch (start us, length us, event | category | flops | bytes accessed | tf_op | source)
XLA Modules:
  0.0 67.1 jit_solution(721830023451873376)
XLA Ops:
  0.0 1.3 %constant_dynamic-slice_fusion.20 = (bf16[4,1,128,512]{3,2,1,0:T(8,128)(2,1)S(1)}, bf16[4,1,128,512]{3,2,1,0:T(8,128)(2,1)S(1)}) fusion(bf16[4,2,128,512]{3,2,1,0:T(8,128)(2,1)} %bitcast.18, s32[]{:T(128)S(6)} %select_n.69, s32[]{:T(128)S(6)} %select_n.73), kind=kLoop, calls=%fused_computation.30 | loop fusion | bytes 2097160 | tf_op jit(solution)/shard_map/jit(dynamic_index_in_dim)/dynamic_slice | solution.py:355
  1.9 1.5 %collective-permute-done.1 = bf16[8,64,512]{2,1,0:T(8,128)(2,1)S(1)} collective-permute-done((bf16[8,64,512]{2,1,0:T(8,128)(2,1)S(1)}, bf16[8,64,512]{2,1,0:T(8,128)(2,1)S(1)}, u32[]{:S(2)}, u32[]{:S(2)}) %collective-permute-start.1) | collective-permute-done | bytes 524320 | tf_op jit(solution)/shard_map/ppermute | solution.py:340
  3.4 4.0 %collective-permute-start.8 = (bf16[2,64,512]{2,1,0:T(8,128)(2,1)S(1)}, bf16[2,64,512]{2,1,0:T(8,128)(2,1)S(1)}, u32[]{:S(2)}, u32[]{:S(2)}) collective-permute-start(bf16[2,64,512]{2,1,0:T(8,128)(2,1)S(1)} %pad_maximum_fusion.9), channel_id=1, source_target_pairs={{0,12},{1,13},{2,14},{3,15},{4,8},{5,9},{6,10},{7,11},{8,4},{9,5},... | collective-permute-start | bytes 393224 | tf_op jit(solution)/shard_map/ppermute | solution.py:340
  7.4 1.6 %collective-permute-start.7 = (bf16[2,64,512]{2,1,0:T(8,128)(2,1)S(1)}, bf16[2,64,512]{2,1,0:T(8,128)(2,1)S(1)}, u32[]{:S(2)}, u32[]{:S(2)}) collective-permute-start(bf16[2,64,512]{2,1,0:T(8,128)(2,1)S(1)} %pad_maximum_fusion.8), channel_id=1, source_target_pairs={{0,2},{1,3},{2,0},{3,1},{4,6},{5,7},{6,4},{7,5},{8,10},{9,11},{10,... | collective-permute-start | bytes 393224 | tf_op jit(solution)/shard_map/ppermute | solution.py:340
  9.1 2.0 %collective-permute-start.5 = (bf16[2,64,512]{2,1,0:T(8,128)(2,1)S(1)}, bf16[2,64,512]{2,1,0:T(8,128)(2,1)S(1)}, u32[]{:S(2)}, u32[]{:S(2)}) collective-permute-start(bf16[2,64,512]{2,1,0:T(8,128)(2,1)S(1)} %pad_maximum_fusion.5), channel_id=1, source_target_pairs={{0,8},{1,9},{2,10},{3,11},{4,12},{5,13},{6,14},{7,15},{8,0},{9,1},... | collective-permute-start | bytes 393224 | tf_op jit(solution)/shard_map/ppermute | solution.py:340
  11.1 2.5 %collective-permute-start.4 = (bf16[2,64,512]{2,1,0:T(8,128)(2,1)S(1)}, bf16[2,64,512]{2,1,0:T(8,128)(2,1)S(1)}, u32[]{:S(2)}, u32[]{:S(2)}) collective-permute-start(bf16[2,64,512]{2,1,0:T(8,128)(2,1)S(1)} %pad_maximum_fusion.4), channel_id=1, source_target_pairs={{0,6},{1,7},{2,4},{3,5},{4,2},{5,3},{6,0},{7,1},{8,14},{9,15},{10,... | collective-permute-start | bytes 393224 | tf_op jit(solution)/shard_map/ppermute | solution.py:340
  14.1 1.5 %collective-permute-done.7.rest_2_ = bf16[2,64,512]{2,1,0:T(8,128)(2,1)S(1)} collective-permute-done((bf16[2,64,512]{2,1,0:T(8,128)(2,1)S(1)}, bf16[2,64,512]{2,1,0:T(8,128)(2,1)S(1)}, u32[]{:S(2)}, u32[]{:S(2)}) %collective-permute-start.7) | collective-permute-done | bytes 131104 | tf_op jit(solution)/shard_map/ppermute | solution.py:340
  17.3 4.4 %transform.3.rest_4_ = f32[64,1280]{1,0:T(8,128)S(1)} custom-call(s32[1]{0:T(128)} %bitcast.place_ref, bf16[163840,128]{1,0:T(8,128)(2,1)} %constant.100.clone.table_ref, bf16[2,64,512]{2,1,0:T(8,128)(2,1)S(1)} %pad_maximum_fusion.6.rest_0_, bf16[2,64,512]{2,1,0:T(8,128)(2,1)S(1)} %collective-permute-done.6.rest_1_, ...), custom_call_target="tpu_custom_call" | custom-call | flops 671088640 | bytes 10485760 | tf_op jit(solution)/shard_map/transform/pallas_call | solution.py:121
  21.8 3.1 %transform.4 = (f32[32,768]{1,0:T(8,128)S(1)}, f32[32,768]{1,0:T(8,128)S(1)}) custom-call(s32[1]{0:T(128)} %bitcast.place_ref, bf16[163840,128]{1,0:T(8,128)(2,1)} %constant.100.clone.table_ref, bf16[2,64,512]{2,1,0:T(8,128)(2,1)S(1)} %collective-permute-done.2.rest_0_, bf16[2,64,512]{2,1,0:T(8,128)(2,1)S(1)} %collective-permute-done.3.rest_1_, ...), custom_call_target="tpu_custom_call" | custom-call | flops 402653184 | bytes 6291456 | tf_op jit(solution)/shard_map/transform/pallas_call | solution.py:121
  25.0 2.7 %collective-permute-start.9 = (f32[32,768]{1,0:T(8,128)S(1)}, f32[32,768]{1,0:T(8,128)S(1)}, u32[]{:S(2)}, u32[]{:S(2)}) collective-permute-start(f32[32,768]{1,0:T(8,128)S(1)} %get-tuple-element.10), channel_id=1, source_target_pairs={{0,16},{1,17},{2,18},{3,19},{4,20},{5,21},{6,22},{7,23},{8,24},{9,... | collective-permute-start | bytes 294920 | tf_op jit(solution)/shard_map/ppermute | solution.py:340
  27.6 2.4 %transform.5 = (f32[32,512]{1,0:T(8,128)S(1)}, f32[32,512]{1,0:T(8,128)S(1)}) custom-call(s32[1]{0:T(128)} %bitcast.place_ref, bf16[163840,128]{1,0:T(8,128)(2,1)} %constant.100.clone.table_ref, bf16[2,64,512]{2,1,0:T(8,128)(2,1)S(1)} %collective-permute-done.2.rest_0_, bf16[2,64,512]{2,1,0:T(8,128)(2,1)S(1)} %collective-permute-done.3.rest_1_, ...), custom_call_target="tpu_custom_call" | custom-call | flops 268435456 | bytes 4194304 | tf_op jit(solution)/shard_map/transform/pallas_call | solution.py:121
  31.9 4.2 %collective-permute-done.10.rest_3_ = f32[32,512]{1,0:T(8,128)S(1)} collective-permute-done((f32[32,512]{1,0:T(8,128)S(1)}, f32[32,512]{1,0:T(8,128)S(1)}, u32[]{:S(2)}, u32[]{:S(2)}) %collective-permute-start.10) | collective-permute-done | bytes 65568 | tf_op jit(solution)/shard_map/ppermute | solution.py:340
  36.3 2.0 %collective-permute-start.11 = (bf16[32,1280]{1,0:T(8,128)(2,1)S(1)}, bf16[32,1280]{1,0:T(8,128)(2,1)S(1)}, u32[]{:S(2)}, u32[]{:S(2)}) collective-permute-start(bf16[32,1280]{1,0:T(8,128)(2,1)S(1)} %whiten.1), channel_id=1, source_target_pairs={{0,16},{1,17},{2,18},{3,19},{4,20},{5,21},{6,22},{7,23},{8,24},{9,... | collective-permute-start | bytes 245768 | tf_op jit(solution)/shard_map/ppermute | solution.py:340
  38.3 2.3 %collective-permute-start.12 = (bf16[32,1280]{1,0:T(8,128)(2,1)S(1)}, bf16[32,1280]{1,0:T(8,128)(2,1)S(1)}, u32[]{:S(2)}, u32[]{:S(2)}) collective-permute-start(bf16[32,1280]{1,0:T(8,128)(2,1)S(1)} %whiten.1), channel_id=1, source_target_pairs={{0,24},{1,25},{2,26},{3,27},{4,28},{5,29},{6,30},{7,31},{8,16},{9,... | collective-permute-start | bytes 245768 | tf_op jit(solution)/shard_map/ppermute | solution.py:340
  40.7 2.1 %collective-permute-start.22 = (bf16[2,32,1280]{2,1,0:T(8,128)(2,1)S(1)}, bf16[2,32,1280]{2,1,0:T(8,128)(2,1)S(1)}, u32[]{:S(2)}, u32[]{:S(2)}) collective-permute-start(bf16[2,32,1280]{2,1,0:T(8,128)(2,1)S(1)} %pad_maximum_fusion.1.second_ref), channel_id=1, source_target_pairs={{0,6},{1,7},{2,4},{3,5},{4,2},{5,3},{6,0},{7,1},{8,14},{9,15},{10,... | collective-permute-start | bytes 491528 | tf_op jit(solution)/shard_map/ppermute | solution.py:340
  42.8 1.8 %collective-permute-done.11 = bf16[32,1280]{1,0:T(8,128)(2,1)S(1)} collective-permute-done((bf16[32,1280]{1,0:T(8,128)(2,1)S(1)}, bf16[32,1280]{1,0:T(8,128)(2,1)S(1)}, u32[]{:S(2)}, u32[]{:S(2)}) %collective-permute-start.11) | collective-permute-done | bytes 81952 | tf_op jit(solution)/shard_map/ppermute | solution.py:340
  44.6 1.8 %collective-permute-start.21 = (bf16[2,32,1280]{2,1,0:T(8,128)(2,1)S(1)}, bf16[2,32,1280]{2,1,0:T(8,128)(2,1)S(1)}, u32[]{:S(2)}, u32[]{:S(2)}) collective-permute-start(bf16[2,32,1280]{2,1,0:T(8,128)(2,1)S(1)} %pad_maximum_fusion.first_ref), channel_id=1, source_target_pairs={{0,6},{1,7},{2,4},{3,5},{4,2},{5,3},{6,0},{7,1},{8,14},{9,15},{10,... | collective-permute-start | bytes 491528 | tf_op jit(solution)/shard_map/ppermute | solution.py:340
  47.1 1.4 %collective-permute-start.18 = (bf16[2,32,1280]{2,1,0:T(8,128)(2,1)S(1)}, bf16[2,32,1280]{2,1,0:T(8,128)(2,1)S(1)}, u32[]{:S(2)}, u32[]{:S(2)}) collective-permute-start(bf16[2,32,1280]{2,1,0:T(8,128)(2,1)S(1)} %pad_maximum_fusion.first_ref), channel_id=1, source_target_pairs={{0,4},{1,5},{2,6},{3,7},{4,0},{5,1},{6,2},{7,3},{8,12},{9,13},{10,... | collective-permute-start | bytes 491528 | tf_op jit(solution)/shard_map/ppermute | solution.py:340
  49.7 1.5 %collective-permute-start.15 = (bf16[2,32,1280]{2,1,0:T(8,128)(2,1)S(1)}, bf16[2,32,1280]{2,1,0:T(8,128)(2,1)S(1)}, u32[]{:S(2)}, u32[]{:S(2)}) collective-permute-start(bf16[2,32,1280]{2,1,0:T(8,128)(2,1)S(1)} %pad_maximum_fusion.first_ref), channel_id=1, source_target_pairs={{0,2},{1,3},{2,0},{3,1},{4,6},{5,7},{6,4},{7,5},{8,10},{9,11},{10,... | collective-permute-start | bytes 491528 | tf_op jit(solution)/shard_map/ppermute | solution.py:340
  51.2 1.5 %collective-permute-done.21.first_ref = bf16[2,32,1280]{2,1,0:T(8,128)(2,1)S(1)} collective-permute-done((bf16[2,32,1280]{2,1,0:T(8,128)(2,1)S(1)}, bf16[2,32,1280]{2,1,0:T(8,128)(2,1)S(1)}, u32[]{:S(2)}, u32[]{:S(2)}) %collective-permute-start.21) | collective-permute-done | bytes 163872 | tf_op jit(solution)/shard_map/ppermute | solution.py:340
  52.8 2.2 %collective-permute-done.19.second_ref = bf16[2,32,1280]{2,1,0:T(8,128)(2,1)S(1)} collective-permute-done((bf16[2,32,1280]{2,1,0:T(8,128)(2,1)S(1)}, bf16[2,32,1280]{2,1,0:T(8,128)(2,1)S(1)}, u32[]{:S(2)}, u32[]{:S(2)}) %collective-permute-start.19) | collective-permute-done | bytes 163872 | tf_op jit(solution)/shard_map/ppermute | solution.py:340
  54.9 2.6 %collective-permute-done.18.first_ref = bf16[2,32,1280]{2,1,0:T(8,128)(2,1)S(1)} collective-permute-done((bf16[2,32,1280]{2,1,0:T(8,128)(2,1)S(1)}, bf16[2,32,1280]{2,1,0:T(8,128)(2,1)S(1)}, u32[]{:S(2)}, u32[]{:S(2)}) %collective-permute-start.18) | collective-permute-done | bytes 163872 | tf_op jit(solution)/shard_map/ppermute | solution.py:340
  59.7 2.5 %correlate.2.rest_4_ = f32[4,64,1280]{2,1,0:T(8,128)S(1)} custom-call(s32[1]{0:T(128)} %bitcast.place_ref, f32[8,4]{1,0:T(8,128)S(1)} %convert_element_type.3.flags_ref, s32[64,1]{1,0:T(8,128)S(1)} %copy.10.ids_ref, bf16[4,32,1280]{2,1,0:T(8,128)(2,1)S(1)} %join.4.rest_0_, bf16[4,32,1280]{2,1,0:T(8,128)(2,1)} %join.5.rest_1_, ...), custom_call_target="tpu_custom_call" | custom-call | flops 83886080 | bytes 1310720 | tf_op jit(solution)/shard_map/correlate/pallas_call | solution.py:315
  62.2 4.9 %correlate.3 = f32[64,4,1001]{2,1,0:T(4,128)} custom-call(s32[1]{0:T(128)} %bitcast.place_ref, f32[8,4]{1,0:T(8,128)S(1)} %convert_element_type.3.flags_ref, s32[64,1]{1,0:T(8,128)S(1)} %copy.10.ids_ref, bf16[4,32,1280]{2,1,0:T(8,128)(2,1)} %collective-permute-done.14.rest_0_, bf16[4,32,1280]{2,1,0:T(8,128)(2,1)} %collective-permute-done.17.rest_1_, ...), custom_call_target="tpu_custom_call" | custom-call | flops 83886080 | bytes 1310720 | tf_op jit(solution)/shard_map/correlate/pallas_call | solution.py:315
  (58 shorter events, 9.1 us)
Async XLA Ops:
  1.3 2.1 %collective-permute-start.1 = (bf16[8,64,512]{2,1,0:T(8,128)(2,1)S(1)}, bf16[8,64,512]{2,1,0:T(8,128)(2,1)S(1)}, u32[]{:S(2)}, u32[]{:S(2)}) collective-permute-start(bf16[8,64,512]{2,1,0:T(8,128)(2,1)S(1)} %bitcast.19), channel_id=1, source_target_pairs={{0,1},{1,0},{2,3},{3,2},{4,5},{5,4},{6,7},{7,6},{8,9},{9,8},{10,11... | collective-permute-start | bytes 1572872 | tf_op jit(solution)/shard_map/ppermute | solution.py:340
  3.4 10.2 %collective-permute-start.8 = (bf16[2,64,512]{2,1,0:T(8,128)(2,1)S(1)}, bf16[2,64,512]{2,1,0:T(8,128)(2,1)S(1)}, u32[]{:S(2)}, u32[]{:S(2)}) collective-permute-start(bf16[2,64,512]{2,1,0:T(8,128)(2,1)S(1)} %pad_maximum_fusion.9), channel_id=1, source_target_pairs={{0,12},{1,13},{2,14},{3,15},{4,8},{5,9},{6,10},{7,11},{8,4},{9,5},... | collective-permute-start | bytes 393224 | tf_op jit(solution)/shard_map/ppermute | solution.py:340
  7.4 8.2 %collective-permute-start.7 = (bf16[2,64,512]{2,1,0:T(8,128)(2,1)S(1)}, bf16[2,64,512]{2,1,0:T(8,128)(2,1)S(1)}, u32[]{:S(2)}, u32[]{:S(2)}) collective-permute-start(bf16[2,64,512]{2,1,0:T(8,128)(2,1)S(1)} %pad_maximum_fusion.8), channel_id=1, source_target_pairs={{0,2},{1,3},{2,0},{3,1},{4,6},{5,7},{6,4},{7,5},{8,10},{9,11},{10,... | collective-permute-start | bytes 393224 | tf_op jit(solution)/shard_map/ppermute | solution.py:340
  9.0 8.3 %collective-permute-start.6 = (bf16[2,64,512]{2,1,0:T(8,128)(2,1)S(1)}, bf16[2,64,512]{2,1,0:T(8,128)(2,1)S(1)}, u32[]{:S(2)}, u32[]{:S(2)}) collective-permute-start(bf16[2,64,512]{2,1,0:T(8,128)(2,1)S(1)} %pad_maximum_fusion.7), channel_id=1, source_target_pairs={{0,14},{1,15},{2,12},{3,13},{4,10},{5,11},{6,8},{7,9},{8,6},{9,7},... | collective-permute-start | bytes 393224 | tf_op jit(solution)/shard_map/ppermute | solution.py:340
  9.1 12.7 %collective-permute-start.5 = (bf16[2,64,512]{2,1,0:T(8,128)(2,1)S(1)}, bf16[2,64,512]{2,1,0:T(8,128)(2,1)S(1)}, u32[]{:S(2)}, u32[]{:S(2)}) collective-permute-start(bf16[2,64,512]{2,1,0:T(8,128)(2,1)S(1)} %pad_maximum_fusion.5), channel_id=1, source_target_pairs={{0,8},{1,9},{2,10},{3,11},{4,12},{5,13},{6,14},{7,15},{8,0},{9,1},... | collective-permute-start | bytes 393224 | tf_op jit(solution)/shard_map/ppermute | solution.py:340
  11.1 10.7 %collective-permute-start.4 = (bf16[2,64,512]{2,1,0:T(8,128)(2,1)S(1)}, bf16[2,64,512]{2,1,0:T(8,128)(2,1)S(1)}, u32[]{:S(2)}, u32[]{:S(2)}) collective-permute-start(bf16[2,64,512]{2,1,0:T(8,128)(2,1)S(1)} %pad_maximum_fusion.4), channel_id=1, source_target_pairs={{0,6},{1,7},{2,4},{3,5},{4,2},{5,3},{6,0},{7,1},{8,14},{9,15},{10,... | collective-permute-start | bytes 393224 | tf_op jit(solution)/shard_map/ppermute | solution.py:340
  13.7 8.1 %collective-permute-start.3 = (bf16[2,64,512]{2,1,0:T(8,128)(2,1)S(1)}, bf16[2,64,512]{2,1,0:T(8,128)(2,1)S(1)}, u32[]{:S(2)}, u32[]{:S(2)}) collective-permute-start(bf16[2,64,512]{2,1,0:T(8,128)(2,1)S(1)} %pad_maximum_fusion.3), channel_id=1, source_target_pairs={{0,10},{1,11},{2,8},{3,9},{4,14},{5,15},{6,12},{7,13},{8,2},{9,3},... | collective-permute-start | bytes 393224 | tf_op jit(solution)/shard_map/ppermute | solution.py:340
  15.7 6.1 %collective-permute-start.2 = (bf16[2,64,512]{2,1,0:T(8,128)(2,1)S(1)}, bf16[2,64,512]{2,1,0:T(8,128)(2,1)S(1)}, u32[]{:S(2)}, u32[]{:S(2)}) collective-permute-start(bf16[2,64,512]{2,1,0:T(8,128)(2,1)S(1)} %pad_maximum_fusion.2), channel_id=1, source_target_pairs={{0,4},{1,5},{2,6},{3,7},{4,0},{5,1},{6,2},{7,3},{8,12},{9,13},{10,... | collective-permute-start | bytes 393224 | tf_op jit(solution)/shard_map/ppermute | solution.py:340
  25.0 11.1 %collective-permute-start.9 = (f32[32,768]{1,0:T(8,128)S(1)}, f32[32,768]{1,0:T(8,128)S(1)}, u32[]{:S(2)}, u32[]{:S(2)}) collective-permute-start(f32[32,768]{1,0:T(8,128)S(1)} %get-tuple-element.10), channel_id=1, source_target_pairs={{0,16},{1,17},{2,18},{3,19},{4,20},{5,21},{6,22},{7,23},{8,24},{9,... | collective-permute-start | bytes 294920 | tf_op jit(solution)/shard_map/ppermute | solution.py:340
  30.1 6.0 %collective-permute-start.10 = (f32[32,512]{1,0:T(8,128)S(1)}, f32[32,512]{1,0:T(8,128)S(1)}, u32[]{:S(2)}, u32[]{:S(2)}) collective-permute-start(f32[32,512]{1,0:T(8,128)S(1)} %get-tuple-element.12), channel_id=1, source_target_pairs={{0,16},{1,17},{2,18},{3,19},{4,20},{5,21},{6,22},{7,23},{8,24},{9,... | collective-permute-start | bytes 196616 | tf_op jit(solution)/shard_map/ppermute | solution.py:340
  30.6 1.2 %collective-permute-start = (f32[8,4]{1,0:T(8,128)S(1)}, f32[8,4]{1,0:T(8,128)S(1)}, u32[]{:S(2)}, u32[]{:S(2)}) collective-permute-start(f32[8,4]{1,0:T(8,128)S(1)} %convert_element_type.3.flags_ref), channel_id=1, source_target_pairs={{0,1},{1,0},{2,3},{3,2},{4,5},{5,4},{6,7},{7,6},{8,9},{9,8},{10,11... | collective-permute-start | bytes 392 | tf_op jit(solution)/shard_map/ppermute | solution.py:340
  36.2 4.5 %collective-permute-start.13 = (bf16[32,1280]{1,0:T(8,128)(2,1)S(1)}, bf16[32,1280]{1,0:T(8,128)(2,1)S(1)}, u32[]{:S(2)}, u32[]{:S(2)}) collective-permute-start(bf16[32,1280]{1,0:T(8,128)(2,1)S(1)} %whiten.1), channel_id=1, source_target_pairs={{0,8},{1,9},{2,10},{3,11},{4,12},{5,13},{6,14},{7,15},{8,0},{9,1},... | collective-permute-start | bytes 245768 | tf_op jit(solution)/shard_map/ppermute | solution.py:340
  36.3 8.3 %collective-permute-start.11 = (bf16[32,1280]{1,0:T(8,128)(2,1)S(1)}, bf16[32,1280]{1,0:T(8,128)(2,1)S(1)}, u32[]{:S(2)}, u32[]{:S(2)}) collective-permute-start(bf16[32,1280]{1,0:T(8,128)(2,1)S(1)} %whiten.1), channel_id=1, source_target_pairs={{0,16},{1,17},{2,18},{3,19},{4,20},{5,21},{6,22},{7,23},{8,24},{9,... | collective-permute-start | bytes 245768 | tf_op jit(solution)/shard_map/ppermute | solution.py:340
  38.3 6.3 %collective-permute-start.12 = (bf16[32,1280]{1,0:T(8,128)(2,1)S(1)}, bf16[32,1280]{1,0:T(8,128)(2,1)S(1)}, u32[]{:S(2)}, u32[]{:S(2)}) collective-permute-start(bf16[32,1280]{1,0:T(8,128)(2,1)S(1)} %whiten.1), channel_id=1, source_target_pairs={{0,24},{1,25},{2,26},{3,27},{4,28},{5,29},{6,30},{7,31},{8,16},{9,... | collective-permute-start | bytes 245768 | tf_op jit(solution)/shard_map/ppermute | solution.py:340
  40.7 8.9 %collective-permute-start.22 = (bf16[2,32,1280]{2,1,0:T(8,128)(2,1)S(1)}, bf16[2,32,1280]{2,1,0:T(8,128)(2,1)S(1)}, u32[]{:S(2)}, u32[]{:S(2)}) collective-permute-start(bf16[2,32,1280]{2,1,0:T(8,128)(2,1)S(1)} %pad_maximum_fusion.1.second_ref), channel_id=1, source_target_pairs={{0,6},{1,7},{2,4},{3,5},{4,2},{5,3},{6,0},{7,1},{8,14},{9,15},{10,... | collective-permute-start | bytes 491528 | tf_op jit(solution)/shard_map/ppermute | solution.py:340
  44.6 8.1 %collective-permute-start.21 = (bf16[2,32,1280]{2,1,0:T(8,128)(2,1)S(1)}, bf16[2,32,1280]{2,1,0:T(8,128)(2,1)S(1)}, u32[]{:S(2)}, u32[]{:S(2)}) collective-permute-start(bf16[2,32,1280]{2,1,0:T(8,128)(2,1)S(1)} %pad_maximum_fusion.first_ref), channel_id=1, source_target_pairs={{0,6},{1,7},{2,4},{3,5},{4,2},{5,3},{6,0},{7,1},{8,14},{9,15},{10,... | collective-permute-start | bytes 491528 | tf_op jit(solution)/shard_map/ppermute | solution.py:340
  46.4 8.5 %collective-permute-start.19 = (bf16[2,32,1280]{2,1,0:T(8,128)(2,1)S(1)}, bf16[2,32,1280]{2,1,0:T(8,128)(2,1)S(1)}, u32[]{:S(2)}, u32[]{:S(2)}) collective-permute-start(bf16[2,32,1280]{2,1,0:T(8,128)(2,1)S(1)} %pad_maximum_fusion.1.second_ref), channel_id=1, source_target_pairs={{0,4},{1,5},{2,6},{3,7},{4,0},{5,1},{6,2},{7,3},{8,12},{9,13},{10,... | collective-permute-start | bytes 491528 | tf_op jit(solution)/shard_map/ppermute | solution.py:340
  47.1 10.5 %collective-permute-start.18 = (bf16[2,32,1280]{2,1,0:T(8,128)(2,1)S(1)}, bf16[2,32,1280]{2,1,0:T(8,128)(2,1)S(1)}, u32[]{:S(2)}, u32[]{:S(2)}) collective-permute-start(bf16[2,32,1280]{2,1,0:T(8,128)(2,1)S(1)} %pad_maximum_fusion.first_ref), channel_id=1, source_target_pairs={{0,4},{1,5},{2,6},{3,7},{4,0},{5,1},{6,2},{7,3},{8,12},{9,13},{10,... | collective-permute-start | bytes 491528 | tf_op jit(solution)/shard_map/ppermute | solution.py:340
  48.4 9.9 %collective-permute-start.16 = (bf16[2,32,1280]{2,1,0:T(8,128)(2,1)S(1)}, bf16[2,32,1280]{2,1,0:T(8,128)(2,1)S(1)}, u32[]{:S(2)}, u32[]{:S(2)}) collective-permute-start(bf16[2,32,1280]{2,1,0:T(8,128)(2,1)S(1)} %pad_maximum_fusion.1.second_ref), channel_id=1, source_target_pairs={{0,2},{1,3},{2,0},{3,1},{4,6},{5,7},{6,4},{7,5},{8,10},{9,11},{10,... | collective-permute-start | bytes 491528 | tf_op jit(solution)/shard_map/ppermute | solution.py:340
  49.7 8.6 %collective-permute-start.15 = (bf16[2,32,1280]{2,1,0:T(8,128)(2,1)S(1)}, bf16[2,32,1280]{2,1,0:T(8,128)(2,1)S(1)}, u32[]{:S(2)}, u32[]{:S(2)}) collective-permute-start(bf16[2,32,1280]{2,1,0:T(8,128)(2,1)S(1)} %pad_maximum_fusion.first_ref), channel_id=1, source_target_pairs={{0,2},{1,3},{2,0},{3,1},{4,6},{5,7},{6,4},{7,5},{8,10},{9,11},{10,... | collective-permute-start | bytes 491528 | tf_op jit(solution)/shard_map/ppermute | solution.py:340
  52.7 9.4 %collective-permute-start.14 = (bf16[4,32,1280]{2,1,0:T(8,128)(2,1)S(1)}, bf16[4,32,1280]{2,1,0:T(8,128)(2,1)}, u32[]{:S(2)}, u32[]{:S(2)}) collective-permute-start(bf16[4,32,1280]{2,1,0:T(8,128)(2,1)S(1)} %join.4.rest_0_), channel_id=1, source_target_pairs={{0,1},{1,0},{2,3},{3,2},{4,5},{5,4},{6,7},{7,6},{8,9},{9,8},{10,11... | collective-permute-start | bytes 983048 | tf_op jit(solution)/shard_map/ppermute | solution.py:340
  54.9 7.3 %collective-permute-start.23 = (bf16[4,32,1280]{2,1,0:T(8,128)(2,1)S(1)}, bf16[4,32,1280]{2,1,0:T(8,128)(2,1)}, u32[]{:S(2)}, u32[]{:S(2)}) collective-permute-start(bf16[4,32,1280]{2,1,0:T(8,128)(2,1)S(1)} %join.7.rest_3_), channel_id=1, source_target_pairs={{0,1},{1,0},{2,3},{3,2},{4,5},{5,4},{6,7},{7,6},{8,9},{9,8},{10,11... | collective-permute-start | bytes 983048 | tf_op jit(solution)/shard_map/ppermute | solution.py:340
  58.3 3.9 %collective-permute-start.20 = (bf16[4,32,1280]{2,1,0:T(8,128)(2,1)}, bf16[4,32,1280]{2,1,0:T(8,128)(2,1)}, u32[]{:S(2)}, u32[]{:S(2)}) collective-permute-start(bf16[4,32,1280]{2,1,0:T(8,128)(2,1)} %join.6.rest_2_), channel_id=1, source_target_pairs={{0,1},{1,0},{2,3},{3,2},{4,5},{5,4},{6,7},{7,6},{8,9},{9,8},{10,11... | collective-permute-start | bytes 983048 | tf_op jit(solution)/shard_map/ppermute | solution.py:340
  59.1 3.2 %collective-permute-start.17 = (bf16[4,32,1280]{2,1,0:T(8,128)(2,1)}, bf16[4,32,1280]{2,1,0:T(8,128)(2,1)}, u32[]{:S(2)}, u32[]{:S(2)}) collective-permute-start(bf16[4,32,1280]{2,1,0:T(8,128)(2,1)} %join.5.rest_1_), channel_id=1, source_target_pairs={{0,1},{1,0},{2,3},{3,2},{4,5},{5,4},{6,7},{7,6},{8,9},{9,8},{10,11... | collective-permute-start | bytes 983048 | tf_op jit(solution)/shard_map/ppermute | solution.py:340
  (3 other events, 52.6 us)

commit v9 on v7

--- a/solution.py
+++ b/solution.py
@@ -184,55 +184,61 @@
     blocks, rest = rest[: len(steps)], rest[len(steps) :]
     if core:
         before_ref, table_ref, out_ref = rest[:3]
-        held_ref, panel_ref, receivers_ref, inverse_ref, stacked_ref, sem = rest[3:]
+        panel_ref, receivers_ref, inverse_ref, stacked_ref, sem = rest[3:]
         fetch = pltpu.make_async_copy(table_ref, inverse_ref, sem)
         fetch.start()
     else:
-        out_ref, held_ref, panel_ref, receivers_ref = rest
-    rows = held_ref.shape[1]
+        out_ref, panel_ref, receivers_ref = rest
+    far, rows, _ = blocks[0].shape
     members = devices // SHARES
     parts = members // segments
     ch_local = channels // devices
     ch_chip = 2 * ch_local
     place = place_ref[0]
-    parity = place % 2 ^ core
+    centre = place ^ core
+    parity = centre % 2
     ids = ids_ref[...]
     sources = ids.shape[0]
 
-    def position(device):
-        member = device % members
-        return (member // 2) * SHARES + device // members
-
-    for step, block in zip(steps, blocks):
-        far = block.shape[0]
-        for line in range(far):
-            device = place ^ ((line + far // 2) % far * 8 + step + core)
-            held_ref[position(device)] = block[line]
-
-    tails = held_ref[:, :, FLAG_TILE : FLAG_TILE + 128].reshape(held_ref.shape[0] * rows, 128)
+    distances = [(line + far // 2) % far * 8 + step for step in steps for line in range(far)]
+    places = [(index, line) for index in range(len(steps)) for line in range(far)]
+
+    heads = [
+        blocks[index][line, :16, FLAG_TILE : FLAG_TILE + 128] for index, line in places
+    ]
+    tails = jnp.concatenate(heads, axis=0)
+    distance = (ids // ch_chip * 2 + parity) ^ centre
+    slot = distance % 8 // 2 * far + (distance // 8 + far // 2) % far
     column = lax.broadcasted_iota(jnp.int32, (sources, tails.shape[0]), 1)
-    choice = (column == position(ids // ch_chip * 2 + parity) * rows).astype(jnp.bfloat16)
+    choice = (column == slot * 16).astype(jnp.bfloat16)
     tail = jnp.dot(choice, tails, preferred_element_type=jnp.float32)
     lane = lax.broadcasted_iota(jnp.int32, (sources, 128), 1)
 
-    channel = lax.broadcasted_iota(jnp.int32, (sources, channels), 1)
-    pick_sources = (channel == ids).astype(jnp.bfloat16)
-    line = lax.broadcasted_iota(jnp.int32, (16, channels), 0)
-    channel = lax.broadcasted_iota(jnp.int32, (16, channels), 1)
-    pick_own = ((channel == place * ch_local + line) & (line < ch_local)).astype(jnp.bfloat16)
-    pick = jnp.concatenate([pick_sources, pick_own], axis=0)
+    line = lax.broadcasted_iota(jnp.int32, (16, 1), 0)
+    own = jnp.where(line < ch_local, place * ch_local + line, -1)
+    wanted = jnp.concatenate([ids, own], axis=0)
+    column = lax.broadcasted_iota(jnp.int32, (1, channels), 1)
 
     counts = [jnp.zeros((sources, 1), jnp.float32) for _ in range(ch_local)]
-    per_segment = channels // rows
+    numbers = []
     for g in range(segments // 2):
-        segment = held_ref[g * per_segment : (g + 1) * per_segment].reshape(channels, WIDTH)
+        chosen = [n for n, d in enumerate(distances) if d % members // 2 // parts == g]
+        channel = column % rows
+        for order, n in enumerate(chosen):
+            device = centre ^ distances[n]
+            base = device % members // 2 % parts * (SHARES * rows) + device // members * rows
+            channel = jnp.where(column // rows == order, channel + base, channel)
+        pick = (channel == wanted).astype(jnp.bfloat16)
+        segment = jnp.concatenate([blocks[places[n][0]][places[n][1]] for n in chosen], axis=0)
         picked = jnp.dot(pick, segment, preferred_element_type=jnp.float32)
-        mine = lane == FLAG_LANE + g * ch_chip + ids % ch_chip
+        number = (centre ^ distances[chosen[0]]) % members // 2 // parts
+        numbers.append(2 * number + parity)
+        mine = lane == FLAG_LANE + number * ch_chip + ids % ch_chip
         weight = jnp.sum(jnp.where(mine, tail, 0.0), axis=1, keepdims=True)
         panel_ref[g] = picked[:sources] * weight
         receivers_ref[g] = picked[sources:]
         for c in range(ch_local):
-            counts[c] += weight * flags_ref[2 * g + parity, c]
+            counts[c] += weight * flags_ref[numbers[g], c]
 
     shares = [None] * ch_local
     for start in [FLAG_TILE] + [start for start in range(0, PART, 128) if start != FLAG_TILE]:
@@ -242,7 +248,7 @@
             real_sum = jnp.zeros((sources, 128), jnp.float32)
             imag_sum = jnp.zeros((sources, 128), jnp.float32)
             for g in range(segments // 2):
-                flag = flags_ref[2 * g + parity, c]
+                flag = flags_ref[numbers[g], c]
                 rec_real = receivers_ref[g, c : c + 1, re] * flag
                 rec_imag = receivers_ref[g, c : c + 1, im] * flag
                 src_real, src_imag = panel_ref[g, :, re], panel_ref[g, :, im]
@@ -277,14 +283,12 @@
 
 def correlate(core, place, weights, ids, steps, blocks, shape, before=None, table=None):
     segments, channels, devices = shape
-    rows = blocks[0].shape[1]
     ch_local = channels // devices
     sources = ids.shape[0]
     smem = pl.BlockSpec(memory_space=pltpu.SMEM)
     vmem = pl.BlockSpec(memory_space=pltpu.VMEM)
     in_specs = [smem, smem, vmem] + [vmem] * len(blocks)
     scratch = [
-        pltpu.VMEM((devices // 2, rows, WIDTH), jnp.bfloat16),
         pltpu.VMEM((segments // 2, sources, WIDTH), jnp.float32),
         pltpu.VMEM((segments // 2, 16, WIDTH), jnp.float32),
     ]

time: 67.2 us -> 67 us (level)
  no operation moved by 1% of the time
where the time goes in v9:
time: 67 us; the launch traced here: 66.8 us
  starting transfers between devices  30.3 us (45%)
  Pallas kernels  17.3 us (26%)
  waiting for transfers between devices  14.3 us (21%)
  local copies, waits for them, and re-layouts  4.36 us (7%)
    ppermute x24, starting transfers between devices, exchange(): return lax.ppermute(block, 'chan', [(i, i ^ bits) for i in range(devices)])  30.3 us
    ppermute x24, waiting for transfers between devices, exchange(): return lax.ppermute(block, 'chan', [(i, i ^ bits) for i in range(devices)])  14.3 us
    pallas_call x3, Pallas kernels, transform(): pl.pallas_call(functools.partial(transform_kernel, steps, first, started)...  10 us
    pallas_call x2, Pallas kernels, correlate(): pl.pallas_call(functools.partial(correlate_kernel, shape, core, steps), i...  7.16 us
    unnamed x10, local copies, waits for them, and re-layouts  1.45 us
    concatenate x3, local copies, waits for them, and re-layouts, per_device(): jnp.concatenate([exchange(half, step) if step else half for half in halves])  1.36 us
  transfers between devices with their start and end apart: 24, of which 9 were waited for; matrix products, arithmetic and copies ran while one was open for 5% of the time, Pallas kernels for 14%

profile of v9, /device:TPU:0, one launch (start us, length us, event | category | flops | bytes accessed | tf_op | source)
XLA Modules:
  0.0 66.8 jit_solution(8547440624901413382)
XLA Ops:
  0.0 1.3 %constant_dynamic-slice_fusion.20 = (bf16[4,1,128,512]{3,2,1,0:T(8,128)(2,1)S(1)}, bf16[4,1,128,512]{3,2,1,0:T(8,128)(2,1)S(1)}) fusion(bf16[4,2,128,512]{3,2,1,0:T(8,128)(2,1)} %bitcast.19, s32[]{:T(128)S(6)} %select_n.69, s32[]{:T(128)S(6)} %select_n.73), kind=kLoop, calls=%fused_computation.37 | loop fusion | bytes 2097160 | tf_op jit(solution)/shard_map/jit(dynamic_index_in_dim)/dynamic_slice | solution.py:343
  1.9 1.5 %collective-permute-done.1 = bf16[8,64,512]{2,1,0:T(8,128)(2,1)S(1)} collective-permute-done((bf16[8,64,512]{2,1,0:T(8,128)(2,1)S(1)}, bf16[8,64,512]{2,1,0:T(8,128)(2,1)S(1)}, u32[]{:S(2)}, u32[]{:S(2)}) %collective-permute-start.1) | collective-permute-done | bytes 524320 | tf_op jit(solution)/shard_map/ppermute | solution.py:328
  3.4 4.0 %collective-permute-start.8 = (bf16[2,64,512]{2,1,0:T(8,128)(2,1)S(1)}, bf16[2,64,512]{2,1,0:T(8,128)(2,1)S(1)}, u32[]{:S(2)}, u32[]{:S(2)}) collective-permute-start(bf16[2,64,512]{2,1,0:T(8,128)(2,1)S(1)} %pad_maximum_fusion.10), channel_id=1, source_target_pairs={{0,12},{1,13},{2,14},{3,15},{4,8},{5,9},{6,10},{7,11},{8,4},{9,5},... | collective-permute-start | bytes 393224 | tf_op jit(solution)/shard_map/ppermute | solution.py:328
  7.4 1.6 %collective-permute-start.7 = (bf16[2,64,512]{2,1,0:T(8,128)(2,1)S(1)}, bf16[2,64,512]{2,1,0:T(8,128)(2,1)S(1)}, u32[]{:S(2)}, u32[]{:S(2)}) collective-permute-start(bf16[2,64,512]{2,1,0:T(8,128)(2,1)S(1)} %pad_maximum_fusion.9), channel_id=1, source_target_pairs={{0,2},{1,3},{2,0},{3,1},{4,6},{5,7},{6,4},{7,5},{8,10},{9,11},{10,... | collective-permute-start | bytes 393224 | tf_op jit(solution)/shard_map/ppermute | solution.py:328
  9.1 2.0 %collective-permute-start.5 = (bf16[2,64,512]{2,1,0:T(8,128)(2,1)S(1)}, bf16[2,64,512]{2,1,0:T(8,128)(2,1)S(1)}, u32[]{:S(2)}, u32[]{:S(2)}) collective-permute-start(bf16[2,64,512]{2,1,0:T(8,128)(2,1)S(1)} %pad_maximum_fusion.6), channel_id=1, source_target_pairs={{0,8},{1,9},{2,10},{3,11},{4,12},{5,13},{6,14},{7,15},{8,0},{9,1},... | collective-permute-start | bytes 393224 | tf_op jit(solution)/shard_map/ppermute | solution.py:328
  11.1 2.5 %collective-permute-start.4 = (bf16[2,64,512]{2,1,0:T(8,128)(2,1)S(1)}, bf16[2,64,512]{2,1,0:T(8,128)(2,1)S(1)}, u32[]{:S(2)}, u32[]{:S(2)}) collective-permute-start(bf16[2,64,512]{2,1,0:T(8,128)(2,1)S(1)} %pad_maximum_fusion.5), channel_id=1, source_target_pairs={{0,6},{1,7},{2,4},{3,5},{4,2},{5,3},{6,0},{7,1},{8,14},{9,15},{10,... | collective-permute-start | bytes 393224 | tf_op jit(solution)/shard_map/ppermute | solution.py:328
  14.1 1.5 %collective-permute-done.7.rest_2_ = bf16[2,64,512]{2,1,0:T(8,128)(2,1)S(1)} collective-permute-done((bf16[2,64,512]{2,1,0:T(8,128)(2,1)S(1)}, bf16[2,64,512]{2,1,0:T(8,128)(2,1)S(1)}, u32[]{:S(2)}, u32[]{:S(2)}) %collective-permute-start.7) | collective-permute-done | bytes 131104 | tf_op jit(solution)/shard_map/ppermute | solution.py:328
  16.2 1.2 %collective-permute-done.6.rest_1_ = bf16[2,64,512]{2,1,0:T(8,128)(2,1)S(1)} collective-permute-done((bf16[2,64,512]{2,1,0:T(8,128)(2,1)S(1)}, bf16[2,64,512]{2,1,0:T(8,128)(2,1)S(1)}, u32[]{:S(2)}, u32[]{:S(2)}) %collective-permute-start.6) | collective-permute-done | bytes 131104 | tf_op jit(solution)/shard_map/ppermute | solution.py:328
  17.3 4.4 %transform.3.rest_4_ = f32[64,1280]{1,0:T(8,128)S(1)} custom-call(s32[1]{0:T(128)} %bitcast.place_ref, bf16[163840,128]{1,0:T(8,128)(2,1)} %constant.100.clone.table_ref, bf16[2,64,512]{2,1,0:T(8,128)(2,1)S(1)} %pad_maximum_fusion.7.rest_0_, bf16[2,64,512]{2,1,0:T(8,128)(2,1)S(1)} %collective-permute-done.6.rest_1_, ...), custom_call_target="tpu_custom_call" | custom-call | flops 671088640 | bytes 10485760 | tf_op jit(solution)/shard_map/transform/pallas_call | solution.py:121
  21.8 3.1 %transform.4 = (f32[32,768]{1,0:T(8,128)S(1)}, f32[32,768]{1,0:T(8,128)S(1)}) custom-call(s32[1]{0:T(128)} %bitcast.place_ref, bf16[163840,128]{1,0:T(8,128)(2,1)} %constant.100.clone.table_ref, bf16[2,64,512]{2,1,0:T(8,128)(2,1)S(1)} %collective-permute-done.2.rest_0_, bf16[2,64,512]{2,1,0:T(8,128)(2,1)S(1)} %collective-permute-done.3.rest_1_, ...), custom_call_target="tpu_custom_call" | custom-call | flops 402653184 | bytes 6291456 | tf_op jit(solution)/shard_map/transform/pallas_call | solution.py:121
  25.0 2.7 %collective-permute-start.9 = (f32[32,768]{1,0:T(8,128)S(1)}, f32[32,768]{1,0:T(8,128)S(1)}, u32[]{:S(2)}, u32[]{:S(2)}) collective-permute-start(f32[32,768]{1,0:T(8,128)S(1)} %get-tuple-element.10), channel_id=1, source_target_pairs={{0,16},{1,17},{2,18},{3,19},{4,20},{5,21},{6,22},{7,23},{8,24},{9,... | collective-permute-start | bytes 294920 | tf_op jit(solution)/shard_map/ppermute | solution.py:328
  27.6 2.4 %transform.5 = (f32[32,512]{1,0:T(8,128)S(1)}, f32[32,512]{1,0:T(8,128)S(1)}) custom-call(s32[1]{0:T(128)} %bitcast.place_ref, bf16[163840,128]{1,0:T(8,128)(2,1)} %constant.100.clone.table_ref, bf16[2,64,512]{2,1,0:T(8,128)(2,1)S(1)} %collective-permute-done.2.rest_0_, bf16[2,64,512]{2,1,0:T(8,128)(2,1)S(1)} %collective-permute-done.3.rest_1_, ...), custom_call_target="tpu_custom_call" | custom-call | flops 268435456 | bytes 4194304 | tf_op jit(solution)/shard_map/transform/pallas_call | solution.py:121
  30.6 1.2 %collective-permute-done = f32[8,4]{1,0:T(8,128)S(1)} collective-permute-done((f32[8,4]{1,0:T(8,128)S(1)}, f32[8,4]{1,0:T(8,128)S(1)}, u32[]{:S(2)}, u32[]{:S(2)}) %collective-permute-start) | collective-permute-done | bytes 160 | tf_op jit(solution)/shard_map/ppermute | solution.py:328
  31.9 4.2 %collective-permute-done.10.rest_3_ = f32[32,512]{1,0:T(8,128)S(1)} collective-permute-done((f32[32,512]{1,0:T(8,128)S(1)}, f32[32,512]{1,0:T(8,128)S(1)}, u32[]{:S(2)}, u32[]{:S(2)}) %collective-permute-start.10) | collective-permute-done | bytes 65568 | tf_op jit(solution)/shard_map/ppermute | solution.py:328
  36.3 2.0 %collective-permute-start.11 = (bf16[32,1280]{1,0:T(8,128)(2,1)S(1)}, bf16[32,1280]{1,0:T(8,128)(2,1)S(1)}, u32[]{:S(2)}, u32[]{:S(2)}) collective-permute-start(bf16[32,1280]{1,0:T(8,128)(2,1)S(1)} %whiten.1), channel_id=1, source_target_pairs={{0,16},{1,17},{2,18},{3,19},{4,20},{5,21},{6,22},{7,23},{8,24},{9,... | collective-permute-start | bytes 245768 | tf_op jit(solution)/shard_map/ppermute | solution.py:328
  38.3 2.3 %collective-permute-start.12 = (bf16[32,1280]{1,0:T(8,128)(2,1)S(1)}, bf16[32,1280]{1,0:T(8,128)(2,1)S(1)}, u32[]{:S(2)}, u32[]{:S(2)}) collective-permute-start(bf16[32,1280]{1,0:T(8,128)(2,1)S(1)} %whiten.1), channel_id=1, source_target_pairs={{0,24},{1,25},{2,26},{3,27},{4,28},{5,29},{6,30},{7,31},{8,16},{9,... | collective-permute-start | bytes 245768 | tf_op jit(solution)/shard_map/ppermute | solution.py:328
  40.7 2.1 %collective-permute-start.22 = (bf16[2,32,1280]{2,1,0:T(8,128)(2,1)S(1)}, bf16[2,32,1280]{2,1,0:T(8,128)(2,1)S(1)}, u32[]{:S(2)}, u32[]{:S(2)}) collective-permute-start(bf16[2,32,1280]{2,1,0:T(8,128)(2,1)S(1)} %pad_maximum_fusion.2), channel_id=1, source_target_pairs={{0,6},{1,7},{2,4},{3,5},{4,2},{5,3},{6,0},{7,1},{8,14},{9,15},{10,... | collective-permute-start | bytes 491528 | tf_op jit(solution)/shard_map/ppermute | solution.py:328
  42.8 2.6 %collective-permute-start.19 = (bf16[2,32,1280]{2,1,0:T(8,128)(2,1)S(1)}, bf16[2,32,1280]{2,1,0:T(8,128)(2,1)S(1)}, u32[]{:S(2)}, u32[]{:S(2)}) collective-permute-start(bf16[2,32,1280]{2,1,0:T(8,128)(2,1)S(1)} %pad_maximum_fusion.2), channel_id=1, source_target_pairs={{0,4},{1,5},{2,6},{3,7},{4,0},{5,1},{6,2},{7,3},{8,12},{9,13},{10,... | collective-permute-start | bytes 491528 | tf_op jit(solution)/shard_map/ppermute | solution.py:328
  45.5 0.9 %collective-permute-start.21 = (bf16[2,32,1280]{2,1,0:T(8,128)(2,1)S(1)}, bf16[2,32,1280]{2,1,0:T(8,128)(2,1)S(1)}, u32[]{:S(2)}, u32[]{:S(2)}) collective-permute-start(bf16[2,32,1280]{2,1,0:T(8,128)(2,1)S(1)} %pad_maximum_fusion.1), channel_id=1, source_target_pairs={{0,6},{1,7},{2,4},{3,5},{4,2},{5,3},{6,0},{7,1},{8,14},{9,15},{10,... | collective-permute-start | bytes 491528 | tf_op jit(solution)/shard_map/ppermute | solution.py:328
  47.1 2.0 %collective-permute-start.16 = (bf16[2,32,1280]{2,1,0:T(8,128)(2,1)S(1)}, bf16[2,32,1280]{2,1,0:T(8,128)(2,1)S(1)}, u32[]{:S(2)}, u32[]{:S(2)}) collective-permute-start(bf16[2,32,1280]{2,1,0:T(8,128)(2,1)S(1)} %pad_maximum_fusion.2), channel_id=1, source_target_pairs={{0,2},{1,3},{2,0},{3,1},{4,6},{5,7},{6,4},{7,5},{8,10},{9,11},{10,... | collective-permute-start | bytes 491528 | tf_op jit(solution)/shard_map/ppermute | solution.py:328
  49.1 3.3 %collective-permute-done.21 = bf16[2,32,1280]{2,1,0:T(8,128)(2,1)S(1)} collective-permute-done((bf16[2,32,1280]{2,1,0:T(8,128)(2,1)S(1)}, bf16[2,32,1280]{2,1,0:T(8,128)(2,1)S(1)}, u32[]{:S(2)}, u32[]{:S(2)}) %collective-permute-start.21) | collective-permute-done | bytes 163872 | tf_op jit(solution)/shard_map/ppermute | solution.py:328
  52.4 2.4 %collective-permute-start.15 = (bf16[2,32,1280]{2,1,0:T(8,128)(2,1)S(1)}, bf16[2,32,1280]{2,1,0:T(8,128)(2,1)S(1)}, u32[]{:S(2)}, u32[]{:S(2)}) collective-permute-start(bf16[2,32,1280]{2,1,0:T(8,128)(2,1)S(1)} %pad_maximum_fusion.1), channel_id=1, source_target_pairs={{0,2},{1,3},{2,0},{3,1},{4,6},{5,7},{6,4},{7,5},{8,10},{9,11},{10,... | collective-permute-start | bytes 491528 | tf_op jit(solution)/shard_map/ppermute | solution.py:328
  59.6 2.4 %correlate.2.rest_4_ = f32[4,64,1280]{2,1,0:T(8,128)S(1)} custom-call(s32[1]{0:T(128)} %bitcast.place_ref, f32[8,4]{1,0:T(8,128)S(1)} %convert_element_type.3.flags_ref, s32[64,1]{1,0:T(8,128)S(1)} %copy.10.ids_ref, bf16[4,32,1280]{2,1,0:T(8,128)(2,1)S(1)} %pad_maximum_fusion.rest_0_, bf16[4,32,1280]{2,1,0:T(8,128)(2,1)} %constant_dynamic-update-slice_fusion.rest_1_, ...), custom_call_target="tpu_custom_call" | custom-call | flops 83886080 | bytes 1310720 | tf_op jit(solution)/shard_map/correlate/pallas_call | solution.py:303
  62.1 4.7 %correlate.3 = f32[64,4,1001]{2,1,0:T(4,128)} custom-call(s32[1]{0:T(128)} %bitcast.place_ref, f32[8,4]{1,0:T(8,128)S(1)} %convert_element_type.3.flags_ref, s32[64,1]{1,0:T(8,128)S(1)} %copy.10.ids_ref, bf16[4,32,1280]{2,1,0:T(8,128)(2,1)} %collective-permute-done.14.rest_0_, bf16[4,32,1280]{2,1,0:T(8,128)(2,1)} %collective-permute-done.17.rest_1_, ...), custom_call_target="tpu_custom_call" | custom-call | flops 83886080 | bytes 1310720 | tf_op jit(solution)/shard_map/correlate/pallas_call | solution.py:303
  (61 shorter events, 8.2 us)
Async XLA Ops:
  1.3 2.1 %collective-permute-start.1 = (bf16[8,64,512]{2,1,0:T(8,128)(2,1)S(1)}, bf16[8,64,512]{2,1,0:T(8,128)(2,1)S(1)}, u32[]{:S(2)}, u32[]{:S(2)}) collective-permute-start(bf16[8,64,512]{2,1,0:T(8,128)(2,1)S(1)} %bitcast.20), channel_id=1, source_target_pairs={{0,1},{1,0},{2,3},{3,2},{4,5},{5,4},{6,7},{7,6},{8,9},{9,8},{10,11... | collective-permute-start | bytes 1572872 | tf_op jit(solution)/shard_map/ppermute | solution.py:328
  3.4 10.2 %collective-permute-start.8 = (bf16[2,64,512]{2,1,0:T(8,128)(2,1)S(1)}, bf16[2,64,512]{2,1,0:T(8,128)(2,1)S(1)}, u32[]{:S(2)}, u32[]{:S(2)}) collective-permute-start(bf16[2,64,512]{2,1,0:T(8,128)(2,1)S(1)} %pad_maximum_fusion.10), channel_id=1, source_target_pairs={{0,12},{1,13},{2,14},{3,15},{4,8},{5,9},{6,10},{7,11},{8,4},{9,5},... | collective-permute-start | bytes 393224 | tf_op jit(solution)/shard_map/ppermute | solution.py:328
  7.4 8.2 %collective-permute-start.7 = (bf16[2,64,512]{2,1,0:T(8,128)(2,1)S(1)}, bf16[2,64,512]{2,1,0:T(8,128)(2,1)S(1)}, u32[]{:S(2)}, u32[]{:S(2)}) collective-permute-start(bf16[2,64,512]{2,1,0:T(8,128)(2,1)S(1)} %pad_maximum_fusion.9), channel_id=1, source_target_pairs={{0,2},{1,3},{2,0},{3,1},{4,6},{5,7},{6,4},{7,5},{8,10},{9,11},{10,... | collective-permute-start | bytes 393224 | tf_op jit(solution)/shard_map/ppermute | solution.py:328
  9.0 8.3 %collective-permute-start.6 = (bf16[2,64,512]{2,1,0:T(8,128)(2,1)S(1)}, bf16[2,64,512]{2,1,0:T(8,128)(2,1)S(1)}, u32[]{:S(2)}, u32[]{:S(2)}) collective-permute-start(bf16[2,64,512]{2,1,0:T(8,128)(2,1)S(1)} %pad_maximum_fusion.8), channel_id=1, source_target_pairs={{0,14},{1,15},{2,12},{3,13},{4,10},{5,11},{6,8},{7,9},{8,6},{9,7},... | collective-permute-start | bytes 393224 | tf_op jit(solution)/shard_map/ppermute | solution.py:328
  9.1 12.7 %collective-permute-start.5 = (bf16[2,64,512]{2,1,0:T(8,128)(2,1)S(1)}, bf16[2,64,512]{2,1,0:T(8,128)(2,1)S(1)}, u32[]{:S(2)}, u32[]{:S(2)}) collective-permute-start(bf16[2,64,512]{2,1,0:T(8,128)(2,1)S(1)} %pad_maximum_fusion.6), channel_id=1, source_target_pairs={{0,8},{1,9},{2,10},{3,11},{4,12},{5,13},{6,14},{7,15},{8,0},{9,1},... | collective-permute-start | bytes 393224 | tf_op jit(solution)/shard_map/ppermute | solution.py:328
  11.1 10.7 %collective-permute-start.4 = (bf16[2,64,512]{2,1,0:T(8,128)(2,1)S(1)}, bf16[2,64,512]{2,1,0:T(8,128)(2,1)S(1)}, u32[]{:S(2)}, u32[]{:S(2)}) collective-permute-start(bf16[2,64,512]{2,1,0:T(8,128)(2,1)S(1)} %pad_maximum_fusion.5), channel_id=1, source_target_pairs={{0,6},{1,7},{2,4},{3,5},{4,2},{5,3},{6,0},{7,1},{8,14},{9,15},{10,... | collective-permute-start | bytes 393224 | tf_op jit(solution)/shard_map/ppermute | solution.py:328
  13.7 8.1 %collective-permute-start.3 = (bf16[2,64,512]{2,1,0:T(8,128)(2,1)S(1)}, bf16[2,64,512]{2,1,0:T(8,128)(2,1)S(1)}, u32[]{:S(2)}, u32[]{:S(2)}) collective-permute-start(bf16[2,64,512]{2,1,0:T(8,128)(2,1)S(1)} %pad_maximum_fusion.4), channel_id=1, source_target_pairs={{0,10},{1,11},{2,8},{3,9},{4,14},{5,15},{6,12},{7,13},{8,2},{9,3},... | collective-permute-start | bytes 393224 | tf_op jit(solution)/shard_map/ppermute | solution.py:328
  15.7 6.1 %collective-permute-start.2 = (bf16[2,64,512]{2,1,0:T(8,128)(2,1)S(1)}, bf16[2,64,512]{2,1,0:T(8,128)(2,1)S(1)}, u32[]{:S(2)}, u32[]{:S(2)}) collective-permute-start(bf16[2,64,512]{2,1,0:T(8,128)(2,1)S(1)} %pad_maximum_fusion.3), channel_id=1, source_target_pairs={{0,4},{1,5},{2,6},{3,7},{4,0},{5,1},{6,2},{7,3},{8,12},{9,13},{10,... | collective-permute-start | bytes 393224 | tf_op jit(solution)/shard_map/ppermute | solution.py:328
  25.0 11.1 %collective-permute-start.9 = (f32[32,768]{1,0:T(8,128)S(1)}, f32[32,768]{1,0:T(8,128)S(1)}, u32[]{:S(2)}, u32[]{:S(2)}) collective-permute-start(f32[32,768]{1,0:T(8,128)S(1)} %get-tuple-element.10), channel_id=1, source_target_pairs={{0,16},{1,17},{2,18},{3,19},{4,20},{5,21},{6,22},{7,23},{8,24},{9,... | collective-permute-start | bytes 294920 | tf_op jit(solution)/shard_map/ppermute | solution.py:328
  30.1 6.0 %collective-permute-start.10 = (f32[32,512]{1,0:T(8,128)S(1)}, f32[32,512]{1,0:T(8,128)S(1)}, u32[]{:S(2)}, u32[]{:S(2)}) collective-permute-start(f32[32,512]{1,0:T(8,128)S(1)} %get-tuple-element.12), channel_id=1, source_target_pairs={{0,16},{1,17},{2,18},{3,19},{4,20},{5,21},{6,22},{7,23},{8,24},{9,... | collective-permute-start | bytes 196616 | tf_op jit(solution)/shard_map/ppermute | solution.py:328
  30.6 1.2 %collective-permute-start = (f32[8,4]{1,0:T(8,128)S(1)}, f32[8,4]{1,0:T(8,128)S(1)}, u32[]{:S(2)}, u32[]{:S(2)}) collective-permute-start(f32[8,4]{1,0:T(8,128)S(1)} %convert_element_type.3.flags_ref), channel_id=1, source_target_pairs={{0,1},{1,0},{2,3},{3,2},{4,5},{5,4},{6,7},{7,6},{8,9},{9,8},{10,11... | collective-permute-start | bytes 392 | tf_op jit(solution)/shard_map/ppermute | solution.py:328
  36.2 4.5 %collective-permute-start.13 = (bf16[32,1280]{1,0:T(8,128)(2,1)S(1)}, bf16[32,1280]{1,0:T(8,128)(2,1)S(1)}, u32[]{:S(2)}, u32[]{:S(2)}) collective-permute-start(bf16[32,1280]{1,0:T(8,128)(2,1)S(1)} %whiten.1), channel_id=1, source_target_pairs={{0,8},{1,9},{2,10},{3,11},{4,12},{5,13},{6,14},{7,15},{8,0},{9,1},... | collective-permute-start | bytes 245768 | tf_op jit(solution)/shard_map/ppermute | solution.py:328
  36.3 9.2 %collective-permute-start.11 = (bf16[32,1280]{1,0:T(8,128)(2,1)S(1)}, bf16[32,1280]{1,0:T(8,128)(2,1)S(1)}, u32[]{:S(2)}, u32[]{:S(2)}) collective-permute-start(bf16[32,1280]{1,0:T(8,128)(2,1)S(1)} %whiten.1), channel_id=1, source_target_pairs={{0,16},{1,17},{2,18},{3,19},{4,20},{5,21},{6,22},{7,23},{8,24},{9,... | collective-permute-start | bytes 245768 | tf_op jit(solution)/shard_map/ppermute | solution.py:328
  38.3 7.1 %collective-permute-start.12 = (bf16[32,1280]{1,0:T(8,128)(2,1)S(1)}, bf16[32,1280]{1,0:T(8,128)(2,1)S(1)}, u32[]{:S(2)}, u32[]{:S(2)}) collective-permute-start(bf16[32,1280]{1,0:T(8,128)(2,1)S(1)} %whiten.1), channel_id=1, source_target_pairs={{0,24},{1,25},{2,26},{3,27},{4,28},{5,29},{6,30},{7,31},{8,16},{9,... | collective-permute-start | bytes 245768 | tf_op jit(solution)/shard_map/ppermute | solution.py:328
  40.7 14.1 %collective-permute-start.22 = (bf16[2,32,1280]{2,1,0:T(8,128)(2,1)S(1)}, bf16[2,32,1280]{2,1,0:T(8,128)(2,1)S(1)}, u32[]{:S(2)}, u32[]{:S(2)}) collective-permute-start(bf16[2,32,1280]{2,1,0:T(8,128)(2,1)S(1)} %pad_maximum_fusion.2), channel_id=1, source_target_pairs={{0,6},{1,7},{2,4},{3,5},{4,2},{5,3},{6,0},{7,1},{8,14},{9,15},{10,... | collective-permute-start | bytes 491528 | tf_op jit(solution)/shard_map/ppermute | solution.py:328
  42.8 13.6 %collective-permute-start.19 = (bf16[2,32,1280]{2,1,0:T(8,128)(2,1)S(1)}, bf16[2,32,1280]{2,1,0:T(8,128)(2,1)S(1)}, u32[]{:S(2)}, u32[]{:S(2)}) collective-permute-start(bf16[2,32,1280]{2,1,0:T(8,128)(2,1)S(1)} %pad_maximum_fusion.2), channel_id=1, source_target_pairs={{0,4},{1,5},{2,6},{3,7},{4,0},{5,1},{6,2},{7,3},{8,12},{9,13},{10,... | collective-permute-start | bytes 491528 | tf_op jit(solution)/shard_map/ppermute | solution.py:328
  45.5 7.0 %collective-permute-start.21 = (bf16[2,32,1280]{2,1,0:T(8,128)(2,1)S(1)}, bf16[2,32,1280]{2,1,0:T(8,128)(2,1)S(1)}, u32[]{:S(2)}, u32[]{:S(2)}) collective-permute-start(bf16[2,32,1280]{2,1,0:T(8,128)(2,1)S(1)} %pad_maximum_fusion.1), channel_id=1, source_target_pairs={{0,6},{1,7},{2,4},{3,5},{4,2},{5,3},{6,0},{7,1},{8,14},{9,15},{10,... | collective-permute-start | bytes 491528 | tf_op jit(solution)/shard_map/ppermute | solution.py:328
  46.4 9.4 %collective-permute-start.18 = (bf16[2,32,1280]{2,1,0:T(8,128)(2,1)S(1)}, bf16[2,32,1280]{2,1,0:T(8,128)(2,1)S(1)}, u32[]{:S(2)}, u32[]{:S(2)}) collective-permute-start(bf16[2,32,1280]{2,1,0:T(8,128)(2,1)S(1)} %pad_maximum_fusion.1), channel_id=1, source_target_pairs={{0,4},{1,5},{2,6},{3,7},{4,0},{5,1},{6,2},{7,3},{8,12},{9,13},{10,... | collective-permute-start | bytes 491528 | tf_op jit(solution)/shard_map/ppermute | solution.py:328
  47.1 11.7 %collective-permute-start.16 = (bf16[2,32,1280]{2,1,0:T(8,128)(2,1)S(1)}, bf16[2,32,1280]{2,1,0:T(8,128)(2,1)S(1)}, u32[]{:S(2)}, u32[]{:S(2)}) collective-permute-start(bf16[2,32,1280]{2,1,0:T(8,128)(2,1)S(1)} %pad_maximum_fusion.2), channel_id=1, source_target_pairs={{0,2},{1,3},{2,0},{3,1},{4,6},{5,7},{6,4},{7,5},{8,10},{9,11},{10,... | collective-permute-start | bytes 491528 | tf_op jit(solution)/shard_map/ppermute | solution.py:328
  52.4 5.7 %collective-permute-start.15 = (bf16[2,32,1280]{2,1,0:T(8,128)(2,1)S(1)}, bf16[2,32,1280]{2,1,0:T(8,128)(2,1)S(1)}, u32[]{:S(2)}, u32[]{:S(2)}) collective-permute-start(bf16[2,32,1280]{2,1,0:T(8,128)(2,1)S(1)} %pad_maximum_fusion.1), channel_id=1, source_target_pairs={{0,2},{1,3},{2,0},{3,1},{4,6},{5,7},{6,4},{7,5},{8,10},{9,11},{10,... | collective-permute-start | bytes 491528 | tf_op jit(solution)/shard_map/ppermute | solution.py:328
  54.8 7.2 %collective-permute-start.14 = (bf16[4,32,1280]{2,1,0:T(8,128)(2,1)S(1)}, bf16[4,32,1280]{2,1,0:T(8,128)(2,1)}, u32[]{:S(2)}, u32[]{:S(2)}) collective-permute-start(bf16[4,32,1280]{2,1,0:T(8,128)(2,1)S(1)} %pad_maximum_fusion.rest_0_), channel_id=1, source_target_pairs={{0,1},{1,0},{2,3},{3,2},{4,5},{5,4},{6,7},{7,6},{8,9},{9,8},{10,11... | collective-permute-start | bytes 983048 | tf_op jit(solution)/shard_map/ppermute | solution.py:328
  55.8 6.2 %collective-permute-start.23 = (bf16[4,32,1280]{2,1,0:T(8,128)(2,1)S(1)}, bf16[4,32,1280]{2,1,0:T(8,128)(2,1)}, u32[]{:S(2)}, u32[]{:S(2)}) collective-permute-start(bf16[4,32,1280]{2,1,0:T(8,128)(2,1)S(1)} %constant_dynamic-update-slice_fusion.4.rest_3_), channel_id=1, source_target_pairs={{0,1},{1,0},{2,3},{3,2},{4,5},{5,4},{6,7},{7,6},{8,9},{9,8},{10,11... | collective-permute-start | bytes 983048 | tf_op jit(solution)/shard_map/ppermute | solution.py:328
  57.1 4.9 %collective-permute-start.20 = (bf16[4,32,1280]{2,1,0:T(8,128)(2,1)}, bf16[4,32,1280]{2,1,0:T(8,128)(2,1)}, u32[]{:S(2)}, u32[]{:S(2)}) collective-permute-start(bf16[4,32,1280]{2,1,0:T(8,128)(2,1)} %constant_dynamic-update-slice_fusion.2.rest_2_), channel_id=1, source_target_pairs={{0,1},{1,0},{2,3},{3,2},{4,5},{5,4},{6,7},{7,6},{8,9},{9,8},{10,11... | collective-permute-start | bytes 983048 | tf_op jit(solution)/shard_map/ppermute | solution.py:328
  59.5 2.6 %collective-permute-start.17 = (bf16[4,32,1280]{2,1,0:T(8,128)(2,1)}, bf16[4,32,1280]{2,1,0:T(8,128)(2,1)}, u32[]{:S(2)}, u32[]{:S(2)}) collective-permute-start(bf16[4,32,1280]{2,1,0:T(8,128)(2,1)} %constant_dynamic-update-slice_fusion.rest_1_), channel_id=1, source_target_pairs={{0,1},{1,0},{2,3},{3,2},{4,5},{5,4},{6,7},{7,6},{8,9},{9,8},{10,11... | collective-permute-start | bytes 983048 | tf_op jit(solution)/shard_map/ppermute | solution.py:328
  (3 other events, 51.5 us)

commit v10 on v9

--- a/solution.py
+++ b/solution.py
@@ -179,9 +179,9 @@
     )(flags, *parts)
 
 
-def correlate_kernel(shape, core, steps, place_ref, flags_ref, ids_ref, *rest):
+def correlate_kernel(shape, core, layout, place_ref, flags_ref, ids_ref, *rest):
     segments, channels, devices = shape
-    blocks, rest = rest[: len(steps)], rest[len(steps) :]
+    blocks, rest = rest[: len(layout)], rest[len(layout) :]
     if core:
         before_ref, table_ref, out_ref = rest[:3]
         panel_ref, receivers_ref, inverse_ref, stacked_ref, sem = rest[3:]
@@ -189,7 +189,7 @@
         fetch.start()
     else:
         out_ref, panel_ref, receivers_ref = rest
-    far, rows, _ = blocks[0].shape
+    rows = blocks[0].shape[1]
     members = devices // SHARES
     parts = members // segments
     ch_local = channels // devices
@@ -200,15 +200,17 @@
     ids = ids_ref[...]
     sources = ids.shape[0]
 
-    distances = [(line + far // 2) % far * 8 + step for step in steps for line in range(far)]
-    places = [(index, line) for index in range(len(steps)) for line in range(far)]
+    distances = [distance for ways in layout for distance in ways]
+    places = [(index, line) for index, ways in enumerate(layout) for line in range(len(ways))]
 
     heads = [
         blocks[index][line, :16, FLAG_TILE : FLAG_TILE + 128] for index, line in places
     ]
     tails = jnp.concatenate(heads, axis=0)
     distance = (ids // ch_chip * 2 + parity) ^ centre
-    slot = distance % 8 // 2 * far + (distance // 8 + far // 2) % far
+    slot = jnp.zeros_like(distance)
+    for n, known in enumerate(distances):
+        slot = jnp.where(distance == known, n, slot)
     column = lax.broadcasted_iota(jnp.int32, (sources, tails.shape[0]), 1)
     choice = (column == slot * 16).astype(jnp.bfloat16)
     tail = jnp.dot(choice, tails, preferred_element_type=jnp.float32)
@@ -281,7 +283,7 @@
         out_ref[...] = lags.reshape(sources, ch_local, LAG_TILES * 128)[:, :, :LAGS]
 
 
-def correlate(core, place, weights, ids, steps, blocks, shape, before=None, table=None):
+def correlate(core, place, weights, ids, layout, blocks, shape, before=None, table=None):
     segments, channels, devices = shape
     ch_local = channels // devices
     sources = ids.shape[0]
@@ -301,7 +303,7 @@
         ]
     out = (sources, ch_local, LAGS) if core else (ch_local, sources, WIDTH)
     return pl.pallas_call(
-        functools.partial(correlate_kernel, shape, core, steps),
+        functools.partial(correlate_kernel, shape, core, layout),
         in_specs=in_specs,
         out_specs=vmem,
         out_shape=jax.ShapeDtypeStruct(out, jnp.float32),
@@ -362,18 +364,21 @@
 
     far = devices // 8
     line = [white] + [exchange(white, 8 * k) for k in range(1, far)]
-    halves = [jnp.stack(line[far // 2 :]), jnp.stack(line[: far // 2])]
-    steps = [2 * near for near in range(4)]
-    blocks = [
-        jnp.concatenate([exchange(half, step) if step else half for half in halves])
-        for step in steps
-    ]
+    halves = [(first, jnp.stack(line[first : first + far // 2])) for first in (far // 2, 0)]
+    layout, blocks = [], []
+    for near in range(0, 8, 2):
+        came = [exchange(half, near) if near else half for _, half in halves]
+        ways = [[8 * (first + k) + near for k in range(far // 2)] for first, _ in halves]
+        if near != 2:
+            came, ways = [jnp.concatenate(came)], [ways[0] + ways[1]]
+        blocks += came
+        layout += ways
     swapped = [exchange(block, 1) for block in blocks]
     ids = source_ids.reshape(-1, 1)
     common = me, weights, ids
     shape = segments, channels, devices
-    before = correlate(0, *common, steps, blocks, shape)
-    return correlate(1, *common, steps, swapped, shape, before, inverse_table(samples))
+    before = correlate(0, *common, layout, blocks, shape)
+    return correlate(1, *common, layout, swapped, shape, before, inverse_table(samples))
 
 
 def solution(mesh):

time: 67 us -> 65.8 us (0.982)
  local copies, waits for them, and re-layouts: 4.36 us -> 3.03 us
    concatenate x3 -> x2, local copies, waits for them, and re-layouts: 1.36 us -> 0.69 us  [per_device(): came, ways = ([jnp.concatenate(came)], [ways[0] + ways[1]])]
    unnamed x10 -> x9, local copies, waits for them, and re-layouts: 1.45 us -> 0.79 us
    ppermute x24 -> x25, waiting for transfers between devices: 14.3 us -> 14.4 us  [exchange(): return lax.ppermute(block, 'chan', [(i, i ^ bits) for i in range(devices)])]
    ppermute x24 -> x25, starting transfers between devices: 30.3 us -> 30.3 us  [exchange(): return lax.ppermute(block, 'chan', [(i, i ^ bits) for i in range(devices)])]
  transfers between devices with their start and end apart: 24 -> 25, of which waited for: 9 -> 9; matrix products, arithmetic and copies ran while one was open for 5% -> 3% of each run, Pallas kernels for 14% -> 14%
where the time goes in v10:
time: 65.8 us; the launch traced here: 65.5 us
  starting transfers between devices  30.3 us (46%)
  Pallas kernels  17.3 us (26%)
  waiting for transfers between devices  14.4 us (22%)
  local copies, waits for them, and re-layouts  3.03 us (5%)
    ppermute x25, starting transfers between devices, exchange(): return lax.ppermute(block, 'chan', [(i, i ^ bits) for i in range(devices)])  30.3 us
    ppermute x25, waiting for transfers between devices, exchange(): return lax.ppermute(block, 'chan', [(i, i ^ bits) for i in range(devices)])  14.4 us
    pallas_call x3, Pallas kernels, transform(): pl.pallas_call(functools.partial(transform_kernel, steps, first, started)...  10 us
    pallas_call x2, Pallas kernels, correlate(): pl.pallas_call(functools.partial(correlate_kernel, shape, core, layout),...  7.13 us
  transfers between devices with their start and end apart: 25, of which 9 were waited for; matrix products, arithmetic and copies ran while one was open for 3% of the time, Pallas kernels for 14%

profile of v10, /device:TPU:0, one launch (start us, length us, event | category | flops | bytes accessed | tf_op | source)
XLA Modules:
  0.0 65.5 jit_solution(9910095562525930910)
XLA Ops:
  0.0 1.3 %constant_dynamic-slice_fusion.20 = (bf16[4,1,128,512]{3,2,1,0:T(8,128)(2,1)S(1)}, bf16[4,1,128,512]{3,2,1,0:T(8,128)(2,1)S(1)}) fusion(bf16[4,2,128,512]{3,2,1,0:T(8,128)(2,1)} %bitcast.19, s32[]{:T(128)S(6)} %select_n.69, s32[]{:T(128)S(6)} %select_n.73), kind=kLoop, calls=%fused_computation.35 | loop fusion | bytes 2097160 | tf_op jit(solution)/shard_map/jit(dynamic_index_in_dim)/dynamic_slice | solution.py:345
  1.9 1.5 %collective-permute-done.1 = bf16[8,64,512]{2,1,0:T(8,128)(2,1)S(1)} collective-permute-done((bf16[8,64,512]{2,1,0:T(8,128)(2,1)S(1)}, bf16[8,64,512]{2,1,0:T(8,128)(2,1)S(1)}, u32[]{:S(2)}, u32[]{:S(2)}) %collective-permute-start.1) | collective-permute-done | bytes 524320 | tf_op jit(solution)/shard_map/ppermute | solution.py:330
  3.4 4.0 %collective-permute-start.8 = (bf16[2,64,512]{2,1,0:T(8,128)(2,1)S(1)}, bf16[2,64,512]{2,1,0:T(8,128)(2,1)S(1)}, u32[]{:S(2)}, u32[]{:S(2)}) collective-permute-start(bf16[2,64,512]{2,1,0:T(8,128)(2,1)S(1)} %pad_maximum_fusion.10), channel_id=1, source_target_pairs={{0,12},{1,13},{2,14},{3,15},{4,8},{5,9},{6,10},{7,11},{8,4},{9,5},... | collective-permute-start | bytes 393224 | tf_op jit(solution)/shard_map/ppermute | solution.py:330
  7.4 1.6 %collective-permute-start.7 = (bf16[2,64,512]{2,1,0:T(8,128)(2,1)S(1)}, bf16[2,64,512]{2,1,0:T(8,128)(2,1)S(1)}, u32[]{:S(2)}, u32[]{:S(2)}) collective-permute-start(bf16[2,64,512]{2,1,0:T(8,128)(2,1)S(1)} %pad_maximum_fusion.9), channel_id=1, source_target_pairs={{0,2},{1,3},{2,0},{3,1},{4,6},{5,7},{6,4},{7,5},{8,10},{9,11},{10,... | collective-permute-start | bytes 393224 | tf_op jit(solution)/shard_map/ppermute | solution.py:330
  9.1 2.0 %collective-permute-start.5 = (bf16[2,64,512]{2,1,0:T(8,128)(2,1)S(1)}, bf16[2,64,512]{2,1,0:T(8,128)(2,1)S(1)}, u32[]{:S(2)}, u32[]{:S(2)}) collective-permute-start(bf16[2,64,512]{2,1,0:T(8,128)(2,1)S(1)} %pad_maximum_fusion.6), channel_id=1, source_target_pairs={{0,8},{1,9},{2,10},{3,11},{4,12},{5,13},{6,14},{7,15},{8,0},{9,1},... | collective-permute-start | bytes 393224 | tf_op jit(solution)/shard_map/ppermute | solution.py:330
  11.1 2.5 %collective-permute-start.4 = (bf16[2,64,512]{2,1,0:T(8,128)(2,1)S(1)}, bf16[2,64,512]{2,1,0:T(8,128)(2,1)S(1)}, u32[]{:S(2)}, u32[]{:S(2)}) collective-permute-start(bf16[2,64,512]{2,1,0:T(8,128)(2,1)S(1)} %pad_maximum_fusion.5), channel_id=1, source_target_pairs={{0,6},{1,7},{2,4},{3,5},{4,2},{5,3},{6,0},{7,1},{8,14},{9,15},{10,... | collective-permute-start | bytes 393224 | tf_op jit(solution)/shard_map/ppermute | solution.py:330
  14.1 1.5 %collective-permute-done.7.rest_2_ = bf16[2,64,512]{2,1,0:T(8,128)(2,1)S(1)} collective-permute-done((bf16[2,64,512]{2,1,0:T(8,128)(2,1)S(1)}, bf16[2,64,512]{2,1,0:T(8,128)(2,1)S(1)}, u32[]{:S(2)}, u32[]{:S(2)}) %collective-permute-start.7) | collective-permute-done | bytes 131104 | tf_op jit(solution)/shard_map/ppermute | solution.py:330
  16.2 1.2 %collective-permute-done.6.rest_1_ = bf16[2,64,512]{2,1,0:T(8,128)(2,1)S(1)} collective-permute-done((bf16[2,64,512]{2,1,0:T(8,128)(2,1)S(1)}, bf16[2,64,512]{2,1,0:T(8,128)(2,1)S(1)}, u32[]{:S(2)}, u32[]{:S(2)}) %collective-permute-start.6) | collective-permute-done | bytes 131104 | tf_op jit(solution)/shard_map/ppermute | solution.py:330
  17.3 4.4 %transform.3.rest_4_ = f32[64,1280]{1,0:T(8,128)S(1)} custom-call(s32[1]{0:T(128)} %bitcast.place_ref, bf16[163840,128]{1,0:T(8,128)(2,1)} %constant.100.clone.table_ref, bf16[2,64,512]{2,1,0:T(8,128)(2,1)S(1)} %pad_maximum_fusion.7.rest_0_, bf16[2,64,512]{2,1,0:T(8,128)(2,1)S(1)} %collective-permute-done.6.rest_1_, ...), custom_call_target="tpu_custom_call" | custom-call | flops 671088640 | bytes 10485760 | tf_op jit(solution)/shard_map/transform/pallas_call | solution.py:121
  21.8 3.1 %transform.4 = (f32[32,768]{1,0:T(8,128)S(1)}, f32[32,768]{1,0:T(8,128)S(1)}) custom-call(s32[1]{0:T(128)} %bitcast.place_ref, bf16[163840,128]{1,0:T(8,128)(2,1)} %constant.100.clone.table_ref, bf16[2,64,512]{2,1,0:T(8,128)(2,1)S(1)} %collective-permute-done.2.rest_0_, bf16[2,64,512]{2,1,0:T(8,128)(2,1)S(1)} %collective-permute-done.3.rest_1_, ...), custom_call_target="tpu_custom_call" | custom-call | flops 402653184 | bytes 6291456 | tf_op jit(solution)/shard_map/transform/pallas_call | solution.py:121
  25.0 2.6 %collective-permute-start.9 = (f32[32,768]{1,0:T(8,128)S(1)}, f32[32,768]{1,0:T(8,128)S(1)}, u32[]{:S(2)}, u32[]{:S(2)}) collective-permute-start(f32[32,768]{1,0:T(8,128)S(1)} %get-tuple-element.10), channel_id=1, source_target_pairs={{0,16},{1,17},{2,18},{3,19},{4,20},{5,21},{6,22},{7,23},{8,24},{9,... | collective-permute-start | bytes 294920 | tf_op jit(solution)/shard_map/ppermute | solution.py:330
  27.6 2.4 %transform.5 = (f32[32,512]{1,0:T(8,128)S(1)}, f32[32,512]{1,0:T(8,128)S(1)}) custom-call(s32[1]{0:T(128)} %bitcast.place_ref, bf16[163840,128]{1,0:T(8,128)(2,1)} %constant.100.clone.table_ref, bf16[2,64,512]{2,1,0:T(8,128)(2,1)S(1)} %collective-permute-done.2.rest_0_, bf16[2,64,512]{2,1,0:T(8,128)(2,1)S(1)} %collective-permute-done.3.rest_1_, ...), custom_call_target="tpu_custom_call" | custom-call | flops 268435456 | bytes 4194304 | tf_op jit(solution)/shard_map/transform/pallas_call | solution.py:121
  30.6 1.2 %collective-permute-done = f32[8,4]{1,0:T(8,128)S(1)} collective-permute-done((f32[8,4]{1,0:T(8,128)S(1)}, f32[8,4]{1,0:T(8,128)S(1)}, u32[]{:S(2)}, u32[]{:S(2)}) %collective-permute-start) | collective-permute-done | bytes 160 | tf_op jit(solution)/shard_map/ppermute | solution.py:330
  31.9 4.2 %collective-permute-done.10.rest_3_ = f32[32,512]{1,0:T(8,128)S(1)} collective-permute-done((f32[32,512]{1,0:T(8,128)S(1)}, f32[32,512]{1,0:T(8,128)S(1)}, u32[]{:S(2)}, u32[]{:S(2)}) %collective-permute-start.10) | collective-permute-done | bytes 65568 | tf_op jit(solution)/shard_map/ppermute | solution.py:330
  36.3 2.0 %collective-permute-start.11 = (bf16[32,1280]{1,0:T(8,128)(2,1)S(1)}, bf16[32,1280]{1,0:T(8,128)(2,1)S(1)}, u32[]{:S(2)}, u32[]{:S(2)}) collective-permute-start(bf16[32,1280]{1,0:T(8,128)(2,1)S(1)} %whiten.1), channel_id=1, source_target_pairs={{0,16},{1,17},{2,18},{3,19},{4,20},{5,21},{6,22},{7,23},{8,24},{9,... | collective-permute-start | bytes 245768 | tf_op jit(solution)/shard_map/ppermute | solution.py:330
  38.3 2.3 %collective-permute-start.12 = (bf16[32,1280]{1,0:T(8,128)(2,1)S(1)}, bf16[32,1280]{1,0:T(8,128)(2,1)S(1)}, u32[]{:S(2)}, u32[]{:S(2)}) collective-permute-start(bf16[32,1280]{1,0:T(8,128)(2,1)S(1)} %whiten.1), channel_id=1, source_target_pairs={{0,24},{1,25},{2,26},{3,27},{4,28},{5,29},{6,30},{7,31},{8,16},{9,... | collective-permute-start | bytes 245768 | tf_op jit(solution)/shard_map/ppermute | solution.py:330
  40.7 2.1 %collective-permute-start.23 = (bf16[2,32,1280]{2,1,0:T(8,128)(2,1)S(1)}, bf16[2,32,1280]{2,1,0:T(8,128)(2,1)S(1)}, u32[]{:S(2)}, u32[]{:S(2)}) collective-permute-start(bf16[2,32,1280]{2,1,0:T(8,128)(2,1)S(1)} %pad_maximum_fusion.2), channel_id=1, source_target_pairs={{0,6},{1,7},{2,4},{3,5},{4,2},{5,3},{6,0},{7,1},{8,14},{9,15},{10,... | collective-permute-start | bytes 491528 | tf_op jit(solution)/shard_map/ppermute | solution.py:330
  42.8 2.6 %collective-permute-start.20 = (bf16[2,32,1280]{2,1,0:T(8,128)(2,1)S(1)}, bf16[2,32,1280]{2,1,0:T(8,128)(2,1)S(1)}, u32[]{:S(2)}, u32[]{:S(2)}) collective-permute-start(bf16[2,32,1280]{2,1,0:T(8,128)(2,1)S(1)} %pad_maximum_fusion.2), channel_id=1, source_target_pairs={{0,4},{1,5},{2,6},{3,7},{4,0},{5,1},{6,2},{7,3},{8,12},{9,13},{10,... | collective-permute-start | bytes 491528 | tf_op jit(solution)/shard_map/ppermute | solution.py:330
  45.5 0.9 %collective-permute-start.22 = (bf16[2,32,1280]{2,1,0:T(8,128)(2,1)S(1)}, bf16[2,32,1280]{2,1,0:T(8,128)(2,1)S(1)}, u32[]{:S(2)}, u32[]{:S(2)}) collective-permute-start(bf16[2,32,1280]{2,1,0:T(8,128)(2,1)S(1)} %pad_maximum_fusion.1), channel_id=1, source_target_pairs={{0,6},{1,7},{2,4},{3,5},{4,2},{5,3},{6,0},{7,1},{8,14},{9,15},{10,... | collective-permute-start | bytes 491528 | tf_op jit(solution)/shard_map/ppermute | solution.py:330
  47.0 2.0 %collective-permute-start.17 = (bf16[2,32,1280]{2,1,0:T(8,128)(2,1)S(1)}, bf16[2,32,1280]{2,1,0:T(8,128)(2,1)S(1)}, u32[]{:S(2)}, u32[]{:S(2)}) collective-permute-start(bf16[2,32,1280]{2,1,0:T(8,128)(2,1)S(1)} %pad_maximum_fusion.2), channel_id=1, source_target_pairs={{0,2},{1,3},{2,0},{3,1},{4,6},{5,7},{6,4},{7,5},{8,10},{9,11},{10,... | collective-permute-start | bytes 491528 | tf_op jit(solution)/shard_map/ppermute | solution.py:330
  49.1 3.4 %collective-permute-done.22 = bf16[2,32,1280]{2,1,0:T(8,128)(2,1)S(1)} collective-permute-done((bf16[2,32,1280]{2,1,0:T(8,128)(2,1)S(1)}, bf16[2,32,1280]{2,1,0:T(8,128)(2,1)S(1)}, u32[]{:S(2)}, u32[]{:S(2)}) %collective-permute-start.22) | collective-permute-done | bytes 163872 | tf_op jit(solution)/shard_map/ppermute | solution.py:330
  52.4 2.4 %collective-permute-start.15 = (bf16[2,32,1280]{2,1,0:T(8,128)(2,1)S(1)}, bf16[2,32,1280]{2,1,0:T(8,128)(2,1)}, u32[]{:S(2)}, u32[]{:S(2)}) collective-permute-start(bf16[2,32,1280]{2,1,0:T(8,128)(2,1)S(1)} %pad_maximum_fusion.1), channel_id=1, source_target_pairs={{0,2},{1,3},{2,0},{3,1},{4,6},{5,7},{6,4},{7,5},{8,10},{9,11},{10,... | collective-permute-start | bytes 491528 | tf_op jit(solution)/shard_map/ppermute | solution.py:330
  58.3 2.4 %correlate.2.rest_5_ = f32[4,64,1280]{2,1,0:T(8,128)S(1)} custom-call(s32[1]{0:T(128)} %bitcast.place_ref, f32[8,4]{1,0:T(8,128)S(1)} %convert_element_type.3.flags_ref, s32[64,1]{1,0:T(8,128)S(1)} %copy.10.ids_ref, bf16[4,32,1280]{2,1,0:T(8,128)(2,1)S(1)} %pad_maximum_fusion.rest_0_, bf16[2,32,1280]{2,1,0:T(8,128)(2,1)} %collective-permute-done.15.rest_1_, ...), custom_call_target="tpu_custom_call" | custom-call | flops 83886080 | bytes 1310720 | tf_op jit(solution)/shard_map/correlate/pallas_call | solution.py:305
  60.8 4.7 %correlate.3 = f32[64,4,1001]{2,1,0:T(4,128)} custom-call(s32[1]{0:T(128)} %bitcast.place_ref, f32[8,4]{1,0:T(8,128)S(1)} %convert_element_type.3.flags_ref, s32[64,1]{1,0:T(8,128)S(1)} %copy.10.ids_ref, bf16[4,32,1280]{2,1,0:T(8,128)(2,1)} %collective-permute-done.14.rest_0_, bf16[2,32,1280]{2,1,0:T(8,128)(2,1)} %collective-permute-done.16.rest_1_, ...), custom_call_target="tpu_custom_call" | custom-call | flops 83886080 | bytes 1310720 | tf_op jit(solution)/shard_map/correlate/pallas_call | solution.py:305
  (61 shorter events, 6.9 us)
Async XLA Ops:
  1.3 2.1 %collective-permute-start.1 = (bf16[8,64,512]{2,1,0:T(8,128)(2,1)S(1)}, bf16[8,64,512]{2,1,0:T(8,128)(2,1)S(1)}, u32[]{:S(2)}, u32[]{:S(2)}) collective-permute-start(bf16[8,64,512]{2,1,0:T(8,128)(2,1)S(1)} %bitcast.20), channel_id=1, source_target_pairs={{0,1},{1,0},{2,3},{3,2},{4,5},{5,4},{6,7},{7,6},{8,9},{9,8},{10,11... | collective-permute-start | bytes 1572872 | tf_op jit(solution)/shard_map/ppermute | solution.py:330
  3.4 10.2 %collective-permute-start.8 = (bf16[2,64,512]{2,1,0:T(8,128)(2,1)S(1)}, bf16[2,64,512]{2,1,0:T(8,128)(2,1)S(1)}, u32[]{:S(2)}, u32[]{:S(2)}) collective-permute-start(bf16[2,64,512]{2,1,0:T(8,128)(2,1)S(1)} %pad_maximum_fusion.10), channel_id=1, source_target_pairs={{0,12},{1,13},{2,14},{3,15},{4,8},{5,9},{6,10},{7,11},{8,4},{9,5},... | collective-permute-start | bytes 393224 | tf_op jit(solution)/shard_map/ppermute | solution.py:330
  7.4 8.2 %collective-permute-start.7 = (bf16[2,64,512]{2,1,0:T(8,128)(2,1)S(1)}, bf16[2,64,512]{2,1,0:T(8,128)(2,1)S(1)}, u32[]{:S(2)}, u32[]{:S(2)}) collective-permute-start(bf16[2,64,512]{2,1,0:T(8,128)(2,1)S(1)} %pad_maximum_fusion.9), channel_id=1, source_target_pairs={{0,2},{1,3},{2,0},{3,1},{4,6},{5,7},{6,4},{7,5},{8,10},{9,11},{10,... | collective-permute-start | bytes 393224 | tf_op jit(solution)/shard_map/ppermute | solution.py:330
  9.0 8.3 %collective-permute-start.6 = (bf16[2,64,512]{2,1,0:T(8,128)(2,1)S(1)}, bf16[2,64,512]{2,1,0:T(8,128)(2,1)S(1)}, u32[]{:S(2)}, u32[]{:S(2)}) collective-permute-start(bf16[2,64,512]{2,1,0:T(8,128)(2,1)S(1)} %pad_maximum_fusion.8), channel_id=1, source_target_pairs={{0,14},{1,15},{2,12},{3,13},{4,10},{5,11},{6,8},{7,9},{8,6},{9,7},... | collective-permute-start | bytes 393224 | tf_op jit(solution)/shard_map/ppermute | solution.py:330
  9.1 12.7 %collective-permute-start.5 = (bf16[2,64,512]{2,1,0:T(8,128)(2,1)S(1)}, bf16[2,64,512]{2,1,0:T(8,128)(2,1)S(1)}, u32[]{:S(2)}, u32[]{:S(2)}) collective-permute-start(bf16[2,64,512]{2,1,0:T(8,128)(2,1)S(1)} %pad_maximum_fusion.6), channel_id=1, source_target_pairs={{0,8},{1,9},{2,10},{3,11},{4,12},{5,13},{6,14},{7,15},{8,0},{9,1},... | collective-permute-start | bytes 393224 | tf_op jit(solution)/shard_map/ppermute | solution.py:330
  11.1 10.7 %collective-permute-start.4 = (bf16[2,64,512]{2,1,0:T(8,128)(2,1)S(1)}, bf16[2,64,512]{2,1,0:T(8,128)(2,1)S(1)}, u32[]{:S(2)}, u32[]{:S(2)}) collective-permute-start(bf16[2,64,512]{2,1,0:T(8,128)(2,1)S(1)} %pad_maximum_fusion.5), channel_id=1, source_target_pairs={{0,6},{1,7},{2,4},{3,5},{4,2},{5,3},{6,0},{7,1},{8,14},{9,15},{10,... | collective-permute-start | bytes 393224 | tf_op jit(solution)/shard_map/ppermute | solution.py:330
  13.7 8.1 %collective-permute-start.3 = (bf16[2,64,512]{2,1,0:T(8,128)(2,1)S(1)}, bf16[2,64,512]{2,1,0:T(8,128)(2,1)S(1)}, u32[]{:S(2)}, u32[]{:S(2)}) collective-permute-start(bf16[2,64,512]{2,1,0:T(8,128)(2,1)S(1)} %pad_maximum_fusion.4), channel_id=1, source_target_pairs={{0,10},{1,11},{2,8},{3,9},{4,14},{5,15},{6,12},{7,13},{8,2},{9,3},... | collective-permute-start | bytes 393224 | tf_op jit(solution)/shard_map/ppermute | solution.py:330
  15.7 6.1 %collective-permute-start.2 = (bf16[2,64,512]{2,1,0:T(8,128)(2,1)S(1)}, bf16[2,64,512]{2,1,0:T(8,128)(2,1)S(1)}, u32[]{:S(2)}, u32[]{:S(2)}) collective-permute-start(bf16[2,64,512]{2,1,0:T(8,128)(2,1)S(1)} %pad_maximum_fusion.3), channel_id=1, source_target_pairs={{0,4},{1,5},{2,6},{3,7},{4,0},{5,1},{6,2},{7,3},{8,12},{9,13},{10,... | collective-permute-start | bytes 393224 | tf_op jit(solution)/shard_map/ppermute | solution.py:330
  25.0 11.1 %collective-permute-start.9 = (f32[32,768]{1,0:T(8,128)S(1)}, f32[32,768]{1,0:T(8,128)S(1)}, u32[]{:S(2)}, u32[]{:S(2)}) collective-permute-start(f32[32,768]{1,0:T(8,128)S(1)} %get-tuple-element.10), channel_id=1, source_target_pairs={{0,16},{1,17},{2,18},{3,19},{4,20},{5,21},{6,22},{7,23},{8,24},{9,... | collective-permute-start | bytes 294920 | tf_op jit(solution)/shard_map/ppermute | solution.py:330
  30.1 6.0 %collective-permute-start.10 = (f32[32,512]{1,0:T(8,128)S(1)}, f32[32,512]{1,0:T(8,128)S(1)}, u32[]{:S(2)}, u32[]{:S(2)}) collective-permute-start(f32[32,512]{1,0:T(8,128)S(1)} %get-tuple-element.12), channel_id=1, source_target_pairs={{0,16},{1,17},{2,18},{3,19},{4,20},{5,21},{6,22},{7,23},{8,24},{9,... | collective-permute-start | bytes 196616 | tf_op jit(solution)/shard_map/ppermute | solution.py:330
  36.2 4.5 %collective-permute-start.13 = (bf16[32,1280]{1,0:T(8,128)(2,1)S(1)}, bf16[32,1280]{1,0:T(8,128)(2,1)S(1)}, u32[]{:S(2)}, u32[]{:S(2)}) collective-permute-start(bf16[32,1280]{1,0:T(8,128)(2,1)S(1)} %whiten.1), channel_id=1, source_target_pairs={{0,8},{1,9},{2,10},{3,11},{4,12},{5,13},{6,14},{7,15},{8,0},{9,1},... | collective-permute-start | bytes 245768 | tf_op jit(solution)/shard_map/ppermute | solution.py:330
  36.3 9.2 %collective-permute-start.11 = (bf16[32,1280]{1,0:T(8,128)(2,1)S(1)}, bf16[32,1280]{1,0:T(8,128)(2,1)S(1)}, u32[]{:S(2)}, u32[]{:S(2)}) collective-permute-start(bf16[32,1280]{1,0:T(8,128)(2,1)S(1)} %whiten.1), channel_id=1, source_target_pairs={{0,16},{1,17},{2,18},{3,19},{4,20},{5,21},{6,22},{7,23},{8,24},{9,... | collective-permute-start | bytes 245768 | tf_op jit(solution)/shard_map/ppermute | solution.py:330
  38.3 7.1 %collective-permute-start.12 = (bf16[32,1280]{1,0:T(8,128)(2,1)S(1)}, bf16[32,1280]{1,0:T(8,128)(2,1)S(1)}, u32[]{:S(2)}, u32[]{:S(2)}) collective-permute-start(bf16[32,1280]{1,0:T(8,128)(2,1)S(1)} %whiten.1), channel_id=1, source_target_pairs={{0,24},{1,25},{2,26},{3,27},{4,28},{5,29},{6,30},{7,31},{8,16},{9,... | collective-permute-start | bytes 245768 | tf_op jit(solution)/shard_map/ppermute | solution.py:330
  40.7 14.1 %collective-permute-start.23 = (bf16[2,32,1280]{2,1,0:T(8,128)(2,1)S(1)}, bf16[2,32,1280]{2,1,0:T(8,128)(2,1)S(1)}, u32[]{:S(2)}, u32[]{:S(2)}) collective-permute-start(bf16[2,32,1280]{2,1,0:T(8,128)(2,1)S(1)} %pad_maximum_fusion.2), channel_id=1, source_target_pairs={{0,6},{1,7},{2,4},{3,5},{4,2},{5,3},{6,0},{7,1},{8,14},{9,15},{10,... | collective-permute-start | bytes 491528 | tf_op jit(solution)/shard_map/ppermute | solution.py:330
  42.8 13.7 %collective-permute-start.20 = (bf16[2,32,1280]{2,1,0:T(8,128)(2,1)S(1)}, bf16[2,32,1280]{2,1,0:T(8,128)(2,1)S(1)}, u32[]{:S(2)}, u32[]{:S(2)}) collective-permute-start(bf16[2,32,1280]{2,1,0:T(8,128)(2,1)S(1)} %pad_maximum_fusion.2), channel_id=1, source_target_pairs={{0,4},{1,5},{2,6},{3,7},{4,0},{5,1},{6,2},{7,3},{8,12},{9,13},{10,... | collective-permute-start | bytes 491528 | tf_op jit(solution)/shard_map/ppermute | solution.py:330
  45.5 7.0 %collective-permute-start.22 = (bf16[2,32,1280]{2,1,0:T(8,128)(2,1)S(1)}, bf16[2,32,1280]{2,1,0:T(8,128)(2,1)S(1)}, u32[]{:S(2)}, u32[]{:S(2)}) collective-permute-start(bf16[2,32,1280]{2,1,0:T(8,128)(2,1)S(1)} %pad_maximum_fusion.1), channel_id=1, source_target_pairs={{0,6},{1,7},{2,4},{3,5},{4,2},{5,3},{6,0},{7,1},{8,14},{9,15},{10,... | collective-permute-start | bytes 491528 | tf_op jit(solution)/shard_map/ppermute | solution.py:330
  46.4 9.4 %collective-permute-start.19 = (bf16[2,32,1280]{2,1,0:T(8,128)(2,1)S(1)}, bf16[2,32,1280]{2,1,0:T(8,128)(2,1)S(1)}, u32[]{:S(2)}, u32[]{:S(2)}) collective-permute-start(bf16[2,32,1280]{2,1,0:T(8,128)(2,1)S(1)} %pad_maximum_fusion.1), channel_id=1, source_target_pairs={{0,4},{1,5},{2,6},{3,7},{4,0},{5,1},{6,2},{7,3},{8,12},{9,13},{10,... | collective-permute-start | bytes 491528 | tf_op jit(solution)/shard_map/ppermute | solution.py:330
  47.0 10.6 %collective-permute-start.17 = (bf16[2,32,1280]{2,1,0:T(8,128)(2,1)S(1)}, bf16[2,32,1280]{2,1,0:T(8,128)(2,1)S(1)}, u32[]{:S(2)}, u32[]{:S(2)}) collective-permute-start(bf16[2,32,1280]{2,1,0:T(8,128)(2,1)S(1)} %pad_maximum_fusion.2), channel_id=1, source_target_pairs={{0,2},{1,3},{2,0},{3,1},{4,6},{5,7},{6,4},{7,5},{8,10},{9,11},{10,... | collective-permute-start | bytes 491528 | tf_op jit(solution)/shard_map/ppermute | solution.py:330
  52.4 5.8 %collective-permute-start.15 = (bf16[2,32,1280]{2,1,0:T(8,128)(2,1)S(1)}, bf16[2,32,1280]{2,1,0:T(8,128)(2,1)}, u32[]{:S(2)}, u32[]{:S(2)}) collective-permute-start(bf16[2,32,1280]{2,1,0:T(8,128)(2,1)S(1)} %pad_maximum_fusion.1), channel_id=1, source_target_pairs={{0,2},{1,3},{2,0},{3,1},{4,6},{5,7},{6,4},{7,5},{8,10},{9,11},{10,... | collective-permute-start | bytes 491528 | tf_op jit(solution)/shard_map/ppermute | solution.py:330
  54.8 5.9 %collective-permute-start.14 = (bf16[4,32,1280]{2,1,0:T(8,128)(2,1)S(1)}, bf16[4,32,1280]{2,1,0:T(8,128)(2,1)}, u32[]{:S(2)}, u32[]{:S(2)}) collective-permute-start(bf16[4,32,1280]{2,1,0:T(8,128)(2,1)S(1)} %pad_maximum_fusion.rest_0_), channel_id=1, source_target_pairs={{0,1},{1,0},{2,3},{3,2},{4,5},{5,4},{6,7},{7,6},{8,9},{9,8},{10,11... | collective-permute-start | bytes 983048 | tf_op jit(solution)/shard_map/ppermute | solution.py:330
  55.8 5.0 %collective-permute-start.24 = (bf16[4,32,1280]{2,1,0:T(8,128)(2,1)S(1)}, bf16[4,32,1280]{2,1,0:T(8,128)(2,1)}, u32[]{:S(2)}, u32[]{:S(2)}) collective-permute-start(bf16[4,32,1280]{2,1,0:T(8,128)(2,1)S(1)} %constant_dynamic-update-slice_fusion.2.rest_4_), channel_id=1, source_target_pairs={{0,1},{1,0},{2,3},{3,2},{4,5},{5,4},{6,7},{7,6},{8,9},{9,8},{10,11... | collective-permute-start | bytes 983048 | tf_op jit(solution)/shard_map/ppermute | solution.py:330
  57.2 3.6 %collective-permute-start.21 = (bf16[4,32,1280]{2,1,0:T(8,128)(2,1)}, bf16[4,32,1280]{2,1,0:T(8,128)(2,1)}, u32[]{:S(2)}, u32[]{:S(2)}) collective-permute-start(bf16[4,32,1280]{2,1,0:T(8,128)(2,1)} %constant_dynamic-update-slice_fusion.rest_3_), channel_id=1, source_target_pairs={{0,1},{1,0},{2,3},{3,2},{4,5},{5,4},{6,7},{7,6},{8,9},{9,8},{10,11... | collective-permute-start | bytes 983048 | tf_op jit(solution)/shard_map/ppermute | solution.py:330
  57.7 3.1 %collective-permute-start.18 = (bf16[2,32,1280]{2,1,0:T(8,128)(2,1)S(1)}, bf16[2,32,1280]{2,1,0:T(8,128)(2,1)}, u32[]{:S(2)}, u32[]{:S(2)}) collective-permute-start(bf16[2,32,1280]{2,1,0:T(8,128)(2,1)S(1)} %collective-permute-done.17.rest_2_), channel_id=1, source_target_pairs={{0,1},{1,0},{2,3},{3,2},{4,5},{5,4},{6,7},{7,6},{8,9},{9,8},{10,11... | collective-permute-start | bytes 491528 | tf_op jit(solution)/shard_map/ppermute | solution.py:330
  58.2 2.5 %collective-permute-start.16 = (bf16[2,32,1280]{2,1,0:T(8,128)(2,1)}, bf16[2,32,1280]{2,1,0:T(8,128)(2,1)}, u32[]{:S(2)}, u32[]{:S(2)}) collective-permute-start(bf16[2,32,1280]{2,1,0:T(8,128)(2,1)} %collective-permute-done.15.rest_1_), channel_id=1, source_target_pairs={{0,1},{1,0},{2,3},{3,2},{4,5},{5,4},{6,7},{7,6},{8,9},{9,8},{10,11... | collective-permute-start | bytes 491528 | tf_op jit(solution)/shard_map/ppermute | solution.py:330
  (4 other events, 54.9 us)

commit v11 on v10

--- a/solution.py
+++ b/solution.py
@@ -370,6 +370,8 @@
         came = [exchange(half, near) if near else half for _, half in halves]
         ways = [[8 * (first + k) + near for k in range(far // 2)] for first, _ in halves]
         if near != 2:
+            if near == 6:
+                came, ways = came[::-1], ways[::-1]
             came, ways = [jnp.concatenate(came)], [ways[0] + ways[1]]
         blocks += came
         layout += ways

time: 65.8 us -> 65.7 us (level)
  no operation moved by 1% of the time
where the time goes in v11:
time: 65.7 us; the launch traced here: 65.5 us
  starting transfers between devices  30.4 us (46%)
  Pallas kernels  17.2 us (26%)
  waiting for transfers between devices  14.2 us (22%)
  local copies, waits for them, and re-layouts  3.03 us (5%)
    ppermute x25, starting transfers between devices, exchange(): return lax.ppermute(block, 'chan', [(i, i ^ bits) for i in range(devices)])  30.4 us
    ppermute x25, waiting for transfers between devices, exchange(): return lax.ppermute(block, 'chan', [(i, i ^ bits) for i in range(devices)])  14.2 us
    pallas_call x3, Pallas kernels, transform(): pl.pallas_call(functools.partial(transform_kernel, steps, first, started)...  10 us
    pallas_call x2, Pallas kernels, correlate(): pl.pallas_call(functools.partial(correlate_kernel, shape, core, layout),...  7.12 us
  transfers between devices with their start and end apart: 25, of which 9 were waited for; matrix products, arithmetic and copies ran while one was open for 3% of the time, Pallas kernels for 14%

profile of v11, /device:TPU:0, one launch (start us, length us, event | category | flops | bytes accessed | tf_op | source)
XLA Modules:
  0.0 65.5 jit_solution(16043379569936636056)
XLA Ops:
  0.0 1.3 %constant_dynamic-slice_fusion.20 = (bf16[4,1,128,512]{3,2,1,0:T(8,128)(2,1)S(1)}, bf16[4,1,128,512]{3,2,1,0:T(8,128)(2,1)S(1)}) fusion(bf16[4,2,128,512]{3,2,1,0:T(8,128)(2,1)} %bitcast.19, s32[]{:T(128)S(6)} %select_n.69, s32[]{:T(128)S(6)} %select_n.73), kind=kLoop, calls=%fused_computation.35 | loop fusion | bytes 2097160 | tf_op jit(solution)/shard_map/jit(dynamic_index_in_dim)/dynamic_slice | solution.py:345
  1.9 1.5 %collective-permute-done.1 = bf16[8,64,512]{2,1,0:T(8,128)(2,1)S(1)} collective-permute-done((bf16[8,64,512]{2,1,0:T(8,128)(2,1)S(1)}, bf16[8,64,512]{2,1,0:T(8,128)(2,1)S(1)}, u32[]{:S(2)}, u32[]{:S(2)}) %collective-permute-start.1) | collective-permute-done | bytes 524320 | tf_op jit(solution)/shard_map/ppermute | solution.py:330
  3.4 4.0 %collective-permute-start.8 = (bf16[2,64,512]{2,1,0:T(8,128)(2,1)S(1)}, bf16[2,64,512]{2,1,0:T(8,128)(2,1)S(1)}, u32[]{:S(2)}, u32[]{:S(2)}) collective-permute-start(bf16[2,64,512]{2,1,0:T(8,128)(2,1)S(1)} %pad_maximum_fusion.10), channel_id=1, source_target_pairs={{0,12},{1,13},{2,14},{3,15},{4,8},{5,9},{6,10},{7,11},{8,4},{9,5},... | collective-permute-start | bytes 393224 | tf_op jit(solution)/shard_map/ppermute | solution.py:330
  7.4 1.6 %collective-permute-start.7 = (bf16[2,64,512]{2,1,0:T(8,128)(2,1)S(1)}, bf16[2,64,512]{2,1,0:T(8,128)(2,1)S(1)}, u32[]{:S(2)}, u32[]{:S(2)}) collective-permute-start(bf16[2,64,512]{2,1,0:T(8,128)(2,1)S(1)} %pad_maximum_fusion.9), channel_id=1, source_target_pairs={{0,2},{1,3},{2,0},{3,1},{4,6},{5,7},{6,4},{7,5},{8,10},{9,11},{10,... | collective-permute-start | bytes 393224 | tf_op jit(solution)/shard_map/ppermute | solution.py:330
  9.1 2.0 %collective-permute-start.5 = (bf16[2,64,512]{2,1,0:T(8,128)(2,1)S(1)}, bf16[2,64,512]{2,1,0:T(8,128)(2,1)S(1)}, u32[]{:S(2)}, u32[]{:S(2)}) collective-permute-start(bf16[2,64,512]{2,1,0:T(8,128)(2,1)S(1)} %pad_maximum_fusion.6), channel_id=1, source_target_pairs={{0,8},{1,9},{2,10},{3,11},{4,12},{5,13},{6,14},{7,15},{8,0},{9,1},... | collective-permute-start | bytes 393224 | tf_op jit(solution)/shard_map/ppermute | solution.py:330
  11.1 2.5 %collective-permute-start.4 = (bf16[2,64,512]{2,1,0:T(8,128)(2,1)S(1)}, bf16[2,64,512]{2,1,0:T(8,128)(2,1)S(1)}, u32[]{:S(2)}, u32[]{:S(2)}) collective-permute-start(bf16[2,64,512]{2,1,0:T(8,128)(2,1)S(1)} %pad_maximum_fusion.5), channel_id=1, source_target_pairs={{0,6},{1,7},{2,4},{3,5},{4,2},{5,3},{6,0},{7,1},{8,14},{9,15},{10,... | collective-permute-start | bytes 393224 | tf_op jit(solution)/shard_map/ppermute | solution.py:330
  14.1 1.5 %collective-permute-done.7.rest_2_ = bf16[2,64,512]{2,1,0:T(8,128)(2,1)S(1)} collective-permute-done((bf16[2,64,512]{2,1,0:T(8,128)(2,1)S(1)}, bf16[2,64,512]{2,1,0:T(8,128)(2,1)S(1)}, u32[]{:S(2)}, u32[]{:S(2)}) %collective-permute-start.7) | collective-permute-done | bytes 131104 | tf_op jit(solution)/shard_map/ppermute | solution.py:330
  16.2 1.2 %collective-permute-done.6.rest_1_ = bf16[2,64,512]{2,1,0:T(8,128)(2,1)S(1)} collective-permute-done((bf16[2,64,512]{2,1,0:T(8,128)(2,1)S(1)}, bf16[2,64,512]{2,1,0:T(8,128)(2,1)S(1)}, u32[]{:S(2)}, u32[]{:S(2)}) %collective-permute-start.6) | collective-permute-done | bytes 131104 | tf_op jit(solution)/shard_map/ppermute | solution.py:330
  17.3 4.4 %transform.3.rest_4_ = f32[64,1280]{1,0:T(8,128)S(1)} custom-call(s32[1]{0:T(128)} %bitcast.place_ref, bf16[163840,128]{1,0:T(8,128)(2,1)} %constant.100.clone.table_ref, bf16[2,64,512]{2,1,0:T(8,128)(2,1)S(1)} %pad_maximum_fusion.7.rest_0_, bf16[2,64,512]{2,1,0:T(8,128)(2,1)S(1)} %collective-permute-done.6.rest_1_, ...), custom_call_target="tpu_custom_call" | custom-call | flops 671088640 | bytes 10485760 | tf_op jit(solution)/shard_map/transform/pallas_call | solution.py:121
  21.8 3.1 %transform.4 = (f32[32,768]{1,0:T(8,128)S(1)}, f32[32,768]{1,0:T(8,128)S(1)}) custom-call(s32[1]{0:T(128)} %bitcast.place_ref, bf16[163840,128]{1,0:T(8,128)(2,1)} %constant.100.clone.table_ref, bf16[2,64,512]{2,1,0:T(8,128)(2,1)S(1)} %collective-permute-done.2.rest_0_, bf16[2,64,512]{2,1,0:T(8,128)(2,1)S(1)} %collective-permute-done.3.rest_1_, ...), custom_call_target="tpu_custom_call" | custom-call | flops 402653184 | bytes 6291456 | tf_op jit(solution)/shard_map/transform/pallas_call | solution.py:121
  25.0 2.6 %collective-permute-start.9 = (f32[32,768]{1,0:T(8,128)S(1)}, f32[32,768]{1,0:T(8,128)S(1)}, u32[]{:S(2)}, u32[]{:S(2)}) collective-permute-start(f32[32,768]{1,0:T(8,128)S(1)} %get-tuple-element.10), channel_id=1, source_target_pairs={{0,16},{1,17},{2,18},{3,19},{4,20},{5,21},{6,22},{7,23},{8,24},{9,... | collective-permute-start | bytes 294920 | tf_op jit(solution)/shard_map/ppermute | solution.py:330
  27.6 2.4 %transform.5 = (f32[32,512]{1,0:T(8,128)S(1)}, f32[32,512]{1,0:T(8,128)S(1)}) custom-call(s32[1]{0:T(128)} %bitcast.place_ref, bf16[163840,128]{1,0:T(8,128)(2,1)} %constant.100.clone.table_ref, bf16[2,64,512]{2,1,0:T(8,128)(2,1)S(1)} %collective-permute-done.2.rest_0_, bf16[2,64,512]{2,1,0:T(8,128)(2,1)S(1)} %collective-permute-done.3.rest_1_, ...), custom_call_target="tpu_custom_call" | custom-call | flops 268435456 | bytes 4194304 | tf_op jit(solution)/shard_map/transform/pallas_call | solution.py:121
  30.6 1.2 %collective-permute-done = f32[8,4]{1,0:T(8,128)S(1)} collective-permute-done((f32[8,4]{1,0:T(8,128)S(1)}, f32[8,4]{1,0:T(8,128)S(1)}, u32[]{:S(2)}, u32[]{:S(2)}) %collective-permute-start) | collective-permute-done | bytes 160 | tf_op jit(solution)/shard_map/ppermute | solution.py:330
  31.9 4.2 %collective-permute-done.10.rest_3_ = f32[32,512]{1,0:T(8,128)S(1)} collective-permute-done((f32[32,512]{1,0:T(8,128)S(1)}, f32[32,512]{1,0:T(8,128)S(1)}, u32[]{:S(2)}, u32[]{:S(2)}) %collective-permute-start.10) | collective-permute-done | bytes 65568 | tf_op jit(solution)/shard_map/ppermute | solution.py:330
  36.3 2.0 %collective-permute-start.11 = (bf16[32,1280]{1,0:T(8,128)(2,1)S(1)}, bf16[32,1280]{1,0:T(8,128)(2,1)S(1)}, u32[]{:S(2)}, u32[]{:S(2)}) collective-permute-start(bf16[32,1280]{1,0:T(8,128)(2,1)S(1)} %whiten.1), channel_id=1, source_target_pairs={{0,16},{1,17},{2,18},{3,19},{4,20},{5,21},{6,22},{7,23},{8,24},{9,... | collective-permute-start | bytes 245768 | tf_op jit(solution)/shard_map/ppermute | solution.py:330
  38.3 2.3 %collective-permute-start.12 = (bf16[32,1280]{1,0:T(8,128)(2,1)S(1)}, bf16[32,1280]{1,0:T(8,128)(2,1)S(1)}, u32[]{:S(2)}, u32[]{:S(2)}) collective-permute-start(bf16[32,1280]{1,0:T(8,128)(2,1)S(1)} %whiten.1), channel_id=1, source_target_pairs={{0,24},{1,25},{2,26},{3,27},{4,28},{5,29},{6,30},{7,31},{8,16},{9,... | collective-permute-start | bytes 245768 | tf_op jit(solution)/shard_map/ppermute | solution.py:330
  40.7 2.1 %collective-permute-start.22 = (bf16[2,32,1280]{2,1,0:T(8,128)(2,1)S(1)}, bf16[2,32,1280]{2,1,0:T(8,128)(2,1)S(1)}, u32[]{:S(2)}, u32[]{:S(2)}) collective-permute-start(bf16[2,32,1280]{2,1,0:T(8,128)(2,1)S(1)} %pad_maximum_fusion.2), channel_id=1, source_target_pairs={{0,6},{1,7},{2,4},{3,5},{4,2},{5,3},{6,0},{7,1},{8,14},{9,15},{10,... | collective-permute-start | bytes 491528 | tf_op jit(solution)/shard_map/ppermute | solution.py:330
  42.8 2.6 %collective-permute-start.20 = (bf16[2,32,1280]{2,1,0:T(8,128)(2,1)S(1)}, bf16[2,32,1280]{2,1,0:T(8,128)(2,1)S(1)}, u32[]{:S(2)}, u32[]{:S(2)}) collective-permute-start(bf16[2,32,1280]{2,1,0:T(8,128)(2,1)S(1)} %pad_maximum_fusion.2), channel_id=1, source_target_pairs={{0,4},{1,5},{2,6},{3,7},{4,0},{5,1},{6,2},{7,3},{8,12},{9,13},{10,... | collective-permute-start | bytes 491528 | tf_op jit(solution)/shard_map/ppermute | solution.py:330
  47.0 2.0 %collective-permute-start.17 = (bf16[2,32,1280]{2,1,0:T(8,128)(2,1)S(1)}, bf16[2,32,1280]{2,1,0:T(8,128)(2,1)S(1)}, u32[]{:S(2)}, u32[]{:S(2)}) collective-permute-start(bf16[2,32,1280]{2,1,0:T(8,128)(2,1)S(1)} %pad_maximum_fusion.2), channel_id=1, source_target_pairs={{0,2},{1,3},{2,0},{3,1},{4,6},{5,7},{6,4},{7,5},{8,10},{9,11},{10,... | collective-permute-start | bytes 491528 | tf_op jit(solution)/shard_map/ppermute | solution.py:330
  49.1 2.4 %collective-permute-start.15 = (bf16[2,32,1280]{2,1,0:T(8,128)(2,1)S(1)}, bf16[2,32,1280]{2,1,0:T(8,128)(2,1)}, u32[]{:S(2)}, u32[]{:S(2)}) collective-permute-start(bf16[2,32,1280]{2,1,0:T(8,128)(2,1)S(1)} %pad_maximum_fusion.1), channel_id=1, source_target_pairs={{0,2},{1,3},{2,0},{3,1},{4,6},{5,7},{6,4},{7,5},{8,10},{9,11},{10,... | collective-permute-start | bytes 491528 | tf_op jit(solution)/shard_map/ppermute | solution.py:330
  51.5 2.1 %collective-permute-done.23 = bf16[2,32,1280]{2,1,0:T(8,128)(2,1)S(1)} collective-permute-done((bf16[2,32,1280]{2,1,0:T(8,128)(2,1)S(1)}, bf16[2,32,1280]{2,1,0:T(8,128)(2,1)S(1)}, u32[]{:S(2)}, u32[]{:S(2)}) %collective-permute-start.23) | collective-permute-done | bytes 163872 | tf_op jit(solution)/shard_map/ppermute | solution.py:330
  53.6 2.2 %collective-permute-done.19 = bf16[2,32,1280]{2,1,0:T(8,128)(2,1)S(1)} collective-permute-done((bf16[2,32,1280]{2,1,0:T(8,128)(2,1)S(1)}, bf16[2,32,1280]{2,1,0:T(8,128)(2,1)S(1)}, u32[]{:S(2)}, u32[]{:S(2)}) %collective-permute-start.19) | collective-permute-done | bytes 163872 | tf_op jit(solution)/shard_map/ppermute | solution.py:330
  58.3 2.4 %correlate.2.rest_5_ = f32[4,64,1280]{2,1,0:T(8,128)S(1)} custom-call(s32[1]{0:T(128)} %bitcast.place_ref, f32[8,4]{1,0:T(8,128)S(1)} %convert_element_type.3.flags_ref, s32[64,1]{1,0:T(8,128)S(1)} %copy.10.ids_ref, bf16[4,32,1280]{2,1,0:T(8,128)(2,1)S(1)} %pad_maximum_fusion.rest_0_, bf16[2,32,1280]{2,1,0:T(8,128)(2,1)} %collective-permute-done.15.rest_1_, ...), custom_call_target="tpu_custom_call" | custom-call | flops 83886080 | bytes 1310720 | tf_op jit(solution)/shard_map/correlate/pallas_call | solution.py:305
  60.8 4.7 %correlate.3 = f32[64,4,1001]{2,1,0:T(4,128)} custom-call(s32[1]{0:T(128)} %bitcast.place_ref, f32[8,4]{1,0:T(8,128)S(1)} %convert_element_type.3.flags_ref, s32[64,1]{1,0:T(8,128)S(1)} %copy.10.ids_ref, bf16[4,32,1280]{2,1,0:T(8,128)(2,1)} %collective-permute-done.14.rest_0_, bf16[2,32,1280]{2,1,0:T(8,128)(2,1)} %collective-permute-done.16.rest_1_, ...), custom_call_target="tpu_custom_call" | custom-call | flops 83886080 | bytes 1310720 | tf_op jit(solution)/shard_map/correlate/pallas_call | solution.py:305
  (61 shorter events, 6.9 us)
Async XLA Ops:
  1.3 2.1 %collective-permute-start.1 = (bf16[8,64,512]{2,1,0:T(8,128)(2,1)S(1)}, bf16[8,64,512]{2,1,0:T(8,128)(2,1)S(1)}, u32[]{:S(2)}, u32[]{:S(2)}) collective-permute-start(bf16[8,64,512]{2,1,0:T(8,128)(2,1)S(1)} %bitcast.20), channel_id=1, source_target_pairs={{0,1},{1,0},{2,3},{3,2},{4,5},{5,4},{6,7},{7,6},{8,9},{9,8},{10,11... | collective-permute-start | bytes 1572872 | tf_op jit(solution)/shard_map/ppermute | solution.py:330
  3.4 10.2 %collective-permute-start.8 = (bf16[2,64,512]{2,1,0:T(8,128)(2,1)S(1)}, bf16[2,64,512]{2,1,0:T(8,128)(2,1)S(1)}, u32[]{:S(2)}, u32[]{:S(2)}) collective-permute-start(bf16[2,64,512]{2,1,0:T(8,128)(2,1)S(1)} %pad_maximum_fusion.10), channel_id=1, source_target_pairs={{0,12},{1,13},{2,14},{3,15},{4,8},{5,9},{6,10},{7,11},{8,4},{9,5},... | collective-permute-start | bytes 393224 | tf_op jit(solution)/shard_map/ppermute | solution.py:330
  7.4 8.2 %collective-permute-start.7 = (bf16[2,64,512]{2,1,0:T(8,128)(2,1)S(1)}, bf16[2,64,512]{2,1,0:T(8,128)(2,1)S(1)}, u32[]{:S(2)}, u32[]{:S(2)}) collective-permute-start(bf16[2,64,512]{2,1,0:T(8,128)(2,1)S(1)} %pad_maximum_fusion.9), channel_id=1, source_target_pairs={{0,2},{1,3},{2,0},{3,1},{4,6},{5,7},{6,4},{7,5},{8,10},{9,11},{10,... | collective-permute-start | bytes 393224 | tf_op jit(solution)/shard_map/ppermute | solution.py:330
  9.0 8.3 %collective-permute-start.6 = (bf16[2,64,512]{2,1,0:T(8,128)(2,1)S(1)}, bf16[2,64,512]{2,1,0:T(8,128)(2,1)S(1)}, u32[]{:S(2)}, u32[]{:S(2)}) collective-permute-start(bf16[2,64,512]{2,1,0:T(8,128)(2,1)S(1)} %pad_maximum_fusion.8), channel_id=1, source_target_pairs={{0,14},{1,15},{2,12},{3,13},{4,10},{5,11},{6,8},{7,9},{8,6},{9,7},... | collective-permute-start | bytes 393224 | tf_op jit(solution)/shard_map/ppermute | solution.py:330
  9.1 12.7 %collective-permute-start.5 = (bf16[2,64,512]{2,1,0:T(8,128)(2,1)S(1)}, bf16[2,64,512]{2,1,0:T(8,128)(2,1)S(1)}, u32[]{:S(2)}, u32[]{:S(2)}) collective-permute-start(bf16[2,64,512]{2,1,0:T(8,128)(2,1)S(1)} %pad_maximum_fusion.6), channel_id=1, source_target_pairs={{0,8},{1,9},{2,10},{3,11},{4,12},{5,13},{6,14},{7,15},{8,0},{9,1},... | collective-permute-start | bytes 393224 | tf_op jit(solution)/shard_map/ppermute | solution.py:330
  11.1 10.7 %collective-permute-start.4 = (bf16[2,64,512]{2,1,0:T(8,128)(2,1)S(1)}, bf16[2,64,512]{2,1,0:T(8,128)(2,1)S(1)}, u32[]{:S(2)}, u32[]{:S(2)}) collective-permute-start(bf16[2,64,512]{2,1,0:T(8,128)(2,1)S(1)} %pad_maximum_fusion.5), channel_id=1, source_target_pairs={{0,6},{1,7},{2,4},{3,5},{4,2},{5,3},{6,0},{7,1},{8,14},{9,15},{10,... | collective-permute-start | bytes 393224 | tf_op jit(solution)/shard_map/ppermute | solution.py:330
  13.7 8.1 %collective-permute-start.3 = (bf16[2,64,512]{2,1,0:T(8,128)(2,1)S(1)}, bf16[2,64,512]{2,1,0:T(8,128)(2,1)S(1)}, u32[]{:S(2)}, u32[]{:S(2)}) collective-permute-start(bf16[2,64,512]{2,1,0:T(8,128)(2,1)S(1)} %pad_maximum_fusion.4), channel_id=1, source_target_pairs={{0,10},{1,11},{2,8},{3,9},{4,14},{5,15},{6,12},{7,13},{8,2},{9,3},... | collective-permute-start | bytes 393224 | tf_op jit(solution)/shard_map/ppermute | solution.py:330
  15.7 6.1 %collective-permute-start.2 = (bf16[2,64,512]{2,1,0:T(8,128)(2,1)S(1)}, bf16[2,64,512]{2,1,0:T(8,128)(2,1)S(1)}, u32[]{:S(2)}, u32[]{:S(2)}) collective-permute-start(bf16[2,64,512]{2,1,0:T(8,128)(2,1)S(1)} %pad_maximum_fusion.3), channel_id=1, source_target_pairs={{0,4},{1,5},{2,6},{3,7},{4,0},{5,1},{6,2},{7,3},{8,12},{9,13},{10,... | collective-permute-start | bytes 393224 | tf_op jit(solution)/shard_map/ppermute | solution.py:330
  25.0 11.1 %collective-permute-start.9 = (f32[32,768]{1,0:T(8,128)S(1)}, f32[32,768]{1,0:T(8,128)S(1)}, u32[]{:S(2)}, u32[]{:S(2)}) collective-permute-start(f32[32,768]{1,0:T(8,128)S(1)} %get-tuple-element.10), channel_id=1, source_target_pairs={{0,16},{1,17},{2,18},{3,19},{4,20},{5,21},{6,22},{7,23},{8,24},{9,... | collective-permute-start | bytes 294920 | tf_op jit(solution)/shard_map/ppermute | solution.py:330
  30.1 6.0 %collective-permute-start.10 = (f32[32,512]{1,0:T(8,128)S(1)}, f32[32,512]{1,0:T(8,128)S(1)}, u32[]{:S(2)}, u32[]{:S(2)}) collective-permute-start(f32[32,512]{1,0:T(8,128)S(1)} %get-tuple-element.12), channel_id=1, source_target_pairs={{0,16},{1,17},{2,18},{3,19},{4,20},{5,21},{6,22},{7,23},{8,24},{9,... | collective-permute-start | bytes 196616 | tf_op jit(solution)/shard_map/ppermute | solution.py:330
  36.2 4.5 %collective-permute-start.13 = (bf16[32,1280]{1,0:T(8,128)(2,1)S(1)}, bf16[32,1280]{1,0:T(8,128)(2,1)S(1)}, u32[]{:S(2)}, u32[]{:S(2)}) collective-permute-start(bf16[32,1280]{1,0:T(8,128)(2,1)S(1)} %whiten.1), channel_id=1, source_target_pairs={{0,8},{1,9},{2,10},{3,11},{4,12},{5,13},{6,14},{7,15},{8,0},{9,1},... | collective-permute-start | bytes 245768 | tf_op jit(solution)/shard_map/ppermute | solution.py:330
  36.3 9.2 %collective-permute-start.11 = (bf16[32,1280]{1,0:T(8,128)(2,1)S(1)}, bf16[32,1280]{1,0:T(8,128)(2,1)S(1)}, u32[]{:S(2)}, u32[]{:S(2)}) collective-permute-start(bf16[32,1280]{1,0:T(8,128)(2,1)S(1)} %whiten.1), channel_id=1, source_target_pairs={{0,16},{1,17},{2,18},{3,19},{4,20},{5,21},{6,22},{7,23},{8,24},{9,... | collective-permute-start | bytes 245768 | tf_op jit(solution)/shard_map/ppermute | solution.py:330
  38.3 7.1 %collective-permute-start.12 = (bf16[32,1280]{1,0:T(8,128)(2,1)S(1)}, bf16[32,1280]{1,0:T(8,128)(2,1)S(1)}, u32[]{:S(2)}, u32[]{:S(2)}) collective-permute-start(bf16[32,1280]{1,0:T(8,128)(2,1)S(1)} %whiten.1), channel_id=1, source_target_pairs={{0,24},{1,25},{2,26},{3,27},{4,28},{5,29},{6,30},{7,31},{8,16},{9,... | collective-permute-start | bytes 245768 | tf_op jit(solution)/shard_map/ppermute | solution.py:330
  40.7 8.3 %collective-permute-start.22 = (bf16[2,32,1280]{2,1,0:T(8,128)(2,1)S(1)}, bf16[2,32,1280]{2,1,0:T(8,128)(2,1)S(1)}, u32[]{:S(2)}, u32[]{:S(2)}) collective-permute-start(bf16[2,32,1280]{2,1,0:T(8,128)(2,1)S(1)} %pad_maximum_fusion.2), channel_id=1, source_target_pairs={{0,6},{1,7},{2,4},{3,5},{4,2},{5,3},{6,0},{7,1},{8,14},{9,15},{10,... | collective-permute-start | bytes 491528 | tf_op jit(solution)/shard_map/ppermute | solution.py:330
  42.8 13.7 %collective-permute-start.20 = (bf16[2,32,1280]{2,1,0:T(8,128)(2,1)S(1)}, bf16[2,32,1280]{2,1,0:T(8,128)(2,1)S(1)}, u32[]{:S(2)}, u32[]{:S(2)}) collective-permute-start(bf16[2,32,1280]{2,1,0:T(8,128)(2,1)S(1)} %pad_maximum_fusion.2), channel_id=1, source_target_pairs={{0,4},{1,5},{2,6},{3,7},{4,0},{5,1},{6,2},{7,3},{8,12},{9,13},{10,... | collective-permute-start | bytes 491528 | tf_op jit(solution)/shard_map/ppermute | solution.py:330
  45.5 8.1 %collective-permute-start.23 = (bf16[2,32,1280]{2,1,0:T(8,128)(2,1)S(1)}, bf16[2,32,1280]{2,1,0:T(8,128)(2,1)S(1)}, u32[]{:S(2)}, u32[]{:S(2)}) collective-permute-start(bf16[2,32,1280]{2,1,0:T(8,128)(2,1)S(1)} %pad_maximum_fusion.1), channel_id=1, source_target_pairs={{0,6},{1,7},{2,4},{3,5},{4,2},{5,3},{6,0},{7,1},{8,14},{9,15},{10,... | collective-permute-start | bytes 491528 | tf_op jit(solution)/shard_map/ppermute | solution.py:330
  46.4 9.4 %collective-permute-start.19 = (bf16[2,32,1280]{2,1,0:T(8,128)(2,1)S(1)}, bf16[2,32,1280]{2,1,0:T(8,128)(2,1)S(1)}, u32[]{:S(2)}, u32[]{:S(2)}) collective-permute-start(bf16[2,32,1280]{2,1,0:T(8,128)(2,1)S(1)} %pad_maximum_fusion.1), channel_id=1, source_target_pairs={{0,4},{1,5},{2,6},{3,7},{4,0},{5,1},{6,2},{7,3},{8,12},{9,13},{10,... | collective-permute-start | bytes 491528 | tf_op jit(solution)/shard_map/ppermute | solution.py:330
  47.0 10.6 %collective-permute-start.17 = (bf16[2,32,1280]{2,1,0:T(8,128)(2,1)S(1)}, bf16[2,32,1280]{2,1,0:T(8,128)(2,1)S(1)}, u32[]{:S(2)}, u32[]{:S(2)}) collective-permute-start(bf16[2,32,1280]{2,1,0:T(8,128)(2,1)S(1)} %pad_maximum_fusion.2), channel_id=1, source_target_pairs={{0,2},{1,3},{2,0},{3,1},{4,6},{5,7},{6,4},{7,5},{8,10},{9,11},{10,... | collective-permute-start | bytes 491528 | tf_op jit(solution)/shard_map/ppermute | solution.py:330
  49.1 8.9 %collective-permute-start.15 = (bf16[2,32,1280]{2,1,0:T(8,128)(2,1)S(1)}, bf16[2,32,1280]{2,1,0:T(8,128)(2,1)}, u32[]{:S(2)}, u32[]{:S(2)}) collective-permute-start(bf16[2,32,1280]{2,1,0:T(8,128)(2,1)S(1)} %pad_maximum_fusion.1), channel_id=1, source_target_pairs={{0,2},{1,3},{2,0},{3,1},{4,6},{5,7},{6,4},{7,5},{8,10},{9,11},{10,... | collective-permute-start | bytes 491528 | tf_op jit(solution)/shard_map/ppermute | solution.py:330
  53.6 7.1 %collective-permute-start.14 = (bf16[4,32,1280]{2,1,0:T(8,128)(2,1)S(1)}, bf16[4,32,1280]{2,1,0:T(8,128)(2,1)}, u32[]{:S(2)}, u32[]{:S(2)}) collective-permute-start(bf16[4,32,1280]{2,1,0:T(8,128)(2,1)S(1)} %pad_maximum_fusion.rest_0_), channel_id=1, source_target_pairs={{0,1},{1,0},{2,3},{3,2},{4,5},{5,4},{6,7},{7,6},{8,9},{9,8},{10,11... | collective-permute-start | bytes 983048 | tf_op jit(solution)/shard_map/ppermute | solution.py:330
  55.8 4.9 %collective-permute-start.24 = (bf16[4,32,1280]{2,1,0:T(8,128)(2,1)S(1)}, bf16[4,32,1280]{2,1,0:T(8,128)(2,1)}, u32[]{:S(2)}, u32[]{:S(2)}) collective-permute-start(bf16[4,32,1280]{2,1,0:T(8,128)(2,1)S(1)} %constant_dynamic-update-slice_fusion.2.rest_4_), channel_id=1, source_target_pairs={{0,1},{1,0},{2,3},{3,2},{4,5},{5,4},{6,7},{7,6},{8,9},{9,8},{10,11... | collective-permute-start | bytes 983048 | tf_op jit(solution)/shard_map/ppermute | solution.py:330
  57.2 3.6 %collective-permute-start.21 = (bf16[4,32,1280]{2,1,0:T(8,128)(2,1)}, bf16[4,32,1280]{2,1,0:T(8,128)(2,1)}, u32[]{:S(2)}, u32[]{:S(2)}) collective-permute-start(bf16[4,32,1280]{2,1,0:T(8,128)(2,1)} %constant_dynamic-update-slice_fusion.rest_3_), channel_id=1, source_target_pairs={{0,1},{1,0},{2,3},{3,2},{4,5},{5,4},{6,7},{7,6},{8,9},{9,8},{10,11... | collective-permute-start | bytes 983048 | tf_op jit(solution)/shard_map/ppermute | solution.py:330
  57.7 3.0 %collective-permute-start.18 = (bf16[2,32,1280]{2,1,0:T(8,128)(2,1)S(1)}, bf16[2,32,1280]{2,1,0:T(8,128)(2,1)}, u32[]{:S(2)}, u32[]{:S(2)}) collective-permute-start(bf16[2,32,1280]{2,1,0:T(8,128)(2,1)S(1)} %collective-permute-done.17.rest_2_), channel_id=1, source_target_pairs={{0,1},{1,0},{2,3},{3,2},{4,5},{5,4},{6,7},{7,6},{8,9},{9,8},{10,11... | collective-permute-start | bytes 491528 | tf_op jit(solution)/shard_map/ppermute | solution.py:330
  58.0 2.7 %collective-permute-start.16 = (bf16[2,32,1280]{2,1,0:T(8,128)(2,1)}, bf16[2,32,1280]{2,1,0:T(8,128)(2,1)}, u32[]{:S(2)}, u32[]{:S(2)}) collective-permute-start(bf16[2,32,1280]{2,1,0:T(8,128)(2,1)} %collective-permute-done.15.rest_1_), channel_id=1, source_target_pairs={{0,1},{1,0},{2,3},{3,2},{4,5},{5,4},{6,7},{7,6},{8,9},{9,8},{10,11... | collective-permute-start | bytes 491528 | tf_op jit(solution)/shard_map/ppermute | solution.py:330
  (4 other events, 54.9 us)
